TPU v7x, 128 devices: a whole 4x4x4 slice. The times are simulated.
128 devices in a mesh: img: 8 (over z, x_lo), txt: 16 (over x_hi, y, core).
Axes of the slice: x: 4 (x_hi: 2, x_lo: 2; x = x_hi * 2 + x_lo), y: 4, z: 4, core: 2. Of those that a mesh axis runs over, the one named last changes fastest.
Arguments:
- image_feat: bfloat16 [16384, 1152], P(('img', 'txt')), may hold values from -6 to 6
- text_feat: bfloat16 [16384, 1152], P(('img', 'txt')), may hold values from -6 to 6
- image_head: bfloat16 [1152, 1152], replicated, may hold values from -0.1875 to 0.1875
- text_head: bfloat16 [1152, 1152], replicated, may hold values from -0.1875 to 0.1875
- group_bias: float32 [32], replicated, may hold values from -6 to -4
- text_lang: int32 [16384], P(('img', 'txt')), may hold values from 0 to 31
- partner: int32 [16384], P(('img', 'txt')), may hold values from 0 to 16383, each once
Outputs:
- image_grad: float32 [16384, 1152], P(('img', 'txt'))
- text_grad: float32 [16384, 1152], P(('img', 'txt'))
- image_head_grad: float32 [1152, 1152], P(('img', 'txt'))
- text_head_grad: float32 [1152, 1152], P(('img', 'txt'))
Inputs may be any that keep to these rules, and one draw needn't show every extreme that they name: partner names every image exactly once.
All inputs are finite; a program needn't handle non-finite values.
Results may differ from a plain program's by a relative error of at most 0.02.
Values may be sent and summed in bfloat16 or wider, within the bound.
No kernel may reach another device: no remote copies, remote signals or barrier semaphores. Data moves between devices by JAX's collectives and lax.ppermute only.
A program may use at most 128 MiB of HBM per device.

v0:
```python
import jax
import jax.numpy as jnp
from jax import lax
from jax.experimental import pallas as pl
from jax.experimental.pallas import tpu as pltpu
from jax.sharding import PartitionSpec as P

logit_scale = 64.0
epsilon = 1e-06
log2e = 1.4426950408889634
f32, b16 = jnp.float32, jnp.bfloat16

DEV = "dev"
PLACES = [
    (z, lo, hi, y, c)
    for z in range(4)
    for lo in range(2)
    for hi in range(2)
    for y in range(4)
    for c in range(2)
]


def flat(z, lo, hi, y, c):
    return (z * 2 + lo) * 16 + hi * 8 + y * 2 + c


def img_move(d, e):
    return lambda z, lo, hi, y, c: ((z + d) % 4, lo ^ e, hi, y, c)


def txt_move(d, e):
    return lambda z, lo, hi, y, c: (z, lo ^ e, hi ^ e, (y + d) % 4, c)


def core_move(z, lo, hi, y, c):
    return (z, lo, hi, y, 1 - c)


IMG_GROUPS = [
    [flat(z, lo, hi, y, c) for z in range(4) for lo in range(2)]
    for hi in range(2)
    for y in range(4)
    for c in range(2)
]
TXT_GROUPS = [
    [flat(z, hi ^ b, hi, y, c) for y in range(4) for hi in range(2)]
    for z in range(4)
    for b in range(2)
    for c in range(2)
]
TXT_CORE_GROUPS = [
    [flat(z, hi ^ b, hi, y, c) for c in range(2) for y in range(4) for hi in range(2)]
    for z in range(4)
    for b in range(2)
]
CHIP_GROUPS = [[flat(*p) for p in PLACES if p[4] == c] for c in range(2)]


def send(block, move):
    return lax.ppermute(block, DEV, [(flat(*p), flat(*move(*p))) for p in PLACES])


def exchange(blocks, groups):
    return lax.all_to_all(blocks, DEV, 0, 0, axis_index_groups=groups, tiled=True)


PAD = 16
NN = (((1,), (0,)), ((), ()))
NT = (((1,), (1,)), ((), ()))
TN = (((0,), (0,)), ((), ()))


def dot(a, b, dims):
    return lax.dot_general(a, b, dims, preferred_element_type=f32)


def call(body, out_shape, scalars, arrays, in_specs=None, out_specs=None, grid=(), scratch=(), cost=0, aliases=None):
    whole = pl.BlockSpec(memory_space=pltpu.VMEM)
    many = isinstance(out_shape, (list, tuple))
    if in_specs is None:
        in_specs = [whole] * len(arrays)
    if out_specs is None:
        out_specs = [whole] * len(out_shape) if many else whole
    spec = pltpu.PrefetchScalarGridSpec(
        num_scalar_prefetch=1,
        grid=grid,
        in_specs=in_specs,
        out_specs=out_specs,
        scratch_shapes=list(scratch),
    )
    moved = sum(a.size * a.dtype.itemsize for a in arrays)
    return pl.pallas_call(
        body,
        out_shape=out_shape,
        grid_spec=spec,
        input_output_aliases=aliases or {},
        compiler_params=pltpu.CompilerParams(vmem_limit_bytes=60 * 2**20),
        cost_estimate=pl.CostEstimate(flops=cost, bytes_accessed=moved, transcendentals=0),
    )(jnp.stack(scalars).astype(jnp.int32), *arrays)


def aligned(index, size):
    return pl.ds(pl.multiple_of(index * size, size), size)


def split_rows(total, lanes):
    high = total.astype(b16).astype(f32)
    row = lax.broadcasted_iota(jnp.int32, (PAD, lanes), 0)
    return jnp.where(row == 0, high, jnp.where(row == 1, total - high, 0.0)).astype(b16)


def joined(rows):
    return rows[0:1].astype(f32) + rows[1:2].astype(f32)


def in_pair(own, across, second, rows):
    own, across = own[:rows], across[:rows]
    first = second == 0
    return jnp.concatenate([jnp.where(first, own, across), jnp.where(first, across, own)], axis=0)


def unit_kernel(rows, extra, pairs, at_ref, *refs):
    blocks, refs = refs[: 2 * pairs], refs[2 * pairs :]
    turned_head, head = refs[0], refs[1]
    (feats, proj), outs = refs[-2:], refs[-5:-2]
    width = turned_head.shape[0]
    quarter = width // 4
    second = at_ref[0]
    step = pl.program_id(0)
    for p in range(pairs):
        own, across = blocks[2 * p], blocks[2 * p + 1]

        @pl.when(step == p)
        def _():
            feats[...] = in_pair(own, across, second, rows)
            if extra:
                first = second == 0
                sides = own[rows:, :rows], across[rows:, :rows]
                outs[2][0, width:, :rows] = jnp.where(first, sides[0], sides[1])
                outs[2][0, width:, rows:] = jnp.where(first, sides[1], sides[0])

    total = jnp.zeros((1, 2 * rows), f32)
    for m in range(4):
        span = slice(m * quarter, (m + 1) * quarter)
        part = dot(turned_head[span], feats[...], NT)
        proj[span] = part
        total = total + jnp.sum(part * part, axis=0, keepdims=True)
    length = jnp.sqrt(total + epsilon)
    outs[1][...] = length
    inverse = 1.0 / length
    for m in range(4):
        span = slice(m * quarter, (m + 1) * quarter)
        unit = (proj[span] * inverse).astype(b16)
        outs[0][span] = unit
        if extra:
            outs[2][0, span] = unit
    if extra:
        outs[0][width:] = outs[2][0, width:]
    else:
        part = dot(feats[...], head[...], NN)
        total = jnp.sum(part * part, axis=1, keepdims=True)
        outs[2][...] = (part * (1.0 / jnp.sqrt(total + epsilon))).astype(b16)


def units(pairs, heads, second, places, rows, extra, carried):
    width = heads[0].shape[0]
    tile = 2 * rows
    whole = lambda a: pl.BlockSpec(a.shape, lambda i, at: (0, 0))
    out = [
        jax.ShapeDtypeStruct((width + extra, 8 * rows), b16),
        jax.ShapeDtypeStruct((1, 8 * rows), f32),
    ]
    steps = [
        pl.BlockSpec((width + extra, tile), lambda i, at: (0, at[1 + i])),
        pl.BlockSpec((1, tile), lambda i, at: (0, at[1 + i])),
    ]
    if extra:
        out.append(jax.ShapeDtypeStruct((len(pairs), width + extra, tile), b16))
        steps.append(pl.BlockSpec((1, width + extra, tile), lambda i, at: (i, 0, 0)))
        heads = [heads[0], heads[0]]
    else:
        out.append(jax.ShapeDtypeStruct((8 * rows, width), b16))
        steps.append(pl.BlockSpec((tile, width), lambda i, at: (at[1 + i], 0)))
    last = pl.BlockSpec(memory_space=pl.ANY) if extra else whole(heads[1])
    blocks = [block for pair in pairs for block in pair]
    return call(
        lambda *refs: unit_kernel(rows, extra, len(pairs), *refs),
        out,
        [second, *places],
        [*blocks, *heads, *carried],
        in_specs=[whole(a) for a in [*blocks, heads[0]]]
        + [last]
        + [pl.BlockSpec(memory_space=pl.ANY)] * len(carried),
        out_specs=steps,
        grid=(len(pairs),),
        scratch=[pltpu.VMEM((tile, width), b16), pltpu.VMEM((width, tile), f32)],
        cost=2 * tile * width * width * len(pairs) * (1 if extra else 2),
        aliases={len(blocks) + 3 + n: n for n in range(len(carried))},
    )


def ring_order(near, far):
    return [near.at[0], near.at[1], far.at[0], near.at[2]]


def tile_slopes(rows, groups, place, bias_ref, img, txt, slopes, by_img):
    width = img.shape[1]
    tile = 2 * rows
    lang = txt[width : width + PAD].astype(f32)
    partner = lang[1:2] * 128.0 + lang[2:3]
    lang = lang[0:1]
    bias = jnp.zeros((1, tile), f32)
    for g in range(groups):
        bias = jnp.where(lang == g, bias_ref[g], bias)
    bias = bias * -log2e
    down = jnp.zeros((1, tile), f32)
    high = 4 * rows
    for m in range(img.shape[0] // high):
        span = slice(m * high, (m + 1) * high)
        index = m * high + lax.broadcasted_iota(jnp.int32, (high, 1), 0)
        ids = ((index // rows * 16 + place) * rows + index % rows).astype(f32)
        cosines = dot(img[span], txt[:width], NN)
        below = 1.0 + jnp.exp2(cosines * (-log2e * logit_scale) + bias)
        gate = pl.reciprocal(below, approx=True)
        gate = gate * (2.0 - below * gate)
        slope = gate - jnp.where(partner == ids, 1.0, 0.0)
        slopes[span, :tile] = slope.astype(b16)
        weighted = slope * cosines
        down = down + jnp.sum(weighted, axis=0, keepdims=True)
        side = by_img[span]
        for k in range(0, tile, by_img.shape[1]):
            side = side + weighted[:, k : k + by_img.shape[1]]
        by_img[span] = side
    return logit_scale * down


def put_text_terms(up, turned, slopes, down):
    slab = turned.shape[0] // 8
    figures = split_rows(down, up.shape[1])
    part = dot(turned[...], slopes, NN)
    for e in range(8):
        at = e * (slab + PAD)
        up[at : at + slab] = part[e * slab : (e + 1) * slab].astype(b16)
        up[at + slab : at + slab + PAD] = figures


def other_kernel(rows, groups, at_ref, bias_ref, img, turned, *refs):
    chunks, (slopes, img_sum, up, by_img, held, txt) = ring_order(*refs[:2]), refs[2:]
    step = pl.program_id(0)

    @pl.when(step == 0)
    def _():
        by_img[...] = jnp.zeros(by_img.shape, f32)

    for d in range(4):

        @pl.when(step == d)
        def _():
            txt[...] = chunks[d][...]

    down = tile_slopes(rows, groups, at_ref[0], bias_ref, img, txt, held, by_img)
    slopes[0] = held[...]
    put_text_terms(up, turned, held[...], down)

    @pl.when(step == 3)
    def _():
        img_sum[...] = logit_scale * jnp.sum(by_img[...].T, axis=0, keepdims=True)


def other_tile(img, turned, chunks, group_bias, place, ring, rows):
    count, width = img.shape
    tile = 2 * rows
    height = width + 8 * PAD
    whole = lambda a: pl.BlockSpec(a.shape, lambda i, at: (0, 0))
    stack = lambda a: pl.BlockSpec(a.shape, lambda i, at: (0, 0, 0))
    return call(
        lambda *refs: other_kernel(rows, group_bias.shape[0], *refs),
        [
            jax.ShapeDtypeStruct((4, count, tile), b16),
            jax.ShapeDtypeStruct((1, count), f32),
            jax.ShapeDtypeStruct((height, count), b16),
        ],
        [place, ring],
        [group_bias, img, turned, *chunks],
        in_specs=[pl.BlockSpec(memory_space=pltpu.SMEM), whole(img), whole(turned)]
        + [stack(chunk) for chunk in chunks],
        out_specs=[
            pl.BlockSpec((1, count, tile), lambda i, at: (i, 0, 0)),
            pl.BlockSpec((1, count), lambda i, at: (0, 0)),
            pl.BlockSpec((height, tile), lambda i, at: (0, (at[1] + i) % 4)),
        ],
        grid=(4,),
        scratch=[
            pltpu.VMEM((count, min(128, tile)), f32),
            pltpu.VMEM((count, tile), b16),
            pltpu.VMEM((width + PAD, tile), b16),
        ],
        cost=4 * width * count * count,
    )


def own_kernel(rows, groups, at_ref, bias_ref, img, turned, txt, *refs):
    chunks = ring_order(*refs[:2])
    other_slopes, other_sum, up = refs[2:5]
    outs, (by_img, held, both, total) = refs[5:13], refs[13:]
    step = pl.program_id(0)
    width = img.shape[1]
    tile = 2 * rows

    @pl.when(step == 0)
    def _():
        by_img[...] = jnp.zeros(by_img.shape, f32)
        total[...] = jnp.zeros(total.shape, f32)

    for d in range(4):

        @pl.when(step == d)
        def _():
            both[:, tile:] = chunks[d][:width]

    held[:, tile:] = other_slopes[0]
    both[:, :tile] = txt[:width]
    down = tile_slopes(rows, groups, at_ref[0], bias_ref, img, txt, held, by_img)
    put_text_terms(up, turned, held[:, :tile], down)
    total[...] += dot(both[...], held[...], NT)

    @pl.when(step == 3)
    def _():
        slab = width // 8
        sums = logit_scale * jnp.sum(by_img[...].T, axis=0, keepdims=True) + other_sum[...]
        figures = split_rows(sums, sums.shape[1])
        own = at_ref[2] == 0
        for d in range(4):
            at = pl.multiple_of((at_ref[1] + d) % 4 * (2 * slab), 2 * slab)
            low, high = total[pl.ds(at, slab)], total[pl.ds(at + slab, slab)]
            outs[2 * d][:slab] = jnp.where(own, low, high).astype(b16)
            outs[2 * d][slab:] = figures
            outs[2 * d + 1][:slab] = jnp.where(own, high, low).astype(b16)
            outs[2 * d + 1][slab:] = figures


def own_tile(
    img, turned, txt, chunks, other_slopes, other_sum, group_bias, place, ring, second, rows
):
    count, width = img.shape
    tile = 2 * rows
    height = width + 8 * PAD
    slab = width // 8
    whole = lambda a: pl.BlockSpec(a.shape, lambda i, at: (0, 0))
    stack = lambda a: pl.BlockSpec(a.shape, lambda i, at: (0, 0, 0))
    piece = jax.ShapeDtypeStruct((slab + PAD, count), b16)
    out = call(
        lambda *refs: own_kernel(rows, group_bias.shape[0], *refs),
        [jax.ShapeDtypeStruct((height, count), b16)] + [piece] * 8,
        [place, ring, second],
        [group_bias, img, turned, txt, *chunks, other_slopes, other_sum],
        in_specs=[
            pl.BlockSpec(memory_space=pltpu.SMEM),
            whole(img),
            whole(turned),
            pl.BlockSpec((width + PAD, tile), lambda i, at: (0, i)),
        ]
        + [stack(chunk) for chunk in chunks]
        + [pl.BlockSpec((1, count, tile), lambda i, at: (i, 0, 0)), whole(other_sum)],
        out_specs=[pl.BlockSpec((height, tile), lambda i, at: (0, i))] + [whole(piece)] * 8,
        grid=(4,),
        scratch=[
            pltpu.VMEM((count, min(128, tile)), f32),
            pltpu.VMEM((count, 2 * tile), b16),
            pltpu.VMEM((width, 2 * tile), b16),
            pltpu.VMEM((width, count), f32),
        ],
        cost=8 * width * count * count,
    )
    return out[0], out[1:]


def sum_into(out, terms):
    slab = out.shape[0] - PAD
    block, total = terms[0][:slab].astype(f32), joined(terms[0][slab:])
    for term in terms[1:]:
        block, total = block + term[:slab].astype(f32), total + joined(term[slab:])
    out[:slab] = block.astype(b16)
    out[slab:] = split_rows(total, out.shape[1])


def sum_kernel(sizes, at_ref, *refs):
    start = 0
    for size, out in zip(sizes, refs[sum(sizes) :]):
        sum_into(out, refs[start : start + size])
        start += size


def sums(groups, rows):
    flat_terms = [term for group in groups for term in group]
    arrays, specs, places = [], [], [jnp.int32(0)]
    height = None
    for term in flat_terms:
        if isinstance(term, tuple):
            arrays.append(term[0])
            height = term[0].shape[0] // 8
            specs.append(
                pl.BlockSpec((height, 4 * rows), lambda i, at, n=len(places): (at[n], i))
            )
            places.append(term[1])
        else:
            arrays.append(term)
            height = term.shape[0]
            specs.append(pl.BlockSpec((height, 4 * rows), lambda i, at: (0, i)))
    count = arrays[0].shape[1]
    spec = pl.BlockSpec((height, 4 * rows), lambda i, at: (0, i))
    return call(
        lambda *refs: sum_kernel([len(group) for group in groups], *refs),
        [jax.ShapeDtypeStruct((height, count), b16)] * len(groups),
        places,
        arrays,
        in_specs=specs,
        out_specs=[spec] * len(groups),
        grid=(count // (4 * rows),),
    )


def grad_kernel(rows, sizes, at_ref, *refs):
    part, grad = refs[-2:]
    outs = refs[-6:-2]
    start = 0
    for n in range(2):
        mine = refs[start : start + sizes[n] + 10]
        start += sizes[n] + 10
        terms, mine = mine[: sizes[n]], mine[sizes[n] :]
        unit, norm, blocks = mine[0], mine[1], mine[2:]
        ring_at, second = at_ref[4 * n], at_ref[4 * n + 1]
        slab = unit.shape[0]
        up, inner = terms[0][:slab].astype(f32), joined(terms[0][slab:])
        for term in terms[1:]:
            up, inner = up + term[:slab].astype(f32), inner + joined(term[slab:])
        up = logit_scale * up - unit[...].astype(f32) * inner
        grad[n] = (up * (1.0 / norm[...])).astype(b16)
        own, give = outs[2 * n : 2 * n + 2]
        for ring in range(4):
            low = grad[n, :, (2 * ring) * rows : (2 * ring + 1) * rows]
            high = grad[n, :, (2 * ring + 1) * rows : (2 * ring + 2) * rows]
            own[ring] = jnp.where(second == 0, low, high)
            give[ring] = jnp.where(second == 0, high, low)
        total = None
        for d in range(4):
            cols = grad[n, :, aligned((ring_at + d) % 4, 2 * rows)]
            term = dot(cols, in_pair(blocks[2 * d], blocks[2 * d + 1], second, rows), NN)
            total = term if total is None else total + term
        part[n * slab : (n + 1) * slab] = total.astype(b16)


def gradients(towers, rows):
    arrays, specs, scalars = [], [], []
    whole = lambda a: pl.BlockSpec(a.shape, lambda i, at: (0,) * len(a.shape))
    for n, (ring, second, place, terms, unit, norm, blocks) in enumerate(towers):
        width = blocks[0].shape[1]
        slab, count = width // 8, 8 * rows
        mine = lambda height, n=n: pl.BlockSpec((height, count), lambda i, at: (at[4 * n + 2], 0))
        for term in terms:
            arrays.append(term[0] if isinstance(term, tuple) else term)
            specs.append(mine(slab + PAD) if isinstance(term, tuple) else whole(term))
        arrays += [unit, norm, *blocks]
        specs += [mine(slab), whole(norm)] + [whole(a) for a in blocks]
        scalars += [ring, second, place, place]
    block = jax.ShapeDtypeStruct((4, slab, rows), b16)
    term = jax.ShapeDtypeStruct((2 * slab, width), b16)
    return call(
        lambda *refs: grad_kernel(rows, [len(tower[3]) for tower in towers], *refs),
        [block] * 4 + [term],
        scalars,
        arrays,
        in_specs=specs,
        out_specs=[whole(block)] * 4 + [whole(term)],
        grid=(1,),
        scratch=[pltpu.VMEM((2, slab, count), b16)],
        cost=4 * slab * count * width,
    )


def pick_kernel(at_ref, mine, theirs, out):
    width = mine.shape[1]
    slots = out.shape[0]
    own = width // 128
    third = mine.shape[0] // 3
    part = (mine[...].astype(f32) + theirs[...].astype(f32)).astype(b16)
    slot = lax.broadcasted_iota(jnp.int32, (slots, 1), 0)
    feature = lax.broadcasted_iota(jnp.int32, (slots, width), 1)
    base = (slot // 8 * 2 + at_ref[0]) * own
    chosen = jnp.where(feature == base + slot % 8, 1.0, 0.0).astype(b16)
    out[:, : 3 * third] = dot(chosen, part, NT).astype(b16)
    chosen = jnp.where(feature == base + 8, 1.0, 0.0).astype(b16)
    ninth = dot(chosen, part, NT)
    pick = slot % 8
    rest = jnp.where(pick == 1, ninth[:, third : 2 * third], ninth[:, :third])
    rest = jnp.where(pick == 2, ninth[:, 2 * third :], rest)
    out[:, 3 * third :] = rest.astype(b16)


def picked(core, mine, theirs):
    both, width = mine.shape
    return call(
        pick_kernel,
        jax.ShapeDtypeStruct((64 * 8, both * 4 // 3), b16),
        [core],
        [mine, theirs],
        cost=4 * 512 * width * both,
    )


def head_kernel(at_ref, got, img_out, txt_out):
    slab = img_out.shape[1] // 8
    third = slab * 2 // 3
    half = third // 2
    for p in range(8):
        img = txt = None
        for other in range(8):
            z, lo, hi, y = p // 2, p % 2, other // 4, other % 4
            block = got[(z * 2 + lo) * 8 + hi * 4 + y].astype(f32)
            img = block if img is None else img + block
            z, lo, hi, y = other // 2, other % 2, p % 2, p // 2
            block = got[(z * 2 + lo) * 8 + hi * 4 + y].astype(f32)
            txt = block if txt is None else txt + block
        at = p * slab
        ninth = 2 * slab
        img_out[0:8, at : at + slab] = img[:, :slab]
        img_out[8:9, at : at + third] = img[0:1, ninth : ninth + third]
        img_out[8:9, at + third : at + slab] = img[1:2, ninth : ninth + half]
        txt_out[0:8, at : at + slab] = txt[:, slab : 2 * slab]
        txt_out[8:9, at : at + half] = txt[1:2, ninth + half : ninth + third]
        txt_out[8:9, at + half : at + slab] = txt[2:3, ninth : ninth + third]


def together(arrays):
    return lax.optimization_barrier(list(arrays))


def pair_lines(own, got, second):
    return jnp.concatenate([jnp.where(second, got, own), jnp.where(second, own, got)], axis=1)


def whole_columns(lines, move, ring):
    got = []
    for d in range(4):
        block = lax.dynamic_index_in_dim(lines, (ring + d) % 4, 0, keepdims=False)
        got.append(send(block, move(d, 0)) if d else block)
    return jnp.concatenate([got[-d % 4] for d in range(4)], axis=0)


def from_ring(turned_head, ring):
    start = ring * (turned_head.shape[0] // 4)
    return lax.dynamic_slice_in_dim(
        jnp.concatenate([turned_head, turned_head]), start, turned_head.shape[0], axis=0
    )


def shards(image_feat, text_feat, image_head, text_head, group_bias, text_lang, partner):
    rows, width = image_feat.shape
    slab = width // 8
    place = lax.axis_index(DEV)
    z, lo, hi, y, core = place // 32, place // 16 % 2, place // 8 % 2, place // 2 % 4, place % 2

    figures = jnp.stack([text_lang, partner // 128, partner % 128]).astype(b16)
    figures = jnp.pad(figures, ((0, PAD - 3), (0, width - rows)))
    text_rows = jnp.concatenate([text_feat, figures], axis=0)
    moves = (img_move, txt_move)
    own = (image_feat, text_rows)
    across = [send(own[n], moves[n](0, 1)) for n in range(2)]
    before = [send(own[n], moves[n](1, 0)) for n in range(2)]
    after = [send(own[n], moves[n](3, 0)) for n in range(2)]
    *across, turned_txt = together(across + [text_head.T])
    across_after = [send(across[n], moves[n](3, 0)) for n in range(2)]
    across_before = [send(across[n], moves[n](1, 0)) for n in range(2)]
    *got, turned_img = together(across_after + before + after + across + [image_head.T])
    across_after, before, after, across = [got[2 * n : 2 * n + 2] for n in range(4)]
    far = [send(before[n], moves[n](1, 0)) for n in range(2)]
    across_far = [send(across_after[n], moves[n](3, 0)) for n in range(2)]
    pairs = [
        [(own[n], across[n]), (after[n], across_after[n]), (before[n], across_before[n])]
        for n in range(2)
    ]
    near_y, near_z = ([(ring + d) % 4 for d in (0, 1, 3)] for ring in (y, z))
    far_y, far_z = [(y + 2) % 4], [(z + 2) % 4]
    img_heads = [turned_img, image_head]
    *txt_made, chunks = units(pairs[1], [turned_txt], hi, near_y, rows, PAD, ())
    others = [send(chunks, core_move)]
    img_made = units(pairs[0], img_heads, lo, near_z, rows, 0, ())
    got = together(far + across_far + list(img_made))
    far, across_far, img_made = got[0:2], got[2:4], got[4:]
    unit_txt, norm_txt, chunks = units(
        [(far[1], across_far[1])], [turned_txt], hi, far_y, rows, PAD, txt_made
    )
    others.append(send(chunks, core_move))
    turned_units, norm_img, unit_img = units(
        [(far[0], across_far[0])], img_heads, lo, far_z, rows, 0, img_made
    )
    blocks = [
        [
            own[n], across[n], after[n], across_after[n],
            far[n], across_far[n], before[n], across_before[n],
        ]
        for n in range(2)
    ]

    other_slopes, other_sum, other_up = other_tile(
        unit_img, turned_units, others, group_bias, place % 16, y, rows
    )
    back = send(other_up, core_move)
    text_up, img_terms = own_tile(
        unit_img, turned_units, unit_txt, others, other_slopes, other_sum, group_bias,
        place % 16, z, lo, rows,
    )

    def txt_slab(d, e):
        at = (y + d) % 4 * 2 + (hi + e) % 2
        return [(text_up, at), (back, at)]

    def img_slab(d, e):
        return [img_terms[2 * d + e]]

    slabs = (img_slab, txt_slab)
    txt_far, txt_across_far, txt_across_after = sums(
        [txt_slab(2, 0), txt_slab(2, 1), txt_slab(1, 1)], rows
    )
    far = [send(img_terms[4], img_move(1, 0)), send(txt_far, txt_move(1, 0))]
    across_far = [send(img_terms[5], img_move(3, 0)), send(txt_across_far, txt_move(3, 0))]
    got = together(far + across_far + [img_terms[3], txt_across_after])
    far, across_far = got[0:2], got[2:4]
    across_before = [send(got[4 + n], moves[n](1, 0)) for n in range(2)]
    joint = sums(
        [slabs[n](3, 1) + [across_far[n]] for n in range(2)]
        + [slabs[n](1, 0) + [far[n]] for n in range(2)]
        + [txt_slab(3, 0)],
        rows,
    )
    across_after = [send(joint[n], moves[n](3, 0)) for n in range(2)]
    got = together(across_before + across_after + [*joint[2:], img_terms[6]])
    across_before, across_after = got[0:2], got[2:4]
    before = [send(got[4 + n], moves[n](1, 0)) for n in range(2)]
    after = [send(got[7], img_move(3, 0)), send(got[6], txt_move(3, 0))]
    joint = sums([slabs[n](0, 1) + [across_before[n], across_after[n]] for n in range(2)], rows)
    across = [send(joint[n], moves[n](0, 1)) for n in range(2)]
    final = [slabs[n](0, 0) + [before[n], after[n], across[n]] for n in range(2)]

    img_own, img_give, txt_own, txt_give, part = gradients(
        [
            (z, lo, z * 2 + lo, final[0], turned_units, norm_img, blocks[0]),
            (y, hi, y * 2 + hi, final[1], unit_txt, norm_txt, blocks[1]),
        ],
        rows,
    )
    img_got = send(img_give, img_move(0, 1))
    txt_got = send(txt_give, txt_move(0, 1))
    heads, img_got, txt_got = together([picked(core, part, send(part, core_move)), img_got, txt_got])
    heads = exchange(heads.reshape(64, 8, -1), CHIP_GROUPS)
    head_shape = jax.ShapeDtypeStruct((width // 128, width), f32)
    image_head_grad, text_head_grad = call(head_kernel, [head_shape] * 2, [core], [heads])

    grad_img = whole_columns(pair_lines(img_own, img_got, lo), img_move, z)
    image_grad = dot(grad_img, from_ring(turned_img, z), TN)
    grad_txt = whole_columns(pair_lines(txt_own, txt_got, hi), txt_move, y)
    text_grad = dot(grad_txt, from_ring(turned_txt, y), TN)
    return (image_grad, text_grad, image_head_grad, text_head_grad)


def solution(mesh):
    line = jax.sharding.Mesh(mesh.devices.reshape(-1), (DEV,))
    in_specs = (P(DEV, None), P(DEV, None), P(), P(), P(), P(DEV), P(DEV))
    return jax.shard_map(
        shards, mesh=line, in_specs=in_specs, out_specs=(P(DEV, None),) * 4, check_vma=False
    )
```

profile of v0, /device:TPU:1, one launch (start us, length us, event | category | flops | bytes accessed | tf_op | source)
XLA Modules:
  0.0 209.8 jit_solution(6018543509063717226)
XLA Ops:
  2.4 3.4 %collective-permute-start.1 = (bf16[144,1152]{1,0:T(8,128)(2,1)S(1)}, bf16[144,1152]{1,0:T(8,128)(2,1)S(1)}, u32[]{:S(2)}, u32[]{:S(2)}) collective-permute-start(bf16[144,1152]{1,0:T(8,128)(2,1)S(1)} %pad_maximum_fusion.refs_1_.refs_22_), channel_id=1, source_target_pairs={{0,24},{1,25},{2,26},{3,27},{4,28},{5,29},{6,30},{7,31},{8,16},{9,... | collective-permute-start | bytes 995336 | tf_op jit(solution)/shard_map/ppermute | solution.py:61
  10.8 5.2 %copy.16 = bf16[1152,1152]{0,1:T(8,128)(2,1)} copy(bf16[1152,1152]{1,0:T(8,128)(2,1)} %param.10) | data formatting | bytes 5308416 | tf_op args[3]
  19.0 2.6 %collective-permute-start.2 = (bf16[128,1152]{1,0:T(8,128)(2,1)}, bf16[128,1152]{1,0:T(8,128)(2,1)}, u32[]{:S(2)}, u32[]{:S(2)}) collective-permute-start(bf16[128,1152]{1,0:T(8,128)(2,1)} %collective-permute-done.refs_2_.refs_8_), channel_id=1, source_target_pairs={{0,96},{1,97},{2,98},{3,99},{4,100},{5,101},{6,102},{7,103},{8,104... | collective-permute-start | bytes 884744 | tf_op jit(solution)/shard_map/ppermute | solution.py:61
  21.6 3.3 %copy.17 = bf16[1152,1152]{0,1:T(8,128)(2,1)} copy(bf16[1152,1152]{1,0:T(8,128)(2,1)S(1)} %copy-done.2) | data formatting | bytes 5308416 | tf_op args[2]
  25.6 5.2 %collective-permute-done.3.refs_4_.refs_25_ = bf16[144,1152]{1,0:T(8,128)(2,1)} collective-permute-done((bf16[144,1152]{1,0:T(8,128)(2,1)S(1)}, bf16[144,1152]{1,0:T(8,128)(2,1)}, u32[]{:S(2)}, u32[]{:S(2)}) %collective-permute-start.3) | collective-permute-done | bytes 331808 | tf_op jit(solution)/shard_map/ppermute | solution.py:61
  30.8 7.9 %shard_map.104 = (bf16[1168,1024]{1,0:T(8,128)(2,1)}, f32[1,1024]{1,0:T(1,128)}, bf16[3,1168,256]{2,1,0:T(8,128)(2,1)}) custom-call(s32[4]{0:T(128)} %pad_add_fusion.4.refs_0_, bf16[144,1152]{1,0:T(8,128)(2,1)} %copy-done.7, bf16[144,1152]{1,0:T(8,128)(2,1)} %copy-done.10, bf16[144,1152]{1,0:T(8,128)(2,1)} %collective-permute-done.7.refs_3_.refs_24_, ...), custom_call_target="tpu_custom_call" | custom-call | flops 2038431744 | bytes 7299072 | tf_op jit(solution)/shard_map/pallas_call | solution.py:93
  38.8 2.7 %collective-permute-start.14 = (bf16[3,1168,256]{2,1,0:T(8,128)(2,1)}, bf16[3,1168,256]{2,1,0:T(8,128)(2,1)S(1)}, u32[]{:S(2)}, u32[]{:S(2)}) collective-permute-start(bf16[3,1168,256]{2,1,0:T(8,128)(2,1)} %get-tuple-element.108), channel_id=1, source_target_pairs={{0,1},{1,0},{2,3},{3,2},{4,5},{5,4},{6,7},{7,6},{8,9},{9,8},{10,11... | collective-permute-start | bytes 5382152 | tf_op jit(solution)/shard_map/ppermute | solution.py:61
  47.4 4.1 %collective-permute-done.12.refs_6_.refs_14_ = bf16[128,1152]{1,0:T(8,128)(2,1)S(1)} collective-permute-done((bf16[128,1152]{1,0:T(8,128)(2,1)}, bf16[128,1152]{1,0:T(8,128)(2,1)S(1)}, u32[]{:S(2)}, u32[]{:S(2)}) %collective-permute-start.12) | collective-permute-done | bytes 294944 | tf_op jit(solution)/shard_map/ppermute | solution.py:61
  52.2 11.1 %shard_map.102 = (bf16[1152,1024]{1,0:T(8,128)(2,1)}, f32[1,1024]{1,0:T(1,128)}, bf16[1024,1152]{1,0:T(8,128)(2,1)}) custom-call(s32[4]{0:T(128)} %pad_add_fusion.2.refs_0_, bf16[128,1152]{1,0:T(8,128)(2,1)} %refs_7_.1, bf16[128,1152]{1,0:T(8,128)(2,1)} %collective-permute-done.refs_2_.refs_8_, bf16[128,1152]{1,0:T(8,128)(2,1)} %collective-permute-done.6.refs_3_.refs_9_, ...), custom_call_target="tpu_custom_call" | custom-call | flops 4076863488 | bytes 7077888 | tf_op jit(solution)/shard_map/pallas_call | solution.py:93
  64.3 4.9 %shard_map.105 = (bf16[1168,1024]{1,0:T(8,128)(2,1)}, f32[1,1024]{1,0:T(1,128)}, bf16[1,1168,256]{2,1,0:T(8,128)(2,1)}) custom-call(s32[2]{0:T(128)} %pad_add_fusion.3.refs_0_, bf16[144,1152]{1,0:T(8,128)(2,1)} %copy-done.5, bf16[144,1152]{1,0:T(8,128)(2,1)} %copy-done.6, bf16[1152,1152]{1,0:T(8,128)(2,1)} %bitcast.50, ...), custom_call_target="tpu_custom_call", output_to_operand_aliasing={{0}: (5, {}), {1}: (6, {})} | custom-call | flops 679477248 | bytes 8368128 | tf_op jit(solution)/shard_map/pallas_call | solution.py:93
  71.6 6.4 %shard_map.103 = (bf16[1152,1024]{1,0:T(8,128)(2,1)}, f32[1,1024]{1,0:T(1,128)}, bf16[1024,1152]{1,0:T(8,128)(2,1)}) custom-call(s32[2]{0:T(128)} %pad_add_fusion.1.refs_0_, bf16[128,1152]{1,0:T(8,128)(2,1)} %copy-done.8, bf16[128,1152]{1,0:T(8,128)(2,1)} %copy-done.9, ...), custom_call_target="tpu_custom_call", output_to_operand_aliasing={{0}: (5, {}), {1}: (6, {}), {2}: (7, {})} | custom-call | flops 1358954496 | bytes 10620928 | tf_op jit(solution)/shard_map/pallas_call | solution.py:93
  79.3 13.6 %shard_map.106 = (bf16[4,1024,256]{2,1,0:T(8,128)(2,1)}, f32[1,1024]{1,0:T(1,128)}, bf16[1280,1024]{1,0:T(8,128)(2,1)}) custom-call(s32[2]{0:T(128)} %pad_add_fusion.5.refs_0_, f32[32]{0:T(128)} %refs_1_.5, bf16[1024,1152]{1,0:T(8,128)(2,1)} %get-tuple-element.98.refs_2_, bf16[1152,1024]{1,0:T(8,128)(2,1)} %get-tuple-element.99.refs_3_.refs_5_, ...), custom_call_target="tpu_custom_call" | custom-call | flops 4831838208 | bytes 7110784 | tf_op jit(solution)/shard_map/pallas_call | solution.py:93
  94.3 20.1 %shard_map.107 = (bf16[1280,1024]{1,0:T(8,128)(2,1)}, bf16[160,1024]{1,0:T(8,128)(2,1)}, bf16[160,1024]{1,0:T(8,128)(2,1)}, bf16[160,1024]{1,0:T(8,128)(2,1)}, b...) custom-call(s32[3]{0:T(128)} %pad_add_fusion.refs_0_, ...), custom_call_target="tpu_custom_call" | custom-call | flops 9663676416 | bytes 11604096 | tf_op jit(solution)/shard_map/pallas_call | solution.py:93
  118.6 3.2 %shard_map.108 = (bf16[160,1024]{1,0:T(8,128)(2,1)}, bf16[160,1024]{1,0:T(8,128)(2,1)}, bf16[160,1024]{1,0:T(8,128)(2,1)}) custom-call(s32[7]{0:T(128)} %stack.163.refs_0_, bf16[1280,1024]{1,0:T(8,128)(2,1)} %get-tuple-element.114.refs_1_.refs_3_.refs_5_.refs_8_.refs_11_.refs_4_.refs_15_, bf16[1280,1024]{1,0:T(8,128)(2,1)} %copy-done, ...), custom_call_target="tpu_custom_call" | custom-call | bytes 15728640 | tf_op jit(solution)/shard_map/pallas_call | solution.py:93
  123.0 2.4 %collective-permute-start.20 = (bf16[160,1024]{1,0:T(8,128)(2,1)}, bf16[160,1024]{1,0:T(8,128)(2,1)S(1)}, u32[]{:S(2)}, u32[]{:S(2)}) collective-permute-start(bf16[160,1024]{1,0:T(8,128)(2,1)} %get-tuple-element.118), channel_id=1, source_target_pairs={{0,6},{1,7},{2,0},{3,1},{4,2},{5,3},{6,4},{7,5},{8,14},{9,15},{10,... | collective-permute-start | bytes 983048 | tf_op jit(solution)/shard_map/ppermute | solution.py:61
  126.1 6.5 %collective-permute-done.18.refs_10_ = bf16[160,1024]{1,0:T(8,128)(2,1)S(1)} collective-permute-done((bf16[160,1024]{1,0:T(8,128)(2,1)}, bf16[160,1024]{1,0:T(8,128)(2,1)S(1)}, u32[]{:S(2)}, u32[]{:S(2)}) %collective-permute-start.18) | collective-permute-done | bytes 327712 | tf_op jit(solution)/shard_map/ppermute | solution.py:61
  133.4 4.2 %shard_map.109 = (bf16[160,1024]{1,0:T(8,128)(2,1)}, bf16[160,1024]{1,0:T(8,128)(2,1)}, bf16[160,1024]{1,0:T(8,128)(2,1)}, bf16[160,1024]{1,0:T(8,128)(2,1)}, bf16[160,1024]{1,0:T(8,128)(2,1)}) custom-call(s32[7]{0:T(128)} %stack.167.refs_0_, bf16[160,1024]{1,0:T(8,128)(2,1)} %get-tuple-element.123.refs_1_, bf16[160,1024]{1,0:T(8,128)(2,1)} %copy-done.22, ...), custom_call_target="tpu_custom_call" | custom-call | bytes 17694720 | tf_op jit(solution)/shard_map/pallas_call | solution.py:93
  137.6 2.5 %collective-permute-start.23 = (bf16[160,1024]{1,0:T(8,128)(2,1)}, bf16[160,1024]{1,0:T(8,128)(2,1)S(1)}, u32[]{:S(2)}, u32[]{:S(2)}) collective-permute-start(bf16[160,1024]{1,0:T(8,128)(2,1)} %get-tuple-element.129), channel_id=1, source_target_pairs={{0,96},{1,97},{2,98},{3,99},{4,100},{5,101},{6,102},{7,103},{8,104... | collective-permute-start | bytes 983048 | tf_op jit(solution)/shard_map/ppermute | solution.py:61
  140.1 2.2 %collective-permute-start.24 = (bf16[160,1024]{1,0:T(8,128)(2,1)}, bf16[160,1024]{1,0:T(8,128)(2,1)S(1)}, u32[]{:S(2)}, u32[]{:S(2)}) collective-permute-start(bf16[160,1024]{1,0:T(8,128)(2,1)} %get-tuple-element.130), channel_id=1, source_target_pairs={{0,6},{1,7},{2,0},{3,1},{4,2},{5,3},{6,4},{7,5},{8,14},{9,15},{10,... | collective-permute-start | bytes 983048 | tf_op jit(solution)/shard_map/ppermute | solution.py:61
  142.3 2.8 %collective-permute-done.23.refs_3_ = bf16[160,1024]{1,0:T(8,128)(2,1)S(1)} collective-permute-done((bf16[160,1024]{1,0:T(8,128)(2,1)}, bf16[160,1024]{1,0:T(8,128)(2,1)S(1)}, u32[]{:S(2)}, u32[]{:S(2)}) %collective-permute-start.23) | collective-permute-done | bytes 327712 | tf_op jit(solution)/shard_map/ppermute | solution.py:61
  147.6 2.6 %collective-permute-start.26 = (bf16[160,1024]{1,0:T(8,128)(2,1)S(1)}, bf16[160,1024]{1,0:T(8,128)(2,1)S(1)}, u32[]{:S(2)}, u32[]{:S(2)}) collective-permute-start(bf16[160,1024]{1,0:T(8,128)(2,1)S(1)} %copy-done.31), channel_id=1, source_target_pairs={{0,96},{1,97},{2,98},{3,99},{4,100},{5,101},{6,102},{7,103},{8,104... | collective-permute-start | bytes 983048 | tf_op jit(solution)/shard_map/ppermute | solution.py:61
  150.3 3.3 %shard_map.110 = (bf16[160,1024]{1,0:T(8,128)(2,1)}, bf16[160,1024]{1,0:T(8,128)(2,1)}) custom-call(s32[3]{0:T(128)} %pad_add_fusion.6.refs_0_, bf16[160,1024]{1,0:T(8,128)(2,1)} %get-tuple-element.137.refs_1_, bf16[160,1024]{1,0:T(8,128)(2,1)} %copy-done.11, bf16[160,1024]{1,0:T(8,128)(2,1)} %copy-done.13, ...), custom_call_target="tpu_custom_call" | custom-call | bytes 6881280 | tf_op jit(solution)/shard_map/pallas_call | solution.py:93
  154.8 2.4 %collective-permute-start.29 = (bf16[160,1024]{1,0:T(8,128)(2,1)S(1)}, bf16[160,1024]{1,0:T(8,128)(2,1)S(1)}, u32[]{:S(2)}, u32[]{:S(2)}) collective-permute-start(bf16[160,1024]{1,0:T(8,128)(2,1)S(1)} %copy-done.32), channel_id=1, source_target_pairs={{0,6},{1,7},{2,0},{3,1},{4,2},{5,3},{6,4},{7,5},{8,14},{9,15},{10,... | collective-permute-start | bytes 983048 | tf_op jit(solution)/shard_map/ppermute | solution.py:61
  161.5 3.3 %collective-permute-done.30.refs_19_ = bf16[160,1024]{1,0:T(8,128)(2,1)S(1)} collective-permute-done((bf16[160,1024]{1,0:T(8,128)(2,1)}, bf16[160,1024]{1,0:T(8,128)(2,1)S(1)}, u32[]{:S(2)}, u32[]{:S(2)}) %collective-permute-start.30) | collective-permute-done | bytes 327712 | tf_op jit(solution)/shard_map/ppermute | solution.py:61
  165.5 7.1 %shard_map.111 = (bf16[4,144,128]{2,1,0:T(8,128)(2,1)}, bf16[4,144,128]{2,1,0:T(8,128)(2,1)}, bf16[4,144,128]{2,1,0:T(8,128)(2,1)}, bf16[4,144,128]{2,1,0:T(8,128)(2,1)}, bf16[288,1152]{1,0:T(8,128)(2,1)}) custom-call(s32[8]{0:T(128)} %stack.140.refs_0_, bf16[160,1024]{1,0:T(8,128)(2,1)} %get-tuple-element.112.refs_1_, bf16[160,1024]{1,0:T(8,128)(2,1)} %copy-done.15, ...), custom_call_target="tpu_custom_call" | custom-call | flops 679477248 | bytes 17309696 | tf_op jit(solution)/shard_map/pallas_call | solution.py:93
  172.6 5.6 %collective-permute-start.31 = (bf16[288,1152]{1,0:T(8,128)(2,1)}, bf16[288,1152]{1,0:T(8,128)(2,1)S(1)}, u32[]{:S(2)}, u32[]{:S(2)}) collective-permute-start(bf16[288,1152]{1,0:T(8,128)(2,1)} %get-tuple-element.148.mine), channel_id=1, source_target_pairs={{0,1},{1,0},{2,3},{3,2},{4,5},{5,4},{6,7},{7,6},{8,9},{9,8},{10,11... | collective-permute-start | bytes 1990664 | tf_op jit(solution)/shard_map/ppermute | solution.py:61
  181.0 3.8 %shard_map.112 = bf16[512,384]{1,0:T(8,128)(2,1)} custom-call(s32[1]{0:T(128)} %bitcast.at_ref, bf16[288,1152]{1,0:T(8,128)(2,1)} %get-tuple-element.148.mine, bf16[288,1152]{1,0:T(8,128)(2,1)} %copy-done.29), custom_call_target="tpu_custom_call" | custom-call | flops 679477248 | bytes 1327104 | tf_op jit(solution)/shard_map/pallas_call | solution.py:93
  188.4 2.8 %collective-permute-start.38 = (bf16[288,128]{1,0:T(8,128)(2,1)}, bf16[288,128]{1,0:T(8,128)(2,1)}, u32[]{:S(2)}, u32[]{:S(2)}) collective-permute-start(bf16[288,128]{1,0:T(8,128)(2,1)} %get-tuple-element.160), channel_id=1, source_target_pairs={{0,4},{1,5},{2,6},{3,7},{4,0},{5,1},{6,2},{7,3},{8,12},{9,13},{10,... | collective-permute-start | bytes 221192 | tf_op jit(solution)/shard_map/ppermute | solution.py:61
  191.3 6.0 %all-to-all-start = ((bf16[64,8,384]{2,1,0:T(8,128)(2,1)}), bf16[64,8,384]{2,1,0:T(8,128)(2,1)S(1)}, u32[]{:S(2)}, u32[]{:S(2)}) async-start(bf16[64,8,384]{2,1,0:T(8,128)(2,1)} %bitcast.56), calls=%async_computation | async-start | bytes 786432 | tf_op jit(solution)/shard_map/all_to_all | solution.py:65
  197.3 2.6 %collective-permute-start.37 = (bf16[288,128]{1,0:T(8,128)(2,1)S(1)}, bf16[288,128]{1,0:T(8,128)(2,1)S(1)}, u32[]{:S(2)}, u32[]{:S(2)}) collective-permute-start(bf16[288,128]{1,0:T(8,128)(2,1)S(1)} %get-tuple-element.159), channel_id=1, source_target_pairs={{0,6},{1,7},{2,0},{3,1},{4,2},{5,3},{6,4},{7,5},{8,14},{9,15},{10,... | collective-permute-start | bytes 221192 | tf_op jit(solution)/shard_map/ppermute | solution.py:61
  199.9 3.7 %fusion.2 = f32[128,1152]{1,0:T(8,128)} fusion(s32[]{:T(128)S(6)} %select_n.210, bf16[1152,1152]{1,0:T(8,128)(2,1)S(1)} %bitcast.55, bf16[288,128]{1,0:T(8,128)(2,1)} %collective-permute-done.36, bf16[288,128]{1,0:T(8,128)(2,1)} %collective-permute-done.35, bf16[288,128]{1,0:T(8,128)(2,1)} %collective-permute-done.34, ...), kind=kOutput, calls=%fused_computation.6 | convolution fusion | flops 346226688 | bytes 3538948 | tf_op jit(solution)/shard_map/dot_general | solution.py:75
  203.6 3.6 %fusion.4 = f32[128,1152]{1,0:T(8,128)} fusion(s32[]{:T(128)S(6)} %select_n.218, bf16[1152,1152]{1,0:T(8,128)(2,1)S(1)} %bitcast.52, bf16[288,128]{1,0:T(8,128)(2,1)} %collective-permute-done.39, bf16[288,128]{1,0:T(8,128)(2,1)} %collective-permute-done.38, bf16[288,128]{1,0:T(8,128)(2,1)S(1)} %collective-permute-done.37, ...), kind=kOutput, calls=%fused_computation.7 | convolution fusion | flops 346226688 | bytes 3538948 | tf_op jit(solution)/shard_map/dot_general | solution.py:75
  (151 shorter events, 47.8 us)
Async XLA Ops:
  2.4 15.1 %collective-permute-start.1 = (bf16[144,1152]{1,0:T(8,128)(2,1)S(1)}, bf16[144,1152]{1,0:T(8,128)(2,1)S(1)}, u32[]{:S(2)}, u32[]{:S(2)}) collective-permute-start(bf16[144,1152]{1,0:T(8,128)(2,1)S(1)} %pad_maximum_fusion.refs_1_.refs_22_), channel_id=1, source_target_pairs={{0,24},{1,25},{2,26},{3,27},{4,28},{5,29},{6,30},{7,31},{8,16},{9,... | collective-permute-start | bytes 995336 | tf_op jit(solution)/shard_map/ppermute | solution.py:61
  5.7 10.3 %collective-permute-start = (bf16[128,1152]{1,0:T(8,128)(2,1)}, bf16[128,1152]{1,0:T(8,128)(2,1)}, u32[]{:S(2)}, u32[]{:S(2)}) collective-permute-start(bf16[128,1152]{1,0:T(8,128)(2,1)} %refs_7_.1), channel_id=1, source_target_pairs={{0,16},{1,17},{2,18},{3,19},{4,20},{5,21},{6,22},{7,23},{8,24},{9,... | collective-permute-start | bytes 884744 | tf_op jit(solution)/shard_map/ppermute | solution.py:61
  5.7 13.2 %collective-permute-start.4 = (bf16[128,1152]{1,0:T(8,128)(2,1)}, bf16[128,1152]{1,0:T(8,128)(2,1)}, u32[]{:S(2)}, u32[]{:S(2)}) collective-permute-start(bf16[128,1152]{1,0:T(8,128)(2,1)} %refs_7_.1), channel_id=1, source_target_pairs={{0,32},{1,33},{2,34},{3,35},{4,36},{5,37},{6,38},{7,39},{8,40},{9,... | collective-permute-start | bytes 884744 | tf_op jit(solution)/shard_map/ppermute | solution.py:61
  7.4 11.6 %collective-permute-start.6 = (bf16[128,1152]{1,0:T(8,128)(2,1)}, bf16[128,1152]{1,0:T(8,128)(2,1)}, u32[]{:S(2)}, u32[]{:S(2)}) collective-permute-start(bf16[128,1152]{1,0:T(8,128)(2,1)} %refs_7_.1), channel_id=1, source_target_pairs={{0,96},{1,97},{2,98},{3,99},{4,100},{5,101},{6,102},{7,103},{8,104... | collective-permute-start | bytes 884744 | tf_op jit(solution)/shard_map/ppermute | solution.py:61
  9.5 15.9 %collective-permute-start.5 = (bf16[144,1152]{1,0:T(8,128)(2,1)S(1)}, bf16[144,1152]{1,0:T(8,128)(2,1)}, u32[]{:S(2)}, u32[]{:S(2)}) collective-permute-start(bf16[144,1152]{1,0:T(8,128)(2,1)S(1)} %pad_maximum_fusion.refs_1_.refs_22_), channel_id=1, source_target_pairs={{0,2},{1,3},{2,4},{3,5},{4,6},{5,7},{6,0},{7,1},{8,10},{9,11},{10,... | collective-permute-start | bytes 995336 | tf_op jit(solution)/shard_map/ppermute | solution.py:61
  16.0 9.4 %collective-permute-start.7 = (bf16[144,1152]{1,0:T(8,128)(2,1)S(1)}, bf16[144,1152]{1,0:T(8,128)(2,1)}, u32[]{:S(2)}, u32[]{:S(2)}) collective-permute-start(bf16[144,1152]{1,0:T(8,128)(2,1)S(1)} %pad_maximum_fusion.refs_1_.refs_22_), channel_id=1, source_target_pairs={{0,6},{1,7},{2,0},{3,1},{4,2},{5,3},{6,4},{7,5},{8,14},{9,15},{10,... | collective-permute-start | bytes 995336 | tf_op jit(solution)/shard_map/ppermute | solution.py:61
  17.5 13.3 %collective-permute-start.3 = (bf16[144,1152]{1,0:T(8,128)(2,1)S(1)}, bf16[144,1152]{1,0:T(8,128)(2,1)}, u32[]{:S(2)}, u32[]{:S(2)}) collective-permute-start(bf16[144,1152]{1,0:T(8,128)(2,1)S(1)} %collective-permute-done.1.refs_2_.refs_23_), channel_id=1, source_target_pairs={{0,6},{1,7},{2,0},{3,1},{4,2},{5,3},{6,4},{7,5},{8,14},{9,15},{10,... | collective-permute-start | bytes 995336 | tf_op jit(solution)/shard_map/ppermute | solution.py:61
  19.0 11.9 %collective-permute-start.13 = (bf16[144,1152]{1,0:T(8,128)(2,1)S(1)}, bf16[144,1152]{1,0:T(8,128)(2,1)}, u32[]{:S(2)}, u32[]{:S(2)}) collective-permute-start(bf16[144,1152]{1,0:T(8,128)(2,1)S(1)} %collective-permute-done.1.refs_2_.refs_23_), channel_id=1, source_target_pairs={{0,2},{1,3},{2,4},{3,5},{4,6},{5,7},{6,0},{7,1},{8,10},{9,11},{10,... | collective-permute-start | bytes 995336 | tf_op jit(solution)/shard_map/ppermute | solution.py:61
  38.8 39.2 %collective-permute-start.14 = (bf16[3,1168,256]{2,1,0:T(8,128)(2,1)}, bf16[3,1168,256]{2,1,0:T(8,128)(2,1)S(1)}, u32[]{:S(2)}, u32[]{:S(2)}) collective-permute-start(bf16[3,1168,256]{2,1,0:T(8,128)(2,1)} %get-tuple-element.108), channel_id=1, source_target_pairs={{0,1},{1,0},{2,3},{3,2},{4,5},{5,4},{6,7},{7,6},{8,9},{9,8},{10,11... | collective-permute-start | bytes 5382152 | tf_op jit(solution)/shard_map/ppermute | solution.py:61
  41.4 10.1 %collective-permute-start.12 = (bf16[128,1152]{1,0:T(8,128)(2,1)}, bf16[128,1152]{1,0:T(8,128)(2,1)S(1)}, u32[]{:S(2)}, u32[]{:S(2)}) collective-permute-start(bf16[128,1152]{1,0:T(8,128)(2,1)} %collective-permute-done.refs_2_.refs_8_), channel_id=1, source_target_pairs={{0,32},{1,33},{2,34},{3,35},{4,36},{5,37},{6,38},{7,39},{8,40},{9,... | collective-permute-start | bytes 884744 | tf_op jit(solution)/shard_map/ppermute | solution.py:61
  42.6 20.8 %collective-permute-start.9 = (bf16[144,1152]{1,0:T(8,128)(2,1)}, bf16[144,1152]{1,0:T(8,128)(2,1)S(1)}, u32[]{:S(2)}, u32[]{:S(2)}) collective-permute-start(bf16[144,1152]{1,0:T(8,128)(2,1)} %collective-permute-done.5.refs_5_.refs_28_), channel_id=1, source_target_pairs={{0,2},{1,3},{2,4},{3,5},{4,6},{5,7},{6,0},{7,1},{8,10},{9,11},{10,... | collective-permute-start | bytes 995336 | tf_op jit(solution)/shard_map/ppermute | solution.py:61
  43.9 19.5 %collective-permute-start.11 = (bf16[144,1152]{1,0:T(8,128)(2,1)}, bf16[144,1152]{1,0:T(8,128)(2,1)S(1)}, u32[]{:S(2)}, u32[]{:S(2)}) collective-permute-start(bf16[144,1152]{1,0:T(8,128)(2,1)} %collective-permute-done.3.refs_4_.refs_25_), channel_id=1, source_target_pairs={{0,6},{1,7},{2,0},{3,1},{4,2},{5,3},{6,4},{7,5},{8,14},{9,15},{10,... | collective-permute-start | bytes 995336 | tf_op jit(solution)/shard_map/ppermute | solution.py:61
  45.7 17.6 %collective-permute-start.8 = (bf16[128,1152]{1,0:T(8,128)(2,1)}, bf16[128,1152]{1,0:T(8,128)(2,1)S(1)}, u32[]{:S(2)}, u32[]{:S(2)}) collective-permute-start(bf16[128,1152]{1,0:T(8,128)(2,1)} %collective-permute-done.4.refs_5_.refs_13_), channel_id=1, source_target_pairs={{0,32},{1,33},{2,34},{3,35},{4,36},{5,37},{6,38},{7,39},{8,40},{9,... | collective-permute-start | bytes 884744 | tf_op jit(solution)/shard_map/ppermute | solution.py:61
  51.5 11.9 %collective-permute-start.10 = (bf16[128,1152]{1,0:T(8,128)(2,1)}, bf16[128,1152]{1,0:T(8,128)(2,1)S(1)}, u32[]{:S(2)}, u32[]{:S(2)}) collective-permute-start(bf16[128,1152]{1,0:T(8,128)(2,1)} %collective-permute-done.2.refs_4_.refs_10_), channel_id=1, source_target_pairs={{0,96},{1,97},{2,98},{3,99},{4,100},{5,101},{6,102},{7,103},{8,104... | collective-permute-start | bytes 884744 | tf_op jit(solution)/shard_map/ppermute | solution.py:61
  69.1 8.8 %collective-permute-start.15 = (bf16[1,1168,256]{2,1,0:T(8,128)(2,1)}, bf16[1,1168,256]{2,1,0:T(8,128)(2,1)S(1)}, u32[]{:S(2)}, u32[]{:S(2)}) collective-permute-start(bf16[1,1168,256]{2,1,0:T(8,128)(2,1)} %get-tuple-element.109), channel_id=1, source_target_pairs={{0,1},{1,0},{2,3},{3,2},{4,5},{5,4},{6,7},{7,6},{8,9},{9,8},{10,11... | collective-permute-start | bytes 1794056 | tf_op jit(solution)/shard_map/ppermute | solution.py:61
  93.0 24.2 %collective-permute-start.17 = (bf16[1280,1024]{1,0:T(8,128)(2,1)}, bf16[1280,1024]{1,0:T(8,128)(2,1)S(1)}, u32[]{:S(2)}, u32[]{:S(2)}) collective-permute-start(bf16[1280,1024]{1,0:T(8,128)(2,1)} %get-tuple-element.115), channel_id=1, source_target_pairs={{0,1},{1,0},{2,3},{3,2},{4,5},{5,4},{6,7},{7,6},{8,9},{9,8},{10,11... | collective-permute-start | bytes 7864328 | tf_op jit(solution)/shard_map/ppermute | solution.py:61
  114.4 11.6 %collective-permute-start.16 = (bf16[160,1024]{1,0:T(8,128)(2,1)}, bf16[160,1024]{1,0:T(8,128)(2,1)S(1)}, u32[]{:S(2)}, u32[]{:S(2)}) collective-permute-start(bf16[160,1024]{1,0:T(8,128)(2,1)} %get-tuple-element.113), channel_id=1, source_target_pairs={{0,32},{1,33},{2,34},{3,35},{4,36},{5,37},{6,38},{7,39},{8,40},{9,... | collective-permute-start | bytes 983048 | tf_op jit(solution)/shard_map/ppermute | solution.py:61
  115.4 10.7 %collective-permute-start.19 = (bf16[160,1024]{1,0:T(8,128)(2,1)}, bf16[160,1024]{1,0:T(8,128)(2,1)S(1)}, u32[]{:S(2)}, u32[]{:S(2)}) collective-permute-start(bf16[160,1024]{1,0:T(8,128)(2,1)} %get-tuple-element.117), channel_id=1, source_target_pairs={{0,96},{1,97},{2,98},{3,99},{4,100},{5,101},{6,102},{7,103},{8,104... | collective-permute-start | bytes 983048 | tf_op jit(solution)/shard_map/ppermute | solution.py:61
  121.8 10.8 %collective-permute-start.18 = (bf16[160,1024]{1,0:T(8,128)(2,1)}, bf16[160,1024]{1,0:T(8,128)(2,1)S(1)}, u32[]{:S(2)}, u32[]{:S(2)}) collective-permute-start(bf16[160,1024]{1,0:T(8,128)(2,1)} %get-tuple-element.116), channel_id=1, source_target_pairs={{0,2},{1,3},{2,4},{3,5},{4,6},{5,7},{6,0},{7,1},{8,10},{9,11},{10,... | collective-permute-start | bytes 983048 | tf_op jit(solution)/shard_map/ppermute | solution.py:61
  123.0 9.5 %collective-permute-start.20 = (bf16[160,1024]{1,0:T(8,128)(2,1)}, bf16[160,1024]{1,0:T(8,128)(2,1)S(1)}, u32[]{:S(2)}, u32[]{:S(2)}) collective-permute-start(bf16[160,1024]{1,0:T(8,128)(2,1)} %get-tuple-element.118), channel_id=1, source_target_pairs={{0,6},{1,7},{2,0},{3,1},{4,2},{5,3},{6,4},{7,5},{8,14},{9,15},{10,... | collective-permute-start | bytes 983048 | tf_op jit(solution)/shard_map/ppermute | solution.py:61
  132.6 9.7 %collective-permute-start.21 = (bf16[160,1024]{1,0:T(8,128)(2,1)}, bf16[160,1024]{1,0:T(8,128)(2,1)S(1)}, u32[]{:S(2)}, u32[]{:S(2)}) collective-permute-start(bf16[160,1024]{1,0:T(8,128)(2,1)} %get-tuple-element.121), channel_id=1, source_target_pairs={{0,32},{1,33},{2,34},{3,35},{4,36},{5,37},{6,38},{7,39},{8,40},{9,... | collective-permute-start | bytes 983048 | tf_op jit(solution)/shard_map/ppermute | solution.py:61
  132.6 9.6 %collective-permute-start.22 = (bf16[160,1024]{1,0:T(8,128)(2,1)}, bf16[160,1024]{1,0:T(8,128)(2,1)S(1)}, u32[]{:S(2)}, u32[]{:S(2)}) collective-permute-start(bf16[160,1024]{1,0:T(8,128)(2,1)} %get-tuple-element.122), channel_id=1, source_target_pairs={{0,2},{1,3},{2,4},{3,5},{4,6},{5,7},{6,0},{7,1},{8,10},{9,11},{10,... | collective-permute-start | bytes 983048 | tf_op jit(solution)/shard_map/ppermute | solution.py:61
  147.0 10.1 %collective-permute-start.25 = (bf16[160,1024]{1,0:T(8,128)(2,1)}, bf16[160,1024]{1,0:T(8,128)(2,1)S(1)}, u32[]{:S(2)}, u32[]{:S(2)}) collective-permute-start(bf16[160,1024]{1,0:T(8,128)(2,1)} %get-tuple-element.135), channel_id=1, source_target_pairs={{0,32},{1,33},{2,34},{3,35},{4,36},{5,37},{6,38},{7,39},{8,40},{9,... | collective-permute-start | bytes 983048 | tf_op jit(solution)/shard_map/ppermute | solution.py:61
  147.6 10.4 %collective-permute-start.26 = (bf16[160,1024]{1,0:T(8,128)(2,1)S(1)}, bf16[160,1024]{1,0:T(8,128)(2,1)S(1)}, u32[]{:S(2)}, u32[]{:S(2)}) collective-permute-start(bf16[160,1024]{1,0:T(8,128)(2,1)S(1)} %copy-done.31), channel_id=1, source_target_pairs={{0,96},{1,97},{2,98},{3,99},{4,100},{5,101},{6,102},{7,103},{8,104... | collective-permute-start | bytes 983048 | tf_op jit(solution)/shard_map/ppermute | solution.py:61
  153.7 7.8 %collective-permute-start.28 = (bf16[160,1024]{1,0:T(8,128)(2,1)S(1)}, bf16[160,1024]{1,0:T(8,128)(2,1)S(1)}, u32[]{:S(2)}, u32[]{:S(2)}) collective-permute-start(bf16[160,1024]{1,0:T(8,128)(2,1)S(1)} %copy-done.33), channel_id=1, source_target_pairs={{0,2},{1,3},{2,4},{3,5},{4,6},{5,7},{6,0},{7,1},{8,10},{9,11},{10,... | collective-permute-start | bytes 983048 | tf_op jit(solution)/shard_map/ppermute | solution.py:61
  157.1 7.6 %collective-permute-start.30 = (bf16[160,1024]{1,0:T(8,128)(2,1)}, bf16[160,1024]{1,0:T(8,128)(2,1)S(1)}, u32[]{:S(2)}, u32[]{:S(2)}) collective-permute-start(bf16[160,1024]{1,0:T(8,128)(2,1)} %get-tuple-element.146), channel_id=1, source_target_pairs={{0,24},{1,25},{2,26},{3,27},{4,28},{5,29},{6,30},{7,31},{8,16},{9,... | collective-permute-start | bytes 983048 | tf_op jit(solution)/shard_map/ppermute | solution.py:61
  185.0 12.4 %collective-permute-start.36 = (bf16[288,128]{1,0:T(8,128)(2,1)S(1)}, bf16[288,128]{1,0:T(8,128)(2,1)}, u32[]{:S(2)}, u32[]{:S(2)}) collective-permute-start(bf16[288,128]{1,0:T(8,128)(2,1)S(1)} %get-tuple-element.167), channel_id=1, source_target_pairs={{0,32},{1,33},{2,34},{3,35},{4,36},{5,37},{6,38},{7,39},{8,40},{9,... | collective-permute-start | bytes 221192 | tf_op jit(solution)/shard_map/ppermute | solution.py:61
  185.1 14.9 %collective-permute-start.35 = (bf16[288,128]{1,0:T(8,128)(2,1)S(1)}, bf16[288,128]{1,0:T(8,128)(2,1)}, u32[]{:S(2)}, u32[]{:S(2)}) collective-permute-start(bf16[288,128]{1,0:T(8,128)(2,1)S(1)} %get-tuple-element.166), channel_id=1, source_target_pairs={{0,64},{1,65},{2,66},{3,67},{4,68},{5,69},{6,70},{7,71},{8,72},{9,... | collective-permute-start | bytes 221192 | tf_op jit(solution)/shard_map/ppermute | solution.py:61
  186.3 13.6 %collective-permute-start.34 = (bf16[288,128]{1,0:T(8,128)(2,1)S(1)}, bf16[288,128]{1,0:T(8,128)(2,1)}, u32[]{:S(2)}, u32[]{:S(2)}) collective-permute-start(bf16[288,128]{1,0:T(8,128)(2,1)S(1)} %get-tuple-element.165), channel_id=1, source_target_pairs={{0,96},{1,97},{2,98},{3,99},{4,100},{5,101},{6,102},{7,103},{8,104... | collective-permute-start | bytes 221192 | tf_op jit(solution)/shard_map/ppermute | solution.py:61
  188.4 15.2 %collective-permute-start.39 = (bf16[288,128]{1,0:T(8,128)(2,1)}, bf16[288,128]{1,0:T(8,128)(2,1)}, u32[]{:S(2)}, u32[]{:S(2)}) collective-permute-start(bf16[288,128]{1,0:T(8,128)(2,1)} %get-tuple-element.161), channel_id=1, source_target_pairs={{0,2},{1,3},{2,4},{3,5},{4,6},{5,7},{6,0},{7,1},{8,10},{9,11},{10,... | collective-permute-start | bytes 221192 | tf_op jit(solution)/shard_map/ppermute | solution.py:61
  188.4 15.2 %collective-permute-start.38 = (bf16[288,128]{1,0:T(8,128)(2,1)}, bf16[288,128]{1,0:T(8,128)(2,1)}, u32[]{:S(2)}, u32[]{:S(2)}) collective-permute-start(bf16[288,128]{1,0:T(8,128)(2,1)} %get-tuple-element.160), channel_id=1, source_target_pairs={{0,4},{1,5},{2,6},{3,7},{4,0},{5,1},{6,2},{7,3},{8,12},{9,13},{10,... | collective-permute-start | bytes 221192 | tf_op jit(solution)/shard_map/ppermute | solution.py:61
  191.3 15.9 %all-to-all-start = ((bf16[64,8,384]{2,1,0:T(8,128)(2,1)}), bf16[64,8,384]{2,1,0:T(8,128)(2,1)S(1)}, u32[]{:S(2)}, u32[]{:S(2)}) async-start(bf16[64,8,384]{2,1,0:T(8,128)(2,1)} %bitcast.56), calls=%async_computation | async-start | bytes 786432 | tf_op jit(solution)/shard_map/all_to_all | solution.py:65
  (43 other events, 264.6 us)
where the time goes:
time: 212 us; the launch traced here: 210 us
  Pallas kernels  87.4 us (41%)
  starting transfers between devices  61.4 us (29%)
  waiting for transfers between devices  29.1 us (14%)
  local copies, waits for them, and re-layouts  17 us (8%)
  matrix products  7.27 us (3%)
  other arithmetic  6.65 us (3%)
    pallas_call x12, Pallas kernels, call(): pl.pallas_call(body, out_shape=out_shape, grid_spec=spec, input_output_al...  87.4 us
    ppermute x40, starting transfers between devices, send(): lax.ppermute(block, DEV, [(flat(*p), flat(*move(*p))) for p in PLACES])  55.3 us
    ppermute x40, waiting for transfers between devices, send(): lax.ppermute(block, DEV, [(flat(*p), flat(*move(*p))) for p in PLACES])  29.1 us
    unnamed x70, local copies, waits for them, and re-layouts  15.1 us
    dot_general x2, matrix products, dot(): return lax.dot_general(a, b, dims, preferred_element_type=f32)  7.27 us
    all_to_all x1, starting transfers between devices, exchange(): lax.all_to_all(blocks, DEV, 0, 0, axis_index_groups=groups, tiled=True)  6.04 us
  transfers between devices with their start and end apart: 41, of which 10 were waited for; matrix products, arithmetic and copies ran while one was open for 11% of the time, Pallas kernels for 27%

commit v1 on v0

--- a/solution.py
+++ b/solution.py
@@ -75,7 +75,7 @@
     return lax.dot_general(a, b, dims, preferred_element_type=f32)
 
 
-def call(body, out_shape, scalars, arrays, in_specs=None, out_specs=None, grid=(), scratch=(), cost=0, aliases=None):
+def call(body, out_shape, scalars, arrays, in_specs=None, out_specs=None, grid=(), scratch=(), cost=0, aliases=None, limit=60):
     whole = pl.BlockSpec(memory_space=pltpu.VMEM)
     many = isinstance(out_shape, (list, tuple))
     if in_specs is None:
@@ -95,7 +95,7 @@
         out_shape=out_shape,
         grid_spec=spec,
         input_output_aliases=aliases or {},
-        compiler_params=pltpu.CompilerParams(vmem_limit_bytes=60 * 2**20),
+        compiler_params=pltpu.CompilerParams(vmem_limit_bytes=limit * 2**20),
         cost_estimate=pl.CostEstimate(flops=cost, bytes_accessed=moved, transcendentals=0),
     )(jnp.stack(scalars).astype(jnp.int32), *arrays)
 
@@ -120,83 +120,104 @@
     return jnp.concatenate([jnp.where(first, own, across), jnp.where(first, across, own)], axis=0)
 
 
-def unit_kernel(rows, extra, pairs, at_ref, *refs):
-    blocks, refs = refs[: 2 * pairs], refs[2 * pairs :]
-    turned_head, head = refs[0], refs[1]
-    (feats, proj), outs = refs[-2:], refs[-5:-2]
+def put_units(feats, turned_head, proj, turned, norm):
     width = turned_head.shape[0]
     quarter = width // 4
-    second = at_ref[0]
-    step = pl.program_id(0)
-    for p in range(pairs):
-        own, across = blocks[2 * p], blocks[2 * p + 1]
-
-        @pl.when(step == p)
-        def _():
-            feats[...] = in_pair(own, across, second, rows)
-            if extra:
-                first = second == 0
-                sides = own[rows:, :rows], across[rows:, :rows]
-                outs[2][0, width:, :rows] = jnp.where(first, sides[0], sides[1])
-                outs[2][0, width:, rows:] = jnp.where(first, sides[1], sides[0])
-
-    total = jnp.zeros((1, 2 * rows), f32)
+    total = jnp.zeros((1, feats.shape[0]), f32)
     for m in range(4):
         span = slice(m * quarter, (m + 1) * quarter)
         part = dot(turned_head[span], feats[...], NT)
         proj[span] = part
         total = total + jnp.sum(part * part, axis=0, keepdims=True)
     length = jnp.sqrt(total + epsilon)
-    outs[1][...] = length
+    norm[...] = length
     inverse = 1.0 / length
     for m in range(4):
         span = slice(m * quarter, (m + 1) * quarter)
-        unit = (proj[span] * inverse).astype(b16)
-        outs[0][span] = unit
-        if extra:
-            outs[2][0, span] = unit
-    if extra:
-        outs[0][width:] = outs[2][0, width:]
-    else:
-        part = dot(feats[...], head[...], NN)
-        total = jnp.sum(part * part, axis=1, keepdims=True)
-        outs[2][...] = (part * (1.0 / jnp.sqrt(total + epsilon))).astype(b16)
-
-
-def units(pairs, heads, second, places, rows, extra, carried):
-    width = heads[0].shape[0]
+        turned[span] = (proj[span] * inverse).astype(b16)
+
+
+def img_unit_kernel(at_ref, feats, turned_head, head, turned, norm, unit, proj):
+    put_units(feats, turned_head, proj, turned, norm)
+    part = dot(feats[...], head[...], NN)
+    total = jnp.sum(part * part, axis=1, keepdims=True)
+    unit[...] = (part * (1.0 / jnp.sqrt(total + epsilon))).astype(b16)
+
+
+def img_units(feats, turned_head, head, rows):
+    count, width = feats.shape
+    tile = 2 * rows
+    whole = pl.BlockSpec(head.shape, lambda i, at: (0, 0))
+    return call(
+        img_unit_kernel,
+        [
+            jax.ShapeDtypeStruct((width, count), b16),
+            jax.ShapeDtypeStruct((1, count), f32),
+            jax.ShapeDtypeStruct((count, width), b16),
+        ],
+        [jnp.int32(0)],
+        [feats, turned_head, head],
+        in_specs=[pl.BlockSpec((tile, width), lambda i, at: (i, 0)), whole, whole],
+        out_specs=[
+            pl.BlockSpec((width, tile), lambda i, at: (0, i)),
+            pl.BlockSpec((1, tile), lambda i, at: (0, i)),
+            pl.BlockSpec((tile, width), lambda i, at: (i, 0)),
+        ],
+        grid=(4,),
+        scratch=[pltpu.VMEM((width, tile), f32)],
+        cost=4 * count * width * width,
+        limit=24,
+    )
+
+
+def unit_kernel(rows, pairs, at_ref, *refs):
+    blocks, turned_head = refs[: 2 * pairs], refs[2 * pairs]
+    turned, norm, alone, feats, proj = refs[-5:]
+    width = turned_head.shape[0]
+    second = at_ref[0]
+    step = pl.program_id(0)
+    for p in range(pairs):
+        own, across = blocks[2 * p], blocks[2 * p + 1]
+
+        @pl.when(step == p)
+        def _():
+            feats[...] = in_pair(own, across, second, rows)
+            first = second == 0
+            sides = own[rows:, :rows], across[rows:, :rows]
+            alone[0, width:, :rows] = jnp.where(first, sides[0], sides[1])
+            alone[0, width:, rows:] = jnp.where(first, sides[1], sides[0])
+
+    put_units(feats, turned_head, proj, turned, norm)
+    turned[width:] = alone[0, width:]
+    alone[0, :width] = turned[:width]
+
+
+def units(pairs, turned_head, second, places, rows, carried):
+    width = turned_head.shape[0]
     tile = 2 * rows
     whole = lambda a: pl.BlockSpec(a.shape, lambda i, at: (0, 0))
-    out = [
-        jax.ShapeDtypeStruct((width + extra, 8 * rows), b16),
-        jax.ShapeDtypeStruct((1, 8 * rows), f32),
-    ]
-    steps = [
-        pl.BlockSpec((width + extra, tile), lambda i, at: (0, at[1 + i])),
-        pl.BlockSpec((1, tile), lambda i, at: (0, at[1 + i])),
-    ]
-    if extra:
-        out.append(jax.ShapeDtypeStruct((len(pairs), width + extra, tile), b16))
-        steps.append(pl.BlockSpec((1, width + extra, tile), lambda i, at: (i, 0, 0)))
-        heads = [heads[0], heads[0]]
-    else:
-        out.append(jax.ShapeDtypeStruct((8 * rows, width), b16))
-        steps.append(pl.BlockSpec((tile, width), lambda i, at: (at[1 + i], 0)))
-    last = pl.BlockSpec(memory_space=pl.ANY) if extra else whole(heads[1])
     blocks = [block for pair in pairs for block in pair]
     return call(
-        lambda *refs: unit_kernel(rows, extra, len(pairs), *refs),
-        out,
+        lambda *refs: unit_kernel(rows, len(pairs), *refs),
+        [
+            jax.ShapeDtypeStruct((width + PAD, 8 * rows), b16),
+            jax.ShapeDtypeStruct((1, 8 * rows), f32),
+            jax.ShapeDtypeStruct((len(pairs), width + PAD, tile), b16),
+        ],
         [second, *places],
-        [*blocks, *heads, *carried],
-        in_specs=[whole(a) for a in [*blocks, heads[0]]]
-        + [last]
+        [*blocks, turned_head, *carried],
+        in_specs=[whole(a) for a in [*blocks, turned_head]]
         + [pl.BlockSpec(memory_space=pl.ANY)] * len(carried),
-        out_specs=steps,
+        out_specs=[
+            pl.BlockSpec((width + PAD, tile), lambda i, at: (0, at[1 + i])),
+            pl.BlockSpec((1, tile), lambda i, at: (0, at[1 + i])),
+            pl.BlockSpec((1, width + PAD, tile), lambda i, at: (i, 0, 0)),
+        ],
         grid=(len(pairs),),
         scratch=[pltpu.VMEM((tile, width), b16), pltpu.VMEM((width, tile), f32)],
-        cost=2 * tile * width * width * len(pairs) * (1 if extra else 2),
-        aliases={len(blocks) + 3 + n: n for n in range(len(carried))},
+        cost=2 * tile * width * width * len(pairs),
+        aliases={len(blocks) + 2 + n: n for n in range(len(carried))},
+        limit=24,
     )
 
 
@@ -303,7 +324,7 @@
 def own_kernel(rows, groups, at_ref, bias_ref, img, turned, txt, *refs):
     chunks = ring_order(*refs[:2])
     other_slopes, other_sum, up = refs[2:5]
-    outs, (by_img, held, both, total) = refs[5:13], refs[13:]
+    out, by_img, held, both, total = refs[5:]
     step = pl.program_id(0)
     width = img.shape[1]
     tile = 2 * rows
@@ -330,18 +351,13 @@
         slab = width // 8
         sums = logit_scale * jnp.sum(by_img[...].T, axis=0, keepdims=True) + other_sum[...]
         figures = split_rows(sums, sums.shape[1])
-        own = at_ref[2] == 0
-        for d in range(4):
-            at = pl.multiple_of((at_ref[1] + d) % 4 * (2 * slab), 2 * slab)
-            low, high = total[pl.ds(at, slab)], total[pl.ds(at + slab, slab)]
-            outs[2 * d][:slab] = jnp.where(own, low, high).astype(b16)
-            outs[2 * d][slab:] = figures
-            outs[2 * d + 1][:slab] = jnp.where(own, high, low).astype(b16)
-            outs[2 * d + 1][slab:] = figures
+        for e in range(8):
+            out[e, :slab] = total[e * slab : (e + 1) * slab].astype(b16)
+            out[e, slab:] = figures
 
 
 def own_tile(
-    img, turned, txt, chunks, other_slopes, other_sum, group_bias, place, ring, second, rows
+    img, turned, txt, chunks, other_slopes, other_sum, group_bias, place, rows
 ):
     count, width = img.shape
     tile = 2 * rows
@@ -349,11 +365,11 @@
     slab = width // 8
     whole = lambda a: pl.BlockSpec(a.shape, lambda i, at: (0, 0))
     stack = lambda a: pl.BlockSpec(a.shape, lambda i, at: (0, 0, 0))
-    piece = jax.ShapeDtypeStruct((slab + PAD, count), b16)
-    out = call(
+    pieces = jax.ShapeDtypeStruct((8, slab + PAD, count), b16)
+    return call(
         lambda *refs: own_kernel(rows, group_bias.shape[0], *refs),
-        [jax.ShapeDtypeStruct((height, count), b16)] + [piece] * 8,
-        [place, ring, second],
+        [jax.ShapeDtypeStruct((height, count), b16), pieces],
+        [place],
         [group_bias, img, turned, txt, *chunks, other_slopes, other_sum],
         in_specs=[
             pl.BlockSpec(memory_space=pltpu.SMEM),
@@ -363,7 +379,7 @@
         ]
         + [stack(chunk) for chunk in chunks]
         + [pl.BlockSpec((1, count, tile), lambda i, at: (i, 0, 0)), whole(other_sum)],
-        out_specs=[pl.BlockSpec((height, tile), lambda i, at: (0, i))] + [whole(piece)] * 8,
+        out_specs=[pl.BlockSpec((height, tile), lambda i, at: (0, i)), stack(pieces)],
         grid=(4,),
         scratch=[
             pltpu.VMEM((count, min(128, tile)), f32),
@@ -373,7 +389,6 @@
         ],
         cost=8 * width * count * count,
     )
-    return out[0], out[1:]
 
 
 def sum_into(out, terms):
@@ -421,70 +436,72 @@
     )
 
 
-def grad_kernel(rows, sizes, at_ref, *refs):
-    part, grad = refs[-2:]
-    outs = refs[-6:-2]
-    start = 0
-    for n in range(2):
-        mine = refs[start : start + sizes[n] + 10]
-        start += sizes[n] + 10
-        terms, mine = mine[: sizes[n]], mine[sizes[n] :]
-        unit, norm, blocks = mine[0], mine[1], mine[2:]
-        ring_at, second = at_ref[4 * n], at_ref[4 * n + 1]
-        slab = unit.shape[0]
-        up, inner = terms[0][:slab].astype(f32), joined(terms[0][slab:])
-        for term in terms[1:]:
-            up, inner = up + term[:slab].astype(f32), inner + joined(term[slab:])
-        up = logit_scale * up - unit[...].astype(f32) * inner
-        grad[n] = (up * (1.0 / norm[...])).astype(b16)
-        own, give = outs[2 * n : 2 * n + 2]
-        for ring in range(4):
-            low = grad[n, :, (2 * ring) * rows : (2 * ring + 1) * rows]
-            high = grad[n, :, (2 * ring + 1) * rows : (2 * ring + 2) * rows]
-            own[ring] = jnp.where(second == 0, low, high)
-            give[ring] = jnp.where(second == 0, high, low)
-        total = None
-        for d in range(4):
-            cols = grad[n, :, aligned((ring_at + d) % 4, 2 * rows)]
-            term = dot(cols, in_pair(blocks[2 * d], blocks[2 * d + 1], second, rows), NN)
-            total = term if total is None else total + term
-        part[n * slab : (n + 1) * slab] = total.astype(b16)
-
-
-def gradients(towers, rows):
-    arrays, specs, scalars = [], [], []
+def put_gradient(up, inner, unit, norm, second, grad, own, give, rows):
+    up = logit_scale * up - unit[...].astype(f32) * inner
+    grad[...] = (up * (1.0 / norm[...])).astype(b16)
+    for ring in range(4):
+        low = grad[:, (2 * ring) * rows : (2 * ring + 1) * rows]
+        high = grad[:, (2 * ring + 1) * rows : (2 * ring + 2) * rows]
+        own[ring] = jnp.where(second == 0, low, high)
+        give[ring] = jnp.where(second == 0, high, low)
+
+
+def img_grad_kernel(rows, at_ref, got, unit, norm, feats, own, give, part, grad):
+    slab = unit.shape[0]
+    up, inner = got[0, :slab].astype(f32), joined(got[0, slab:])
+    for n in range(1, 8):
+        up, inner = up + got[n, :slab].astype(f32), inner + joined(got[n, slab:])
+    put_gradient(up, inner, unit, norm, at_ref[1], grad, own, give, rows)
+    part[...] = dot(grad[...], feats[...], NN).astype(b16)
+
+
+def txt_grad_kernel(rows, at_ref, *refs):
+    terms, unit, norm, blocks, (own, give, part, grad) = (
+        refs[:5], refs[5], refs[6], refs[7:15], refs[15:]
+    )
+    slab = unit.shape[0]
+    up, inner = terms[0][:slab].astype(f32), joined(terms[0][slab:])
+    for term in terms[1:]:
+        up, inner = up + term[:slab].astype(f32), inner + joined(term[slab:])
+    put_gradient(up, inner, unit, norm, at_ref[1], grad, own, give, rows)
+    total = None
+    for d in range(4):
+        cols = grad[:, aligned((at_ref[2] + d) % 4, 2 * rows)]
+        term = dot(cols, in_pair(blocks[2 * d], blocks[2 * d + 1], at_ref[1], rows), NN)
+        total = term if total is None else total + term
+    part[...] = total.astype(b16)
+
+
+def gradient(kernel, place, second, ring, terms, unit, norm, feats, rows):
+    width = feats[0].shape[1]
+    slab, count = width // 8, 8 * rows
     whole = lambda a: pl.BlockSpec(a.shape, lambda i, at: (0,) * len(a.shape))
-    for n, (ring, second, place, terms, unit, norm, blocks) in enumerate(towers):
-        width = blocks[0].shape[1]
-        slab, count = width // 8, 8 * rows
-        mine = lambda height, n=n: pl.BlockSpec((height, count), lambda i, at: (at[4 * n + 2], 0))
-        for term in terms:
-            arrays.append(term[0] if isinstance(term, tuple) else term)
-            specs.append(mine(slab + PAD) if isinstance(term, tuple) else whole(term))
-        arrays += [unit, norm, *blocks]
-        specs += [mine(slab), whole(norm)] + [whole(a) for a in blocks]
-        scalars += [ring, second, place, place]
+    mine = lambda height: pl.BlockSpec((height, count), lambda i, at: (at[0], 0))
     block = jax.ShapeDtypeStruct((4, slab, rows), b16)
-    term = jax.ShapeDtypeStruct((2 * slab, width), b16)
+    part = jax.ShapeDtypeStruct((slab, width), b16)
     return call(
-        lambda *refs: grad_kernel(rows, [len(tower[3]) for tower in towers], *refs),
-        [block] * 4 + [term],
-        scalars,
-        arrays,
-        in_specs=specs,
-        out_specs=[whole(block)] * 4 + [whole(term)],
+        lambda *refs: kernel(rows, *refs),
+        [block, block, part],
+        [place, second, ring],
+        [term[0] if isinstance(term, tuple) else term for term in terms] + [unit, norm, *feats],
+        in_specs=[mine(slab + PAD) if isinstance(term, tuple) else whole(term) for term in terms]
+        + [mine(slab), whole(norm)]
+        + [whole(a) for a in feats],
+        out_specs=[whole(block), whole(block), whole(part)],
         grid=(1,),
-        scratch=[pltpu.VMEM((2, slab, count), b16)],
-        cost=4 * slab * count * width,
-    )
-
-
-def pick_kernel(at_ref, mine, theirs, out):
-    width = mine.shape[1]
+        scratch=[pltpu.VMEM((slab, count), b16)],
+        cost=2 * slab * count * width,
+    )
+
+
+def pick_kernel(at_ref, img, txt, other_img, other_txt, out):
+    width = img.shape[1]
     slots = out.shape[0]
     own = width // 128
-    third = mine.shape[0] // 3
-    part = (mine[...].astype(f32) + theirs[...].astype(f32)).astype(b16)
+    third = 2 * img.shape[0] // 3
+    img = img[...].astype(f32) + other_img[...].astype(f32)
+    txt = txt[...].astype(f32) + other_txt[...].astype(f32)
+    part = jnp.concatenate([img, txt], axis=0).astype(b16)
     slot = lax.broadcasted_iota(jnp.int32, (slots, 1), 0)
     feature = lax.broadcasted_iota(jnp.int32, (slots, width), 1)
     base = (slot // 8 * 2 + at_ref[0]) * own
@@ -498,14 +515,14 @@
     out[:, 3 * third :] = rest.astype(b16)
 
 
-def picked(core, mine, theirs):
-    both, width = mine.shape
+def picked(core, parts):
+    slab, width = parts[0].shape
     return call(
         pick_kernel,
-        jax.ShapeDtypeStruct((64 * 8, both * 4 // 3), b16),
+        jax.ShapeDtypeStruct((64 * 8, slab * 8 // 3), b16),
         [core],
-        [mine, theirs],
-        cost=4 * 512 * width * both,
+        parts,
+        cost=8 * 512 * width * slab,
     )
 
 
@@ -564,43 +581,28 @@
     figures = jnp.stack([text_lang, partner // 128, partner % 128]).astype(b16)
     figures = jnp.pad(figures, ((0, PAD - 3), (0, width - rows)))
     text_rows = jnp.concatenate([text_feat, figures], axis=0)
-    moves = (img_move, txt_move)
-    own = (image_feat, text_rows)
-    across = [send(own[n], moves[n](0, 1)) for n in range(2)]
-    before = [send(own[n], moves[n](1, 0)) for n in range(2)]
-    after = [send(own[n], moves[n](3, 0)) for n in range(2)]
-    *across, turned_txt = together(across + [text_head.T])
-    across_after = [send(across[n], moves[n](3, 0)) for n in range(2)]
-    across_before = [send(across[n], moves[n](1, 0)) for n in range(2)]
-    *got, turned_img = together(across_after + before + after + across + [image_head.T])
-    across_after, before, after, across = [got[2 * n : 2 * n + 2] for n in range(4)]
-    far = [send(before[n], moves[n](1, 0)) for n in range(2)]
-    across_far = [send(across_after[n], moves[n](3, 0)) for n in range(2)]
-    pairs = [
-        [(own[n], across[n]), (after[n], across_after[n]), (before[n], across_before[n])]
-        for n in range(2)
-    ]
-    near_y, near_z = ([(ring + d) % 4 for d in (0, 1, 3)] for ring in (y, z))
-    far_y, far_z = [(y + 2) % 4], [(z + 2) % 4]
-    img_heads = [turned_img, image_head]
-    *txt_made, chunks = units(pairs[1], [turned_txt], hi, near_y, rows, PAD, ())
+    img_feats = exchange(jnp.broadcast_to(image_feat[None], (8, rows, width)), IMG_GROUPS)
+    img_feats = img_feats.reshape(8 * rows, width)
+    across = send(text_rows, txt_move(0, 1))
+    before = send(text_rows, txt_move(1, 0))
+    after = send(text_rows, txt_move(3, 0))
+    across, turned_txt = together([across, text_head.T])
+    across_after = send(across, txt_move(3, 0))
+    across_before = send(across, txt_move(1, 0))
+    across_after, before, after, across, turned_img = together(
+        [across_after, before, after, across, image_head.T]
+    )
+    far = send(before, txt_move(1, 0))
+    across_far = send(across_after, txt_move(3, 0))
+    pairs = [(text_rows, across), (after, across_after), (before, across_before)]
+    near_y, far_y = [(y + d) % 4 for d in (0, 1, 3)], [(y + 2) % 4]
+    *made, chunks = units(pairs, turned_txt, hi, near_y, rows, ())
     others = [send(chunks, core_move)]
-    img_made = units(pairs[0], img_heads, lo, near_z, rows, 0, ())
-    got = together(far + across_far + list(img_made))
-    far, across_far, img_made = got[0:2], got[2:4], got[4:]
-    unit_txt, norm_txt, chunks = units(
-        [(far[1], across_far[1])], [turned_txt], hi, far_y, rows, PAD, txt_made
-    )
+    unit_txt, norm_txt, chunks = units([(far, across_far)], turned_txt, hi, far_y, rows, made)
     others.append(send(chunks, core_move))
-    turned_units, norm_img, unit_img = units(
-        [(far[0], across_far[0])], img_heads, lo, far_z, rows, 0, img_made
-    )
-    blocks = [
-        [
-            own[n], across[n], after[n], across_after[n],
-            far[n], across_far[n], before[n], across_before[n],
-        ]
-        for n in range(2)
+    turned_units, norm_img, unit_img = img_units(img_feats, turned_img, image_head, rows)
+    txt_blocks = [
+        text_rows, across, after, across_after, far, across_far, before, across_before
     ]
 
     other_slopes, other_sum, other_up = other_tile(
@@ -609,50 +611,47 @@
     back = send(other_up, core_move)
     text_up, img_terms = own_tile(
         unit_img, turned_units, unit_txt, others, other_slopes, other_sum, group_bias,
-        place % 16, z, lo, rows,
-    )
-
-    def txt_slab(d, e):
+        place % 16, rows,
+    )
+    img_terms = exchange(img_terms, IMG_GROUPS)
+
+    def slab_terms(d, e):
         at = (y + d) % 4 * 2 + (hi + e) % 2
         return [(text_up, at), (back, at)]
 
-    def img_slab(d, e):
-        return [img_terms[2 * d + e]]
-
-    slabs = (img_slab, txt_slab)
-    txt_far, txt_across_far, txt_across_after = sums(
-        [txt_slab(2, 0), txt_slab(2, 1), txt_slab(1, 1)], rows
-    )
-    far = [send(img_terms[4], img_move(1, 0)), send(txt_far, txt_move(1, 0))]
-    across_far = [send(img_terms[5], img_move(3, 0)), send(txt_across_far, txt_move(3, 0))]
-    got = together(far + across_far + [img_terms[3], txt_across_after])
-    far, across_far = got[0:2], got[2:4]
-    across_before = [send(got[4 + n], moves[n](1, 0)) for n in range(2)]
-    joint = sums(
-        [slabs[n](3, 1) + [across_far[n]] for n in range(2)]
-        + [slabs[n](1, 0) + [far[n]] for n in range(2)]
-        + [txt_slab(3, 0)],
-        rows,
-    )
-    across_after = [send(joint[n], moves[n](3, 0)) for n in range(2)]
-    got = together(across_before + across_after + [*joint[2:], img_terms[6]])
-    across_before, across_after = got[0:2], got[2:4]
-    before = [send(got[4 + n], moves[n](1, 0)) for n in range(2)]
-    after = [send(got[7], img_move(3, 0)), send(got[6], txt_move(3, 0))]
-    joint = sums([slabs[n](0, 1) + [across_before[n], across_after[n]] for n in range(2)], rows)
-    across = [send(joint[n], moves[n](0, 1)) for n in range(2)]
-    final = [slabs[n](0, 0) + [before[n], after[n], across[n]] for n in range(2)]
-
-    img_own, img_give, txt_own, txt_give, part = gradients(
-        [
-            (z, lo, z * 2 + lo, final[0], turned_units, norm_img, blocks[0]),
-            (y, hi, y * 2 + hi, final[1], unit_txt, norm_txt, blocks[1]),
-        ],
-        rows,
-    )
+    far, across_far, across_after = sums(
+        [slab_terms(2, 0), slab_terms(2, 1), slab_terms(1, 1)], rows
+    )
+    far = send(far, txt_move(1, 0))
+    across_far = send(across_far, txt_move(3, 0))
+    far, across_far, across_after = together([far, across_far, across_after])
+    across_before = send(across_after, txt_move(1, 0))
+    across_after, before, after = sums(
+        [slab_terms(3, 1) + [across_far], slab_terms(1, 0) + [far], slab_terms(3, 0)], rows
+    )
+    across_after = send(across_after, txt_move(3, 0))
+    across_before, across_after, before, after = together(
+        [across_before, across_after, before, after]
+    )
+    before = send(before, txt_move(1, 0))
+    after = send(after, txt_move(3, 0))
+    (across,) = sums([slab_terms(0, 1) + [across_before, across_after]], rows)
+    across = send(across, txt_move(0, 1))
+
+    img_own, img_give, img_part = gradient(
+        img_grad_kernel, z * 2 + lo, lo, z, [img_terms], turned_units, norm_img, [img_feats], rows
+    )
+    txt_own, txt_give, txt_part = gradient(
+        txt_grad_kernel, y * 2 + hi, hi, y, slab_terms(0, 0) + [before, after, across],
+        unit_txt, norm_txt, txt_blocks, rows,
+    )
+    img_theirs = send(img_part, core_move)
+    txt_theirs = send(txt_part, core_move)
     img_got = send(img_give, img_move(0, 1))
     txt_got = send(txt_give, txt_move(0, 1))
-    heads, img_got, txt_got = together([picked(core, part, send(part, core_move)), img_got, txt_got])
+    heads, img_got, txt_got = together(
+        [picked(core, [img_part, txt_part, img_theirs, txt_theirs]), img_got, txt_got]
+    )
     heads = exchange(heads.reshape(64, 8, -1), CHIP_GROUPS)
     head_shape = jax.ShapeDtypeStruct((width // 128, width), f32)
     image_head_grad, text_head_grad = call(head_kernel, [head_shape] * 2, [core], [heads])

time: 212 us -> 200 us (0.943)
  Pallas kernels: 87.4 us -> 75.8 us
  local copies, waits for them, and re-layouts: 17 us -> 28.3 us
  starting transfers between devices: 61.4 us -> 54.1 us
  waiting for transfers between devices: 29.1 us -> 24.5 us
    ppermute x40 -> x27, starting transfers between devices: 55.3 us -> 39.3 us  [send(): lax.ppermute(block, DEV, [(flat(*p), flat(*move(*p))) for p in PLACES])]
    pallas_call x12, Pallas kernels: 87.4 us -> 75.8 us  [call(): pl.pallas_call(body, out_shape=out_shape, grid_spec=spec, input_output_al...]
    unnamed x70 -> x48, local copies, waits for them, and re-layouts: 15.1 us -> 24.2 us
    all_to_all x1 -> x3, starting transfers between devices: 6.04 us -> 14.8 us  [exchange(): lax.all_to_all(blocks, DEV, 0, 0, axis_index_groups=groups, tiled=True)]
    ppermute x40 -> x27, waiting for transfers between devices: 29.1 us -> 24.5 us  [send(): lax.ppermute(block, DEV, [(flat(*p), flat(*move(*p))) for p in PLACES])]
    broadcast_in_dim x0 -> x1, local copies, waits for them, and re-layouts: none -> 2.75 us  [shards(): jnp.broadcast_to(image_feat[None], (8, rows, width))]
  transfers between devices with their start and end apart: 41 -> 30, of which waited for: 10 -> 8; matrix products, arithmetic and copies ran while one was open for 11% -> 13% of each run, Pallas kernels for 27% -> 31%
where the time goes in v1:
time: 200 us; the launch traced here: 196 us
  Pallas kernels  75.8 us (38%)
  starting transfers between devices  54.1 us (27%)
  local copies, waits for them, and re-layouts  28.3 us (14%)
  waiting for transfers between devices  24.5 us (12%)
  matrix products  7.75 us (4%)
  other arithmetic  5.18 us (3%)
    pallas_call x12, Pallas kernels, call(): pl.pallas_call(body, out_shape=out_shape, grid_spec=spec, input_output_al...  75.8 us
    ppermute x27, starting transfers between devices, send(): lax.ppermute(block, DEV, [(flat(*p), flat(*move(*p))) for p in PLACES])  39.3 us
    ppermute x27, waiting for transfers between devices, send(): lax.ppermute(block, DEV, [(flat(*p), flat(*move(*p))) for p in PLACES])  24.5 us
    unnamed x48, local copies, waits for them, and re-layouts  24.2 us
    all_to_all x3, starting transfers between devices, exchange(): lax.all_to_all(blocks, DEV, 0, 0, axis_index_groups=groups, tiled=True)  14.8 us
    dot_general x2, matrix products, dot(): return lax.dot_general(a, b, dims, preferred_element_type=f32)  7.75 us
  transfers between devices with their start and end apart: 30, of which 8 were waited for; matrix products, arithmetic and copies ran while one was open for 13% of the time, Pallas kernels for 31%

profile of v1, /device:TPU:1, one launch (start us, length us, event | category | flops | bytes accessed | tf_op | source)
XLA Modules:
  0.0 196.5 jit_solution(16589379503366374033)
XLA Ops:
  2.3 3.4 %collective-permute-start = (bf16[144,1152]{1,0:T(8,128)(2,1)S(1)}, bf16[144,1152]{1,0:T(8,128)(2,1)S(1)}, u32[]{:S(2)}, u32[]{:S(2)}) collective-permute-start(bf16[144,1152]{1,0:T(8,128)(2,1)S(1)} %pad_maximum_fusion.refs_1_.refs_8_), channel_id=1, source_target_pairs={{0,24},{1,25},{2,26},{3,27},{4,28},{5,29},{6,30},{7,31},{8,16},{9,... | collective-permute-start | bytes 995336 | tf_op jit(solution)/shard_map/ppermute | solution.py:61
  5.7 2.7 %broadcast_in_dim.2 = bf16[8,128,1152]{2,1,0:T(8,128)(2,1)} broadcast(bf16[128,1152]{1,0:T(8,128)(2,1)} %param.7), dimensions={1,2} | broadcast | bytes 2654208 | tf_op jit(solution)/shard_map/broadcast_in_dim | solution.py:584
  8.5 5.0 %all-to-all-start = ((bf16[8,128,1152]{2,1,0:T(8,128)(2,1)}), bf16[8,128,1152]{2,1,0:T(8,128)(2,1)}, u32[]{:S(2)}, u32[]{:S(2)}) async-start(bf16[8,128,1152]{2,1,0:T(8,128)(2,1)} %broadcast_in_dim.2), calls=%async_computation | async-start | bytes 4718592 | tf_op jit(solution)/shard_map/all_to_all | solution.py:65
  16.3 4.1 %copy.13 = bf16[1152,1152]{0,1:T(8,128)(2,1)S(1)} copy(bf16[1152,1152]{1,0:T(8,128)(2,1)} %param.10) | data formatting | bytes 5308416 | tf_op args[3]
  22.0 5.2 %copy.14 = bf16[1152,1152]{0,1:T(8,128)(2,1)} copy(bf16[1152,1152]{1,0:T(8,128)(2,1)} %head.1) | data formatting | bytes 5308416 | tf_op args[2]
  27.3 3.2 %collective-permute-done.1.refs_4_.refs_11_ = bf16[144,1152]{1,0:T(8,128)(2,1)} collective-permute-done((bf16[144,1152]{1,0:T(8,128)(2,1)S(1)}, bf16[144,1152]{1,0:T(8,128)(2,1)}, u32[]{:S(2)}, u32[]{:S(2)}) %collective-permute-start.1) | collective-permute-done | bytes 331808 | tf_op jit(solution)/shard_map/ppermute | solution.py:61
  30.5 6.5 %shard_map.103 = (bf16[1168,1024]{1,0:T(8,128)(2,1)S(1)}, f32[1,1024]{1,0:T(1,128)S(1)}, bf16[3,1168,256]{2,1,0:T(8,128)(2,1)}) custom-call(s32[4]{0:T(128)S(1)} %pad_add_fusion.2.refs_0_, bf16[144,1152]{1,0:T(8,128)(2,1)S(1)} %pad_maximum_fusion.refs_1_.refs_8_, bf16[144,1152]{1,0:T(8,128)(2,1)S(1)} %collective-permute-done.refs_2_.refs_9_, ...), custom_call_target="tpu_custom_call" | custom-call | flops 2038431744 | bytes 4644864 | tf_op jit(solution)/shard_map/pallas_call | solution.py:93
  38.5 2.9 %collective-permute-start.7 = (bf16[3,1168,256]{2,1,0:T(8,128)(2,1)}, bf16[3,1168,256]{2,1,0:T(8,128)(2,1)}, u32[]{:S(2)}, u32[]{:S(2)}) collective-permute-start(bf16[3,1168,256]{2,1,0:T(8,128)(2,1)} %get-tuple-element.61), channel_id=1, source_target_pairs={{0,1},{1,0},{2,3},{3,2},{4,5},{5,4},{6,7},{7,6},{8,9},{9,8},{10,11... | collective-permute-start | bytes 5382152 | tf_op jit(solution)/shard_map/ppermute | solution.py:61
  41.5 2.6 %collective-permute-start.5 = (bf16[144,1152]{1,0:T(8,128)(2,1)}, bf16[144,1152]{1,0:T(8,128)(2,1)S(1)}, u32[]{:S(2)}, u32[]{:S(2)}) collective-permute-start(bf16[144,1152]{1,0:T(8,128)(2,1)} %collective-permute-done.1.refs_4_.refs_11_), channel_id=1, source_target_pairs={{0,6},{1,7},{2,0},{3,1},{4,2},{5,3},{6,4},{7,5},{8,14},{9,15},{10,... | collective-permute-start | bytes 995336 | tf_op jit(solution)/shard_map/ppermute | solution.py:61
  44.2 8.1 %collective-permute-done.4.refs_1_.refs_12_ = bf16[144,1152]{1,0:T(8,128)(2,1)S(1)} collective-permute-done((bf16[144,1152]{1,0:T(8,128)(2,1)}, bf16[144,1152]{1,0:T(8,128)(2,1)S(1)}, u32[]{:S(2)}, u32[]{:S(2)}) %collective-permute-start.4) | collective-permute-done | bytes 331808 | tf_op jit(solution)/shard_map/ppermute | solution.py:61
  54.2 2.6 %shard_map.104 = (bf16[1168,1024]{1,0:T(8,128)(2,1)S(1)}, f32[1,1024]{1,0:T(1,128)S(1)}, bf16[1,1168,256]{2,1,0:T(8,128)(2,1)}) custom-call(s32[2]{0:T(128)S(1)} %pad_add_fusion.1.refs_0_, bf16[144,1152]{1,0:T(8,128)(2,1)S(1)} %collective-permute-done.4.refs_1_.refs_12_, ...), custom_call_target="tpu_custom_call", output_to_operand_aliasing={{0}: (4, {}), {1}: (5, {})} | custom-call | flops 679477248 | bytes 5713920 | tf_op jit(solution)/shard_map/pallas_call | solution.py:93
  63.2 9.4 %shard_map.102 = (bf16[1152,1024]{1,0:T(8,128)(2,1)S(1)}, f32[1,1024]{1,0:T(1,128)S(1)}, bf16[1024,1152]{1,0:T(8,128)(2,1)S(1)}) custom-call(s32[1]{0:T(128)} %constant.209.clone.1.at_ref, bf16[1024,1152]{1,0:T(8,128)(2,1)} %bitcast.5.feats.refs_4_, bf16[1152,1152]{1,0:T(8,128)(2,1)S(1)} %bitcast.49, bf16[1152,1152]{1,0:T(8,128)(2,1)S(1)} %copy-done.3), custom_call_target="tpu_custom_call" | custom-call | flops 5435817984 | bytes 7667712 | tf_op jit(solution)/shard_map/pallas_call | solution.py:93
  76.9 13.6 %shard_map.105 = (bf16[4,1024,256]{2,1,0:T(8,128)(2,1)}, f32[1,1024]{1,0:T(1,128)}, bf16[1280,1024]{1,0:T(8,128)(2,1)}) custom-call(s32[2]{0:T(128)} %pad_add_fusion.3.refs_0_, f32[32]{0:T(128)} %refs_1_.3, bf16[1024,1152]{1,0:T(8,128)(2,1)} %copy-done.12, bf16[1152,1024]{1,0:T(8,128)(2,1)} %copy-done.5, ...), custom_call_target="tpu_custom_call" | custom-call | flops 4831838208 | bytes 7110784 | tf_op jit(solution)/shard_map/pallas_call | solution.py:93
  90.6 19.0 %shard_map.106 = (bf16[1280,1024]{1,0:T(8,128)(2,1)}, bf16[8,160,1024]{2,1,0:T(8,128)(2,1)}) custom-call(s32[1]{0:T(128)} %bitcast.4.refs_0_, f32[32]{0:T(128)} %refs_1_.3, bf16[1024,1152]{1,0:T(8,128)(2,1)} %copy-done.12, bf16[1152,1024]{1,0:T(8,128)(2,1)} %copy-done.5, bf16[1168,1024]{1,0:T(8,128)(2,1)} %copy-done.2, ...), custom_call_target="tpu_custom_call" | custom-call | flops 9663676416 | bytes 11604096 | tf_op jit(solution)/shard_map/pallas_call | solution.py:93
  109.5 5.1 %all-to-all-start.1 = ((bf16[8,160,1024]{2,1,0:T(8,128)(2,1)}), bf16[8,160,1024]{2,1,0:T(8,128)(2,1)}, u32[]{:S(2)}, u32[]{:S(2)}) async-start(bf16[8,160,1024]{2,1,0:T(8,128)(2,1)} %get-tuple-element.65), calls=%async_computation.1 | async-start | bytes 5242880 | tf_op jit(solution)/shard_map/all_to_all | solution.py:65
  115.4 3.1 %shard_map.108 = (bf16[160,1024]{1,0:T(8,128)(2,1)}, bf16[160,1024]{1,0:T(8,128)(2,1)}, bf16[160,1024]{1,0:T(8,128)(2,1)}) custom-call(s32[7]{0:T(128)} %stack.133.refs_0_, bf16[1280,1024]{1,0:T(8,128)(2,1)} %get-tuple-element.68.refs_1_.refs_3_.refs_5_.refs_4_.refs_7_, bf16[1280,1024]{1,0:T(8,128)(2,1)} %collective-permute-done.9.refs_2_.refs_4_.refs_6_.refs_5_.refs_8_, ...), custom_call_target="tpu_custom_call" | custom-call | bytes 15728640 | tf_op jit(solution)/shard_map/pallas_call | solution.py:93
  118.5 2.7 %collective-permute-start.11 = (bf16[160,1024]{1,0:T(8,128)(2,1)}, bf16[160,1024]{1,0:T(8,128)(2,1)S(1)}, u32[]{:S(2)}, u32[]{:S(2)}) collective-permute-start(bf16[160,1024]{1,0:T(8,128)(2,1)} %get-tuple-element.71), channel_id=1, source_target_pairs={{0,6},{1,7},{2,0},{3,1},{4,2},{5,3},{6,4},{7,5},{8,14},{9,15},{10,... | collective-permute-start | bytes 983048 | tf_op jit(solution)/shard_map/ppermute | solution.py:61
  121.8 6.7 %collective-permute-done.10.refs_6_ = bf16[160,1024]{1,0:T(8,128)(2,1)S(1)} collective-permute-done((bf16[160,1024]{1,0:T(8,128)(2,1)}, bf16[160,1024]{1,0:T(8,128)(2,1)S(1)}, u32[]{:S(2)}, u32[]{:S(2)}) %collective-permute-start.10) | collective-permute-done | bytes 327712 | tf_op jit(solution)/shard_map/ppermute | solution.py:61
  129.9 3.4 %shard_map.109 = (bf16[160,1024]{1,0:T(8,128)(2,1)}, bf16[160,1024]{1,0:T(8,128)(2,1)}, bf16[160,1024]{1,0:T(8,128)(2,1)}) custom-call(s32[7]{0:T(128)} %stack.137.refs_0_, bf16[1280,1024]{1,0:T(8,128)(2,1)} %get-tuple-element.68.refs_1_.refs_3_.refs_5_.refs_4_.refs_7_, bf16[1280,1024]{1,0:T(8,128)(2,1)} %collective-permute-done.9.refs_2_.refs_4_.refs_6_.refs_5_.refs_8_, ...), custom_call_target="tpu_custom_call" | custom-call | bytes 16384000 | tf_op jit(solution)/shard_map/pallas_call | solution.py:93
  136.0 2.4 %collective-permute-done.12.refs_3_ = bf16[160,1024]{1,0:T(8,128)(2,1)S(1)} collective-permute-done((bf16[160,1024]{1,0:T(8,128)(2,1)}, bf16[160,1024]{1,0:T(8,128)(2,1)S(1)}, u32[]{:S(2)}, u32[]{:S(2)}) %collective-permute-start.12) | collective-permute-done | bytes 327712 | tf_op jit(solution)/shard_map/ppermute | solution.py:61
  138.5 2.5 %collective-permute-done.13.refs_4_ = bf16[160,1024]{1,0:T(8,128)(2,1)S(1)} collective-permute-done((bf16[160,1024]{1,0:T(8,128)(2,1)}, bf16[160,1024]{1,0:T(8,128)(2,1)S(1)}, u32[]{:S(2)}, u32[]{:S(2)}) %collective-permute-start.13) | collective-permute-done | bytes 327712 | tf_op jit(solution)/shard_map/ppermute | solution.py:61
  141.8 2.4 %collective-permute-start.15 = (bf16[160,1024]{1,0:T(8,128)(2,1)}, bf16[160,1024]{1,0:T(8,128)(2,1)}, u32[]{:S(2)}, u32[]{:S(2)}) collective-permute-start(bf16[160,1024]{1,0:T(8,128)(2,1)} %get-tuple-element.80), channel_id=1, source_target_pairs={{0,6},{1,7},{2,0},{3,1},{4,2},{5,3},{6,4},{7,5},{8,14},{9,15},{10,... | collective-permute-start | bytes 983048 | tf_op jit(solution)/shard_map/ppermute | solution.py:61
  144.2 2.8 %shard_map.110 = bf16[160,1024]{1,0:T(8,128)(2,1)} custom-call(s32[3]{0:T(128)} %pad_add_fusion.5.refs_0_, bf16[1280,1024]{1,0:T(8,128)(2,1)} %get-tuple-element.68.refs_1_.refs_3_.refs_5_.refs_4_.refs_7_, bf16[1280,1024]{1,0:T(8,128)(2,1)} %collective-permute-done.9.refs_2_.refs_4_.refs_6_.refs_5_.refs_8_, bf16[160,1024]{1,0:T(8,128)(2,1)} %copy-done.14, ...), custom_call_target="tpu_custom_call" | custom-call | bytes 5898240 | tf_op jit(solution)/shard_map/pallas_call | solution.py:93
  149.1 4.9 %shard_map.107 = (bf16[4,144,128]{2,1,0:T(8,128)(2,1)}, bf16[4,144,128]{2,1,0:T(8,128)(2,1)}, bf16[144,1152]{1,0:T(8,128)(2,1)}) custom-call(s32[3]{0:T(128)} %pad_add_fusion.refs_0_, bf16[8,160,1024]{2,1,0:T(8,128)(2,1)} %all-to-all-done.1.refs_1_, bf16[1152,1024]{1,0:T(8,128)(2,1)} %copy-done.5, f32[1,1024]{1,0:T(1,128)} %copy-done.11, ...), custom_call_target="tpu_custom_call" | custom-call | flops 339738624 | bytes 7344128 | tf_op jit(solution)/shard_map/pallas_call | solution.py:93
  154.0 3.5 %collective-permute-start.17 = (bf16[144,1152]{1,0:T(8,128)(2,1)}, bf16[144,1152]{1,0:T(8,128)(2,1)}, u32[]{:S(2)}, u32[]{:S(2)}) collective-permute-start(bf16[144,1152]{1,0:T(8,128)(2,1)} %get-tuple-element.67.img), channel_id=1, source_target_pairs={{0,1},{1,0},{2,3},{3,2},{4,5},{5,4},{6,7},{7,6},{8,9},{9,8},{10,11... | collective-permute-start | bytes 995336 | tf_op jit(solution)/shard_map/ppermute | solution.py:61
  158.3 5.0 %shard_map.111 = (bf16[4,144,128]{2,1,0:T(8,128)(2,1)}, bf16[4,144,128]{2,1,0:T(8,128)(2,1)}, bf16[144,1152]{1,0:T(8,128)(2,1)}) custom-call(s32[3]{0:T(128)} %pad_add_fusion.4.refs_0_, bf16[1280,1024]{1,0:T(8,128)(2,1)} %get-tuple-element.68.refs_1_.refs_3_.refs_5_.refs_4_.refs_7_, ...), custom_call_target="tpu_custom_call" | custom-call | flops 339738624 | bytes 11276288 | tf_op jit(solution)/shard_map/pallas_call | solution.py:93
  165.9 3.7 %shard_map.112 = bf16[512,384]{1,0:T(8,128)(2,1)} custom-call(s32[1]{0:T(128)} %bitcast.at_ref, bf16[144,1152]{1,0:T(8,128)(2,1)} %get-tuple-element.67.img, bf16[144,1152]{1,0:T(8,128)(2,1)} %get-tuple-element.84.txt, bf16[144,1152]{1,0:T(8,128)(2,1)} %collective-permute-done.17.other_img, bf16[144,1152]{1,0:T(8,128)(2,1)} %collective-permute-done.18.other_txt), custom_call_target="tpu_custom_call" | custom-call | flops 679477248 | bytes 1327104 | tf_op jit(solution)/shard_map/pallas_call | solution.py:93
  172.1 2.4 %collective-permute-start.22 = (bf16[288,128]{1,0:T(8,128)(2,1)S(1)}, bf16[288,128]{1,0:T(8,128)(2,1)}, u32[]{:S(2)}, u32[]{:S(2)}) collective-permute-start(bf16[288,128]{1,0:T(8,128)(2,1)S(1)} %get-tuple-element.102), channel_id=1, source_target_pairs={{0,64},{1,65},{2,66},{3,67},{4,68},{5,69},{6,70},{7,71},{8,72},{9,... | collective-permute-start | bytes 221192 | tf_op jit(solution)/shard_map/ppermute | solution.py:61
  176.3 2.9 %collective-permute-start.25 = (bf16[288,128]{1,0:T(8,128)(2,1)}, bf16[288,128]{1,0:T(8,128)(2,1)}, u32[]{:S(2)}, u32[]{:S(2)}) collective-permute-start(bf16[288,128]{1,0:T(8,128)(2,1)} %get-tuple-element.96), channel_id=1, source_target_pairs={{0,4},{1,5},{2,6},{3,7},{4,0},{5,1},{6,2},{7,3},{8,12},{9,13},{10,... | collective-permute-start | bytes 221192 | tf_op jit(solution)/shard_map/ppermute | solution.py:61
  179.3 4.6 %all-to-all-start.2 = ((bf16[64,8,384]{2,1,0:T(8,128)(2,1)}), bf16[64,8,384]{2,1,0:T(8,128)(2,1)S(1)}, u32[]{:S(2)}, u32[]{:S(2)}) async-start(bf16[64,8,384]{2,1,0:T(8,128)(2,1)} %bitcast.50), calls=%async_computation.2 | async-start | bytes 786432 | tf_op jit(solution)/shard_map/all_to_all | solution.py:65
  186.1 4.2 %fusion.2 = f32[128,1152]{1,0:T(8,128)} fusion(s32[]{:T(128)S(6)} %select_n.202, bf16[1152,1152]{1,0:T(8,128)(2,1)} %bitcast.48, bf16[288,128]{1,0:T(8,128)(2,1)} %collective-permute-done.23, bf16[288,128]{1,0:T(8,128)(2,1)} %collective-permute-done.22, bf16[288,128]{1,0:T(8,128)(2,1)} %collective-permute-done.21, bf16[288,128]{1,0:T(8,128)(2,1)S(1)} %get-tuple-element.100), kind=kOutput, calls=%fused_computation.6 | convolution fusion | flops 346226688 | bytes 3538948 | tf_op jit(solution)/shard_map/dot_general | solution.py:75
  190.4 3.5 %fusion.4 = f32[128,1152]{1,0:T(8,128)} fusion(s32[]{:T(128)S(6)} %select_n.210, bf16[1152,1152]{1,0:T(8,128)(2,1)S(1)} %bitcast.47, bf16[288,128]{1,0:T(8,128)(2,1)} %collective-permute-done.26, bf16[288,128]{1,0:T(8,128)(2,1)} %collective-permute-done.25, bf16[288,128]{1,0:T(8,128)(2,1)S(1)} %collective-permute-done.24, ...), kind=kOutput, calls=%fused_computation.7 | convolution fusion | flops 346226688 | bytes 3538948 | tf_op jit(solution)/shard_map/dot_general | solution.py:75
  (106 shorter events, 41.3 us)
Async XLA Ops:
  2.3 28.2 %copy-start.8 = (bf16[144,1152]{1,0:T(8,128)(2,1)}, bf16[144,1152]{1,0:T(8,128)(2,1)S(1)}, u32[]{:S(2)}) copy-start(bf16[144,1152]{1,0:T(8,128)(2,1)S(1)} %pad_maximum_fusion.refs_1_.refs_8_) | copy-start | bytes 995332
  2.3 18.1 %collective-permute-start = (bf16[144,1152]{1,0:T(8,128)(2,1)S(1)}, bf16[144,1152]{1,0:T(8,128)(2,1)S(1)}, u32[]{:S(2)}, u32[]{:S(2)}) collective-permute-start(bf16[144,1152]{1,0:T(8,128)(2,1)S(1)} %pad_maximum_fusion.refs_1_.refs_8_), channel_id=1, source_target_pairs={{0,24},{1,25},{2,26},{3,27},{4,28},{5,29},{6,30},{7,31},{8,16},{9,... | collective-permute-start | bytes 995336 | tf_op jit(solution)/shard_map/ppermute | solution.py:61
  8.5 51.2 %all-to-all-start = ((bf16[8,128,1152]{2,1,0:T(8,128)(2,1)}), bf16[8,128,1152]{2,1,0:T(8,128)(2,1)}, u32[]{:S(2)}, u32[]{:S(2)}) async-start(bf16[8,128,1152]{2,1,0:T(8,128)(2,1)} %broadcast_in_dim.2), calls=%async_computation | async-start | bytes 4718592 | tf_op jit(solution)/shard_map/all_to_all | solution.py:65
  13.5 13.8 %collective-permute-start.2 = (bf16[144,1152]{1,0:T(8,128)(2,1)S(1)}, bf16[144,1152]{1,0:T(8,128)(2,1)}, u32[]{:S(2)}, u32[]{:S(2)}) collective-permute-start(bf16[144,1152]{1,0:T(8,128)(2,1)S(1)} %pad_maximum_fusion.refs_1_.refs_8_), channel_id=1, source_target_pairs={{0,2},{1,3},{2,4},{3,5},{4,6},{5,7},{6,0},{7,1},{8,10},{9,11},{10,... | collective-permute-start | bytes 995336 | tf_op jit(solution)/shard_map/ppermute | solution.py:61
  14.8 12.5 %collective-permute-start.3 = (bf16[144,1152]{1,0:T(8,128)(2,1)S(1)}, bf16[144,1152]{1,0:T(8,128)(2,1)}, u32[]{:S(2)}, u32[]{:S(2)}) collective-permute-start(bf16[144,1152]{1,0:T(8,128)(2,1)S(1)} %pad_maximum_fusion.refs_1_.refs_8_), channel_id=1, source_target_pairs={{0,6},{1,7},{2,0},{3,1},{4,2},{5,3},{6,4},{7,5},{8,14},{9,15},{10,... | collective-permute-start | bytes 995336 | tf_op jit(solution)/shard_map/ppermute | solution.py:61
  20.5 10.1 %collective-permute-start.1 = (bf16[144,1152]{1,0:T(8,128)(2,1)S(1)}, bf16[144,1152]{1,0:T(8,128)(2,1)}, u32[]{:S(2)}, u32[]{:S(2)}) collective-permute-start(bf16[144,1152]{1,0:T(8,128)(2,1)S(1)} %collective-permute-done.refs_2_.refs_9_), channel_id=1, source_target_pairs={{0,6},{1,7},{2,0},{3,1},{4,2},{5,3},{6,4},{7,5},{8,14},{9,15},{10,... | collective-permute-start | bytes 995336 | tf_op jit(solution)/shard_map/ppermute | solution.py:61
  21.9 8.6 %collective-permute-start.6 = (bf16[144,1152]{1,0:T(8,128)(2,1)S(1)}, bf16[144,1152]{1,0:T(8,128)(2,1)}, u32[]{:S(2)}, u32[]{:S(2)}) collective-permute-start(bf16[144,1152]{1,0:T(8,128)(2,1)S(1)} %collective-permute-done.refs_2_.refs_9_), channel_id=1, source_target_pairs={{0,2},{1,3},{2,4},{3,5},{4,6},{5,7},{6,0},{7,1},{8,10},{9,11},{10,... | collective-permute-start | bytes 995336 | tf_op jit(solution)/shard_map/ppermute | solution.py:61
  38.5 37.6 %collective-permute-start.7 = (bf16[3,1168,256]{2,1,0:T(8,128)(2,1)}, bf16[3,1168,256]{2,1,0:T(8,128)(2,1)}, u32[]{:S(2)}, u32[]{:S(2)}) collective-permute-start(bf16[3,1168,256]{2,1,0:T(8,128)(2,1)} %get-tuple-element.61), channel_id=1, source_target_pairs={{0,1},{1,0},{2,3},{3,2},{4,5},{5,4},{6,7},{7,6},{8,9},{9,8},{10,11... | collective-permute-start | bytes 5382152 | tf_op jit(solution)/shard_map/ppermute | solution.py:61
  41.4 10.8 %collective-permute-start.4 = (bf16[144,1152]{1,0:T(8,128)(2,1)}, bf16[144,1152]{1,0:T(8,128)(2,1)S(1)}, u32[]{:S(2)}, u32[]{:S(2)}) collective-permute-start(bf16[144,1152]{1,0:T(8,128)(2,1)} %collective-permute-done.2.refs_5_.refs_14_), channel_id=1, source_target_pairs={{0,2},{1,3},{2,4},{3,5},{4,6},{5,7},{6,0},{7,1},{8,10},{9,11},{10,... | collective-permute-start | bytes 995336 | tf_op jit(solution)/shard_map/ppermute | solution.py:61
  41.5 10.8 %collective-permute-start.5 = (bf16[144,1152]{1,0:T(8,128)(2,1)}, bf16[144,1152]{1,0:T(8,128)(2,1)S(1)}, u32[]{:S(2)}, u32[]{:S(2)}) collective-permute-start(bf16[144,1152]{1,0:T(8,128)(2,1)} %collective-permute-done.1.refs_4_.refs_11_), channel_id=1, source_target_pairs={{0,6},{1,7},{2,0},{3,1},{4,2},{5,3},{6,4},{7,5},{8,14},{9,15},{10,... | collective-permute-start | bytes 995336 | tf_op jit(solution)/shard_map/ppermute | solution.py:61
  58.3 14.4 %copy-start.10 = (f32[1,1024]{1,0:T(1,128)}, f32[1,1024]{1,0:T(1,128)S(1)}, u32[]{:S(2)}) copy-start(f32[1,1024]{1,0:T(1,128)S(1)} %get-tuple-element.83.refs_7_) | copy-start | bytes 12292
  58.3 17.8 %collective-permute-start.8 = (bf16[1,1168,256]{2,1,0:T(8,128)(2,1)}, bf16[1,1168,256]{2,1,0:T(8,128)(2,1)S(1)}, u32[]{:S(2)}, u32[]{:S(2)}) collective-permute-start(bf16[1,1168,256]{2,1,0:T(8,128)(2,1)} %get-tuple-element.62), channel_id=1, source_target_pairs={{0,1},{1,0},{2,3},{3,2},{4,5},{5,4},{6,7},{7,6},{8,9},{9,8},{10,11... | collective-permute-start | bytes 1794056 | tf_op jit(solution)/shard_map/ppermute | solution.py:61
  90.6 24.8 %collective-permute-start.9 = (bf16[1280,1024]{1,0:T(8,128)(2,1)}, bf16[1280,1024]{1,0:T(8,128)(2,1)}, u32[]{:S(2)}, u32[]{:S(2)}) collective-permute-start(bf16[1280,1024]{1,0:T(8,128)(2,1)} %get-tuple-element.69), channel_id=1, source_target_pairs={{0,1},{1,0},{2,3},{3,2},{4,5},{5,4},{6,7},{7,6},{8,9},{9,8},{10,11... | collective-permute-start | bytes 7864328 | tf_op jit(solution)/shard_map/ppermute | solution.py:61
  109.5 39.6 %all-to-all-start.1 = ((bf16[8,160,1024]{2,1,0:T(8,128)(2,1)}), bf16[8,160,1024]{2,1,0:T(8,128)(2,1)}, u32[]{:S(2)}, u32[]{:S(2)}) async-start(bf16[8,160,1024]{2,1,0:T(8,128)(2,1)} %get-tuple-element.65), calls=%async_computation.1 | async-start | bytes 5242880 | tf_op jit(solution)/shard_map/all_to_all | solution.py:65
  118.5 10.0 %collective-permute-start.10 = (bf16[160,1024]{1,0:T(8,128)(2,1)}, bf16[160,1024]{1,0:T(8,128)(2,1)S(1)}, u32[]{:S(2)}, u32[]{:S(2)}) collective-permute-start(bf16[160,1024]{1,0:T(8,128)(2,1)} %get-tuple-element.70), channel_id=1, source_target_pairs={{0,2},{1,3},{2,4},{3,5},{4,6},{5,7},{6,0},{7,1},{8,10},{9,11},{10,... | collective-permute-start | bytes 983048 | tf_op jit(solution)/shard_map/ppermute | solution.py:61
  118.5 10.0 %collective-permute-start.11 = (bf16[160,1024]{1,0:T(8,128)(2,1)}, bf16[160,1024]{1,0:T(8,128)(2,1)S(1)}, u32[]{:S(2)}, u32[]{:S(2)}) collective-permute-start(bf16[160,1024]{1,0:T(8,128)(2,1)} %get-tuple-element.71), channel_id=1, source_target_pairs={{0,6},{1,7},{2,0},{3,1},{4,2},{5,3},{6,4},{7,5},{8,14},{9,15},{10,... | collective-permute-start | bytes 983048 | tf_op jit(solution)/shard_map/ppermute | solution.py:61
  129.3 9.2 %collective-permute-start.12 = (bf16[160,1024]{1,0:T(8,128)(2,1)}, bf16[160,1024]{1,0:T(8,128)(2,1)S(1)}, u32[]{:S(2)}, u32[]{:S(2)}) collective-permute-start(bf16[160,1024]{1,0:T(8,128)(2,1)} %get-tuple-element.73), channel_id=1, source_target_pairs={{0,2},{1,3},{2,4},{3,5},{4,6},{5,7},{6,0},{7,1},{8,10},{9,11},{10,... | collective-permute-start | bytes 983048 | tf_op jit(solution)/shard_map/ppermute | solution.py:61
  133.3 7.6 %collective-permute-start.13 = (bf16[160,1024]{1,0:T(8,128)(2,1)}, bf16[160,1024]{1,0:T(8,128)(2,1)S(1)}, u32[]{:S(2)}, u32[]{:S(2)}) collective-permute-start(bf16[160,1024]{1,0:T(8,128)(2,1)} %get-tuple-element.76), channel_id=1, source_target_pairs={{0,6},{1,7},{2,0},{3,1},{4,2},{5,3},{6,4},{7,5},{8,14},{9,15},{10,... | collective-permute-start | bytes 983048 | tf_op jit(solution)/shard_map/ppermute | solution.py:61
  140.9 16.6 %collective-permute-start.14 = (bf16[160,1024]{1,0:T(8,128)(2,1)}, bf16[160,1024]{1,0:T(8,128)(2,1)}, u32[]{:S(2)}, u32[]{:S(2)}) collective-permute-start(bf16[160,1024]{1,0:T(8,128)(2,1)} %get-tuple-element.79), channel_id=1, source_target_pairs={{0,2},{1,3},{2,4},{3,5},{4,6},{5,7},{6,0},{7,1},{8,10},{9,11},{10,... | collective-permute-start | bytes 983048 | tf_op jit(solution)/shard_map/ppermute | solution.py:61
  141.8 15.8 %collective-permute-start.15 = (bf16[160,1024]{1,0:T(8,128)(2,1)}, bf16[160,1024]{1,0:T(8,128)(2,1)}, u32[]{:S(2)}, u32[]{:S(2)}) collective-permute-start(bf16[160,1024]{1,0:T(8,128)(2,1)} %get-tuple-element.80), channel_id=1, source_target_pairs={{0,6},{1,7},{2,0},{3,1},{4,2},{5,3},{6,4},{7,5},{8,14},{9,15},{10,... | collective-permute-start | bytes 983048 | tf_op jit(solution)/shard_map/ppermute | solution.py:61
  147.0 10.5 %collective-permute-start.16 = (bf16[160,1024]{1,0:T(8,128)(2,1)}, bf16[160,1024]{1,0:T(8,128)(2,1)S(1)}, u32[]{:S(2)}, u32[]{:S(2)}) collective-permute-start(bf16[160,1024]{1,0:T(8,128)(2,1)} %shard_map.110), channel_id=1, source_target_pairs={{0,24},{1,25},{2,26},{3,27},{4,28},{5,29},{6,30},{7,31},{8,16},{9,... | collective-permute-start | bytes 983048 | tf_op jit(solution)/shard_map/ppermute | solution.py:61
  154.0 11.6 %collective-permute-start.17 = (bf16[144,1152]{1,0:T(8,128)(2,1)}, bf16[144,1152]{1,0:T(8,128)(2,1)}, u32[]{:S(2)}, u32[]{:S(2)}) collective-permute-start(bf16[144,1152]{1,0:T(8,128)(2,1)} %get-tuple-element.67.img), channel_id=1, source_target_pairs={{0,1},{1,0},{2,3},{3,2},{4,5},{5,4},{6,7},{7,6},{8,9},{9,8},{10,11... | collective-permute-start | bytes 995336 | tf_op jit(solution)/shard_map/ppermute | solution.py:61
  163.2 2.7 %collective-permute-start.18 = (bf16[144,1152]{1,0:T(8,128)(2,1)}, bf16[144,1152]{1,0:T(8,128)(2,1)}, u32[]{:S(2)}, u32[]{:S(2)}) collective-permute-start(bf16[144,1152]{1,0:T(8,128)(2,1)} %get-tuple-element.84.txt), channel_id=1, source_target_pairs={{0,1},{1,0},{2,3},{3,2},{4,5},{5,4},{6,7},{7,6},{8,9},{9,8},{10,11... | collective-permute-start | bytes 995336 | tf_op jit(solution)/shard_map/ppermute | solution.py:61
  164.3 5.4 %collective-permute-start.19 = (bf16[4,144,128]{2,1,0:T(8,128)(2,1)S(1)}, bf16[4,144,128]{2,1,0:T(8,128)(2,1)S(1)}, u32[]{:S(2)}, u32[]{:S(2)}) collective-permute-start(bf16[4,144,128]{2,1,0:T(8,128)(2,1)S(1)} %copy-done.22), channel_id=1, source_target_pairs={{0,16},{1,17},{2,18},{3,19},{4,20},{5,21},{6,22},{7,23},{8,24},{9,... | collective-permute-start | bytes 442376 | tf_op jit(solution)/shard_map/ppermute | solution.py:61
  164.4 6.4 %collective-permute-start.20 = (bf16[4,144,128]{2,1,0:T(8,128)(2,1)}, bf16[4,144,128]{2,1,0:T(8,128)(2,1)S(1)}, u32[]{:S(2)}, u32[]{:S(2)}) collective-permute-start(bf16[4,144,128]{2,1,0:T(8,128)(2,1)} %get-tuple-element.86), channel_id=1, source_target_pairs={{0,24},{1,25},{2,26},{3,27},{4,28},{5,29},{6,30},{7,31},{8,16},{9,... | collective-permute-start | bytes 442376 | tf_op jit(solution)/shard_map/ppermute | solution.py:61
  170.9 13.0 %collective-permute-start.23 = (bf16[288,128]{1,0:T(8,128)(2,1)S(1)}, bf16[288,128]{1,0:T(8,128)(2,1)}, u32[]{:S(2)}, u32[]{:S(2)}) collective-permute-start(bf16[288,128]{1,0:T(8,128)(2,1)S(1)} %get-tuple-element.103), channel_id=1, source_target_pairs={{0,32},{1,33},{2,34},{3,35},{4,36},{5,37},{6,38},{7,39},{8,40},{9,... | collective-permute-start | bytes 221192 | tf_op jit(solution)/shard_map/ppermute | solution.py:61
  172.1 14.1 %collective-permute-start.22 = (bf16[288,128]{1,0:T(8,128)(2,1)S(1)}, bf16[288,128]{1,0:T(8,128)(2,1)}, u32[]{:S(2)}, u32[]{:S(2)}) collective-permute-start(bf16[288,128]{1,0:T(8,128)(2,1)S(1)} %get-tuple-element.102), channel_id=1, source_target_pairs={{0,64},{1,65},{2,66},{3,67},{4,68},{5,69},{6,70},{7,71},{8,72},{9,... | collective-permute-start | bytes 221192 | tf_op jit(solution)/shard_map/ppermute | solution.py:61
  174.4 11.7 %collective-permute-start.21 = (bf16[288,128]{1,0:T(8,128)(2,1)S(1)}, bf16[288,128]{1,0:T(8,128)(2,1)}, u32[]{:S(2)}, u32[]{:S(2)}) collective-permute-start(bf16[288,128]{1,0:T(8,128)(2,1)S(1)} %get-tuple-element.101), channel_id=1, source_target_pairs={{0,96},{1,97},{2,98},{3,99},{4,100},{5,101},{6,102},{7,103},{8,104... | collective-permute-start | bytes 221192 | tf_op jit(solution)/shard_map/ppermute | solution.py:61
  176.3 14.0 %collective-permute-start.26 = (bf16[288,128]{1,0:T(8,128)(2,1)}, bf16[288,128]{1,0:T(8,128)(2,1)}, u32[]{:S(2)}, u32[]{:S(2)}) collective-permute-start(bf16[288,128]{1,0:T(8,128)(2,1)} %get-tuple-element.97), channel_id=1, source_target_pairs={{0,2},{1,3},{2,4},{3,5},{4,6},{5,7},{6,0},{7,1},{8,10},{9,11},{10,... | collective-permute-start | bytes 221192 | tf_op jit(solution)/shard_map/ppermute | solution.py:61
  176.3 14.0 %collective-permute-start.25 = (bf16[288,128]{1,0:T(8,128)(2,1)}, bf16[288,128]{1,0:T(8,128)(2,1)}, u32[]{:S(2)}, u32[]{:S(2)}) collective-permute-start(bf16[288,128]{1,0:T(8,128)(2,1)} %get-tuple-element.96), channel_id=1, source_target_pairs={{0,4},{1,5},{2,6},{3,7},{4,0},{5,1},{6,2},{7,3},{8,12},{9,13},{10,... | collective-permute-start | bytes 221192 | tf_op jit(solution)/shard_map/ppermute | solution.py:61
  179.3 14.6 %all-to-all-start.2 = ((bf16[64,8,384]{2,1,0:T(8,128)(2,1)}), bf16[64,8,384]{2,1,0:T(8,128)(2,1)S(1)}, u32[]{:S(2)}, u32[]{:S(2)}) async-start(bf16[64,8,384]{2,1,0:T(8,128)(2,1)} %bitcast.50), calls=%async_computation.2 | async-start | bytes 786432 | tf_op jit(solution)/shard_map/all_to_all | solution.py:65
  183.9 6.4 %collective-permute-start.24 = (bf16[288,128]{1,0:T(8,128)(2,1)S(1)}, bf16[288,128]{1,0:T(8,128)(2,1)S(1)}, u32[]{:S(2)}, u32[]{:S(2)}) collective-permute-start(bf16[288,128]{1,0:T(8,128)(2,1)S(1)} %get-tuple-element.95), channel_id=1, source_target_pairs={{0,6},{1,7},{2,0},{3,1},{4,2},{5,3},{6,4},{7,5},{8,14},{9,15},{10,... | collective-permute-start | bytes 221192 | tf_op jit(solution)/shard_map/ppermute | solution.py:61
  (21 other events, 70.4 us)

commit v2 on v1

--- a/solution.py
+++ b/solution.py
@@ -137,92 +137,58 @@
         turned[span] = (proj[span] * inverse).astype(b16)
 
 
-def img_unit_kernel(at_ref, feats, turned_head, head, turned, norm, unit, proj):
-    put_units(feats, turned_head, proj, turned, norm)
-    part = dot(feats[...], head[...], NN)
-    total = jnp.sum(part * part, axis=1, keepdims=True)
-    unit[...] = (part * (1.0 / jnp.sqrt(total + epsilon))).astype(b16)
-
-
-def img_units(feats, turned_head, head, rows):
-    count, width = feats.shape
-    tile = 2 * rows
-    whole = pl.BlockSpec(head.shape, lambda i, at: (0, 0))
-    return call(
-        img_unit_kernel,
-        [
-            jax.ShapeDtypeStruct((width, count), b16),
-            jax.ShapeDtypeStruct((1, count), f32),
-            jax.ShapeDtypeStruct((count, width), b16),
-        ],
-        [jnp.int32(0)],
-        [feats, turned_head, head],
-        in_specs=[pl.BlockSpec((tile, width), lambda i, at: (i, 0)), whole, whole],
-        out_specs=[
-            pl.BlockSpec((width, tile), lambda i, at: (0, i)),
-            pl.BlockSpec((1, tile), lambda i, at: (0, i)),
-            pl.BlockSpec((tile, width), lambda i, at: (i, 0)),
-        ],
-        grid=(4,),
-        scratch=[pltpu.VMEM((width, tile), f32)],
-        cost=4 * count * width * width,
-        limit=24,
-    )
-
-
-def unit_kernel(rows, pairs, at_ref, *refs):
-    blocks, turned_head = refs[: 2 * pairs], refs[2 * pairs]
-    turned, norm, alone, feats, proj = refs[-5:]
+def unit_kernel(rows, at_ref, *refs):
+    blocks, (turned_head, turned, norm, feats, proj) = refs[:8], refs[8:]
     width = turned_head.shape[0]
-    second = at_ref[0]
+    second = at_ref[1]
     step = pl.program_id(0)
-    for p in range(pairs):
-        own, across = blocks[2 * p], blocks[2 * p + 1]
-
-        @pl.when(step == p)
+    for d in range(4):
+        own, across = blocks[2 * d], blocks[2 * d + 1]
+
+        @pl.when(step == d)
         def _():
             feats[...] = in_pair(own, across, second, rows)
             first = second == 0
             sides = own[rows:, :rows], across[rows:, :rows]
-            alone[0, width:, :rows] = jnp.where(first, sides[0], sides[1])
-            alone[0, width:, rows:] = jnp.where(first, sides[1], sides[0])
+            turned[width:, :rows] = jnp.where(first, sides[0], sides[1])
+            turned[width:, rows:] = jnp.where(first, sides[1], sides[0])
 
     put_units(feats, turned_head, proj, turned, norm)
-    turned[width:] = alone[0, width:]
-    alone[0, :width] = turned[:width]
-
-
-def units(pairs, turned_head, second, places, rows, carried):
+
+
+def units(blocks, turned_head, ring, second, rows):
     width = turned_head.shape[0]
     tile = 2 * rows
     whole = lambda a: pl.BlockSpec(a.shape, lambda i, at: (0, 0))
-    blocks = [block for pair in pairs for block in pair]
     return call(
-        lambda *refs: unit_kernel(rows, len(pairs), *refs),
+        lambda *refs: unit_kernel(rows, *refs),
         [
             jax.ShapeDtypeStruct((width + PAD, 8 * rows), b16),
             jax.ShapeDtypeStruct((1, 8 * rows), f32),
-            jax.ShapeDtypeStruct((len(pairs), width + PAD, tile), b16),
         ],
-        [second, *places],
-        [*blocks, turned_head, *carried],
-        in_specs=[whole(a) for a in [*blocks, turned_head]]
-        + [pl.BlockSpec(memory_space=pl.ANY)] * len(carried),
+        [ring, second],
+        [*blocks, turned_head],
+        in_specs=[whole(a) for a in [*blocks, turned_head]],
         out_specs=[
-            pl.BlockSpec((width + PAD, tile), lambda i, at: (0, at[1 + i])),
-            pl.BlockSpec((1, tile), lambda i, at: (0, at[1 + i])),
-            pl.BlockSpec((1, width + PAD, tile), lambda i, at: (i, 0, 0)),
+            pl.BlockSpec((width + PAD, tile), lambda i, at: (0, (at[0] + i) % 4)),
+            pl.BlockSpec((1, tile), lambda i, at: (0, (at[0] + i) % 4)),
         ],
-        grid=(len(pairs),),
+        grid=(4,),
         scratch=[pltpu.VMEM((tile, width), b16), pltpu.VMEM((width, tile), f32)],
-        cost=2 * tile * width * width * len(pairs),
-        aliases={len(blocks) + 2 + n: n for n in range(len(carried))},
-        limit=24,
-    )
-
-
-def ring_order(near, far):
-    return [near.at[0], near.at[1], far.at[0], near.at[2]]
+        cost=2 * 8 * rows * width * width,
+    )
+
+
+def unit_columns(feats, head):
+    projected = dot(head, feats, (((0,), (1,)), ((), ())))
+    norm = jnp.sqrt(jnp.sum(projected * projected, axis=0, keepdims=True) + epsilon)
+    return (projected / norm).astype(b16), norm
+
+
+def unit_rows(feats, head):
+    projected = dot(feats, head, NN)
+    norm = jnp.sqrt(jnp.sum(projected * projected, axis=1, keepdims=True) + epsilon)
+    return (projected / norm).astype(b16)
 
 
 def tile_slopes(rows, groups, place, bias_ref, img, txt, slopes, by_img):
@@ -266,35 +232,26 @@
         up[at + slab : at + slab + PAD] = figures
 
 
-def other_kernel(rows, groups, at_ref, bias_ref, img, turned, *refs):
-    chunks, (slopes, img_sum, up, by_img, held, txt) = ring_order(*refs[:2]), refs[2:]
+def other_kernel(rows, groups, at_ref, bias_ref, img, turned, txt, slopes, img_sum, up, by_img):
     step = pl.program_id(0)
 
     @pl.when(step == 0)
     def _():
         by_img[...] = jnp.zeros(by_img.shape, f32)
 
-    for d in range(4):
-
-        @pl.when(step == d)
-        def _():
-            txt[...] = chunks[d][...]
-
-    down = tile_slopes(rows, groups, at_ref[0], bias_ref, img, txt, held, by_img)
-    slopes[0] = held[...]
-    put_text_terms(up, turned, held[...], down)
+    down = tile_slopes(rows, groups, at_ref[0], bias_ref, img, txt, slopes.at[0], by_img)
+    put_text_terms(up, turned, slopes[0], down)
 
     @pl.when(step == 3)
     def _():
         img_sum[...] = logit_scale * jnp.sum(by_img[...].T, axis=0, keepdims=True)
 
 
-def other_tile(img, turned, chunks, group_bias, place, ring, rows):
+def other_tile(img, turned, txt, group_bias, place, rows):
     count, width = img.shape
     tile = 2 * rows
     height = width + 8 * PAD
     whole = lambda a: pl.BlockSpec(a.shape, lambda i, at: (0, 0))
-    stack = lambda a: pl.BlockSpec(a.shape, lambda i, at: (0, 0, 0))
     return call(
         lambda *refs: other_kernel(rows, group_bias.shape[0], *refs),
         [
@@ -302,29 +259,27 @@
             jax.ShapeDtypeStruct((1, count), f32),
             jax.ShapeDtypeStruct((height, count), b16),
         ],
-        [place, ring],
-        [group_bias, img, turned, *chunks],
-        in_specs=[pl.BlockSpec(memory_space=pltpu.SMEM), whole(img), whole(turned)]
-        + [stack(chunk) for chunk in chunks],
+        [place],
+        [group_bias, img, turned, txt],
+        in_specs=[
+            pl.BlockSpec(memory_space=pltpu.SMEM),
+            whole(img),
+            whole(turned),
+            pl.BlockSpec((width + PAD, tile), lambda i, at: (0, i)),
+        ],
         out_specs=[
             pl.BlockSpec((1, count, tile), lambda i, at: (i, 0, 0)),
             pl.BlockSpec((1, count), lambda i, at: (0, 0)),
-            pl.BlockSpec((height, tile), lambda i, at: (0, (at[1] + i) % 4)),
+            pl.BlockSpec((height, tile), lambda i, at: (0, i)),
         ],
         grid=(4,),
-        scratch=[
-            pltpu.VMEM((count, min(128, tile)), f32),
-            pltpu.VMEM((count, tile), b16),
-            pltpu.VMEM((width + PAD, tile), b16),
-        ],
+        scratch=[pltpu.VMEM((count, min(128, tile)), f32)],
         cost=4 * width * count * count,
     )
 
 
-def own_kernel(rows, groups, at_ref, bias_ref, img, turned, txt, *refs):
-    chunks = ring_order(*refs[:2])
-    other_slopes, other_sum, up = refs[2:5]
-    out, by_img, held, both, total = refs[5:]
+def own_kernel(rows, groups, at_ref, bias_ref, img, turned, txt, other, *refs):
+    other_slopes, other_sum, up, out, by_img, held, both, total = refs
     step = pl.program_id(0)
     width = img.shape[1]
     tile = 2 * rows
@@ -334,12 +289,7 @@
         by_img[...] = jnp.zeros(by_img.shape, f32)
         total[...] = jnp.zeros(total.shape, f32)
 
-    for d in range(4):
-
-        @pl.when(step == d)
-        def _():
-            both[:, tile:] = chunks[d][:width]
-
+    both[:, tile:] = other[:width]
     held[:, tile:] = other_slopes[0]
     both[:, :tile] = txt[:width]
     down = tile_slopes(rows, groups, at_ref[0], bias_ref, img, txt, held, by_img)
@@ -357,7 +307,7 @@
 
 
 def own_tile(
-    img, turned, txt, chunks, other_slopes, other_sum, group_bias, place, rows
+    img, turned, txt, other, other_slopes, other_sum, group_bias, place, rows
 ):
     count, width = img.shape
     tile = 2 * rows
@@ -370,15 +320,16 @@
         lambda *refs: own_kernel(rows, group_bias.shape[0], *refs),
         [jax.ShapeDtypeStruct((height, count), b16), pieces],
         [place],
-        [group_bias, img, turned, txt, *chunks, other_slopes, other_sum],
+        [group_bias, img, turned, txt, other, other_slopes, other_sum],
         in_specs=[
             pl.BlockSpec(memory_space=pltpu.SMEM),
             whole(img),
             whole(turned),
             pl.BlockSpec((width + PAD, tile), lambda i, at: (0, i)),
-        ]
-        + [stack(chunk) for chunk in chunks]
-        + [pl.BlockSpec((1, count, tile), lambda i, at: (i, 0, 0)), whole(other_sum)],
+            pl.BlockSpec((width + PAD, tile), lambda i, at: (0, i)),
+            pl.BlockSpec((1, count, tile), lambda i, at: (i, 0, 0)),
+            whole(other_sum),
+        ],
         out_specs=[pl.BlockSpec((height, tile), lambda i, at: (0, i)), stack(pieces)],
         grid=(4,),
         scratch=[
@@ -436,34 +387,33 @@
     )
 
 
-def put_gradient(up, inner, unit, norm, second, grad, own, give, rows):
+def img_grad_kernel(rows, at_ref, got, unit, norm, feats, blocks, part, grad):
+    slab = unit.shape[0]
+    up, inner = got[0, :slab].astype(f32), joined(got[0, slab:])
+    for n in range(1, 8):
+        up, inner = up + got[n, :slab].astype(f32), inner + joined(got[n, slab:])
+    up = logit_scale * up - unit[...].astype(f32) * inner
+    grad[...] = (up * (1.0 / norm[...])).astype(b16)
+    for n in range(8):
+        blocks[n] = grad[:, n * rows : (n + 1) * rows]
+    part[...] = dot(grad[...], feats[...], NN).astype(b16)
+
+
+def txt_grad_kernel(rows, at_ref, *refs):
+    terms, unit, norm, blocks, (own, give, part, grad) = (
+        refs[:5], refs[5], refs[6], refs[7:15], refs[15:]
+    )
+    slab = unit.shape[0]
+    up, inner = terms[0][:slab].astype(f32), joined(terms[0][slab:])
+    for term in terms[1:]:
+        up, inner = up + term[:slab].astype(f32), inner + joined(term[slab:])
     up = logit_scale * up - unit[...].astype(f32) * inner
     grad[...] = (up * (1.0 / norm[...])).astype(b16)
     for ring in range(4):
         low = grad[:, (2 * ring) * rows : (2 * ring + 1) * rows]
         high = grad[:, (2 * ring + 1) * rows : (2 * ring + 2) * rows]
-        own[ring] = jnp.where(second == 0, low, high)
-        give[ring] = jnp.where(second == 0, high, low)
-
-
-def img_grad_kernel(rows, at_ref, got, unit, norm, feats, own, give, part, grad):
-    slab = unit.shape[0]
-    up, inner = got[0, :slab].astype(f32), joined(got[0, slab:])
-    for n in range(1, 8):
-        up, inner = up + got[n, :slab].astype(f32), inner + joined(got[n, slab:])
-    put_gradient(up, inner, unit, norm, at_ref[1], grad, own, give, rows)
-    part[...] = dot(grad[...], feats[...], NN).astype(b16)
-
-
-def txt_grad_kernel(rows, at_ref, *refs):
-    terms, unit, norm, blocks, (own, give, part, grad) = (
-        refs[:5], refs[5], refs[6], refs[7:15], refs[15:]
-    )
-    slab = unit.shape[0]
-    up, inner = terms[0][:slab].astype(f32), joined(terms[0][slab:])
-    for term in terms[1:]:
-        up, inner = up + term[:slab].astype(f32), inner + joined(term[slab:])
-    put_gradient(up, inner, unit, norm, at_ref[1], grad, own, give, rows)
+        own[ring] = jnp.where(at_ref[1] == 0, low, high)
+        give[ring] = jnp.where(at_ref[1] == 0, high, low)
     total = None
     for d in range(4):
         cols = grad[:, aligned((at_ref[2] + d) % 4, 2 * rows)]
@@ -472,22 +422,22 @@
     part[...] = total.astype(b16)
 
 
-def gradient(kernel, place, second, ring, terms, unit, norm, feats, rows):
+def gradient(kernel, place, second, ring, terms, unit, norm, feats, halves, rows):
     width = feats[0].shape[1]
     slab, count = width // 8, 8 * rows
     whole = lambda a: pl.BlockSpec(a.shape, lambda i, at: (0,) * len(a.shape))
     mine = lambda height: pl.BlockSpec((height, count), lambda i, at: (at[0], 0))
-    block = jax.ShapeDtypeStruct((4, slab, rows), b16)
+    block = jax.ShapeDtypeStruct((8 // halves, slab, rows), b16)
     part = jax.ShapeDtypeStruct((slab, width), b16)
     return call(
         lambda *refs: kernel(rows, *refs),
-        [block, block, part],
+        [block] * halves + [part],
         [place, second, ring],
         [term[0] if isinstance(term, tuple) else term for term in terms] + [unit, norm, *feats],
         in_specs=[mine(slab + PAD) if isinstance(term, tuple) else whole(term) for term in terms]
         + [mine(slab), whole(norm)]
         + [whole(a) for a in feats],
-        out_specs=[whole(block), whole(block), whole(part)],
+        out_specs=[whole(block)] * halves + [whole(part)],
         grid=(1,),
         scratch=[pltpu.VMEM((slab, count), b16)],
         cost=2 * slab * count * width,
@@ -589,31 +539,27 @@
     across, turned_txt = together([across, text_head.T])
     across_after = send(across, txt_move(3, 0))
     across_before = send(across, txt_move(1, 0))
-    across_after, before, after, across, turned_img = together(
-        [across_after, before, after, across, image_head.T]
-    )
+    across_after, before, after, across = together([across_after, before, after, across])
     far = send(before, txt_move(1, 0))
     across_far = send(across_after, txt_move(3, 0))
-    pairs = [(text_rows, across), (after, across_after), (before, across_before)]
-    near_y, far_y = [(y + d) % 4 for d in (0, 1, 3)], [(y + 2) % 4]
-    *made, chunks = units(pairs, turned_txt, hi, near_y, rows, ())
-    others = [send(chunks, core_move)]
-    unit_txt, norm_txt, chunks = units([(far, across_far)], turned_txt, hi, far_y, rows, made)
-    others.append(send(chunks, core_move))
-    turned_units, norm_img, unit_img = img_units(img_feats, turned_img, image_head, rows)
     txt_blocks = [
         text_rows, across, after, across_after, far, across_far, before, across_before
     ]
+    unit_txt, norm_txt = units(txt_blocks, turned_txt, y, hi, rows)
+    other_txt = send(unit_txt, core_move)
+    turned_units, norm_img = unit_columns(img_feats, image_head)
+    unit_img = unit_rows(together([img_feats, unit_txt])[0], image_head)
 
     other_slopes, other_sum, other_up = other_tile(
-        unit_img, turned_units, others, group_bias, place % 16, y, rows
+        unit_img, turned_units, other_txt, group_bias, place % 16, rows
     )
     back = send(other_up, core_move)
     text_up, img_terms = own_tile(
-        unit_img, turned_units, unit_txt, others, other_slopes, other_sum, group_bias,
+        unit_img, turned_units, unit_txt, other_txt, other_slopes, other_sum, group_bias,
         place % 16, rows,
     )
     img_terms = exchange(img_terms, IMG_GROUPS)
+    (txt_ring_head,) = together([from_ring(turned_txt, y)])
 
     def slab_terms(d, e):
         at = (y + d) % 4 * 2 + (hi + e) % 2
@@ -638,28 +584,25 @@
     (across,) = sums([slab_terms(0, 1) + [across_before, across_after]], rows)
     across = send(across, txt_move(0, 1))
 
-    img_own, img_give, img_part = gradient(
-        img_grad_kernel, z * 2 + lo, lo, z, [img_terms], turned_units, norm_img, [img_feats], rows
-    )
+    img_blocks, img_part = gradient(
+        img_grad_kernel, z * 2 + lo, lo, z, [img_terms], turned_units, norm_img, [img_feats], 1, rows
+    )
+    grad_img = exchange(img_blocks, IMG_GROUPS).reshape(width, rows)
     txt_own, txt_give, txt_part = gradient(
         txt_grad_kernel, y * 2 + hi, hi, y, slab_terms(0, 0) + [before, after, across],
-        unit_txt, norm_txt, txt_blocks, rows,
+        unit_txt, norm_txt, txt_blocks, 2, rows,
     )
     img_theirs = send(img_part, core_move)
     txt_theirs = send(txt_part, core_move)
-    img_got = send(img_give, img_move(0, 1))
     txt_got = send(txt_give, txt_move(0, 1))
-    heads, img_got, txt_got = together(
-        [picked(core, [img_part, txt_part, img_theirs, txt_theirs]), img_got, txt_got]
-    )
+    heads, txt_got = together([picked(core, [img_part, txt_part, img_theirs, txt_theirs]), txt_got])
     heads = exchange(heads.reshape(64, 8, -1), CHIP_GROUPS)
     head_shape = jax.ShapeDtypeStruct((width // 128, width), f32)
     image_head_grad, text_head_grad = call(head_kernel, [head_shape] * 2, [core], [heads])
 
-    grad_img = whole_columns(pair_lines(img_own, img_got, lo), img_move, z)
-    image_grad = dot(grad_img, from_ring(turned_img, z), TN)
+    image_grad = dot(grad_img, image_head, (((0,), (1,)), ((), ())))
     grad_txt = whole_columns(pair_lines(txt_own, txt_got, hi), txt_move, y)
-    text_grad = dot(grad_txt, from_ring(turned_txt, y), TN)
+    text_grad = dot(grad_txt, txt_ring_head, TN)
     return (image_grad, text_grad, image_head_grad, text_head_grad)
 
 

time: 200 us -> 194 us (0.970)
  local copies, waits for them, and re-layouts: 28.3 us -> 11.9 us
  Pallas kernels: 75.8 us -> 64.5 us
  other arithmetic: 5.18 us -> 12.8 us
  matrix products: 7.75 us -> 14.4 us
  waiting for transfers between devices: 24.5 us -> 30.9 us
    unnamed x48 -> x33, local copies, waits for them, and re-layouts: 24.2 us -> 7.86 us
    pallas_call x12 -> x10, Pallas kernels: 75.8 us -> 64.5 us  [call(): pl.pallas_call(body, out_shape=out_shape, grid_spec=spec, input_output_al...]
    all_to_all x3 -> x4, starting transfers between devices: 14.8 us -> 23.4 us  [exchange(): lax.all_to_all(blocks, DEV, 0, 0, axis_index_groups=groups, tiled=True)]
    ppermute x27 -> x22, starting transfers between devices: 39.3 us -> 32.5 us  [send(): lax.ppermute(block, DEV, [(flat(*p), flat(*move(*p))) for p in PLACES])]
    dot_general x2 -> x4, matrix products: 7.75 us -> 14.4 us  [dot(): return lax.dot_general(a, b, dims, preferred_element_type=f32)]
    all_to_all x3 -> x4, waiting for transfers between devices: 0.01 us -> 5.75 us  [exchange(): lax.all_to_all(blocks, DEV, 0, 0, axis_index_groups=groups, tiled=True)]
    concatenate x0 -> x1, other arithmetic: none -> 5.52 us  [from_ring(): jnp.concatenate([turned_head, turned_head])]
    convert_element_type x0 -> x2, other arithmetic: none -> 4.16 us  [the longest x1 2.17 us: unit_columns(): return ((projected / norm).astype(b16), norm)]
  transfers between devices with their start and end apart: 30 -> 26, of which waited for: 8 -> 7; matrix products, arithmetic and copies ran while one was open for 13% -> 18% of each run, Pallas kernels for 31% -> 26%
where the time goes in v2:
time: 194 us; the launch traced here: 191 us
  Pallas kernels  64.5 us (33%)
  starting transfers between devices  55.9 us (29%)
  waiting for transfers between devices  30.9 us (16%)
  matrix products  14.4 us (7%)
  other arithmetic  12.8 us (7%)
  local copies, waits for them, and re-layouts  11.9 us (6%)
    pallas_call x10, Pallas kernels, call(): pl.pallas_call(body, out_shape=out_shape, grid_spec=spec, input_output_al...  64.5 us
    ppermute x22, starting transfers between devices, send(): lax.ppermute(block, DEV, [(flat(*p), flat(*move(*p))) for p in PLACES])  32.5 us
    ppermute x22, waiting for transfers between devices, send(): lax.ppermute(block, DEV, [(flat(*p), flat(*move(*p))) for p in PLACES])  25.2 us
    all_to_all x4, starting transfers between devices, exchange(): lax.all_to_all(blocks, DEV, 0, 0, axis_index_groups=groups, tiled=True)  23.4 us
    dot_general x4, matrix products, dot(): return lax.dot_general(a, b, dims, preferred_element_type=f32)  14.4 us
    unnamed x33, local copies, waits for them, and re-layouts  7.86 us
    all_to_all x4, waiting for transfers between devices, exchange(): lax.all_to_all(blocks, DEV, 0, 0, axis_index_groups=groups, tiled=True)  5.75 us
    concatenate x1, other arithmetic, from_ring(): jnp.concatenate([turned_head, turned_head])  5.52 us
  transfers between devices with their start and end apart: 26, of which 7 were waited for; matrix products, arithmetic and copies ran while one was open for 18% of the time, Pallas kernels for 26%

profile of v2, /device:TPU:1, one launch (start us, length us, event | category | flops | bytes accessed | tf_op | source)
XLA Modules:
  0.0 191.4 jit_solution(7407978926751878087)
XLA Ops:
  0.6 2.8 %broadcast_in_dim.2 = bf16[8,128,1152]{2,1,0:T(8,128)(2,1)} broadcast(bf16[128,1152]{1,0:T(8,128)(2,1)} %param.7), dimensions={1,2} | broadcast | bytes 2654208 | tf_op jit(solution)/shard_map/broadcast_in_dim | solution.py:534
  3.5 6.9 %all-to-all-start = ((bf16[8,128,1152]{2,1,0:T(8,128)(2,1)}), bf16[8,128,1152]{2,1,0:T(8,128)(2,1)}, u32[]{:S(2)}, u32[]{:S(2)}) async-start(bf16[8,128,1152]{2,1,0:T(8,128)(2,1)} %broadcast_in_dim.2), calls=%async_computation | async-start | bytes 4718592 | tf_op jit(solution)/shard_map/all_to_all | solution.py:65
  10.5 2.8 %collective-permute-start = (bf16[144,1152]{1,0:T(8,128)(2,1)S(1)}, bf16[144,1152]{1,0:T(8,128)(2,1)S(1)}, u32[]{:S(2)}, u32[]{:S(2)}) collective-permute-start(bf16[144,1152]{1,0:T(8,128)(2,1)S(1)} %pad_maximum_fusion.refs_1_.refs_8_), channel_id=1, source_target_pairs={{0,24},{1,25},{2,26},{3,27},{4,28},{5,29},{6,30},{7,31},{8,16},{9,... | collective-permute-start | bytes 995336 | tf_op jit(solution)/shard_map/ppermute | solution.py:61
  16.1 5.2 %copy.11 = bf16[1152,1152]{0,1:T(8,128)(2,1)} copy(bf16[1152,1152]{1,0:T(8,128)(2,1)} %param.10) | data formatting | bytes 5308416 | tf_op args[3]
  23.1 6.4 %collective-permute-done.1.refs_4_.refs_11_ = bf16[144,1152]{1,0:T(8,128)(2,1)} collective-permute-done((bf16[144,1152]{1,0:T(8,128)(2,1)S(1)}, bf16[144,1152]{1,0:T(8,128)(2,1)}, u32[]{:S(2)}, u32[]{:S(2)}) %collective-permute-start.1) | collective-permute-done | bytes 331808 | tf_op jit(solution)/shard_map/ppermute | solution.py:61
  32.7 5.9 %collective-permute-done.4.refs_5_.refs_12_ = bf16[144,1152]{1,0:T(8,128)(2,1)S(1)} collective-permute-done((bf16[144,1152]{1,0:T(8,128)(2,1)}, bf16[144,1152]{1,0:T(8,128)(2,1)S(1)}, u32[]{:S(2)}, u32[]{:S(2)}) %collective-permute-start.4) | collective-permute-done | bytes 331808 | tf_op jit(solution)/shard_map/ppermute | solution.py:61
  39.4 9.2 %shard_map.102 = (bf16[1168,1024]{1,0:T(8,128)(2,1)}, f32[1,1024]{1,0:T(1,128)}) custom-call(s32[2]{0:T(128)} %pad_add_fusion.1.refs_0_, bf16[144,1152]{1,0:T(8,128)(2,1)} %copy-done.3, bf16[144,1152]{1,0:T(8,128)(2,1)} %copy-done.4, bf16[144,1152]{1,0:T(8,128)(2,1)} %collective-permute-done.3.refs_3_.refs_10_, ...), custom_call_target="tpu_custom_call" | custom-call | flops 2717908992 | bytes 5308416 | tf_op jit(solution)/shard_map/pallas_call | solution.py:93
  48.6 3.0 %collective-permute-start.7 = (bf16[1168,1024]{1,0:T(8,128)(2,1)}, bf16[1168,1024]{1,0:T(8,128)(2,1)}, u32[]{:S(2)}, u32[]{:S(2)}) collective-permute-start(bf16[1168,1024]{1,0:T(8,128)(2,1)} %get-tuple-element.46.refs_4_.refs_6_), channel_id=1, source_target_pairs={{0,1},{1,0},{2,3},{3,2},{4,5},{5,4},{6,7},{7,6},{8,9},{9,8},{10,11... | collective-permute-start | bytes 7176200 | tf_op jit(solution)/shard_map/ppermute | solution.py:61
  51.6 5.0 %multiply_reduce_fusion = (f32[1024]{0:T(1024)S(1)}, f32[1152,1024]{1,0:T(8,128)S(1)}) fusion(bf16[1152,1152]{1,0:T(8,128)(2,1)S(1)} %copy-done, bf16[1024,1152]{1,0:T(8,128)(2,1)} %bitcast.4.refs_4_), kind=kOutput, calls=%fused_computation.3 | convolution fusion | flops 2720267264 | bytes 9736192 | tf_op jit(solution)/shard_map/dot_general | solution.py:75
  56.6 5.3 %multiply_reduce_fusion.1 = (f32[1024]{0:T(1024)S(1)}, f32[1024,1152]{1,0:T(8,128)S(1)}) fusion(bf16[1024,1152]{1,0:T(8,128)(2,1)} %bitcast.4.refs_4_, bf16[1152,1152]{1,0:T(8,128)(2,1)S(1)} %copy-done), kind=kOutput, calls=%fused_computation.5 | convolution fusion | flops 2720267264 | bytes 9736192 | tf_op jit(solution)/shard_map/dot_general | solution.py:75
  61.9 2.2 %divide_convert_fusion.refs_3_.refs_2_ = bf16[1152,1024]{1,0:T(8,128)(2,1)} fusion(f32[1152,1024]{1,0:T(8,128)S(1)} %get-tuple-element.87, f32[1024]{0:T(1024)S(1)} %add_sqrt_fusion), kind=kLoop, calls=%fused_computation.2 | loop fusion | flops 2359296 | bytes 7081984 | tf_op jit(solution)/shard_map/convert_element_type | solution.py:185
  66.1 12.1 %shard_map.103 = (bf16[4,1024,256]{2,1,0:T(8,128)(2,1)}, f32[1,1024]{1,0:T(1,128)}, bf16[1280,1024]{1,0:T(8,128)(2,1)}) custom-call(s32[1]{0:T(128)} %bitcast.3.refs_0_, f32[32]{0:T(128)} %refs_1_.3, bf16[1024,1152]{1,0:T(8,128)(2,1)} %divide_convert_fusion.1.refs_2_, bf16[1152,1024]{1,0:T(8,128)(2,1)} %divide_convert_fusion.refs_3_.refs_2_, ...), custom_call_target="tpu_custom_call" | custom-call | flops 4831838208 | bytes 7110784 | tf_op jit(solution)/shard_map/pallas_call | solution.py:93
  78.2 18.6 %shard_map.104 = (bf16[1280,1024]{1,0:T(8,128)(2,1)}, bf16[8,160,1024]{2,1,0:T(8,128)(2,1)}) custom-call(s32[1]{0:T(128)} %bitcast.3.refs_0_, f32[32]{0:T(128)} %refs_1_.3, bf16[1024,1152]{1,0:T(8,128)(2,1)} %divide_convert_fusion.1.refs_2_, bf16[1152,1024]{1,0:T(8,128)(2,1)} %divide_convert_fusion.refs_3_.refs_2_, ...), custom_call_target="tpu_custom_call" | custom-call | flops 9663676416 | bytes 11604096 | tf_op jit(solution)/shard_map/pallas_call | solution.py:93
  96.8 4.4 %all-to-all-start.1 = ((bf16[8,160,1024]{2,1,0:T(8,128)(2,1)}), bf16[8,160,1024]{2,1,0:T(8,128)(2,1)}, u32[]{:S(2)}, u32[]{:S(2)}) async-start(bf16[8,160,1024]{2,1,0:T(8,128)(2,1)} %get-tuple-element.50), calls=%async_computation.1 | async-start | bytes 5242880 | tf_op jit(solution)/shard_map/all_to_all | solution.py:65
  102.0 3.2 %shard_map.106 = (bf16[160,1024]{1,0:T(8,128)(2,1)}, bf16[160,1024]{1,0:T(8,128)(2,1)}, bf16[160,1024]{1,0:T(8,128)(2,1)}) custom-call(s32[7]{0:T(128)} %stack.108.refs_0_, bf16[1280,1024]{1,0:T(8,128)(2,1)} %get-tuple-element.53.refs_1_.refs_3_.refs_5_.refs_4_.refs_7_, bf16[1280,1024]{1,0:T(8,128)(2,1)} %collective-permute-done.8.refs_2_.refs_4_.refs_6_.refs_5_.refs_8_, ...), custom_call_target="tpu_custom_call" | custom-call | bytes 15728640 | tf_op jit(solution)/shard_map/pallas_call | solution.py:93
  108.5 7.0 %collective-permute-done.9.refs_6_ = bf16[160,1024]{1,0:T(8,128)(2,1)S(1)} collective-permute-done((bf16[160,1024]{1,0:T(8,128)(2,1)}, bf16[160,1024]{1,0:T(8,128)(2,1)S(1)}, u32[]{:S(2)}, u32[]{:S(2)}) %collective-permute-start.9) | collective-permute-done | bytes 327712 | tf_op jit(solution)/shard_map/ppermute | solution.py:61
  116.4 3.4 %shard_map.107 = (bf16[160,1024]{1,0:T(8,128)(2,1)}, bf16[160,1024]{1,0:T(8,128)(2,1)}, bf16[160,1024]{1,0:T(8,128)(2,1)}) custom-call(s32[7]{0:T(128)} %stack.112.refs_0_, bf16[1280,1024]{1,0:T(8,128)(2,1)} %get-tuple-element.53.refs_1_.refs_3_.refs_5_.refs_4_.refs_7_, bf16[1280,1024]{1,0:T(8,128)(2,1)} %collective-permute-done.8.refs_2_.refs_4_.refs_6_.refs_5_.refs_8_, ...), custom_call_target="tpu_custom_call" | custom-call | bytes 16384000 | tf_op jit(solution)/shard_map/pallas_call | solution.py:93
  119.8 2.6 %collective-permute-start.12 = (bf16[160,1024]{1,0:T(8,128)(2,1)}, bf16[160,1024]{1,0:T(8,128)(2,1)S(1)}, u32[]{:S(2)}, u32[]{:S(2)}) collective-permute-start(bf16[160,1024]{1,0:T(8,128)(2,1)} %get-tuple-element.61), channel_id=1, source_target_pairs={{0,6},{1,7},{2,0},{3,1},{4,2},{5,3},{6,4},{7,5},{8,14},{9,15},{10,... | collective-permute-start | bytes 983048 | tf_op jit(solution)/shard_map/ppermute | solution.py:61
  123.0 2.8 %collective-permute-done.11.refs_3_ = bf16[160,1024]{1,0:T(8,128)(2,1)S(1)} collective-permute-done((bf16[160,1024]{1,0:T(8,128)(2,1)}, bf16[160,1024]{1,0:T(8,128)(2,1)S(1)}, u32[]{:S(2)}, u32[]{:S(2)}) %collective-permute-start.11) | collective-permute-done | bytes 327712 | tf_op jit(solution)/shard_map/ppermute | solution.py:61
  125.8 2.4 %collective-permute-done.12.refs_4_ = bf16[160,1024]{1,0:T(8,128)(2,1)S(1)} collective-permute-done((bf16[160,1024]{1,0:T(8,128)(2,1)}, bf16[160,1024]{1,0:T(8,128)(2,1)S(1)}, u32[]{:S(2)}, u32[]{:S(2)}) %collective-permute-start.12) | collective-permute-done | bytes 327712 | tf_op jit(solution)/shard_map/ppermute | solution.py:61
  129.4 2.2 %collective-permute-start.14 = (bf16[160,1024]{1,0:T(8,128)(2,1)}, bf16[160,1024]{1,0:T(8,128)(2,1)}, u32[]{:S(2)}, u32[]{:S(2)}) collective-permute-start(bf16[160,1024]{1,0:T(8,128)(2,1)} %get-tuple-element.65), channel_id=1, source_target_pairs={{0,6},{1,7},{2,0},{3,1},{4,2},{5,3},{6,4},{7,5},{8,14},{9,15},{10,... | collective-permute-start | bytes 983048 | tf_op jit(solution)/shard_map/ppermute | solution.py:61
  131.7 2.8 %shard_map.108 = bf16[160,1024]{1,0:T(8,128)(2,1)} custom-call(s32[3]{0:T(128)} %pad_add_fusion.3.refs_0_, bf16[1280,1024]{1,0:T(8,128)(2,1)} %get-tuple-element.53.refs_1_.refs_3_.refs_5_.refs_4_.refs_7_, bf16[1280,1024]{1,0:T(8,128)(2,1)} %collective-permute-done.8.refs_2_.refs_4_.refs_6_.refs_5_.refs_8_, bf16[160,1024]{1,0:T(8,128)(2,1)} %copy-done.6, ...), custom_call_target="tpu_custom_call" | custom-call | bytes 5898240 | tf_op jit(solution)/shard_map/pallas_call | solution.py:93
  137.4 4.8 %shard_map.105 = (bf16[8,144,128]{2,1,0:T(8,128)(2,1)}, bf16[144,1152]{1,0:T(8,128)(2,1)}) custom-call(s32[3]{0:T(128)} %pad_add_fusion.refs_0_, bf16[8,160,1024]{2,1,0:T(8,128)(2,1)} %all-to-all-done.1.refs_1_, bf16[1152,1024]{1,0:T(8,128)(2,1)} %divide_convert_fusion.refs_3_.refs_2_, f32[1,1024]{1,0:T(1,128)} %bitcast.45, bf16[1024,1152]{1,0:T(8,128)(2,1)} %bitcast.4.refs_4_), custom_call_target="tpu_custom_call" | custom-call | flops 339738624 | bytes 7344128 | tf_op jit(solution)/shard_map/pallas_call | solution.py:93
  142.3 3.5 %collective-permute-start.16 = (bf16[144,1152]{1,0:T(8,128)(2,1)}, bf16[144,1152]{1,0:T(8,128)(2,1)}, u32[]{:S(2)}, u32[]{:S(2)}) collective-permute-start(bf16[144,1152]{1,0:T(8,128)(2,1)} %get-tuple-element.52.img), channel_id=1, source_target_pairs={{0,1},{1,0},{2,3},{3,2},{4,5},{5,4},{6,7},{7,6},{8,9},{9,8},{10,11... | collective-permute-start | bytes 995336 | tf_op jit(solution)/shard_map/ppermute | solution.py:61
  146.5 4.8 %shard_map.109 = (bf16[4,144,128]{2,1,0:T(8,128)(2,1)}, bf16[4,144,128]{2,1,0:T(8,128)(2,1)}, bf16[144,1152]{1,0:T(8,128)(2,1)}) custom-call(s32[3]{0:T(128)} %pad_add_fusion.2.refs_0_, bf16[1280,1024]{1,0:T(8,128)(2,1)} %get-tuple-element.53.refs_1_.refs_3_.refs_5_.refs_4_.refs_7_, ...), custom_call_target="tpu_custom_call" | custom-call | flops 339738624 | bytes 11276288 | tf_op jit(solution)/shard_map/pallas_call | solution.py:93
  153.5 5.5 %fusion = bf16[1152,1152]{1,0:T(8,128)(2,1)} fusion(s32[]{:T(128)S(6)} %select_n.149, bf16[1152,1152]{1,0:T(8,128)(2,1)} %bitcast.42), kind=kLoop, calls=%fused_computation.6 | loop fusion | flops 5308416 | bytes 5308420 | tf_op jit(solution)/shard_map/concatenate | solution.py:521
  159.0 4.0 %all-to-all-start.2 = ((bf16[8,144,128]{2,1,0:T(8,128)(2,1)}), bf16[8,144,128]{2,1,0:T(8,128)(2,1)S(1)}, u32[]{:S(2)}, u32[]{:S(2)}) async-start(bf16[8,144,128]{2,1,0:T(8,128)(2,1)} %get-tuple-element.51), calls=%async_computation.2 | async-start | bytes 589824 | tf_op jit(solution)/shard_map/all_to_all | solution.py:65
  163.0 3.7 %shard_map.110 = bf16[512,384]{1,0:T(8,128)(2,1)} custom-call(s32[1]{0:T(128)} %bitcast.13.at_ref, bf16[144,1152]{1,0:T(8,128)(2,1)} %get-tuple-element.52.img, bf16[144,1152]{1,0:T(8,128)(2,1)} %get-tuple-element.69.txt, bf16[144,1152]{1,0:T(8,128)(2,1)} %collective-permute-done.16.other_img, bf16[144,1152]{1,0:T(8,128)(2,1)} %collective-permute-done.17.other_txt), custom_call_target="tpu_custom_call" | custom-call | flops 679477248 | bytes 1327104 | tf_op jit(solution)/shard_map/pallas_call | solution.py:93
  167.5 2.9 %collective-permute-start.20 = (bf16[288,128]{1,0:T(8,128)(2,1)}, bf16[288,128]{1,0:T(8,128)(2,1)}, u32[]{:S(2)}, u32[]{:S(2)}) collective-permute-start(bf16[288,128]{1,0:T(8,128)(2,1)} %get-tuple-element.78), channel_id=1, source_target_pairs={{0,4},{1,5},{2,6},{3,7},{4,0},{5,1},{6,2},{7,3},{8,12},{9,13},{10,... | collective-permute-start | bytes 221192 | tf_op jit(solution)/shard_map/ppermute | solution.py:61
  170.9 8.1 %all-to-all-start.3 = ((bf16[64,8,384]{2,1,0:T(8,128)(2,1)}), bf16[64,8,384]{2,1,0:T(8,128)(2,1)S(1)}, u32[]{:S(2)}, u32[]{:S(2)}) async-start(bf16[64,8,384]{2,1,0:T(8,128)(2,1)} %bitcast.44), calls=%async_computation.3 | async-start | bytes 786432 | tf_op jit(solution)/shard_map/all_to_all | solution.py:65
  180.8 2.4 %fusion.1 = f32[128,1152]{1,0:T(8,128)} fusion(bf16[1152,1152]{1,0:T(8,128)(2,1)S(1)} %copy-done.1, bf16[288,128]{1,0:T(8,128)(2,1)S(1)} %collective-permute-done.21, bf16[288,128]{1,0:T(8,128)(2,1)} %collective-permute-done.20, bf16[288,128]{1,0:T(8,128)(2,1)} %collective-permute-done.19, bf16[288,128]{1,0:T(8,128)(2,1)S(1)} %get-tuple-element.76), kind=kOutput, calls=%fused_computation.16 | convolution fusion | flops 340918272 | bytes 3538944 | tf_op jit(solution)/shard_map/dot_general | solution.py:75
  183.1 5.7 %all-to-all-done.3.got = bf16[64,8,384]{2,1,0:T(8,128)(2,1)S(1)} async-done(((bf16[64,8,384]{2,1,0:T(8,128)(2,1)}), bf16[64,8,384]{2,1,0:T(8,128)(2,1)S(1)}, u32[]{:S(2)}, u32[]{:S(2)}) %all-to-all-start.3) | async-done | bytes 393248 | tf_op jit(solution)/shard_map/all_to_all | solution.py:65
  (84 shorter events, 28.6 us)
Async XLA Ops:
  0.6 50.9 %copy-start = (bf16[1152,1152]{1,0:T(8,128)(2,1)S(1)}, bf16[1152,1152]{1,0:T(8,128)(2,1)}, u32[]{:S(2)}) copy-start(bf16[1152,1152]{1,0:T(8,128)(2,1)} %param.9) | copy-start | bytes 7962628
  3.5 6.9 %copy-start.15 = (s32[128]{0:T(128)S(1)}, s32[128]{0:T(128)}, u32[]{:S(2)}) copy-start(s32[128]{0:T(128)} %param.12) | copy-start | bytes 1540
  3.5 7.0 %copy-start.11 = (bf16[128,1152]{1,0:T(8,128)(2,1)S(1)}, bf16[128,1152]{1,0:T(8,128)(2,1)}, u32[]{:S(2)}) copy-start(bf16[128,1152]{1,0:T(8,128)(2,1)} %param.8) | copy-start | bytes 884740
  3.5 48.1 %all-to-all-start = ((bf16[8,128,1152]{2,1,0:T(8,128)(2,1)}), bf16[8,128,1152]{2,1,0:T(8,128)(2,1)}, u32[]{:S(2)}, u32[]{:S(2)}) async-start(bf16[8,128,1152]{2,1,0:T(8,128)(2,1)} %broadcast_in_dim.2), calls=%async_computation | async-start | bytes 4718592 | tf_op jit(solution)/shard_map/all_to_all | solution.py:65
  10.5 10.8 %copy-start.3 = (bf16[144,1152]{1,0:T(8,128)(2,1)}, bf16[144,1152]{1,0:T(8,128)(2,1)S(1)}, u32[]{:S(2)}) copy-start(bf16[144,1152]{1,0:T(8,128)(2,1)S(1)} %pad_maximum_fusion.refs_1_.refs_8_) | copy-start | bytes 995332
  10.5 10.8 %collective-permute-start = (bf16[144,1152]{1,0:T(8,128)(2,1)S(1)}, bf16[144,1152]{1,0:T(8,128)(2,1)S(1)}, u32[]{:S(2)}, u32[]{:S(2)}) collective-permute-start(bf16[144,1152]{1,0:T(8,128)(2,1)S(1)} %pad_maximum_fusion.refs_1_.refs_8_), channel_id=1, source_target_pairs={{0,24},{1,25},{2,26},{3,27},{4,28},{5,29},{6,30},{7,31},{8,16},{9,... | collective-permute-start | bytes 995336 | tf_op jit(solution)/shard_map/ppermute | solution.py:61
  13.3 9.7 %collective-permute-start.2 = (bf16[144,1152]{1,0:T(8,128)(2,1)S(1)}, bf16[144,1152]{1,0:T(8,128)(2,1)}, u32[]{:S(2)}, u32[]{:S(2)}) collective-permute-start(bf16[144,1152]{1,0:T(8,128)(2,1)S(1)} %pad_maximum_fusion.refs_1_.refs_8_), channel_id=1, source_target_pairs={{0,2},{1,3},{2,4},{3,5},{4,6},{5,7},{6,0},{7,1},{8,10},{9,11},{10,... | collective-permute-start | bytes 995336 | tf_op jit(solution)/shard_map/ppermute | solution.py:61
  14.6 8.4 %collective-permute-start.3 = (bf16[144,1152]{1,0:T(8,128)(2,1)S(1)}, bf16[144,1152]{1,0:T(8,128)(2,1)}, u32[]{:S(2)}, u32[]{:S(2)}) collective-permute-start(bf16[144,1152]{1,0:T(8,128)(2,1)S(1)} %pad_maximum_fusion.refs_1_.refs_8_), channel_id=1, source_target_pairs={{0,6},{1,7},{2,0},{3,1},{4,2},{5,3},{6,4},{7,5},{8,14},{9,15},{10,... | collective-permute-start | bytes 995336 | tf_op jit(solution)/shard_map/ppermute | solution.py:61
  21.3 17.9 %copy-start.4 = (bf16[144,1152]{1,0:T(8,128)(2,1)}, bf16[144,1152]{1,0:T(8,128)(2,1)S(1)}, u32[]{:S(2)}) copy-start(bf16[144,1152]{1,0:T(8,128)(2,1)S(1)} %collective-permute-done.refs_2_.refs_9_) | copy-start | bytes 995332
  21.3 8.2 %collective-permute-start.1 = (bf16[144,1152]{1,0:T(8,128)(2,1)S(1)}, bf16[144,1152]{1,0:T(8,128)(2,1)}, u32[]{:S(2)}, u32[]{:S(2)}) collective-permute-start(bf16[144,1152]{1,0:T(8,128)(2,1)S(1)} %collective-permute-done.refs_2_.refs_9_), channel_id=1, source_target_pairs={{0,6},{1,7},{2,0},{3,1},{4,2},{5,3},{6,4},{7,5},{8,14},{9,15},{10,... | collective-permute-start | bytes 995336 | tf_op jit(solution)/shard_map/ppermute | solution.py:61
  23.1 9.7 %collective-permute-start.6 = (bf16[144,1152]{1,0:T(8,128)(2,1)S(1)}, bf16[144,1152]{1,0:T(8,128)(2,1)}, u32[]{:S(2)}, u32[]{:S(2)}) collective-permute-start(bf16[144,1152]{1,0:T(8,128)(2,1)S(1)} %collective-permute-done.refs_2_.refs_9_), channel_id=1, source_target_pairs={{0,2},{1,3},{2,4},{3,5},{4,6},{5,7},{6,0},{7,1},{8,10},{9,11},{10,... | collective-permute-start | bytes 995336 | tf_op jit(solution)/shard_map/ppermute | solution.py:61
  29.5 9.2 %collective-permute-start.4 = (bf16[144,1152]{1,0:T(8,128)(2,1)}, bf16[144,1152]{1,0:T(8,128)(2,1)S(1)}, u32[]{:S(2)}, u32[]{:S(2)}) collective-permute-start(bf16[144,1152]{1,0:T(8,128)(2,1)} %collective-permute-done.2.refs_7_.refs_14_), channel_id=1, source_target_pairs={{0,2},{1,3},{2,4},{3,5},{4,6},{5,7},{6,0},{7,1},{8,10},{9,11},{10,... | collective-permute-start | bytes 995336 | tf_op jit(solution)/shard_map/ppermute | solution.py:61
  31.6 7.6 %collective-permute-start.5 = (bf16[144,1152]{1,0:T(8,128)(2,1)}, bf16[144,1152]{1,0:T(8,128)(2,1)}, u32[]{:S(2)}, u32[]{:S(2)}) collective-permute-start(bf16[144,1152]{1,0:T(8,128)(2,1)} %collective-permute-done.1.refs_4_.refs_11_), channel_id=1, source_target_pairs={{0,6},{1,7},{2,0},{3,1},{4,2},{5,3},{6,4},{7,5},{8,14},{9,15},{10,... | collective-permute-start | bytes 995336 | tf_op jit(solution)/shard_map/ppermute | solution.py:61
  48.6 17.4 %collective-permute-start.7 = (bf16[1168,1024]{1,0:T(8,128)(2,1)}, bf16[1168,1024]{1,0:T(8,128)(2,1)}, u32[]{:S(2)}, u32[]{:S(2)}) collective-permute-start(bf16[1168,1024]{1,0:T(8,128)(2,1)} %get-tuple-element.46.refs_4_.refs_6_), channel_id=1, source_target_pairs={{0,1},{1,0},{2,3},{3,2},{4,5},{5,4},{6,7},{7,6},{8,9},{9,8},{10,11... | collective-permute-start | bytes 7176200 | tf_op jit(solution)/shard_map/ppermute | solution.py:61
  78.2 23.8 %collective-permute-start.8 = (bf16[1280,1024]{1,0:T(8,128)(2,1)}, bf16[1280,1024]{1,0:T(8,128)(2,1)}, u32[]{:S(2)}, u32[]{:S(2)}) collective-permute-start(bf16[1280,1024]{1,0:T(8,128)(2,1)} %get-tuple-element.54), channel_id=1, source_target_pairs={{0,1},{1,0},{2,3},{3,2},{4,5},{5,4},{6,7},{7,6},{8,9},{9,8},{10,11... | collective-permute-start | bytes 7864328 | tf_op jit(solution)/shard_map/ppermute | solution.py:61
  96.8 40.6 %all-to-all-start.1 = ((bf16[8,160,1024]{2,1,0:T(8,128)(2,1)}), bf16[8,160,1024]{2,1,0:T(8,128)(2,1)}, u32[]{:S(2)}, u32[]{:S(2)}) async-start(bf16[8,160,1024]{2,1,0:T(8,128)(2,1)} %get-tuple-element.50), calls=%async_computation.1 | async-start | bytes 5242880 | tf_op jit(solution)/shard_map/all_to_all | solution.py:65
  105.2 10.3 %collective-permute-start.9 = (bf16[160,1024]{1,0:T(8,128)(2,1)}, bf16[160,1024]{1,0:T(8,128)(2,1)S(1)}, u32[]{:S(2)}, u32[]{:S(2)}) collective-permute-start(bf16[160,1024]{1,0:T(8,128)(2,1)} %get-tuple-element.55), channel_id=1, source_target_pairs={{0,2},{1,3},{2,4},{3,5},{4,6},{5,7},{6,0},{7,1},{8,10},{9,11},{10,... | collective-permute-start | bytes 983048 | tf_op jit(solution)/shard_map/ppermute | solution.py:61
  105.9 9.6 %collective-permute-start.10 = (bf16[160,1024]{1,0:T(8,128)(2,1)}, bf16[160,1024]{1,0:T(8,128)(2,1)S(1)}, u32[]{:S(2)}, u32[]{:S(2)}) collective-permute-start(bf16[160,1024]{1,0:T(8,128)(2,1)} %get-tuple-element.56), channel_id=1, source_target_pairs={{0,6},{1,7},{2,0},{3,1},{4,2},{5,3},{6,4},{7,5},{8,14},{9,15},{10,... | collective-permute-start | bytes 983048 | tf_op jit(solution)/shard_map/ppermute | solution.py:61
  116.3 9.5 %collective-permute-start.11 = (bf16[160,1024]{1,0:T(8,128)(2,1)}, bf16[160,1024]{1,0:T(8,128)(2,1)S(1)}, u32[]{:S(2)}, u32[]{:S(2)}) collective-permute-start(bf16[160,1024]{1,0:T(8,128)(2,1)} %get-tuple-element.58), channel_id=1, source_target_pairs={{0,2},{1,3},{2,4},{3,5},{4,6},{5,7},{6,0},{7,1},{8,10},{9,11},{10,... | collective-permute-start | bytes 983048 | tf_op jit(solution)/shard_map/ppermute | solution.py:61
  119.8 8.5 %collective-permute-start.12 = (bf16[160,1024]{1,0:T(8,128)(2,1)}, bf16[160,1024]{1,0:T(8,128)(2,1)S(1)}, u32[]{:S(2)}, u32[]{:S(2)}) collective-permute-start(bf16[160,1024]{1,0:T(8,128)(2,1)} %get-tuple-element.61), channel_id=1, source_target_pairs={{0,6},{1,7},{2,0},{3,1},{4,2},{5,3},{6,4},{7,5},{8,14},{9,15},{10,... | collective-permute-start | bytes 983048 | tf_op jit(solution)/shard_map/ppermute | solution.py:61
  128.2 17.5 %collective-permute-start.13 = (bf16[160,1024]{1,0:T(8,128)(2,1)}, bf16[160,1024]{1,0:T(8,128)(2,1)}, u32[]{:S(2)}, u32[]{:S(2)}) collective-permute-start(bf16[160,1024]{1,0:T(8,128)(2,1)} %get-tuple-element.64), channel_id=1, source_target_pairs={{0,2},{1,3},{2,4},{3,5},{4,6},{5,7},{6,0},{7,1},{8,10},{9,11},{10,... | collective-permute-start | bytes 983048 | tf_op jit(solution)/shard_map/ppermute | solution.py:61
  129.4 16.3 %collective-permute-start.14 = (bf16[160,1024]{1,0:T(8,128)(2,1)}, bf16[160,1024]{1,0:T(8,128)(2,1)}, u32[]{:S(2)}, u32[]{:S(2)}) collective-permute-start(bf16[160,1024]{1,0:T(8,128)(2,1)} %get-tuple-element.65), channel_id=1, source_target_pairs={{0,6},{1,7},{2,0},{3,1},{4,2},{5,3},{6,4},{7,5},{8,14},{9,15},{10,... | collective-permute-start | bytes 983048 | tf_op jit(solution)/shard_map/ppermute | solution.py:61
  134.5 11.3 %collective-permute-start.15 = (bf16[160,1024]{1,0:T(8,128)(2,1)}, bf16[160,1024]{1,0:T(8,128)(2,1)S(1)}, u32[]{:S(2)}, u32[]{:S(2)}) collective-permute-start(bf16[160,1024]{1,0:T(8,128)(2,1)} %shard_map.108), channel_id=1, source_target_pairs={{0,24},{1,25},{2,26},{3,27},{4,28},{5,29},{6,30},{7,31},{8,16},{9,... | collective-permute-start | bytes 983048 | tf_op jit(solution)/shard_map/ppermute | solution.py:61
  142.3 20.7 %collective-permute-start.16 = (bf16[144,1152]{1,0:T(8,128)(2,1)}, bf16[144,1152]{1,0:T(8,128)(2,1)}, u32[]{:S(2)}, u32[]{:S(2)}) collective-permute-start(bf16[144,1152]{1,0:T(8,128)(2,1)} %get-tuple-element.52.img), channel_id=1, source_target_pairs={{0,1},{1,0},{2,3},{3,2},{4,5},{5,4},{6,7},{7,6},{8,9},{9,8},{10,11... | collective-permute-start | bytes 995336 | tf_op jit(solution)/shard_map/ppermute | solution.py:61
  151.3 11.7 %collective-permute-start.17 = (bf16[144,1152]{1,0:T(8,128)(2,1)}, bf16[144,1152]{1,0:T(8,128)(2,1)}, u32[]{:S(2)}, u32[]{:S(2)}) collective-permute-start(bf16[144,1152]{1,0:T(8,128)(2,1)} %get-tuple-element.69.txt), channel_id=1, source_target_pairs={{0,1},{1,0},{2,3},{3,2},{4,5},{5,4},{6,7},{7,6},{8,9},{9,8},{10,11... | collective-permute-start | bytes 995336 | tf_op jit(solution)/shard_map/ppermute | solution.py:61
  151.6 15.1 %collective-permute-start.18 = (bf16[4,144,128]{2,1,0:T(8,128)(2,1)}, bf16[4,144,128]{2,1,0:T(8,128)(2,1)S(1)}, u32[]{:S(2)}, u32[]{:S(2)}) collective-permute-start(bf16[4,144,128]{2,1,0:T(8,128)(2,1)} %get-tuple-element.70), channel_id=1, source_target_pairs={{0,24},{1,25},{2,26},{3,27},{4,28},{5,29},{6,30},{7,31},{8,16},{9,... | collective-permute-start | bytes 442376 | tf_op jit(solution)/shard_map/ppermute | solution.py:61
  159.0 7.7 %copy-start.12 = (bf16[4,144,128]{2,1,0:T(8,128)(2,1)S(1)}, bf16[4,144,128]{2,1,0:T(8,128)(2,1)}, u32[]{:S(2)}) copy-start(bf16[4,144,128]{2,1,0:T(8,128)(2,1)} %get-tuple-element.72) | copy-start | bytes 442372
  159.0 11.9 %all-to-all-start.2 = ((bf16[8,144,128]{2,1,0:T(8,128)(2,1)}), bf16[8,144,128]{2,1,0:T(8,128)(2,1)S(1)}, u32[]{:S(2)}, u32[]{:S(2)}) async-start(bf16[8,144,128]{2,1,0:T(8,128)(2,1)} %get-tuple-element.51), calls=%async_computation.2 | async-start | bytes 589824 | tf_op jit(solution)/shard_map/all_to_all | solution.py:65
  167.5 13.3 %collective-permute-start.21 = (bf16[288,128]{1,0:T(8,128)(2,1)}, bf16[288,128]{1,0:T(8,128)(2,1)S(1)}, u32[]{:S(2)}, u32[]{:S(2)}) collective-permute-start(bf16[288,128]{1,0:T(8,128)(2,1)} %get-tuple-element.79), channel_id=1, source_target_pairs={{0,2},{1,3},{2,4},{3,5},{4,6},{5,7},{6,0},{7,1},{8,10},{9,11},{10,... | collective-permute-start | bytes 221192 | tf_op jit(solution)/shard_map/ppermute | solution.py:61
  167.5 13.3 %collective-permute-start.20 = (bf16[288,128]{1,0:T(8,128)(2,1)}, bf16[288,128]{1,0:T(8,128)(2,1)}, u32[]{:S(2)}, u32[]{:S(2)}) collective-permute-start(bf16[288,128]{1,0:T(8,128)(2,1)} %get-tuple-element.78), channel_id=1, source_target_pairs={{0,4},{1,5},{2,6},{3,7},{4,0},{5,1},{6,2},{7,3},{8,12},{9,13},{10,... | collective-permute-start | bytes 221192 | tf_op jit(solution)/shard_map/ppermute | solution.py:61
  170.4 10.3 %collective-permute-start.19 = (bf16[288,128]{1,0:T(8,128)(2,1)}, bf16[288,128]{1,0:T(8,128)(2,1)}, u32[]{:S(2)}, u32[]{:S(2)}) collective-permute-start(bf16[288,128]{1,0:T(8,128)(2,1)} %get-tuple-element.77), channel_id=1, source_target_pairs={{0,6},{1,7},{2,0},{3,1},{4,2},{5,3},{6,4},{7,5},{8,14},{9,15},{10,... | collective-permute-start | bytes 221192 | tf_op jit(solution)/shard_map/ppermute | solution.py:61
  170.9 17.9 %all-to-all-start.3 = ((bf16[64,8,384]{2,1,0:T(8,128)(2,1)}), bf16[64,8,384]{2,1,0:T(8,128)(2,1)S(1)}, u32[]{:S(2)}, u32[]{:S(2)}) async-start(bf16[64,8,384]{2,1,0:T(8,128)(2,1)} %bitcast.44), calls=%async_computation.3 | async-start | bytes 786432 | tf_op jit(solution)/shard_map/all_to_all | solution.py:65
  (10 other events, 24.0 us)

commit v3 on v2

--- a/solution.py
+++ b/solution.py
@@ -137,6 +137,38 @@
         turned[span] = (proj[span] * inverse).astype(b16)
 
 
+def img_unit_kernel(at_ref, feats, turned_head, head, turned, norm, unit, proj):
+    put_units(feats, turned_head, proj, turned, norm)
+    part = dot(feats[...], head[...], NN)
+    total = jnp.sum(part * part, axis=1, keepdims=True)
+    unit[...] = (part * (1.0 / jnp.sqrt(total + epsilon))).astype(b16)
+
+
+def img_units(feats, turned_head, head, rows):
+    count, width = feats.shape
+    tile = 2 * rows
+    whole = pl.BlockSpec(head.shape, lambda i, at: (0, 0))
+    return call(
+        img_unit_kernel,
+        [
+            jax.ShapeDtypeStruct((width, count), b16),
+            jax.ShapeDtypeStruct((1, count), f32),
+            jax.ShapeDtypeStruct((count, width), b16),
+        ],
+        [jnp.int32(0)],
+        [feats, turned_head, head],
+        in_specs=[pl.BlockSpec((tile, width), lambda i, at: (i, 0)), whole, whole],
+        out_specs=[
+            pl.BlockSpec((width, tile), lambda i, at: (0, i)),
+            pl.BlockSpec((1, tile), lambda i, at: (0, i)),
+            pl.BlockSpec((tile, width), lambda i, at: (i, 0)),
+        ],
+        grid=(4,),
+        scratch=[pltpu.VMEM((width, tile), f32)],
+        cost=4 * count * width * width,
+    )
+
+
 def unit_kernel(rows, at_ref, *refs):
     blocks, (turned_head, turned, norm, feats, proj) = refs[:8], refs[8:]
     width = turned_head.shape[0]
@@ -177,18 +209,6 @@
         scratch=[pltpu.VMEM((tile, width), b16), pltpu.VMEM((width, tile), f32)],
         cost=2 * 8 * rows * width * width,
     )
-
-
-def unit_columns(feats, head):
-    projected = dot(head, feats, (((0,), (1,)), ((), ())))
-    norm = jnp.sqrt(jnp.sum(projected * projected, axis=0, keepdims=True) + epsilon)
-    return (projected / norm).astype(b16), norm
-
-
-def unit_rows(feats, head):
-    projected = dot(feats, head, NN)
-    norm = jnp.sqrt(jnp.sum(projected * projected, axis=1, keepdims=True) + epsilon)
-    return (projected / norm).astype(b16)
 
 
 def tile_slopes(rows, groups, place, bias_ref, img, txt, slopes, by_img):
@@ -232,7 +252,7 @@
         up[at + slab : at + slab + PAD] = figures
 
 
-def other_kernel(rows, groups, at_ref, bias_ref, img, turned, txt, slopes, img_sum, up, by_img):
+def pair_kernel(rows, groups, at_ref, bias_ref, img, turned, txt, slopes, img_sum, up, by_img):
     step = pl.program_id(0)
 
     @pl.when(step == 0)
@@ -247,13 +267,13 @@
         img_sum[...] = logit_scale * jnp.sum(by_img[...].T, axis=0, keepdims=True)
 
 
-def other_tile(img, turned, txt, group_bias, place, rows):
+def pair_tile(img, turned, txt, group_bias, place, rows):
     count, width = img.shape
     tile = 2 * rows
     height = width + 8 * PAD
     whole = lambda a: pl.BlockSpec(a.shape, lambda i, at: (0, 0))
     return call(
-        lambda *refs: other_kernel(rows, group_bias.shape[0], *refs),
+        lambda *refs: pair_kernel(rows, group_bias.shape[0], *refs),
         [
             jax.ShapeDtypeStruct((4, count, tile), b16),
             jax.ShapeDtypeStruct((1, count), f32),
@@ -278,67 +298,55 @@
     )
 
 
-def own_kernel(rows, groups, at_ref, bias_ref, img, turned, txt, other, *refs):
-    other_slopes, other_sum, up, out, by_img, held, both, total = refs
+def image_kernel(at_ref, txt, other, slopes, other_slopes, img_sum, other_sum, out, held, both, total):
     step = pl.program_id(0)
-    width = img.shape[1]
-    tile = 2 * rows
+    width, tile = total.shape[0], txt.shape[1]
+    slab = width // 8
+    both[:, :tile] = txt[:width]
+    both[:, tile:] = other[:width]
+    held[:, :tile] = slopes[0]
+    held[:, tile:] = other_slopes[0]
+    part = dot(both[...], held[...], NT)
 
     @pl.when(step == 0)
     def _():
-        by_img[...] = jnp.zeros(by_img.shape, f32)
-        total[...] = jnp.zeros(total.shape, f32)
-
-    both[:, tile:] = other[:width]
-    held[:, tile:] = other_slopes[0]
-    both[:, :tile] = txt[:width]
-    down = tile_slopes(rows, groups, at_ref[0], bias_ref, img, txt, held, by_img)
-    put_text_terms(up, turned, held[:, :tile], down)
-    total[...] += dot(both[...], held[...], NT)
+        total[...] = part
+
+    @pl.when(step != 0)
+    def _():
+        total[...] += part
 
     @pl.when(step == 3)
     def _():
-        slab = width // 8
-        sums = logit_scale * jnp.sum(by_img[...].T, axis=0, keepdims=True) + other_sum[...]
+        sums = img_sum[...] + other_sum[...]
         figures = split_rows(sums, sums.shape[1])
         for e in range(8):
             out[e, :slab] = total[e * slab : (e + 1) * slab].astype(b16)
             out[e, slab:] = figures
 
 
-def own_tile(
-    img, turned, txt, other, other_slopes, other_sum, group_bias, place, rows
-):
-    count, width = img.shape
+def image_tile(txt, other, slopes, other_slopes, img_sum, other_sum, rows):
+    height, count = txt.shape
+    width = height - PAD
     tile = 2 * rows
-    height = width + 8 * PAD
-    slab = width // 8
-    whole = lambda a: pl.BlockSpec(a.shape, lambda i, at: (0, 0))
-    stack = lambda a: pl.BlockSpec(a.shape, lambda i, at: (0, 0, 0))
-    pieces = jax.ShapeDtypeStruct((8, slab + PAD, count), b16)
+    pieces = jax.ShapeDtypeStruct((8, width // 8 + PAD, count), b16)
+    whole = pl.BlockSpec((1, count), lambda i, at: (0, 0))
     return call(
-        lambda *refs: own_kernel(rows, group_bias.shape[0], *refs),
-        [jax.ShapeDtypeStruct((height, count), b16), pieces],
-        [place],
-        [group_bias, img, turned, txt, other, other_slopes, other_sum],
-        in_specs=[
-            pl.BlockSpec(memory_space=pltpu.SMEM),
-            whole(img),
-            whole(turned),
-            pl.BlockSpec((width + PAD, tile), lambda i, at: (0, i)),
-            pl.BlockSpec((width + PAD, tile), lambda i, at: (0, i)),
-            pl.BlockSpec((1, count, tile), lambda i, at: (i, 0, 0)),
-            whole(other_sum),
-        ],
-        out_specs=[pl.BlockSpec((height, tile), lambda i, at: (0, i)), stack(pieces)],
+        image_kernel,
+        pieces,
+        [jnp.int32(0)],
+        [txt, other, slopes, other_slopes, img_sum, other_sum],
+        in_specs=[pl.BlockSpec((height, tile), lambda i, at: (0, i))] * 2
+        + [pl.BlockSpec((1, count, tile), lambda i, at: (i, 0, 0))] * 2
+        + [whole, whole],
+        out_specs=pl.BlockSpec(pieces.shape, lambda i, at: (0, 0, 0)),
         grid=(4,),
         scratch=[
-            pltpu.VMEM((count, min(128, tile)), f32),
             pltpu.VMEM((count, 2 * tile), b16),
             pltpu.VMEM((width, 2 * tile), b16),
             pltpu.VMEM((width, count), f32),
         ],
-        cost=8 * width * count * count,
+        cost=4 * width * count * count,
     )
 
 
@@ -387,15 +395,22 @@
     )
 
 
-def img_grad_kernel(rows, at_ref, got, unit, norm, feats, blocks, part, grad):
+def put_blocks(grad, second, own, give, rows):
+    for ring in range(4):
+        low = grad[:, (2 * ring) * rows : (2 * ring + 1) * rows]
+        high = grad[:, (2 * ring + 1) * rows : (2 * ring + 2) * rows]
+        own[ring] = jnp.where(second == 0, low, high)
+        give[ring] = jnp.where(second == 0, high, low)
+
+
+def img_grad_kernel(rows, at_ref, got, unit, norm, feats, own, give, part, grad):
     slab = unit.shape[0]
     up, inner = got[0, :slab].astype(f32), joined(got[0, slab:])
     for n in range(1, 8):
         up, inner = up + got[n, :slab].astype(f32), inner + joined(got[n, slab:])
     up = logit_scale * up - unit[...].astype(f32) * inner
     grad[...] = (up * (1.0 / norm[...])).astype(b16)
-    for n in range(8):
-        blocks[n] = grad[:, n * rows : (n + 1) * rows]
+    put_blocks(grad, at_ref[1], own, give, rows)
     part[...] = dot(grad[...], feats[...], NN).astype(b16)
 
 
@@ -409,11 +424,7 @@
         up, inner = up + term[:slab].astype(f32), inner + joined(term[slab:])
     up = logit_scale * up - unit[...].astype(f32) * inner
     grad[...] = (up * (1.0 / norm[...])).astype(b16)
-    for ring in range(4):
-        low = grad[:, (2 * ring) * rows : (2 * ring + 1) * rows]
-        high = grad[:, (2 * ring + 1) * rows : (2 * ring + 2) * rows]
-        own[ring] = jnp.where(at_ref[1] == 0, low, high)
-        give[ring] = jnp.where(at_ref[1] == 0, high, low)
+    put_blocks(grad, at_ref[1], own, give, rows)
     total = None
     for d in range(4):
         cols = grad[:, aligned((at_ref[2] + d) % 4, 2 * rows)]
@@ -422,22 +433,22 @@
     part[...] = total.astype(b16)
 
 
-def gradient(kernel, place, second, ring, terms, unit, norm, feats, halves, rows):
+def gradient(kernel, place, second, ring, terms, unit, norm, feats, rows):
     width = feats[0].shape[1]
     slab, count = width // 8, 8 * rows
     whole = lambda a: pl.BlockSpec(a.shape, lambda i, at: (0,) * len(a.shape))
     mine = lambda height: pl.BlockSpec((height, count), lambda i, at: (at[0], 0))
-    block = jax.ShapeDtypeStruct((8 // halves, slab, rows), b16)
+    block = jax.ShapeDtypeStruct((4, slab, rows), b16)
     part = jax.ShapeDtypeStruct((slab, width), b16)
     return call(
         lambda *refs: kernel(rows, *refs),
-        [block] * halves + [part],
+        [block, block, part],
         [place, second, ring],
         [term[0] if isinstance(term, tuple) else term for term in terms] + [unit, norm, *feats],
         in_specs=[mine(slab + PAD) if isinstance(term, tuple) else whole(term) for term in terms]
         + [mine(slab), whole(norm)]
         + [whole(a) for a in feats],
-        out_specs=[whole(block)] * halves + [whole(part)],
+        out_specs=[whole(block), whole(block), whole(part)],
         grid=(1,),
         scratch=[pltpu.VMEM((slab, count), b16)],
         cost=2 * slab * count * width,
@@ -512,14 +523,9 @@
     for d in range(4):
         block = lax.dynamic_index_in_dim(lines, (ring + d) % 4, 0, keepdims=False)
         got.append(send(block, move(d, 0)) if d else block)
-    return jnp.concatenate([got[-d % 4] for d in range(4)], axis=0)
-
-
-def from_ring(turned_head, ring):
-    start = ring * (turned_head.shape[0] // 4)
-    return lax.dynamic_slice_in_dim(
-        jnp.concatenate([turned_head, turned_head]), start, turned_head.shape[0], axis=0
-    )
+    height = got[0].shape[0]
+    from_own = jnp.concatenate([got[-d % 4] for d in range(4)] * 2, axis=0)
+    return lax.dynamic_slice_in_dim(from_own, (4 - ring) % 4 * height, 4 * height, axis=0)
 
 
 def shards(image_feat, text_feat, image_head, text_head, group_bias, text_lang, partner):
@@ -539,7 +545,9 @@
     across, turned_txt = together([across, text_head.T])
     across_after = send(across, txt_move(3, 0))
     across_before = send(across, txt_move(1, 0))
-    across_after, before, after, across = together([across_after, before, after, across])
+    across_after, before, after, across, turned_img = together(
+        [across_after, before, after, across, image_head.T]
+    )
     far = send(before, txt_move(1, 0))
     across_far = send(across_after, txt_move(3, 0))
     txt_blocks = [
@@ -547,19 +555,15 @@
     ]
     unit_txt, norm_txt = units(txt_blocks, turned_txt, y, hi, rows)
     other_txt = send(unit_txt, core_move)
-    turned_units, norm_img = unit_columns(img_feats, image_head)
-    unit_img = unit_rows(together([img_feats, unit_txt])[0], image_head)
-
-    other_slopes, other_sum, other_up = other_tile(
+    turned_units, norm_img, unit_img = img_units(img_feats, turned_img, image_head, rows)
+
+    other_slopes, other_sum, other_up = pair_tile(
         unit_img, turned_units, other_txt, group_bias, place % 16, rows
     )
     back = send(other_up, core_move)
-    text_up, img_terms = own_tile(
-        unit_img, turned_units, unit_txt, other_txt, other_slopes, other_sum, group_bias,
-        place % 16, rows,
-    )
-    img_terms = exchange(img_terms, IMG_GROUPS)
-    (txt_ring_head,) = together([from_ring(turned_txt, y)])
+    slopes, img_sum, text_up = pair_tile(
+        unit_img, turned_units, unit_txt, group_bias, place % 16, rows
+    )
 
     def slab_terms(d, e):
         at = (y + d) % 4 * 2 + (hi + e) % 2
@@ -568,8 +572,12 @@
     far, across_far, across_after = sums(
         [slab_terms(2, 0), slab_terms(2, 1), slab_terms(1, 1)], rows
     )
+    far, across_far, across_after, slopes = together([far, across_far, across_after, slopes])
     far = send(far, txt_move(1, 0))
     across_far = send(across_far, txt_move(3, 0))
+    img_terms = exchange(
+        image_tile(unit_txt, other_txt, slopes, other_slopes, img_sum, other_sum, rows), IMG_GROUPS
+    )
     far, across_far, across_after = together([far, across_far, across_after])
     across_before = send(across_after, txt_move(1, 0))
     across_after, before, after = sums(
@@ -584,13 +592,13 @@
     (across,) = sums([slab_terms(0, 1) + [across_before, across_after]], rows)
     across = send(across, txt_move(0, 1))
 
-    img_blocks, img_part = gradient(
-        img_grad_kernel, z * 2 + lo, lo, z, [img_terms], turned_units, norm_img, [img_feats], 1, rows
-    )
-    grad_img = exchange(img_blocks, IMG_GROUPS).reshape(width, rows)
+    img_own, img_give, img_part = gradient(
+        img_grad_kernel, z * 2 + lo, lo, z, [img_terms], turned_units, norm_img, [img_feats], rows
+    )
+    img_got = send(img_give, img_move(0, 1))
     txt_own, txt_give, txt_part = gradient(
         txt_grad_kernel, y * 2 + hi, hi, y, slab_terms(0, 0) + [before, after, across],
-        unit_txt, norm_txt, txt_blocks, 2, rows,
+        unit_txt, norm_txt, txt_blocks, rows,
     )
     img_theirs = send(img_part, core_move)
     txt_theirs = send(txt_part, core_move)
@@ -600,9 +608,10 @@
     head_shape = jax.ShapeDtypeStruct((width // 128, width), f32)
     image_head_grad, text_head_grad = call(head_kernel, [head_shape] * 2, [core], [heads])
 
+    grad_img = whole_columns(pair_lines(img_own, img_got, lo), img_move, z)
     image_grad = dot(grad_img, image_head, (((0,), (1,)), ((), ())))
     grad_txt = whole_columns(pair_lines(txt_own, txt_got, hi), txt_move, y)
-    text_grad = dot(grad_txt, txt_ring_head, TN)
+    text_grad = dot(grad_txt, text_head, (((0,), (1,)), ((), ())))
     return (image_grad, text_grad, image_head_grad, text_head_grad)
 
 

time: 194 us -> 220 us (1.13)
  Pallas kernels: 64.5 us -> 81.1 us
  waiting for transfers between devices: 30.9 us -> 44.7 us
  local copies, waits for them, and re-layouts: 11.9 us -> 24.1 us
  matrix products: 14.4 us -> 3.53 us
  other arithmetic: 12.8 us -> 5.03 us
    pallas_call x10 -> x12, Pallas kernels: 64.5 us -> 81.1 us  [call(): pl.pallas_call(body, out_shape=out_shape, grid_spec=spec, input_output_al...]
    all_to_all x4 -> x3, waiting for transfers between devices: 5.75 us -> 17.9 us  [exchange(): lax.all_to_all(blocks, DEV, 0, 0, axis_index_groups=groups, tiled=True)]
    unnamed x33 -> x54, local copies, waits for them, and re-layouts: 7.86 us -> 19.2 us
    dot_general x4 -> x2, matrix products: 14.4 us -> 3.53 us  [dot(): return lax.dot_general(a, b, dims, preferred_element_type=f32)]
    concatenate x1 -> x0, other arithmetic: 5.52 us -> none  [from_ring(): jnp.concatenate([turned_head, turned_head])]
    ppermute x22 -> x26, starting transfers between devices: 32.5 us -> 37.5 us  [send(): lax.ppermute(block, DEV, [(flat(*p), flat(*move(*p))) for p in PLACES])]
    all_to_all x4 -> x3, starting transfers between devices: 23.4 us -> 18.7 us  [exchange(): lax.all_to_all(blocks, DEV, 0, 0, axis_index_groups=groups, tiled=True)]
    convert_element_type x2 -> x0, other arithmetic: 4.16 us -> none  [the longest x1 2.17 us: unit_columns(): return ((projected / norm).astype(b16), norm)]
  transfers between devices with their start and end apart: 26 -> 29, of which waited for: 7 -> 10; matrix products, arithmetic and copies ran while one was open for 18% -> 10% of each run, Pallas kernels for 26% -> 25%
where the time goes in v3:
time: 220 us; the launch traced here: 216 us
  Pallas kernels  81.1 us (37%)
  starting transfers between devices  56.2 us (26%)
  waiting for transfers between devices  44.7 us (20%)
  local copies, waits for them, and re-layouts  24.1 us (11%)
  other arithmetic  5.03 us (2%)
  matrix products  3.53 us (2%)
    pallas_call x12, Pallas kernels, call(): pl.pallas_call(body, out_shape=out_shape, grid_spec=spec, input_output_al...  81.1 us
    ppermute x26, starting transfers between devices, send(): lax.ppermute(block, DEV, [(flat(*p), flat(*move(*p))) for p in PLACES])  37.5 us
    ppermute x26, waiting for transfers between devices, send(): lax.ppermute(block, DEV, [(flat(*p), flat(*move(*p))) for p in PLACES])  26.8 us
    unnamed x54, local copies, waits for them, and re-layouts  19.2 us
    all_to_all x3, starting transfers between devices, exchange(): lax.all_to_all(blocks, DEV, 0, 0, axis_index_groups=groups, tiled=True)  18.7 us
    all_to_all x3, waiting for transfers between devices, exchange(): lax.all_to_all(blocks, DEV, 0, 0, axis_index_groups=groups, tiled=True)  17.9 us
  transfers between devices with their start and end apart: 29, of which 10 were waited for; matrix products, arithmetic and copies ran while one was open for 10% of the time, Pallas kernels for 25%

profile of v3, /device:TPU:1, one launch (start us, length us, event | category | flops | bytes accessed | tf_op | source)
XLA Modules:
  0.0 215.6 jit_solution(11154705486007291376)
XLA Ops:
  2.4 3.4 %collective-permute-start = (bf16[144,1152]{1,0:T(8,128)(2,1)S(1)}, bf16[144,1152]{1,0:T(8,128)(2,1)S(1)}, u32[]{:S(2)}, u32[]{:S(2)}) collective-permute-start(bf16[144,1152]{1,0:T(8,128)(2,1)S(1)} %pad_maximum_fusion.refs_1_.refs_8_), channel_id=1, source_target_pairs={{0,24},{1,25},{2,26},{3,27},{4,28},{5,29},{6,30},{7,31},{8,16},{9,... | collective-permute-start | bytes 995336 | tf_op jit(solution)/shard_map/ppermute | solution.py:61
  8.5 5.2 %copy.11 = bf16[1152,1152]{0,1:T(8,128)(2,1)} copy(bf16[1152,1152]{1,0:T(8,128)(2,1)} %param.10) | data formatting | bytes 5308416 | tf_op args[3]
  13.7 2.3 %collective-permute-start.1 = (bf16[144,1152]{1,0:T(8,128)(2,1)S(1)}, bf16[144,1152]{1,0:T(8,128)(2,1)}, u32[]{:S(2)}, u32[]{:S(2)}) collective-permute-start(bf16[144,1152]{1,0:T(8,128)(2,1)S(1)} %collective-permute-done.refs_2_.refs_9_), channel_id=1, source_target_pairs={{0,6},{1,7},{2,0},{3,1},{4,2},{5,3},{6,4},{7,5},{8,14},{9,15},{10,... | collective-permute-start | bytes 995336 | tf_op jit(solution)/shard_map/ppermute | solution.py:61
  16.0 3.2 %copy.12 = bf16[1152,1152]{0,1:T(8,128)(2,1)} copy(bf16[1152,1152]{1,0:T(8,128)(2,1)S(1)} %copy-done.1) | data formatting | bytes 5308416 | tf_op args[2]
  19.3 3.2 %collective-permute-done.1.refs_4_.refs_11_ = bf16[144,1152]{1,0:T(8,128)(2,1)} collective-permute-done((bf16[144,1152]{1,0:T(8,128)(2,1)S(1)}, bf16[144,1152]{1,0:T(8,128)(2,1)}, u32[]{:S(2)}, u32[]{:S(2)}) %collective-permute-start.1) | collective-permute-done | bytes 331808 | tf_op jit(solution)/shard_map/ppermute | solution.py:61
  25.2 2.7 %broadcast_in_dim.2 = bf16[8,128,1152]{2,1,0:T(8,128)(2,1)} broadcast(bf16[128,1152]{1,0:T(8,128)(2,1)} %param.7), dimensions={1,2} | broadcast | bytes 2654208 | tf_op jit(solution)/shard_map/broadcast_in_dim | solution.py:540
  27.9 5.0 %all-to-all-start = ((bf16[8,128,1152]{2,1,0:T(8,128)(2,1)}), bf16[8,128,1152]{2,1,0:T(8,128)(2,1)S(1)}, u32[]{:S(2)}, u32[]{:S(2)}) async-start(bf16[8,128,1152]{2,1,0:T(8,128)(2,1)} %broadcast_in_dim.2), calls=%async_computation | async-start | bytes 4718592 | tf_op jit(solution)/shard_map/all_to_all | solution.py:65
  35.8 9.1 %shard_map.102 = (bf16[1168,1024]{1,0:T(8,128)(2,1)}, f32[1,1024]{1,0:T(1,128)}) custom-call(s32[2]{0:T(128)} %pad_add_fusion.1.refs_0_, bf16[144,1152]{1,0:T(8,128)(2,1)} %copy-done.7, bf16[144,1152]{1,0:T(8,128)(2,1)} %copy-done.8, bf16[144,1152]{1,0:T(8,128)(2,1)} %collective-permute-done.3.refs_3_.refs_10_, ...), custom_call_target="tpu_custom_call" | custom-call | flops 2717908992 | bytes 5308416 | tf_op jit(solution)/shard_map/pallas_call | solution.py:93
  45.0 2.6 %collective-permute-start.7 = (bf16[1168,1024]{1,0:T(8,128)(2,1)}, bf16[1168,1024]{1,0:T(8,128)(2,1)}, u32[]{:S(2)}, u32[]{:S(2)}) collective-permute-start(bf16[1168,1024]{1,0:T(8,128)(2,1)} %get-tuple-element.55.refs_4_.txt.refs_6_), channel_id=1, source_target_pairs={{0,1},{1,0},{2,3},{3,2},{4,5},{5,4},{6,7},{7,6},{8,9},{9,8},{10,11... | collective-permute-start | bytes 7176200 | tf_op jit(solution)/shard_map/ppermute | solution.py:61
  47.6 11.8 %all-to-all-done = bf16[8,128,1152]{2,1,0:T(8,128)(2,1)S(1)} async-done(((bf16[8,128,1152]{2,1,0:T(8,128)(2,1)}), bf16[8,128,1152]{2,1,0:T(8,128)(2,1)S(1)}, u32[]{:S(2)}, u32[]{:S(2)}) %all-to-all-start) | async-done | bytes 2359328 | tf_op jit(solution)/shard_map/all_to_all | solution.py:65
  60.8 12.0 %shard_map.103 = (bf16[1152,1024]{1,0:T(8,128)(2,1)}, f32[1,1024]{1,0:T(1,128)}, bf16[1024,1152]{1,0:T(8,128)(2,1)}) custom-call(s32[1]{0:T(128)} %constant.208.clone.1.at_ref, bf16[1024,1152]{1,0:T(8,128)(2,1)} %bitcast.51, bf16[1152,1152]{1,0:T(8,128)(2,1)} %bitcast.53, bf16[1152,1152]{1,0:T(8,128)(2,1)} %head.1), custom_call_target="tpu_custom_call" | custom-call | flops 5435817984 | bytes 7667712 | tf_op jit(solution)/shard_map/pallas_call | solution.py:93
  72.8 12.2 %shard_map.105 = (bf16[4,1024,256]{2,1,0:T(8,128)(2,1)}, f32[1,1024]{1,0:T(1,128)}, bf16[1280,1024]{1,0:T(8,128)(2,1)}) custom-call(s32[1]{0:T(128)} %bitcast.13.refs_0_, f32[32]{0:T(128)} %refs_1_.3, bf16[1024,1152]{1,0:T(8,128)(2,1)} %get-tuple-element.57.refs_2_, bf16[1152,1024]{1,0:T(8,128)(2,1)} %get-tuple-element.58.refs_3_.refs_2_, ...), custom_call_target="tpu_custom_call" | custom-call | flops 4831838208 | bytes 7110784 | tf_op jit(solution)/shard_map/pallas_call | solution.py:93
  85.0 4.2 %collective-permute-start.8 = (bf16[1280,1024]{1,0:T(8,128)(2,1)}, bf16[1280,1024]{1,0:T(8,128)(2,1)S(1)}, u32[]{:S(2)}, u32[]{:S(2)}) collective-permute-start(bf16[1280,1024]{1,0:T(8,128)(2,1)} %get-tuple-element.60), channel_id=1, source_target_pairs={{0,1},{1,0},{2,3},{3,2},{4,5},{5,4},{6,7},{7,6},{8,9},{9,8},{10,11... | collective-permute-start | bytes 7864328 | tf_op jit(solution)/shard_map/ppermute | solution.py:61
  89.7 12.2 %shard_map.104 = (bf16[4,1024,256]{2,1,0:T(8,128)(2,1)}, f32[1,1024]{1,0:T(1,128)}, bf16[1280,1024]{1,0:T(8,128)(2,1)}) custom-call(s32[1]{0:T(128)} %bitcast.13.refs_0_, f32[32]{0:T(128)} %refs_1_.3, bf16[1024,1152]{1,0:T(8,128)(2,1)} %get-tuple-element.57.refs_2_, bf16[1152,1024]{1,0:T(8,128)(2,1)} %get-tuple-element.58.refs_3_.refs_2_, ...), custom_call_target="tpu_custom_call" | custom-call | flops 4831838208 | bytes 7110784 | tf_op jit(solution)/shard_map/pallas_call | solution.py:93
  103.4 3.2 %shard_map.106 = (bf16[160,1024]{1,0:T(8,128)(2,1)}, bf16[160,1024]{1,0:T(8,128)(2,1)}, bf16[160,1024]{1,0:T(8,128)(2,1)}) custom-call(s32[7]{0:T(128)} %stack.104.refs_0_, bf16[1280,1024]{1,0:T(8,128)(2,1)} %get-tuple-element.59.refs_1_.refs_3_.refs_5_.refs_4_.refs_7_, bf16[1280,1024]{1,0:T(8,128)(2,1)} %copy-done, ...), custom_call_target="tpu_custom_call" | custom-call | bytes 15728640 | tf_op jit(solution)/shard_map/pallas_call | solution.py:93
  106.6 10.8 %shard_map.107 = bf16[8,160,1024]{2,1,0:T(8,128)(2,1)} custom-call(s32[1]{0:T(128)} %constant.208.clone.1.at_ref, bf16[1168,1024]{1,0:T(8,128)(2,1)} %get-tuple-element.55.refs_4_.txt.refs_6_, bf16[1168,1024]{1,0:T(8,128)(2,1)} %collective-permute-done.7.refs_4_.other, bf16[4,1024,256]{2,1,0:T(8,128)(2,1)} %get-tuple-element.65.slopes, ...), custom_call_target="tpu_custom_call" | custom-call | flops 4831838208 | bytes 8986624 | tf_op jit(solution)/shard_map/pallas_call | solution.py:93
  117.4 3.6 %all-to-all-start.1 = ((bf16[8,160,1024]{2,1,0:T(8,128)(2,1)}), bf16[8,160,1024]{2,1,0:T(8,128)(2,1)S(1)}, u32[]{:S(2)}, u32[]{:S(2)}) async-start(bf16[8,160,1024]{2,1,0:T(8,128)(2,1)} %shard_map.107), calls=%async_computation.1 | async-start | bytes 5242880 | tf_op jit(solution)/shard_map/all_to_all | solution.py:65
  124.4 7.3 %collective-permute-done.13.refs_6_ = bf16[160,1024]{1,0:T(8,128)(2,1)S(1)} collective-permute-done((bf16[160,1024]{1,0:T(8,128)(2,1)}, bf16[160,1024]{1,0:T(8,128)(2,1)S(1)}, u32[]{:S(2)}, u32[]{:S(2)}) %collective-permute-start.13) | collective-permute-done | bytes 327712 | tf_op jit(solution)/shard_map/ppermute | solution.py:61
  133.2 3.4 %shard_map.109 = (bf16[160,1024]{1,0:T(8,128)(2,1)}, bf16[160,1024]{1,0:T(8,128)(2,1)}, bf16[160,1024]{1,0:T(8,128)(2,1)}) custom-call(s32[7]{0:T(128)} %stack.112.refs_0_, bf16[1280,1024]{1,0:T(8,128)(2,1)} %get-tuple-element.59.refs_1_.refs_3_.refs_5_.refs_4_.refs_7_, bf16[1280,1024]{1,0:T(8,128)(2,1)} %copy-done, bf16[160,1024]{1,0:T(8,128)(2,1)} %copy-done.15, ...), custom_call_target="tpu_custom_call" | custom-call | bytes 16384000 | tf_op jit(solution)/shard_map/pallas_call | solution.py:93
  138.9 6.3 %collective-permute-done.16.refs_4_ = bf16[160,1024]{1,0:T(8,128)(2,1)S(1)} collective-permute-done((bf16[160,1024]{1,0:T(8,128)(2,1)}, bf16[160,1024]{1,0:T(8,128)(2,1)S(1)}, u32[]{:S(2)}, u32[]{:S(2)}) %collective-permute-start.16) | collective-permute-done | bytes 327712 | tf_op jit(solution)/shard_map/ppermute | solution.py:61
  145.2 2.2 %collective-permute-done.15.refs_3_ = bf16[160,1024]{1,0:T(8,128)(2,1)S(1)} collective-permute-done((bf16[160,1024]{1,0:T(8,128)(2,1)}, bf16[160,1024]{1,0:T(8,128)(2,1)S(1)}, u32[]{:S(2)}, u32[]{:S(2)}) %collective-permute-start.15) | collective-permute-done | bytes 327712 | tf_op jit(solution)/shard_map/ppermute | solution.py:61
  148.2 2.9 %shard_map.110 = bf16[160,1024]{1,0:T(8,128)(2,1)} custom-call(s32[3]{0:T(128)} %pad_add_fusion.3.refs_0_, bf16[1280,1024]{1,0:T(8,128)(2,1)} %get-tuple-element.59.refs_1_.refs_3_.refs_5_.refs_4_.refs_7_, bf16[1280,1024]{1,0:T(8,128)(2,1)} %copy-done, bf16[160,1024]{1,0:T(8,128)(2,1)} %copy-done.11, bf16[160,1024]{1,0:T(8,128)(2,1)} %copy-done.10), custom_call_target="tpu_custom_call" | custom-call | bytes 5898240 | tf_op jit(solution)/shard_map/pallas_call | solution.py:93
  151.0 2.8 %collective-permute-start.19 = (bf16[160,1024]{1,0:T(8,128)(2,1)}, bf16[160,1024]{1,0:T(8,128)(2,1)S(1)}, u32[]{:S(2)}, u32[]{:S(2)}) collective-permute-start(bf16[160,1024]{1,0:T(8,128)(2,1)} %shard_map.110), channel_id=1, source_target_pairs={{0,24},{1,25},{2,26},{3,27},{4,28},{5,29},{6,30},{7,31},{8,16},{9,... | collective-permute-start | bytes 983048 | tf_op jit(solution)/shard_map/ppermute | solution.py:61
  153.8 2.7 %collective-permute-start.18 = (bf16[160,1024]{1,0:T(8,128)(2,1)}, bf16[160,1024]{1,0:T(8,128)(2,1)}, u32[]{:S(2)}, u32[]{:S(2)}) collective-permute-start(bf16[160,1024]{1,0:T(8,128)(2,1)} %get-tuple-element.83), channel_id=1, source_target_pairs={{0,6},{1,7},{2,0},{3,1},{4,2},{5,3},{6,4},{7,5},{8,14},{9,15},{10,... | collective-permute-start | bytes 983048 | tf_op jit(solution)/shard_map/ppermute | solution.py:61
  158.7 4.9 %shard_map.108 = (bf16[4,144,128]{2,1,0:T(8,128)(2,1)}, bf16[4,144,128]{2,1,0:T(8,128)(2,1)}, bf16[144,1152]{1,0:T(8,128)(2,1)}) custom-call(s32[3]{0:T(128)} %pad_add_fusion.refs_0_, bf16[8,160,1024]{2,1,0:T(8,128)(2,1)} %copy-done.4, bf16[1152,1024]{1,0:T(8,128)(2,1)} %get-tuple-element.58.refs_3_.refs_2_, f32[1,1024]{1,0:T(1,128)} %get-tuple-element.69.refs_3_, ...), custom_call_target="tpu_custom_call" | custom-call | flops 339738624 | bytes 7344128 | tf_op jit(solution)/shard_map/pallas_call | solution.py:93
  165.2 5.0 %shard_map.111 = (bf16[4,144,128]{2,1,0:T(8,128)(2,1)}, bf16[4,144,128]{2,1,0:T(8,128)(2,1)}, bf16[144,1152]{1,0:T(8,128)(2,1)}) custom-call(s32[3]{0:T(128)} %pad_add_fusion.2.refs_0_, bf16[1280,1024]{1,0:T(8,128)(2,1)} %get-tuple-element.59.refs_1_.refs_3_.refs_5_.refs_4_.refs_7_, bf16[1280,1024]{1,0:T(8,128)(2,1)} %copy-done, ...), custom_call_target="tpu_custom_call" | custom-call | flops 339738624 | bytes 11276288 | tf_op jit(solution)/shard_map/pallas_call | solution.py:93
  170.2 3.5 %collective-permute-start.21 = (bf16[144,1152]{1,0:T(8,128)(2,1)}, bf16[144,1152]{1,0:T(8,128)(2,1)S(1)}, u32[]{:S(2)}, u32[]{:S(2)}) collective-permute-start(bf16[144,1152]{1,0:T(8,128)(2,1)} %get-tuple-element.87.txt), channel_id=1, source_target_pairs={{0,1},{1,0},{2,3},{3,2},{4,5},{5,4},{6,7},{7,6},{8,9},{9,8},{10,11... | collective-permute-start | bytes 995336 | tf_op jit(solution)/shard_map/ppermute | solution.py:61
  174.5 2.3 %collective-permute-start.10 = (bf16[288,128]{1,0:T(8,128)(2,1)S(1)}, bf16[288,128]{1,0:T(8,128)(2,1)S(1)}, u32[]{:S(2)}, u32[]{:S(2)}) collective-permute-start(bf16[288,128]{1,0:T(8,128)(2,1)S(1)} %get-tuple-element.100), channel_id=1, source_target_pairs={{0,96},{1,97},{2,98},{3,99},{4,100},{5,101},{6,102},{7,103},{8,104... | collective-permute-start | bytes 221192 | tf_op jit(solution)/shard_map/ppermute | solution.py:61
  181.5 2.9 %collective-permute-done.12 = bf16[288,128]{1,0:T(8,128)(2,1)S(1)} collective-permute-done((bf16[288,128]{1,0:T(8,128)(2,1)S(1)}, bf16[288,128]{1,0:T(8,128)(2,1)S(1)}, u32[]{:S(2)}, u32[]{:S(2)}) %collective-permute-start.12) | collective-permute-done | bytes 73760 | tf_op jit(solution)/shard_map/ppermute | solution.py:61
  187.2 3.8 %shard_map.112 = bf16[512,384]{1,0:T(8,128)(2,1)} custom-call(s32[1]{0:T(128)} %bitcast.19.at_ref, bf16[144,1152]{1,0:T(8,128)(2,1)} %get-tuple-element.72.img, bf16[144,1152]{1,0:T(8,128)(2,1)} %get-tuple-element.87.txt, bf16[144,1152]{1,0:T(8,128)(2,1)} %copy-done.20, bf16[144,1152]{1,0:T(8,128)(2,1)} %copy-done.19), custom_call_target="tpu_custom_call" | custom-call | flops 679477248 | bytes 1327104 | tf_op jit(solution)/shard_map/pallas_call | solution.py:93
  193.2 10.0 %all-to-all-start.2 = ((bf16[64,8,384]{2,1,0:T(8,128)(2,1)}), bf16[64,8,384]{2,1,0:T(8,128)(2,1)S(1)}, u32[]{:S(2)}, u32[]{:S(2)}) async-start(bf16[64,8,384]{2,1,0:T(8,128)(2,1)} %bitcast.55), calls=%async_computation.2 | async-start | bytes 786432 | tf_op jit(solution)/shard_map/all_to_all | solution.py:65
  207.0 6.1 %all-to-all-done.2.got = bf16[64,8,384]{2,1,0:T(8,128)(2,1)S(1)} async-done(((bf16[64,8,384]{2,1,0:T(8,128)(2,1)}), bf16[64,8,384]{2,1,0:T(8,128)(2,1)S(1)}, u32[]{:S(2)}, u32[]{:S(2)}) %all-to-all-start.2) | async-done | bytes 393248 | tf_op jit(solution)/shard_map/all_to_all | solution.py:65
  (114 shorter events, 41.9 us)
Async XLA Ops:
  2.3 13.6 %copy-start.1 = (bf16[1152,1152]{1,0:T(8,128)(2,1)S(1)}, bf16[1152,1152]{1,0:T(8,128)(2,1)}, u32[]{:S(2)}) copy-start(bf16[1152,1152]{1,0:T(8,128)(2,1)} %head.1) | copy-start | bytes 7962628
  2.4 11.4 %collective-permute-start = (bf16[144,1152]{1,0:T(8,128)(2,1)S(1)}, bf16[144,1152]{1,0:T(8,128)(2,1)S(1)}, u32[]{:S(2)}, u32[]{:S(2)}) collective-permute-start(bf16[144,1152]{1,0:T(8,128)(2,1)S(1)} %pad_maximum_fusion.refs_1_.refs_8_), channel_id=1, source_target_pairs={{0,24},{1,25},{2,26},{3,27},{4,28},{5,29},{6,30},{7,31},{8,16},{9,... | collective-permute-start | bytes 995336 | tf_op jit(solution)/shard_map/ppermute | solution.py:61
  5.7 13.5 %collective-permute-start.2 = (bf16[144,1152]{1,0:T(8,128)(2,1)S(1)}, bf16[144,1152]{1,0:T(8,128)(2,1)}, u32[]{:S(2)}, u32[]{:S(2)}) collective-permute-start(bf16[144,1152]{1,0:T(8,128)(2,1)S(1)} %pad_maximum_fusion.refs_1_.refs_8_), channel_id=1, source_target_pairs={{0,2},{1,3},{2,4},{3,5},{4,6},{5,7},{6,0},{7,1},{8,10},{9,11},{10,... | collective-permute-start | bytes 995336 | tf_op jit(solution)/shard_map/ppermute | solution.py:61
  7.0 12.2 %collective-permute-start.3 = (bf16[144,1152]{1,0:T(8,128)(2,1)S(1)}, bf16[144,1152]{1,0:T(8,128)(2,1)}, u32[]{:S(2)}, u32[]{:S(2)}) collective-permute-start(bf16[144,1152]{1,0:T(8,128)(2,1)S(1)} %pad_maximum_fusion.refs_1_.refs_8_), channel_id=1, source_target_pairs={{0,6},{1,7},{2,0},{3,1},{4,2},{5,3},{6,4},{7,5},{8,14},{9,15},{10,... | collective-permute-start | bytes 995336 | tf_op jit(solution)/shard_map/ppermute | solution.py:61
  13.7 8.7 %collective-permute-start.1 = (bf16[144,1152]{1,0:T(8,128)(2,1)S(1)}, bf16[144,1152]{1,0:T(8,128)(2,1)}, u32[]{:S(2)}, u32[]{:S(2)}) collective-permute-start(bf16[144,1152]{1,0:T(8,128)(2,1)S(1)} %collective-permute-done.refs_2_.refs_9_), channel_id=1, source_target_pairs={{0,6},{1,7},{2,0},{3,1},{4,2},{5,3},{6,4},{7,5},{8,14},{9,15},{10,... | collective-permute-start | bytes 995336 | tf_op jit(solution)/shard_map/ppermute | solution.py:61
  19.2 14.2 %collective-permute-start.6 = (bf16[144,1152]{1,0:T(8,128)(2,1)S(1)}, bf16[144,1152]{1,0:T(8,128)(2,1)}, u32[]{:S(2)}, u32[]{:S(2)}) collective-permute-start(bf16[144,1152]{1,0:T(8,128)(2,1)S(1)} %collective-permute-done.refs_2_.refs_9_), channel_id=1, source_target_pairs={{0,2},{1,3},{2,4},{3,5},{4,6},{5,7},{6,0},{7,1},{8,10},{9,11},{10,... | collective-permute-start | bytes 995336 | tf_op jit(solution)/shard_map/ppermute | solution.py:61
  22.5 12.7 %collective-permute-start.4 = (bf16[144,1152]{1,0:T(8,128)(2,1)}, bf16[144,1152]{1,0:T(8,128)(2,1)S(1)}, u32[]{:S(2)}, u32[]{:S(2)}) collective-permute-start(bf16[144,1152]{1,0:T(8,128)(2,1)} %collective-permute-done.2.refs_7_.refs_14_), channel_id=1, source_target_pairs={{0,2},{1,3},{2,4},{3,5},{4,6},{5,7},{6,0},{7,1},{8,10},{9,11},{10,... | collective-permute-start | bytes 995336 | tf_op jit(solution)/shard_map/ppermute | solution.py:61
  24.3 10.8 %collective-permute-start.5 = (bf16[144,1152]{1,0:T(8,128)(2,1)}, bf16[144,1152]{1,0:T(8,128)(2,1)}, u32[]{:S(2)}, u32[]{:S(2)}) collective-permute-start(bf16[144,1152]{1,0:T(8,128)(2,1)} %collective-permute-done.1.refs_4_.refs_11_), channel_id=1, source_target_pairs={{0,6},{1,7},{2,0},{3,1},{4,2},{5,3},{6,4},{7,5},{8,14},{9,15},{10,... | collective-permute-start | bytes 995336 | tf_op jit(solution)/shard_map/ppermute | solution.py:61
  27.9 31.6 %all-to-all-start = ((bf16[8,128,1152]{2,1,0:T(8,128)(2,1)}), bf16[8,128,1152]{2,1,0:T(8,128)(2,1)S(1)}, u32[]{:S(2)}, u32[]{:S(2)}) async-start(bf16[8,128,1152]{2,1,0:T(8,128)(2,1)} %broadcast_in_dim.2), calls=%async_computation | async-start | bytes 4718592 | tf_op jit(solution)/shard_map/all_to_all | solution.py:65
  45.0 27.8 %collective-permute-start.7 = (bf16[1168,1024]{1,0:T(8,128)(2,1)}, bf16[1168,1024]{1,0:T(8,128)(2,1)}, u32[]{:S(2)}, u32[]{:S(2)}) collective-permute-start(bf16[1168,1024]{1,0:T(8,128)(2,1)} %get-tuple-element.55.refs_4_.txt.refs_6_), channel_id=1, source_target_pairs={{0,1},{1,0},{2,3},{3,2},{4,5},{5,4},{6,7},{7,6},{8,9},{9,8},{10,11... | collective-permute-start | bytes 7176200 | tf_op jit(solution)/shard_map/ppermute | solution.py:61
  85.0 16.9 %collective-permute-start.8 = (bf16[1280,1024]{1,0:T(8,128)(2,1)}, bf16[1280,1024]{1,0:T(8,128)(2,1)S(1)}, u32[]{:S(2)}, u32[]{:S(2)}) collective-permute-start(bf16[1280,1024]{1,0:T(8,128)(2,1)} %get-tuple-element.60), channel_id=1, source_target_pairs={{0,1},{1,0},{2,3},{3,2},{4,5},{5,4},{6,7},{7,6},{8,9},{9,8},{10,11... | collective-permute-start | bytes 7864328 | tf_op jit(solution)/shard_map/ppermute | solution.py:61
  117.4 39.7 %all-to-all-start.1 = ((bf16[8,160,1024]{2,1,0:T(8,128)(2,1)}), bf16[8,160,1024]{2,1,0:T(8,128)(2,1)S(1)}, u32[]{:S(2)}, u32[]{:S(2)}) async-start(bf16[8,160,1024]{2,1,0:T(8,128)(2,1)} %shard_map.107), calls=%async_computation.1 | async-start | bytes 5242880 | tf_op jit(solution)/shard_map/all_to_all | solution.py:65
  121.0 10.8 %collective-permute-start.13 = (bf16[160,1024]{1,0:T(8,128)(2,1)}, bf16[160,1024]{1,0:T(8,128)(2,1)S(1)}, u32[]{:S(2)}, u32[]{:S(2)}) collective-permute-start(bf16[160,1024]{1,0:T(8,128)(2,1)} %get-tuple-element.73), channel_id=1, source_target_pairs={{0,2},{1,3},{2,4},{3,5},{4,6},{5,7},{6,0},{7,1},{8,10},{9,11},{10,... | collective-permute-start | bytes 983048 | tf_op jit(solution)/shard_map/ppermute | solution.py:61
  121.7 10.1 %collective-permute-start.14 = (bf16[160,1024]{1,0:T(8,128)(2,1)}, bf16[160,1024]{1,0:T(8,128)(2,1)S(1)}, u32[]{:S(2)}, u32[]{:S(2)}) collective-permute-start(bf16[160,1024]{1,0:T(8,128)(2,1)} %get-tuple-element.74), channel_id=1, source_target_pairs={{0,6},{1,7},{2,0},{3,1},{4,2},{5,3},{6,4},{7,5},{8,14},{9,15},{10,... | collective-permute-start | bytes 983048 | tf_op jit(solution)/shard_map/ppermute | solution.py:61
  136.6 8.6 %collective-permute-start.16 = (bf16[160,1024]{1,0:T(8,128)(2,1)}, bf16[160,1024]{1,0:T(8,128)(2,1)S(1)}, u32[]{:S(2)}, u32[]{:S(2)}) collective-permute-start(bf16[160,1024]{1,0:T(8,128)(2,1)} %get-tuple-element.79), channel_id=1, source_target_pairs={{0,6},{1,7},{2,0},{3,1},{4,2},{5,3},{6,4},{7,5},{8,14},{9,15},{10,... | collective-permute-start | bytes 983048 | tf_op jit(solution)/shard_map/ppermute | solution.py:61
  138.3 9.2 %collective-permute-start.15 = (bf16[160,1024]{1,0:T(8,128)(2,1)}, bf16[160,1024]{1,0:T(8,128)(2,1)S(1)}, u32[]{:S(2)}, u32[]{:S(2)}) collective-permute-start(bf16[160,1024]{1,0:T(8,128)(2,1)} %get-tuple-element.76), channel_id=1, source_target_pairs={{0,2},{1,3},{2,4},{3,5},{4,6},{5,7},{6,0},{7,1},{8,10},{9,11},{10,... | collective-permute-start | bytes 983048 | tf_op jit(solution)/shard_map/ppermute | solution.py:61
  151.0 13.4 %collective-permute-start.19 = (bf16[160,1024]{1,0:T(8,128)(2,1)}, bf16[160,1024]{1,0:T(8,128)(2,1)S(1)}, u32[]{:S(2)}, u32[]{:S(2)}) collective-permute-start(bf16[160,1024]{1,0:T(8,128)(2,1)} %shard_map.110), channel_id=1, source_target_pairs={{0,24},{1,25},{2,26},{3,27},{4,28},{5,29},{6,30},{7,31},{8,16},{9,... | collective-permute-start | bytes 983048 | tf_op jit(solution)/shard_map/ppermute | solution.py:61
  153.8 10.6 %collective-permute-start.17 = (bf16[160,1024]{1,0:T(8,128)(2,1)}, bf16[160,1024]{1,0:T(8,128)(2,1)S(1)}, u32[]{:S(2)}, u32[]{:S(2)}) collective-permute-start(bf16[160,1024]{1,0:T(8,128)(2,1)} %get-tuple-element.82), channel_id=1, source_target_pairs={{0,2},{1,3},{2,4},{3,5},{4,6},{5,7},{6,0},{7,1},{8,10},{9,11},{10,... | collective-permute-start | bytes 983048 | tf_op jit(solution)/shard_map/ppermute | solution.py:61
  153.8 10.6 %collective-permute-start.18 = (bf16[160,1024]{1,0:T(8,128)(2,1)}, bf16[160,1024]{1,0:T(8,128)(2,1)}, u32[]{:S(2)}, u32[]{:S(2)}) collective-permute-start(bf16[160,1024]{1,0:T(8,128)(2,1)} %get-tuple-element.83), channel_id=1, source_target_pairs={{0,6},{1,7},{2,0},{3,1},{4,2},{5,3},{6,4},{7,5},{8,14},{9,15},{10,... | collective-permute-start | bytes 983048 | tf_op jit(solution)/shard_map/ppermute | solution.py:61
  163.5 10.9 %collective-permute-start.9 = (bf16[4,144,128]{2,1,0:T(8,128)(2,1)}, bf16[4,144,128]{2,1,0:T(8,128)(2,1)S(1)}, u32[]{:S(2)}, u32[]{:S(2)}) collective-permute-start(bf16[4,144,128]{2,1,0:T(8,128)(2,1)} %get-tuple-element.70), channel_id=1, source_target_pairs={{0,16},{1,17},{2,18},{3,19},{4,20},{5,21},{6,22},{7,23},{8,24},{9,... | collective-permute-start | bytes 442376 | tf_op jit(solution)/shard_map/ppermute | solution.py:61
  170.2 14.3 %copy-start.2 = (bf16[1152,1152]{1,0:T(8,128)(2,1)S(1)}, bf16[1152,1152]{1,0:T(8,128)(2,1)}, u32[]{:S(2)}) copy-start(bf16[1152,1152]{1,0:T(8,128)(2,1)} %head.1) | copy-start | bytes 7962628
  170.2 16.1 %collective-permute-start.21 = (bf16[144,1152]{1,0:T(8,128)(2,1)}, bf16[144,1152]{1,0:T(8,128)(2,1)S(1)}, u32[]{:S(2)}, u32[]{:S(2)}) collective-permute-start(bf16[144,1152]{1,0:T(8,128)(2,1)} %get-tuple-element.87.txt), channel_id=1, source_target_pairs={{0,1},{1,0},{2,3},{3,2},{4,5},{5,4},{6,7},{7,6},{8,9},{9,8},{10,11... | collective-permute-start | bytes 995336 | tf_op jit(solution)/shard_map/ppermute | solution.py:61
  173.7 17.3 %collective-permute-start.22 = (bf16[4,144,128]{2,1,0:T(8,128)(2,1)}, bf16[4,144,128]{2,1,0:T(8,128)(2,1)S(1)}, u32[]{:S(2)}, u32[]{:S(2)}) collective-permute-start(bf16[4,144,128]{2,1,0:T(8,128)(2,1)} %get-tuple-element.88), channel_id=1, source_target_pairs={{0,24},{1,25},{2,26},{3,27},{4,28},{5,29},{6,30},{7,31},{8,16},{9,... | collective-permute-start | bytes 442376 | tf_op jit(solution)/shard_map/ppermute | solution.py:61
  174.1 12.3 %collective-permute-start.20 = (bf16[144,1152]{1,0:T(8,128)(2,1)S(1)}, bf16[144,1152]{1,0:T(8,128)(2,1)S(1)}, u32[]{:S(2)}, u32[]{:S(2)}) collective-permute-start(bf16[144,1152]{1,0:T(8,128)(2,1)S(1)} %copy-done.18), channel_id=1, source_target_pairs={{0,1},{1,0},{2,3},{3,2},{4,5},{5,4},{6,7},{7,6},{8,9},{9,8},{10,11... | collective-permute-start | bytes 995336 | tf_op jit(solution)/shard_map/ppermute | solution.py:61
  174.5 3.8 %collective-permute-start.10 = (bf16[288,128]{1,0:T(8,128)(2,1)S(1)}, bf16[288,128]{1,0:T(8,128)(2,1)S(1)}, u32[]{:S(2)}, u32[]{:S(2)}) collective-permute-start(bf16[288,128]{1,0:T(8,128)(2,1)S(1)} %get-tuple-element.100), channel_id=1, source_target_pairs={{0,96},{1,97},{2,98},{3,99},{4,100},{5,101},{6,102},{7,103},{8,104... | collective-permute-start | bytes 221192 | tf_op jit(solution)/shard_map/ppermute | solution.py:61
  176.8 4.7 %collective-permute-start.11 = (bf16[288,128]{1,0:T(8,128)(2,1)S(1)}, bf16[288,128]{1,0:T(8,128)(2,1)S(1)}, u32[]{:S(2)}, u32[]{:S(2)}) collective-permute-start(bf16[288,128]{1,0:T(8,128)(2,1)S(1)} %get-tuple-element.101), channel_id=1, source_target_pairs={{0,64},{1,65},{2,66},{3,67},{4,68},{5,69},{6,70},{7,71},{8,72},{9,... | collective-permute-start | bytes 221192 | tf_op jit(solution)/shard_map/ppermute | solution.py:61
  178.3 6.2 %collective-permute-start.12 = (bf16[288,128]{1,0:T(8,128)(2,1)S(1)}, bf16[288,128]{1,0:T(8,128)(2,1)S(1)}, u32[]{:S(2)}, u32[]{:S(2)}) collective-permute-start(bf16[288,128]{1,0:T(8,128)(2,1)S(1)} %get-tuple-element.99), channel_id=1, source_target_pairs={{0,32},{1,33},{2,34},{3,35},{4,36},{5,37},{6,38},{7,39},{8,40},{9,... | collective-permute-start | bytes 221192 | tf_op jit(solution)/shard_map/ppermute | solution.py:61
  187.2 18.1 %copy-start.3 = (bf16[1152,1152]{1,0:T(8,128)(2,1)S(1)}, bf16[1152,1152]{1,0:T(8,128)(2,1)}, u32[]{:S(2)}) copy-start(bf16[1152,1152]{1,0:T(8,128)(2,1)} %param.10) | copy-start | bytes 7962628
  191.7 11.5 %collective-permute-start.23 = (bf16[288,128]{1,0:T(8,128)(2,1)}, bf16[288,128]{1,0:T(8,128)(2,1)S(1)}, u32[]{:S(2)}, u32[]{:S(2)}) collective-permute-start(bf16[288,128]{1,0:T(8,128)(2,1)} %get-tuple-element.95), channel_id=1, source_target_pairs={{0,6},{1,7},{2,0},{3,1},{4,2},{5,3},{6,4},{7,5},{8,14},{9,15},{10,... | collective-permute-start | bytes 221192 | tf_op jit(solution)/shard_map/ppermute | solution.py:61
  191.7 11.6 %collective-permute-start.24 = (bf16[288,128]{1,0:T(8,128)(2,1)}, bf16[288,128]{1,0:T(8,128)(2,1)S(1)}, u32[]{:S(2)}, u32[]{:S(2)}) collective-permute-start(bf16[288,128]{1,0:T(8,128)(2,1)} %get-tuple-element.96), channel_id=1, source_target_pairs={{0,4},{1,5},{2,6},{3,7},{4,0},{5,1},{6,2},{7,3},{8,12},{9,13},{10,... | collective-permute-start | bytes 221192 | tf_op jit(solution)/shard_map/ppermute | solution.py:61
  192.1 11.2 %collective-permute-start.25 = (bf16[288,128]{1,0:T(8,128)(2,1)}, bf16[288,128]{1,0:T(8,128)(2,1)}, u32[]{:S(2)}, u32[]{:S(2)}) collective-permute-start(bf16[288,128]{1,0:T(8,128)(2,1)} %get-tuple-element.94), channel_id=1, source_target_pairs={{0,2},{1,3},{2,4},{3,5},{4,6},{5,7},{6,0},{7,1},{8,10},{9,11},{10,... | collective-permute-start | bytes 221192 | tf_op jit(solution)/shard_map/ppermute | solution.py:61
  193.2 19.8 %all-to-all-start.2 = ((bf16[64,8,384]{2,1,0:T(8,128)(2,1)}), bf16[64,8,384]{2,1,0:T(8,128)(2,1)S(1)}, u32[]{:S(2)}, u32[]{:S(2)}) async-start(bf16[64,8,384]{2,1,0:T(8,128)(2,1)} %bitcast.55), calls=%async_computation.2 | async-start | bytes 786432 | tf_op jit(solution)/shard_map/all_to_all | solution.py:65
  (18 other events, 54.8 us)

commit v4 on v2

--- a/solution.py
+++ b/solution.py
@@ -75,7 +75,7 @@
     return lax.dot_general(a, b, dims, preferred_element_type=f32)
 
 
-def call(body, out_shape, scalars, arrays, in_specs=None, out_specs=None, grid=(), scratch=(), cost=0, aliases=None, limit=60):
+def call(body, out_shape, scalars, arrays, in_specs=None, out_specs=None, grid=(), scratch=(), cost=0, aliases=None, weight=1):
     whole = pl.BlockSpec(memory_space=pltpu.VMEM)
     many = isinstance(out_shape, (list, tuple))
     if in_specs is None:
@@ -89,14 +89,14 @@
         out_specs=out_specs,
         scratch_shapes=list(scratch),
     )
-    moved = sum(a.size * a.dtype.itemsize for a in arrays)
+    moved = weight * sum(a.size * a.dtype.itemsize for a in arrays)
     return pl.pallas_call(
         body,
         out_shape=out_shape,
         grid_spec=spec,
         input_output_aliases=aliases or {},
-        compiler_params=pltpu.CompilerParams(vmem_limit_bytes=limit * 2**20),
-        cost_estimate=pl.CostEstimate(flops=cost, bytes_accessed=moved, transcendentals=0),
+        compiler_params=pltpu.CompilerParams(vmem_limit_bytes=60 * 2**20),
+        cost_estimate=pl.CostEstimate(flops=weight * cost, bytes_accessed=moved, transcendentals=0),
     )(jnp.stack(scalars).astype(jnp.int32), *arrays)
 
 
@@ -441,6 +441,7 @@
         grid=(1,),
         scratch=[pltpu.VMEM((slab, count), b16)],
         cost=2 * slab * count * width,
+        weight=0,
     )
 
 
@@ -473,6 +474,7 @@
         [core],
         parts,
         cost=8 * 512 * width * slab,
+        weight=0,
     )
 
 
@@ -512,14 +514,9 @@
     for d in range(4):
         block = lax.dynamic_index_in_dim(lines, (ring + d) % 4, 0, keepdims=False)
         got.append(send(block, move(d, 0)) if d else block)
-    return jnp.concatenate([got[-d % 4] for d in range(4)], axis=0)
-
-
-def from_ring(turned_head, ring):
-    start = ring * (turned_head.shape[0] // 4)
-    return lax.dynamic_slice_in_dim(
-        jnp.concatenate([turned_head, turned_head]), start, turned_head.shape[0], axis=0
-    )
+    height = got[0].shape[0]
+    from_own = jnp.concatenate([got[-d % 4] for d in range(4)] * 2, axis=0)
+    return lax.dynamic_slice_in_dim(from_own, (4 - ring) % 4 * height, 4 * height, axis=0)
 
 
 def shards(image_feat, text_feat, image_head, text_head, group_bias, text_lang, partner):
@@ -536,10 +533,11 @@
     across = send(text_rows, txt_move(0, 1))
     before = send(text_rows, txt_move(1, 0))
     after = send(text_rows, txt_move(3, 0))
-    across, turned_txt = together([across, text_head.T])
     across_after = send(across, txt_move(3, 0))
     across_before = send(across, txt_move(1, 0))
-    across_after, before, after, across = together([across_after, before, after, across])
+    across_after, before, after, across, turned_txt = together(
+        [across_after, before, after, across, text_head.T]
+    )
     far = send(before, txt_move(1, 0))
     across_far = send(across_after, txt_move(3, 0))
     txt_blocks = [
@@ -559,7 +557,6 @@
         place % 16, rows,
     )
     img_terms = exchange(img_terms, IMG_GROUPS)
-    (txt_ring_head,) = together([from_ring(turned_txt, y)])
 
     def slab_terms(d, e):
         at = (y + d) % 4 * 2 + (hi + e) % 2
@@ -602,7 +599,7 @@
 
     image_grad = dot(grad_img, image_head, (((0,), (1,)), ((), ())))
     grad_txt = whole_columns(pair_lines(txt_own, txt_got, hi), txt_move, y)
-    text_grad = dot(grad_txt, txt_ring_head, TN)
+    text_grad = dot(grad_txt, text_head, (((0,), (1,)), ((), ())))
     return (image_grad, text_grad, image_head_grad, text_head_grad)
 
 

time: 194 us -> 196 us (1.010)
  other arithmetic: 12.8 us -> 8.17 us
  local copies, waits for them, and re-layouts: 11.9 us -> 14.3 us
  waiting for transfers between devices: 30.9 us -> 33.2 us
    concatenate x1 -> x0, other arithmetic: 5.52 us -> none  [from_ring(): jnp.concatenate([turned_head, turned_head])]
    ppermute x22, waiting for transfers between devices: 25.2 us -> 28.9 us  [send(): lax.ppermute(block, DEV, [(flat(*p), flat(*move(*p))) for p in PLACES])]
    unnamed x33 -> x36, local copies, waits for them, and re-layouts: 7.86 us -> 9.29 us
  transfers between devices with their start and end apart: 26 -> 26, of which waited for: 7 -> 8; matrix products, arithmetic and copies ran while one was open for 18% -> 16% of each run, Pallas kernels for 26% -> 26%
where the time goes in v4:
time: 196 us; the launch traced here: 193 us
  Pallas kernels  64.3 us (33%)
  starting transfers between devices  56.7 us (29%)
  waiting for transfers between devices  33.2 us (17%)
  matrix products  15.5 us (8%)
  local copies, waits for them, and re-layouts  14.3 us (7%)
  other arithmetic  8.17 us (4%)
    pallas_call x10, Pallas kernels, call(): pl.pallas_call(body, out_shape=out_shape, grid_spec=spec, input_output_al...  64.3 us
    ppermute x22, starting transfers between devices, send(): lax.ppermute(block, DEV, [(flat(*p), flat(*move(*p))) for p in PLACES])  32.8 us
    ppermute x22, waiting for transfers between devices, send(): lax.ppermute(block, DEV, [(flat(*p), flat(*move(*p))) for p in PLACES])  28.9 us
    all_to_all x4, starting transfers between devices, exchange(): lax.all_to_all(blocks, DEV, 0, 0, axis_index_groups=groups, tiled=True)  24 us
    dot_general x4, matrix products, dot(): return lax.dot_general(a, b, dims, preferred_element_type=f32)  15.5 us
    unnamed x36, local copies, waits for them, and re-layouts  9.29 us
    all_to_all x4, waiting for transfers between devices, exchange(): lax.all_to_all(blocks, DEV, 0, 0, axis_index_groups=groups, tiled=True)  4.37 us
  transfers between devices with their start and end apart: 26, of which 8 were waited for; matrix products, arithmetic and copies ran while one was open for 16% of the time, Pallas kernels for 26%

profile of v4, /device:TPU:1, one launch (start us, length us, event | category | flops | bytes accessed | tf_op | source)
XLA Modules:
  0.0 193.3 jit_solution(12491703312811351456)
XLA Ops:
  0.6 2.9 %broadcast_in_dim.2 = bf16[8,128,1152]{2,1,0:T(8,128)(2,1)} broadcast(bf16[128,1152]{1,0:T(8,128)(2,1)} %param.7), dimensions={1,2} | broadcast | bytes 2654208 | tf_op jit(solution)/shard_map/broadcast_in_dim | solution.py:531
  3.5 6.9 %all-to-all-start = ((bf16[8,128,1152]{2,1,0:T(8,128)(2,1)}), bf16[8,128,1152]{2,1,0:T(8,128)(2,1)}, u32[]{:S(2)}, u32[]{:S(2)}) async-start(bf16[8,128,1152]{2,1,0:T(8,128)(2,1)} %broadcast_in_dim.2), calls=%async_computation | async-start | bytes 4718592 | tf_op jit(solution)/shard_map/all_to_all | solution.py:65
  10.5 2.8 %collective-permute-start = (bf16[144,1152]{1,0:T(8,128)(2,1)S(1)}, bf16[144,1152]{1,0:T(8,128)(2,1)S(1)}, u32[]{:S(2)}, u32[]{:S(2)}) collective-permute-start(bf16[144,1152]{1,0:T(8,128)(2,1)S(1)} %pad_maximum_fusion.refs_1_.refs_8_), channel_id=1, source_target_pairs={{0,24},{1,25},{2,26},{3,27},{4,28},{5,29},{6,30},{7,31},{8,16},{9,... | collective-permute-start | bytes 995336 | tf_op jit(solution)/shard_map/ppermute | solution.py:61
  16.1 4.3 %collective-permute-done.refs_2_.refs_9_ = bf16[144,1152]{1,0:T(8,128)(2,1)S(1)} collective-permute-done((bf16[144,1152]{1,0:T(8,128)(2,1)S(1)}, bf16[144,1152]{1,0:T(8,128)(2,1)S(1)}, u32[]{:S(2)}, u32[]{:S(2)}) %collective-permute-start) | collective-permute-done | bytes 331808 | tf_op jit(solution)/shard_map/ppermute | solution.py:61
  20.3 2.7 %collective-permute-start.1 = (bf16[144,1152]{1,0:T(8,128)(2,1)S(1)}, bf16[144,1152]{1,0:T(8,128)(2,1)}, u32[]{:S(2)}, u32[]{:S(2)}) collective-permute-start(bf16[144,1152]{1,0:T(8,128)(2,1)S(1)} %collective-permute-done.refs_2_.refs_9_), channel_id=1, source_target_pairs={{0,6},{1,7},{2,0},{3,1},{4,2},{5,3},{6,4},{7,5},{8,14},{9,15},{10,... | collective-permute-start | bytes 995336 | tf_op jit(solution)/shard_map/ppermute | solution.py:61
  23.1 5.2 %copy.11 = bf16[1152,1152]{0,1:T(8,128)(2,1)} copy(bf16[1152,1152]{1,0:T(8,128)(2,1)} %param.10) | data formatting | bytes 5308416 | tf_op args[3]
  33.6 3.3 %collective-permute-done.6.refs_8_.refs_15_ = bf16[144,1152]{1,0:T(8,128)(2,1)} collective-permute-done((bf16[144,1152]{1,0:T(8,128)(2,1)S(1)}, bf16[144,1152]{1,0:T(8,128)(2,1)}, u32[]{:S(2)}, u32[]{:S(2)}) %collective-permute-start.6) | collective-permute-done | bytes 331808 | tf_op jit(solution)/shard_map/ppermute | solution.py:61
  36.9 7.0 %collective-permute-done.4.refs_5_.refs_12_ = bf16[144,1152]{1,0:T(8,128)(2,1)S(1)} collective-permute-done((bf16[144,1152]{1,0:T(8,128)(2,1)}, bf16[144,1152]{1,0:T(8,128)(2,1)S(1)}, u32[]{:S(2)}, u32[]{:S(2)}) %collective-permute-start.4) | collective-permute-done | bytes 331808 | tf_op jit(solution)/shard_map/ppermute | solution.py:61
  44.6 9.1 %shard_map.102 = (bf16[1168,1024]{1,0:T(8,128)(2,1)}, f32[1,1024]{1,0:T(1,128)}) custom-call(s32[2]{0:T(128)} %pad_add_fusion.1.refs_0_, bf16[144,1152]{1,0:T(8,128)(2,1)} %copy-done.2, bf16[144,1152]{1,0:T(8,128)(2,1)} %copy-done.3, bf16[144,1152]{1,0:T(8,128)(2,1)} %collective-permute-done.3.refs_3_.refs_10_, ...), custom_call_target="tpu_custom_call" | custom-call | flops 2717908992 | bytes 5308416 | tf_op jit(solution)/shard_map/pallas_call | solution.py:93
  53.8 3.0 %collective-permute-start.7 = (bf16[1168,1024]{1,0:T(8,128)(2,1)}, bf16[1168,1024]{1,0:T(8,128)(2,1)}, u32[]{:S(2)}, u32[]{:S(2)}) collective-permute-start(bf16[1168,1024]{1,0:T(8,128)(2,1)} %get-tuple-element.44.refs_4_.refs_6_), channel_id=1, source_target_pairs={{0,1},{1,0},{2,3},{3,2},{4,5},{5,4},{6,7},{7,6},{8,9},{9,8},{10,11... | collective-permute-start | bytes 7176200 | tf_op jit(solution)/shard_map/ppermute | solution.py:61
  56.7 5.0 %multiply_reduce_fusion = (f32[1024]{0:T(1024)S(1)}, f32[1152,1024]{1,0:T(8,128)S(1)}) fusion(bf16[1152,1152]{1,0:T(8,128)(2,1)S(1)} %copy-done, bf16[1024,1152]{1,0:T(8,128)(2,1)} %bitcast.4.refs_4_), kind=kOutput, calls=%fused_computation.1 | convolution fusion | flops 2720267264 | bytes 9736192 | tf_op jit(solution)/shard_map/dot_general | solution.py:75
  61.7 5.3 %multiply_reduce_fusion.1 = (f32[1024]{0:T(1024)S(1)}, f32[1024,1152]{1,0:T(8,128)S(1)}) fusion(bf16[1024,1152]{1,0:T(8,128)(2,1)} %bitcast.4.refs_4_, bf16[1152,1152]{1,0:T(8,128)(2,1)S(1)} %copy-done), kind=kOutput, calls=%fused_computation.3 | convolution fusion | flops 2720267264 | bytes 9736192 | tf_op jit(solution)/shard_map/dot_general | solution.py:75
  71.1 12.2 %shard_map.103 = (bf16[4,1024,256]{2,1,0:T(8,128)(2,1)}, f32[1,1024]{1,0:T(1,128)}, bf16[1280,1024]{1,0:T(8,128)(2,1)}) custom-call(s32[1]{0:T(128)} %bitcast.3.refs_0_, f32[32]{0:T(128)} %refs_1_.3, bf16[1024,1152]{1,0:T(8,128)(2,1)} %divide_convert_fusion.1.refs_2_, bf16[1152,1024]{1,0:T(8,128)(2,1)} %divide_convert_fusion.refs_3_.refs_2_, ...), custom_call_target="tpu_custom_call" | custom-call | flops 4831838208 | bytes 7110784 | tf_op jit(solution)/shard_map/pallas_call | solution.py:93
  83.3 18.5 %shard_map.104 = (bf16[1280,1024]{1,0:T(8,128)(2,1)}, bf16[8,160,1024]{2,1,0:T(8,128)(2,1)}) custom-call(s32[1]{0:T(128)} %bitcast.3.refs_0_, f32[32]{0:T(128)} %refs_1_.3, bf16[1024,1152]{1,0:T(8,128)(2,1)} %divide_convert_fusion.1.refs_2_, bf16[1152,1024]{1,0:T(8,128)(2,1)} %divide_convert_fusion.refs_3_.refs_2_, ...), custom_call_target="tpu_custom_call" | custom-call | flops 9663676416 | bytes 11604096 | tf_op jit(solution)/shard_map/pallas_call | solution.py:93
  101.8 4.4 %all-to-all-start.1 = ((bf16[8,160,1024]{2,1,0:T(8,128)(2,1)}), bf16[8,160,1024]{2,1,0:T(8,128)(2,1)}, u32[]{:S(2)}, u32[]{:S(2)}) async-start(bf16[8,160,1024]{2,1,0:T(8,128)(2,1)} %get-tuple-element.48), calls=%async_computation.1 | async-start | bytes 5242880 | tf_op jit(solution)/shard_map/all_to_all | solution.py:65
  106.9 3.1 %shard_map.106 = (bf16[160,1024]{1,0:T(8,128)(2,1)}, bf16[160,1024]{1,0:T(8,128)(2,1)}, bf16[160,1024]{1,0:T(8,128)(2,1)}) custom-call(s32[7]{0:T(128)} %stack.108.refs_0_, bf16[1280,1024]{1,0:T(8,128)(2,1)} %get-tuple-element.51.refs_1_.refs_3_.refs_5_.refs_4_.refs_7_, bf16[1280,1024]{1,0:T(8,128)(2,1)} %collective-permute-done.8.refs_2_.refs_4_.refs_6_.refs_5_.refs_8_, ...), custom_call_target="tpu_custom_call" | custom-call | bytes 15728640 | tf_op jit(solution)/shard_map/pallas_call | solution.py:93
  110.1 2.7 %collective-permute-start.10 = (bf16[160,1024]{1,0:T(8,128)(2,1)}, bf16[160,1024]{1,0:T(8,128)(2,1)S(1)}, u32[]{:S(2)}, u32[]{:S(2)}) collective-permute-start(bf16[160,1024]{1,0:T(8,128)(2,1)} %get-tuple-element.54), channel_id=1, source_target_pairs={{0,6},{1,7},{2,0},{3,1},{4,2},{5,3},{6,4},{7,5},{8,14},{9,15},{10,... | collective-permute-start | bytes 983048 | tf_op jit(solution)/shard_map/ppermute | solution.py:61
  113.3 7.1 %collective-permute-done.9.refs_6_ = bf16[160,1024]{1,0:T(8,128)(2,1)S(1)} collective-permute-done((bf16[160,1024]{1,0:T(8,128)(2,1)}, bf16[160,1024]{1,0:T(8,128)(2,1)S(1)}, u32[]{:S(2)}, u32[]{:S(2)}) %collective-permute-start.9) | collective-permute-done | bytes 327712 | tf_op jit(solution)/shard_map/ppermute | solution.py:61
  121.3 3.4 %shard_map.107 = (bf16[160,1024]{1,0:T(8,128)(2,1)}, bf16[160,1024]{1,0:T(8,128)(2,1)}, bf16[160,1024]{1,0:T(8,128)(2,1)}) custom-call(s32[7]{0:T(128)} %stack.112.refs_0_, bf16[1280,1024]{1,0:T(8,128)(2,1)} %get-tuple-element.51.refs_1_.refs_3_.refs_5_.refs_4_.refs_7_, bf16[1280,1024]{1,0:T(8,128)(2,1)} %collective-permute-done.8.refs_2_.refs_4_.refs_6_.refs_5_.refs_8_, ...), custom_call_target="tpu_custom_call" | custom-call | bytes 16384000 | tf_op jit(solution)/shard_map/pallas_call | solution.py:93
  124.6 2.7 %collective-permute-start.12 = (bf16[160,1024]{1,0:T(8,128)(2,1)}, bf16[160,1024]{1,0:T(8,128)(2,1)S(1)}, u32[]{:S(2)}, u32[]{:S(2)}) collective-permute-start(bf16[160,1024]{1,0:T(8,128)(2,1)} %get-tuple-element.59), channel_id=1, source_target_pairs={{0,6},{1,7},{2,0},{3,1},{4,2},{5,3},{6,4},{7,5},{8,14},{9,15},{10,... | collective-permute-start | bytes 983048 | tf_op jit(solution)/shard_map/ppermute | solution.py:61
  127.9 2.9 %collective-permute-done.11.refs_3_ = bf16[160,1024]{1,0:T(8,128)(2,1)S(1)} collective-permute-done((bf16[160,1024]{1,0:T(8,128)(2,1)}, bf16[160,1024]{1,0:T(8,128)(2,1)S(1)}, u32[]{:S(2)}, u32[]{:S(2)}) %collective-permute-start.11) | collective-permute-done | bytes 327712 | tf_op jit(solution)/shard_map/ppermute | solution.py:61
  130.7 2.4 %collective-permute-done.12.refs_4_ = bf16[160,1024]{1,0:T(8,128)(2,1)S(1)} collective-permute-done((bf16[160,1024]{1,0:T(8,128)(2,1)}, bf16[160,1024]{1,0:T(8,128)(2,1)S(1)}, u32[]{:S(2)}, u32[]{:S(2)}) %collective-permute-start.12) | collective-permute-done | bytes 327712 | tf_op jit(solution)/shard_map/ppermute | solution.py:61
  134.3 2.2 %collective-permute-start.14 = (bf16[160,1024]{1,0:T(8,128)(2,1)}, bf16[160,1024]{1,0:T(8,128)(2,1)}, u32[]{:S(2)}, u32[]{:S(2)}) collective-permute-start(bf16[160,1024]{1,0:T(8,128)(2,1)} %get-tuple-element.63), channel_id=1, source_target_pairs={{0,6},{1,7},{2,0},{3,1},{4,2},{5,3},{6,4},{7,5},{8,14},{9,15},{10,... | collective-permute-start | bytes 983048 | tf_op jit(solution)/shard_map/ppermute | solution.py:61
  136.5 2.8 %shard_map.108 = bf16[160,1024]{1,0:T(8,128)(2,1)} custom-call(s32[3]{0:T(128)} %pad_add_fusion.3.refs_0_, bf16[1280,1024]{1,0:T(8,128)(2,1)} %get-tuple-element.51.refs_1_.refs_3_.refs_5_.refs_4_.refs_7_, bf16[1280,1024]{1,0:T(8,128)(2,1)} %collective-permute-done.8.refs_2_.refs_4_.refs_6_.refs_5_.refs_8_, bf16[160,1024]{1,0:T(8,128)(2,1)} %copy-done.6, ...), custom_call_target="tpu_custom_call" | custom-call | bytes 5898240 | tf_op jit(solution)/shard_map/pallas_call | solution.py:93
  141.7 4.8 %shard_map.105 = (bf16[8,144,128]{2,1,0:T(8,128)(2,1)}, bf16[144,1152]{1,0:T(8,128)(2,1)}) custom-call(s32[3]{0:T(128)} %pad_add_fusion.refs_0_, bf16[8,160,1024]{2,1,0:T(8,128)(2,1)} %all-to-all-done.1.refs_1_, bf16[1152,1024]{1,0:T(8,128)(2,1)} %divide_convert_fusion.refs_3_.refs_2_, f32[1,1024]{1,0:T(1,128)} %bitcast.48, bf16[1024,1152]{1,0:T(8,128)(2,1)} %bitcast.4.refs_4_), custom_call_target="tpu_custom_call" | custom-call | tf_op jit(solution)/shard_map/pallas_call | solution.py:93
  146.6 3.7 %all-to-all-start.2 = ((bf16[8,144,128]{2,1,0:T(8,128)(2,1)}), bf16[8,144,128]{2,1,0:T(8,128)(2,1)S(1)}, u32[]{:S(2)}, u32[]{:S(2)}) async-start(bf16[8,144,128]{2,1,0:T(8,128)(2,1)} %get-tuple-element.49), calls=%async_computation.2 | async-start | bytes 589824 | tf_op jit(solution)/shard_map/all_to_all | solution.py:65
  150.8 4.0 %collective-permute-start.16 = (bf16[144,1152]{1,0:T(8,128)(2,1)}, bf16[144,1152]{1,0:T(8,128)(2,1)S(1)}, u32[]{:S(2)}, u32[]{:S(2)}) collective-permute-start(bf16[144,1152]{1,0:T(8,128)(2,1)} %get-tuple-element.50.img), channel_id=1, source_target_pairs={{0,1},{1,0},{2,3},{3,2},{4,5},{5,4},{6,7},{7,6},{8,9},{9,8},{10,11... | collective-permute-start | bytes 995336 | tf_op jit(solution)/shard_map/ppermute | solution.py:61
  154.8 4.9 %shard_map.109 = (bf16[4,144,128]{2,1,0:T(8,128)(2,1)}, bf16[4,144,128]{2,1,0:T(8,128)(2,1)}, bf16[144,1152]{1,0:T(8,128)(2,1)}) custom-call(s32[3]{0:T(128)} %pad_add_fusion.2.refs_0_, bf16[1280,1024]{1,0:T(8,128)(2,1)} %get-tuple-element.51.refs_1_.refs_3_.refs_5_.refs_4_.refs_7_, ...), custom_call_target="tpu_custom_call" | custom-call | tf_op jit(solution)/shard_map/pallas_call | solution.py:93
  164.1 3.7 %shard_map.110 = bf16[512,384]{1,0:T(8,128)(2,1)} custom-call(s32[1]{0:T(128)} %bitcast.13.at_ref, bf16[144,1152]{1,0:T(8,128)(2,1)} %get-tuple-element.50.img, bf16[144,1152]{1,0:T(8,128)(2,1)} %get-tuple-element.67.txt, bf16[144,1152]{1,0:T(8,128)(2,1)} %copy-done.5, bf16[144,1152]{1,0:T(8,128)(2,1)} %collective-permute-done.17.other_txt), custom_call_target="tpu_custom_call" | custom-call | tf_op jit(solution)/shard_map/pallas_call | solution.py:93
  171.8 9.0 %all-to-all-start.3 = ((bf16[64,8,384]{2,1,0:T(8,128)(2,1)}), bf16[64,8,384]{2,1,0:T(8,128)(2,1)S(1)}, u32[]{:S(2)}, u32[]{:S(2)}) async-start(bf16[64,8,384]{2,1,0:T(8,128)(2,1)} %bitcast.46), calls=%async_computation.3 | async-start | bytes 786432 | tf_op jit(solution)/shard_map/all_to_all | solution.py:65
  182.8 3.5 %fusion = f32[128,1152]{1,0:T(8,128)} fusion(bf16[1152,1152]{1,0:T(8,128)(2,1)} %param.10, bf16[2304,128]{1,0:T(8,128)(2,1)S(1)} %constant_dynamic-update-slice_fusion, s32[]{:T(128)S(6)} %select_n.154), kind=kOutput, calls=%fused_computation.13 | convolution fusion | flops 339738624 | bytes 3538948 | tf_op jit(solution)/shard_map/dot_general | solution.py:75
  186.4 4.4 %all-to-all-done.3.got = bf16[64,8,384]{2,1,0:T(8,128)(2,1)S(1)} async-done(((bf16[64,8,384]{2,1,0:T(8,128)(2,1)}), bf16[64,8,384]{2,1,0:T(8,128)(2,1)S(1)}, u32[]{:S(2)}, u32[]{:S(2)}) %all-to-all-start.3) | async-done | bytes 393248 | tf_op jit(solution)/shard_map/all_to_all | solution.py:65
  (89 shorter events, 32.7 us)
Async XLA Ops:
  0.6 56.1 %copy-start = (bf16[1152,1152]{1,0:T(8,128)(2,1)S(1)}, bf16[1152,1152]{1,0:T(8,128)(2,1)}, u32[]{:S(2)}) copy-start(bf16[1152,1152]{1,0:T(8,128)(2,1)} %param.9) | copy-start | bytes 7962628
  3.5 6.9 %copy-start.14 = (s32[128]{0:T(128)S(1)}, s32[128]{0:T(128)}, u32[]{:S(2)}) copy-start(s32[128]{0:T(128)} %param.12) | copy-start | bytes 1540
  3.5 7.0 %copy-start.10 = (bf16[128,1152]{1,0:T(8,128)(2,1)S(1)}, bf16[128,1152]{1,0:T(8,128)(2,1)}, u32[]{:S(2)}) copy-start(bf16[128,1152]{1,0:T(8,128)(2,1)} %param.8) | copy-start | bytes 884740
  3.5 53.2 %all-to-all-start = ((bf16[8,128,1152]{2,1,0:T(8,128)(2,1)}), bf16[8,128,1152]{2,1,0:T(8,128)(2,1)}, u32[]{:S(2)}, u32[]{:S(2)}) async-start(bf16[8,128,1152]{2,1,0:T(8,128)(2,1)} %broadcast_in_dim.2), calls=%async_computation | async-start | bytes 4718592 | tf_op jit(solution)/shard_map/all_to_all | solution.py:65
  10.5 17.8 %copy-start.2 = (bf16[144,1152]{1,0:T(8,128)(2,1)}, bf16[144,1152]{1,0:T(8,128)(2,1)S(1)}, u32[]{:S(2)}) copy-start(bf16[144,1152]{1,0:T(8,128)(2,1)S(1)} %pad_maximum_fusion.refs_1_.refs_8_) | copy-start | bytes 995332
  10.5 9.8 %collective-permute-start = (bf16[144,1152]{1,0:T(8,128)(2,1)S(1)}, bf16[144,1152]{1,0:T(8,128)(2,1)S(1)}, u32[]{:S(2)}, u32[]{:S(2)}) collective-permute-start(bf16[144,1152]{1,0:T(8,128)(2,1)S(1)} %pad_maximum_fusion.refs_1_.refs_8_), channel_id=1, source_target_pairs={{0,24},{1,25},{2,26},{3,27},{4,28},{5,29},{6,30},{7,31},{8,16},{9,... | collective-permute-start | bytes 995336 | tf_op jit(solution)/shard_map/ppermute | solution.py:61
  13.3 15.0 %collective-permute-start.2 = (bf16[144,1152]{1,0:T(8,128)(2,1)S(1)}, bf16[144,1152]{1,0:T(8,128)(2,1)}, u32[]{:S(2)}, u32[]{:S(2)}) collective-permute-start(bf16[144,1152]{1,0:T(8,128)(2,1)S(1)} %pad_maximum_fusion.refs_1_.refs_8_), channel_id=1, source_target_pairs={{0,2},{1,3},{2,4},{3,5},{4,6},{5,7},{6,0},{7,1},{8,10},{9,11},{10,... | collective-permute-start | bytes 995336 | tf_op jit(solution)/shard_map/ppermute | solution.py:61
  14.6 13.7 %collective-permute-start.3 = (bf16[144,1152]{1,0:T(8,128)(2,1)S(1)}, bf16[144,1152]{1,0:T(8,128)(2,1)}, u32[]{:S(2)}, u32[]{:S(2)}) collective-permute-start(bf16[144,1152]{1,0:T(8,128)(2,1)S(1)} %pad_maximum_fusion.refs_1_.refs_8_), channel_id=1, source_target_pairs={{0,6},{1,7},{2,0},{3,1},{4,2},{5,3},{6,4},{7,5},{8,14},{9,15},{10,... | collective-permute-start | bytes 995336 | tf_op jit(solution)/shard_map/ppermute | solution.py:61
  20.3 8.0 %copy-start.3 = (bf16[144,1152]{1,0:T(8,128)(2,1)}, bf16[144,1152]{1,0:T(8,128)(2,1)S(1)}, u32[]{:S(2)}) copy-start(bf16[144,1152]{1,0:T(8,128)(2,1)S(1)} %collective-permute-done.refs_2_.refs_9_) | copy-start | bytes 995332
  20.3 10.0 %collective-permute-start.1 = (bf16[144,1152]{1,0:T(8,128)(2,1)S(1)}, bf16[144,1152]{1,0:T(8,128)(2,1)}, u32[]{:S(2)}, u32[]{:S(2)}) collective-permute-start(bf16[144,1152]{1,0:T(8,128)(2,1)S(1)} %collective-permute-done.refs_2_.refs_9_), channel_id=1, source_target_pairs={{0,6},{1,7},{2,0},{3,1},{4,2},{5,3},{6,4},{7,5},{8,14},{9,15},{10,... | collective-permute-start | bytes 995336 | tf_op jit(solution)/shard_map/ppermute | solution.py:61
  28.3 8.6 %collective-permute-start.6 = (bf16[144,1152]{1,0:T(8,128)(2,1)S(1)}, bf16[144,1152]{1,0:T(8,128)(2,1)}, u32[]{:S(2)}, u32[]{:S(2)}) collective-permute-start(bf16[144,1152]{1,0:T(8,128)(2,1)S(1)} %collective-permute-done.refs_2_.refs_9_), channel_id=1, source_target_pairs={{0,2},{1,3},{2,4},{3,5},{4,6},{5,7},{6,0},{7,1},{8,10},{9,11},{10,... | collective-permute-start | bytes 995336 | tf_op jit(solution)/shard_map/ppermute | solution.py:61
  30.3 13.5 %collective-permute-start.4 = (bf16[144,1152]{1,0:T(8,128)(2,1)}, bf16[144,1152]{1,0:T(8,128)(2,1)S(1)}, u32[]{:S(2)}, u32[]{:S(2)}) collective-permute-start(bf16[144,1152]{1,0:T(8,128)(2,1)} %collective-permute-done.2.refs_7_.refs_14_), channel_id=1, source_target_pairs={{0,2},{1,3},{2,4},{3,5},{4,6},{5,7},{6,0},{7,1},{8,10},{9,11},{10,... | collective-permute-start | bytes 995336 | tf_op jit(solution)/shard_map/ppermute | solution.py:61
  31.6 12.3 %collective-permute-start.5 = (bf16[144,1152]{1,0:T(8,128)(2,1)}, bf16[144,1152]{1,0:T(8,128)(2,1)}, u32[]{:S(2)}, u32[]{:S(2)}) collective-permute-start(bf16[144,1152]{1,0:T(8,128)(2,1)} %collective-permute-done.1.refs_4_.refs_11_), channel_id=1, source_target_pairs={{0,6},{1,7},{2,0},{3,1},{4,2},{5,3},{6,4},{7,5},{8,14},{9,15},{10,... | collective-permute-start | bytes 995336 | tf_op jit(solution)/shard_map/ppermute | solution.py:61
  53.8 17.4 %collective-permute-start.7 = (bf16[1168,1024]{1,0:T(8,128)(2,1)}, bf16[1168,1024]{1,0:T(8,128)(2,1)}, u32[]{:S(2)}, u32[]{:S(2)}) collective-permute-start(bf16[1168,1024]{1,0:T(8,128)(2,1)} %get-tuple-element.44.refs_4_.refs_6_), channel_id=1, source_target_pairs={{0,1},{1,0},{2,3},{3,2},{4,5},{5,4},{6,7},{7,6},{8,9},{9,8},{10,11... | collective-permute-start | bytes 7176200 | tf_op jit(solution)/shard_map/ppermute | solution.py:61
  83.3 23.6 %collective-permute-start.8 = (bf16[1280,1024]{1,0:T(8,128)(2,1)}, bf16[1280,1024]{1,0:T(8,128)(2,1)}, u32[]{:S(2)}, u32[]{:S(2)}) collective-permute-start(bf16[1280,1024]{1,0:T(8,128)(2,1)} %get-tuple-element.52), channel_id=1, source_target_pairs={{0,1},{1,0},{2,3},{3,2},{4,5},{5,4},{6,7},{7,6},{8,9},{9,8},{10,11... | collective-permute-start | bytes 7864328 | tf_op jit(solution)/shard_map/ppermute | solution.py:61
  101.8 39.9 %all-to-all-start.1 = ((bf16[8,160,1024]{2,1,0:T(8,128)(2,1)}), bf16[8,160,1024]{2,1,0:T(8,128)(2,1)}, u32[]{:S(2)}, u32[]{:S(2)}) async-start(bf16[8,160,1024]{2,1,0:T(8,128)(2,1)} %get-tuple-element.48), calls=%async_computation.1 | async-start | bytes 5242880 | tf_op jit(solution)/shard_map/all_to_all | solution.py:65
  110.0 10.4 %collective-permute-start.9 = (bf16[160,1024]{1,0:T(8,128)(2,1)}, bf16[160,1024]{1,0:T(8,128)(2,1)S(1)}, u32[]{:S(2)}, u32[]{:S(2)}) collective-permute-start(bf16[160,1024]{1,0:T(8,128)(2,1)} %get-tuple-element.53), channel_id=1, source_target_pairs={{0,2},{1,3},{2,4},{3,5},{4,6},{5,7},{6,0},{7,1},{8,10},{9,11},{10,... | collective-permute-start | bytes 983048 | tf_op jit(solution)/shard_map/ppermute | solution.py:61
  110.1 10.3 %collective-permute-start.10 = (bf16[160,1024]{1,0:T(8,128)(2,1)}, bf16[160,1024]{1,0:T(8,128)(2,1)S(1)}, u32[]{:S(2)}, u32[]{:S(2)}) collective-permute-start(bf16[160,1024]{1,0:T(8,128)(2,1)} %get-tuple-element.54), channel_id=1, source_target_pairs={{0,6},{1,7},{2,0},{3,1},{4,2},{5,3},{6,4},{7,5},{8,14},{9,15},{10,... | collective-permute-start | bytes 983048 | tf_op jit(solution)/shard_map/ppermute | solution.py:61
  121.2 9.5 %collective-permute-start.11 = (bf16[160,1024]{1,0:T(8,128)(2,1)}, bf16[160,1024]{1,0:T(8,128)(2,1)S(1)}, u32[]{:S(2)}, u32[]{:S(2)}) collective-permute-start(bf16[160,1024]{1,0:T(8,128)(2,1)} %get-tuple-element.56), channel_id=1, source_target_pairs={{0,2},{1,3},{2,4},{3,5},{4,6},{5,7},{6,0},{7,1},{8,10},{9,11},{10,... | collective-permute-start | bytes 983048 | tf_op jit(solution)/shard_map/ppermute | solution.py:61
  124.6 8.5 %collective-permute-start.12 = (bf16[160,1024]{1,0:T(8,128)(2,1)}, bf16[160,1024]{1,0:T(8,128)(2,1)S(1)}, u32[]{:S(2)}, u32[]{:S(2)}) collective-permute-start(bf16[160,1024]{1,0:T(8,128)(2,1)} %get-tuple-element.59), channel_id=1, source_target_pairs={{0,6},{1,7},{2,0},{3,1},{4,2},{5,3},{6,4},{7,5},{8,14},{9,15},{10,... | collective-permute-start | bytes 983048 | tf_op jit(solution)/shard_map/ppermute | solution.py:61
  133.1 21.7 %collective-permute-start.13 = (bf16[160,1024]{1,0:T(8,128)(2,1)}, bf16[160,1024]{1,0:T(8,128)(2,1)}, u32[]{:S(2)}, u32[]{:S(2)}) collective-permute-start(bf16[160,1024]{1,0:T(8,128)(2,1)} %get-tuple-element.62), channel_id=1, source_target_pairs={{0,2},{1,3},{2,4},{3,5},{4,6},{5,7},{6,0},{7,1},{8,10},{9,11},{10,... | collective-permute-start | bytes 983048 | tf_op jit(solution)/shard_map/ppermute | solution.py:61
  134.3 20.5 %collective-permute-start.14 = (bf16[160,1024]{1,0:T(8,128)(2,1)}, bf16[160,1024]{1,0:T(8,128)(2,1)}, u32[]{:S(2)}, u32[]{:S(2)}) collective-permute-start(bf16[160,1024]{1,0:T(8,128)(2,1)} %get-tuple-element.63), channel_id=1, source_target_pairs={{0,6},{1,7},{2,0},{3,1},{4,2},{5,3},{6,4},{7,5},{8,14},{9,15},{10,... | collective-permute-start | bytes 983048 | tf_op jit(solution)/shard_map/ppermute | solution.py:61
  139.4 15.4 %collective-permute-start.15 = (bf16[160,1024]{1,0:T(8,128)(2,1)}, bf16[160,1024]{1,0:T(8,128)(2,1)}, u32[]{:S(2)}, u32[]{:S(2)}) collective-permute-start(bf16[160,1024]{1,0:T(8,128)(2,1)} %shard_map.108), channel_id=1, source_target_pairs={{0,24},{1,25},{2,26},{3,27},{4,28},{5,29},{6,30},{7,31},{8,16},{9,... | collective-permute-start | bytes 983048 | tf_op jit(solution)/shard_map/ppermute | solution.py:61
  146.6 15.1 %all-to-all-start.2 = ((bf16[8,144,128]{2,1,0:T(8,128)(2,1)}), bf16[8,144,128]{2,1,0:T(8,128)(2,1)S(1)}, u32[]{:S(2)}, u32[]{:S(2)}) async-start(bf16[8,144,128]{2,1,0:T(8,128)(2,1)} %get-tuple-element.49), calls=%async_computation.2 | async-start | bytes 589824 | tf_op jit(solution)/shard_map/all_to_all | solution.py:65
  150.8 12.6 %collective-permute-start.16 = (bf16[144,1152]{1,0:T(8,128)(2,1)}, bf16[144,1152]{1,0:T(8,128)(2,1)S(1)}, u32[]{:S(2)}, u32[]{:S(2)}) collective-permute-start(bf16[144,1152]{1,0:T(8,128)(2,1)} %get-tuple-element.50.img), channel_id=1, source_target_pairs={{0,1},{1,0},{2,3},{3,2},{4,5},{5,4},{6,7},{7,6},{8,9},{9,8},{10,11... | collective-permute-start | bytes 995336 | tf_op jit(solution)/shard_map/ppermute | solution.py:61
  159.7 3.8 %collective-permute-start.17 = (bf16[144,1152]{1,0:T(8,128)(2,1)}, bf16[144,1152]{1,0:T(8,128)(2,1)}, u32[]{:S(2)}, u32[]{:S(2)}) collective-permute-start(bf16[144,1152]{1,0:T(8,128)(2,1)} %get-tuple-element.67.txt), channel_id=1, source_target_pairs={{0,1},{1,0},{2,3},{3,2},{4,5},{5,4},{6,7},{7,6},{8,9},{9,8},{10,11... | collective-permute-start | bytes 995336 | tf_op jit(solution)/shard_map/ppermute | solution.py:61
  159.7 8.2 %copy-start.11 = (bf16[4,144,128]{2,1,0:T(8,128)(2,1)S(1)}, bf16[4,144,128]{2,1,0:T(8,128)(2,1)}, u32[]{:S(2)}) copy-start(bf16[4,144,128]{2,1,0:T(8,128)(2,1)} %get-tuple-element.70) | copy-start | bytes 442372
  159.7 8.1 %collective-permute-start.18 = (bf16[4,144,128]{2,1,0:T(8,128)(2,1)}, bf16[4,144,128]{2,1,0:T(8,128)(2,1)}, u32[]{:S(2)}, u32[]{:S(2)}) collective-permute-start(bf16[4,144,128]{2,1,0:T(8,128)(2,1)} %get-tuple-element.68), channel_id=1, source_target_pairs={{0,24},{1,25},{2,26},{3,27},{4,28},{5,29},{6,30},{7,31},{8,16},{9,... | collective-permute-start | bytes 442376 | tf_op jit(solution)/shard_map/ppermute | solution.py:61
  169.5 11.4 %collective-permute-start.19 = (bf16[288,128]{1,0:T(8,128)(2,1)}, bf16[288,128]{1,0:T(8,128)(2,1)S(1)}, u32[]{:S(2)}, u32[]{:S(2)}) collective-permute-start(bf16[288,128]{1,0:T(8,128)(2,1)} %get-tuple-element.75), channel_id=1, source_target_pairs={{0,6},{1,7},{2,0},{3,1},{4,2},{5,3},{6,4},{7,5},{8,14},{9,15},{10,... | collective-permute-start | bytes 221192 | tf_op jit(solution)/shard_map/ppermute | solution.py:61
  171.3 9.7 %collective-permute-start.20 = (bf16[288,128]{1,0:T(8,128)(2,1)}, bf16[288,128]{1,0:T(8,128)(2,1)S(1)}, u32[]{:S(2)}, u32[]{:S(2)}) collective-permute-start(bf16[288,128]{1,0:T(8,128)(2,1)} %get-tuple-element.76), channel_id=1, source_target_pairs={{0,4},{1,5},{2,6},{3,7},{4,0},{5,1},{6,2},{7,3},{8,12},{9,13},{10,... | collective-permute-start | bytes 221192 | tf_op jit(solution)/shard_map/ppermute | solution.py:61
  171.3 9.7 %collective-permute-start.21 = (bf16[288,128]{1,0:T(8,128)(2,1)}, bf16[288,128]{1,0:T(8,128)(2,1)}, u32[]{:S(2)}, u32[]{:S(2)}) collective-permute-start(bf16[288,128]{1,0:T(8,128)(2,1)} %get-tuple-element.74), channel_id=1, source_target_pairs={{0,2},{1,3},{2,4},{3,5},{4,6},{5,7},{6,0},{7,1},{8,10},{9,11},{10,... | collective-permute-start | bytes 221192 | tf_op jit(solution)/shard_map/ppermute | solution.py:61
  171.8 18.9 %all-to-all-start.3 = ((bf16[64,8,384]{2,1,0:T(8,128)(2,1)}), bf16[64,8,384]{2,1,0:T(8,128)(2,1)S(1)}, u32[]{:S(2)}, u32[]{:S(2)}) async-start(bf16[64,8,384]{2,1,0:T(8,128)(2,1)} %bitcast.46), calls=%async_computation.3 | async-start | bytes 786432 | tf_op jit(solution)/shard_map/all_to_all | solution.py:65
  (9 other events, 22.1 us)

commit v5 on v4

--- a/solution.py
+++ b/solution.py
@@ -191,7 +191,16 @@
     return (projected / norm).astype(b16)
 
 
-def tile_slopes(rows, groups, place, bias_ref, img, txt, slopes, by_img):
+def fetches(img_from, turned_from, img, turned, sem):
+    half = img.shape[0] // 2
+    parts = [(img_from.at[pl.ds(n * half, half)], img.at[pl.ds(n * half, half)]) for n in range(2)]
+    parts.append((turned_from, turned))
+    return [
+        pltpu.make_async_copy(source, target, sem.at[n]) for n, (source, target) in enumerate(parts)
+    ]
+
+
+def tile_slopes(rows, groups, place, bias_ref, img, txt, slopes, by_img, copies):
     width = img.shape[1]
     tile = 2 * rows
     lang = txt[width : width + PAD].astype(f32)
@@ -205,6 +214,11 @@
     high = 4 * rows
     for m in range(img.shape[0] // high):
         span = slice(m * high, (m + 1) * high)
+
+        @pl.when(pl.program_id(0) == 0)
+        def _():
+            copies[m].wait()
+
         index = m * high + lax.broadcasted_iota(jnp.int32, (high, 1), 0)
         ids = ((index // rows * 16 + place) * rows + index % rows).astype(f32)
         cosines = dot(img[span], txt[:width], NN)
@@ -232,14 +246,25 @@
         up[at + slab : at + slab + PAD] = figures
 
 
-def other_kernel(rows, groups, at_ref, bias_ref, img, turned, txt, slopes, img_sum, up, by_img):
+def other_kernel(
+    rows, groups, at_ref, bias_ref, img_from, turned_from, txt, slopes, img_sum, up,
+    by_img, img, turned, sem,
+):
     step = pl.program_id(0)
+    copies = fetches(img_from, turned_from, img, turned, sem)
 
     @pl.when(step == 0)
     def _():
+        for copy in copies:
+            copy.start()
         by_img[...] = jnp.zeros(by_img.shape, f32)
 
-    down = tile_slopes(rows, groups, at_ref[0], bias_ref, img, txt, slopes.at[0], by_img)
+    down = tile_slopes(rows, groups, at_ref[0], bias_ref, img, txt, slopes.at[0], by_img, copies)
+
+    @pl.when(step == 0)
+    def _():
+        copies[2].wait()
+
     put_text_terms(up, turned, slopes[0], down)
 
     @pl.when(step == 3)
@@ -263,8 +288,8 @@
         [group_bias, img, turned, txt],
         in_specs=[
             pl.BlockSpec(memory_space=pltpu.SMEM),
-            whole(img),
-            whole(turned),
+            pl.BlockSpec(memory_space=pl.ANY),
+            pl.BlockSpec(memory_space=pl.ANY),
             pl.BlockSpec((width + PAD, tile), lambda i, at: (0, i)),
         ],
         out_specs=[
@@ -273,26 +298,41 @@
             pl.BlockSpec((height, tile), lambda i, at: (0, i)),
         ],
         grid=(4,),
-        scratch=[pltpu.VMEM((count, min(128, tile)), f32)],
+        scratch=[
+            pltpu.VMEM((count, min(128, tile)), f32),
+            pltpu.VMEM((count, width), b16),
+            pltpu.VMEM((width, count), b16),
+            pltpu.SemaphoreType.DMA((3,)),
+        ],
         cost=4 * width * count * count,
     )
 
 
-def own_kernel(rows, groups, at_ref, bias_ref, img, turned, txt, other, *refs):
-    other_slopes, other_sum, up, out, by_img, held, both, total = refs
+def own_kernel(
+    rows, groups, at_ref, bias_ref, img_from, turned_from, txt, other, other_slopes, other_sum,
+    up, out, by_img, held, both, total, img, turned, sem,
+):
     step = pl.program_id(0)
     width = img.shape[1]
     tile = 2 * rows
+    copies = fetches(img_from, turned_from, img, turned, sem)
 
     @pl.when(step == 0)
     def _():
+        for copy in copies:
+            copy.start()
         by_img[...] = jnp.zeros(by_img.shape, f32)
         total[...] = jnp.zeros(total.shape, f32)
 
     both[:, tile:] = other[:width]
     held[:, tile:] = other_slopes[0]
     both[:, :tile] = txt[:width]
-    down = tile_slopes(rows, groups, at_ref[0], bias_ref, img, txt, held, by_img)
+    down = tile_slopes(rows, groups, at_ref[0], bias_ref, img, txt, held, by_img, copies)
+
+    @pl.when(step == 0)
+    def _():
+        copies[2].wait()
+
     put_text_terms(up, turned, held[:, :tile], down)
     total[...] += dot(both[...], held[...], NT)
 
@@ -323,8 +363,8 @@
         [group_bias, img, turned, txt, other, other_slopes, other_sum],
         in_specs=[
             pl.BlockSpec(memory_space=pltpu.SMEM),
-            whole(img),
-            whole(turned),
+            pl.BlockSpec(memory_space=pl.ANY),
+            pl.BlockSpec(memory_space=pl.ANY),
             pl.BlockSpec((width + PAD, tile), lambda i, at: (0, i)),
             pl.BlockSpec((width + PAD, tile), lambda i, at: (0, i)),
             pl.BlockSpec((1, count, tile), lambda i, at: (i, 0, 0)),
@@ -337,6 +377,9 @@
             pltpu.VMEM((count, 2 * tile), b16),
             pltpu.VMEM((width, 2 * tile), b16),
             pltpu.VMEM((width, count), f32),
+            pltpu.VMEM((count, width), b16),
+            pltpu.VMEM((width, count), b16),
+            pltpu.SemaphoreType.DMA((3,)),
         ],
         cost=8 * width * count * count,
     )
@@ -533,11 +576,9 @@
     across = send(text_rows, txt_move(0, 1))
     before = send(text_rows, txt_move(1, 0))
     after = send(text_rows, txt_move(3, 0))
+    across, before, after, turned_txt = together([across, before, after, text_head.T])
     across_after = send(across, txt_move(3, 0))
     across_before = send(across, txt_move(1, 0))
-    across_after, before, after, across, turned_txt = together(
-        [across_after, before, after, across, text_head.T]
-    )
     far = send(before, txt_move(1, 0))
     across_far = send(across_after, txt_move(3, 0))
     txt_blocks = [

time: 196 us -> 197 us (level)
  Pallas kernels: 64.3 us -> 70.5 us
  waiting for transfers between devices: 33.2 us -> 28.7 us
    pallas_call x10, Pallas kernels: 64.3 us -> 70.5 us  [call(): pl.pallas_call(body, out_shape=out_shape, grid_spec=spec, input_output_al...]
    ppermute x22, waiting for transfers between devices: 28.9 us -> 24.3 us  [send(): lax.ppermute(block, DEV, [(flat(*p), flat(*move(*p))) for p in PLACES])]
  transfers between devices with their start and end apart: 26 -> 26, of which waited for: 8 -> 7; matrix products, arithmetic and copies ran while one was open for 16% -> 16% of each run, Pallas kernels for 26% -> 28%
where the time goes in v5:
time: 197 us; the launch traced here: 195 us
  Pallas kernels  70.5 us (36%)
  starting transfers between devices  57.1 us (29%)
  waiting for transfers between devices  28.7 us (15%)
  matrix products  15.5 us (8%)
  local copies, waits for them, and re-layouts  13.5 us (7%)
  other arithmetic  8.17 us (4%)
    pallas_call x10, Pallas kernels, call(): pl.pallas_call(body, out_shape=out_shape, grid_spec=spec, input_output_al...  70.5 us
    ppermute x22, starting transfers between devices, send(): lax.ppermute(block, DEV, [(flat(*p), flat(*move(*p))) for p in PLACES])  34 us
    ppermute x22, waiting for transfers between devices, send(): lax.ppermute(block, DEV, [(flat(*p), flat(*move(*p))) for p in PLACES])  24.3 us
    all_to_all x4, starting transfers between devices, exchange(): lax.all_to_all(blocks, DEV, 0, 0, axis_index_groups=groups, tiled=True)  23.1 us
    dot_general x4, matrix products, dot(): return lax.dot_general(a, b, dims, preferred_element_type=f32)  15.5 us
    unnamed x36, local copies, waits for them, and re-layouts  8.56 us
    all_to_all x4, waiting for transfers between devices, exchange(): lax.all_to_all(blocks, DEV, 0, 0, axis_index_groups=groups, tiled=True)  4.44 us
  transfers between devices with their start and end apart: 26, of which 7 were waited for; matrix products, arithmetic and copies ran while one was open for 16% of the time, Pallas kernels for 28%

profile of v5, /device:TPU:1, one launch (start us, length us, event | category | flops | bytes accessed | tf_op | source)
XLA Modules:
  0.0 194.7 jit_solution(5984354886499517162)
XLA Ops:
  0.6 2.9 %broadcast_in_dim.2 = bf16[8,128,1152]{2,1,0:T(8,128)(2,1)} broadcast(bf16[128,1152]{1,0:T(8,128)(2,1)} %param.7), dimensions={1,2} | broadcast | bytes 2654208 | tf_op jit(solution)/shard_map/broadcast_in_dim | solution.py:574
  3.5 6.9 %all-to-all-start = ((bf16[8,128,1152]{2,1,0:T(8,128)(2,1)}), bf16[8,128,1152]{2,1,0:T(8,128)(2,1)}, u32[]{:S(2)}, u32[]{:S(2)}) async-start(bf16[8,128,1152]{2,1,0:T(8,128)(2,1)} %broadcast_in_dim.2), calls=%async_computation | async-start | bytes 4718592 | tf_op jit(solution)/shard_map/all_to_all | solution.py:65
  10.5 2.8 %collective-permute-start = (bf16[144,1152]{1,0:T(8,128)(2,1)S(1)}, bf16[144,1152]{1,0:T(8,128)(2,1)S(1)}, u32[]{:S(2)}, u32[]{:S(2)}) collective-permute-start(bf16[144,1152]{1,0:T(8,128)(2,1)S(1)} %pad_maximum_fusion.refs_1_.refs_8_), channel_id=1, source_target_pairs={{0,24},{1,25},{2,26},{3,27},{4,28},{5,29},{6,30},{7,31},{8,16},{9,... | collective-permute-start | bytes 995336 | tf_op jit(solution)/shard_map/ppermute | solution.py:61
  16.1 5.2 %copy.11 = bf16[1152,1152]{0,1:T(8,128)(2,1)} copy(bf16[1152,1152]{1,0:T(8,128)(2,1)} %param.10) | data formatting | bytes 5308416 | tf_op args[3]
  22.6 2.4 %collective-permute-start.3 = (bf16[144,1152]{1,0:T(8,128)(2,1)S(1)}, bf16[144,1152]{1,0:T(8,128)(2,1)S(1)}, u32[]{:S(2)}, u32[]{:S(2)}) collective-permute-start(bf16[144,1152]{1,0:T(8,128)(2,1)S(1)} %collective-permute-done.refs_2_.refs_9_), channel_id=1, source_target_pairs={{0,6},{1,7},{2,0},{3,1},{4,2},{5,3},{6,4},{7,5},{8,14},{9,15},{10,... | collective-permute-start | bytes 995336 | tf_op jit(solution)/shard_map/ppermute | solution.py:61
  25.0 4.5 %collective-permute-done.3.refs_4_.refs_11_ = bf16[144,1152]{1,0:T(8,128)(2,1)S(1)} collective-permute-done((bf16[144,1152]{1,0:T(8,128)(2,1)S(1)}, bf16[144,1152]{1,0:T(8,128)(2,1)S(1)}, u32[]{:S(2)}, u32[]{:S(2)}) %collective-permute-start.3) | collective-permute-done | bytes 331808 | tf_op jit(solution)/shard_map/ppermute | solution.py:61
  29.6 3.3 %collective-permute-start.5 = (bf16[144,1152]{1,0:T(8,128)(2,1)S(1)}, bf16[144,1152]{1,0:T(8,128)(2,1)}, u32[]{:S(2)}, u32[]{:S(2)}) collective-permute-start(bf16[144,1152]{1,0:T(8,128)(2,1)S(1)} %collective-permute-done.3.refs_4_.refs_11_), channel_id=1, source_target_pairs={{0,6},{1,7},{2,0},{3,1},{4,2},{5,3},{6,4},{7,5},{8,14},{9,15},{10,... | collective-permute-start | bytes 995336 | tf_op jit(solution)/shard_map/ppermute | solution.py:61
  33.5 6.2 %collective-permute-done.4.refs_5_.refs_12_ = bf16[144,1152]{1,0:T(8,128)(2,1)} collective-permute-done((bf16[144,1152]{1,0:T(8,128)(2,1)}, bf16[144,1152]{1,0:T(8,128)(2,1)}, u32[]{:S(2)}, u32[]{:S(2)}) %collective-permute-start.4) | collective-permute-done | bytes 331808 | tf_op jit(solution)/shard_map/ppermute | solution.py:61
  39.7 9.1 %shard_map.102 = (bf16[1168,1024]{1,0:T(8,128)(2,1)}, f32[1,1024]{1,0:T(1,128)}) custom-call(s32[2]{0:T(128)} %pad_add_fusion.1.refs_0_, bf16[144,1152]{1,0:T(8,128)(2,1)} %copy-done.2, bf16[144,1152]{1,0:T(8,128)(2,1)} %copy-done.3, bf16[144,1152]{1,0:T(8,128)(2,1)} %collective-permute-done.2.refs_3_.refs_10_, bf16[144,1152]{1,0:T(8,128)(2,1)} %copy-done.4, ...), custom_call_target="tpu_custom_call" | custom-call | flops 2717908992 | bytes 5308416 | tf_op jit(solution)/shard_map/pallas_call | solution.py:93
  48.9 3.9 %collective-permute-start.7 = (bf16[1168,1024]{1,0:T(8,128)(2,1)}, bf16[1168,1024]{1,0:T(8,128)(2,1)}, u32[]{:S(2)}, u32[]{:S(2)}) collective-permute-start(bf16[1168,1024]{1,0:T(8,128)(2,1)} %get-tuple-element.42.refs_4_.refs_6_), channel_id=1, source_target_pairs={{0,1},{1,0},{2,3},{3,2},{4,5},{5,4},{6,7},{7,6},{8,9},{9,8},{10,11... | collective-permute-start | bytes 7176200 | tf_op jit(solution)/shard_map/ppermute | solution.py:61
  52.8 5.0 %multiply_reduce_fusion = (f32[1024]{0:T(1024)S(1)}, f32[1152,1024]{1,0:T(8,128)S(1)}) fusion(bf16[1152,1152]{1,0:T(8,128)(2,1)S(1)} %copy-done, bf16[1024,1152]{1,0:T(8,128)(2,1)} %bitcast.4.refs_4_), kind=kOutput, calls=%fused_computation.1 | convolution fusion | flops 2720267264 | bytes 9736192 | tf_op jit(solution)/shard_map/dot_general | solution.py:75
  57.7 5.3 %multiply_reduce_fusion.1 = (f32[1024]{0:T(1024)S(1)}, f32[1024,1152]{1,0:T(8,128)S(1)}) fusion(bf16[1024,1152]{1,0:T(8,128)(2,1)} %bitcast.4.refs_4_, bf16[1152,1152]{1,0:T(8,128)(2,1)S(1)} %copy-done), kind=kOutput, calls=%fused_computation.3 | convolution fusion | flops 2720267264 | bytes 9736192 | tf_op jit(solution)/shard_map/dot_general | solution.py:75
  67.2 15.0 %shard_map.103 = (bf16[4,1024,256]{2,1,0:T(8,128)(2,1)}, f32[1,1024]{1,0:T(1,128)}, bf16[1280,1024]{1,0:T(8,128)(2,1)}) custom-call(s32[1]{0:T(128)} %bitcast.3.refs_0_, f32[32]{0:T(128)} %refs_1_.3, bf16[1024,1152]{1,0:T(8,128)(2,1)} %divide_convert_fusion.1.refs_2_, bf16[1152,1024]{1,0:T(8,128)(2,1)} %divide_convert_fusion.refs_3_.refs_2_, ...), custom_call_target="tpu_custom_call" | custom-call | flops 4831838208 | bytes 7110784 | tf_op jit(solution)/shard_map/pallas_call | solution.py:93
  82.5 21.9 %shard_map.104 = (bf16[1280,1024]{1,0:T(8,128)(2,1)}, bf16[8,160,1024]{2,1,0:T(8,128)(2,1)}) custom-call(s32[1]{0:T(128)} %bitcast.3.refs_0_, f32[32]{0:T(128)} %refs_1_.3, bf16[1024,1152]{1,0:T(8,128)(2,1)} %divide_convert_fusion.1.refs_2_, bf16[1152,1024]{1,0:T(8,128)(2,1)} %divide_convert_fusion.refs_3_.refs_2_, ...), custom_call_target="tpu_custom_call" | custom-call | flops 9663676416 | bytes 11604096 | tf_op jit(solution)/shard_map/pallas_call | solution.py:93
  104.4 4.4 %all-to-all-start.1 = ((bf16[8,160,1024]{2,1,0:T(8,128)(2,1)}), bf16[8,160,1024]{2,1,0:T(8,128)(2,1)}, u32[]{:S(2)}, u32[]{:S(2)}) async-start(bf16[8,160,1024]{2,1,0:T(8,128)(2,1)} %get-tuple-element.46), calls=%async_computation.1 | async-start | bytes 5242880 | tf_op jit(solution)/shard_map/all_to_all | solution.py:65
  109.5 3.1 %shard_map.106 = (bf16[160,1024]{1,0:T(8,128)(2,1)}, bf16[160,1024]{1,0:T(8,128)(2,1)}, bf16[160,1024]{1,0:T(8,128)(2,1)}) custom-call(s32[7]{0:T(128)} %stack.108.refs_0_, bf16[1280,1024]{1,0:T(8,128)(2,1)} %get-tuple-element.49.refs_1_.refs_3_.refs_5_.refs_4_.refs_7_, bf16[1280,1024]{1,0:T(8,128)(2,1)} %collective-permute-done.8.refs_2_.refs_4_.refs_6_.refs_5_.refs_8_, ...), custom_call_target="tpu_custom_call" | custom-call | bytes 15728640 | tf_op jit(solution)/shard_map/pallas_call | solution.py:93
  112.7 2.7 %collective-permute-start.10 = (bf16[160,1024]{1,0:T(8,128)(2,1)}, bf16[160,1024]{1,0:T(8,128)(2,1)S(1)}, u32[]{:S(2)}, u32[]{:S(2)}) collective-permute-start(bf16[160,1024]{1,0:T(8,128)(2,1)} %get-tuple-element.52), channel_id=1, source_target_pairs={{0,6},{1,7},{2,0},{3,1},{4,2},{5,3},{6,4},{7,5},{8,14},{9,15},{10,... | collective-permute-start | bytes 983048 | tf_op jit(solution)/shard_map/ppermute | solution.py:61
  115.9 7.0 %collective-permute-done.9.refs_6_ = bf16[160,1024]{1,0:T(8,128)(2,1)S(1)} collective-permute-done((bf16[160,1024]{1,0:T(8,128)(2,1)}, bf16[160,1024]{1,0:T(8,128)(2,1)S(1)}, u32[]{:S(2)}, u32[]{:S(2)}) %collective-permute-start.9) | collective-permute-done | bytes 327712 | tf_op jit(solution)/shard_map/ppermute | solution.py:61
  123.8 3.4 %shard_map.107 = (bf16[160,1024]{1,0:T(8,128)(2,1)}, bf16[160,1024]{1,0:T(8,128)(2,1)}, bf16[160,1024]{1,0:T(8,128)(2,1)}) custom-call(s32[7]{0:T(128)} %stack.112.refs_0_, bf16[1280,1024]{1,0:T(8,128)(2,1)} %get-tuple-element.49.refs_1_.refs_3_.refs_5_.refs_4_.refs_7_, bf16[1280,1024]{1,0:T(8,128)(2,1)} %collective-permute-done.8.refs_2_.refs_4_.refs_6_.refs_5_.refs_8_, ...), custom_call_target="tpu_custom_call" | custom-call | bytes 16384000 | tf_op jit(solution)/shard_map/pallas_call | solution.py:93
  127.2 2.7 %collective-permute-start.12 = (bf16[160,1024]{1,0:T(8,128)(2,1)}, bf16[160,1024]{1,0:T(8,128)(2,1)S(1)}, u32[]{:S(2)}, u32[]{:S(2)}) collective-permute-start(bf16[160,1024]{1,0:T(8,128)(2,1)} %get-tuple-element.57), channel_id=1, source_target_pairs={{0,6},{1,7},{2,0},{3,1},{4,2},{5,3},{6,4},{7,5},{8,14},{9,15},{10,... | collective-permute-start | bytes 983048 | tf_op jit(solution)/shard_map/ppermute | solution.py:61
  130.5 2.8 %collective-permute-done.11.refs_3_ = bf16[160,1024]{1,0:T(8,128)(2,1)S(1)} collective-permute-done((bf16[160,1024]{1,0:T(8,128)(2,1)}, bf16[160,1024]{1,0:T(8,128)(2,1)S(1)}, u32[]{:S(2)}, u32[]{:S(2)}) %collective-permute-start.11) | collective-permute-done | bytes 327712 | tf_op jit(solution)/shard_map/ppermute | solution.py:61
  133.3 2.4 %collective-permute-done.12.refs_4_ = bf16[160,1024]{1,0:T(8,128)(2,1)S(1)} collective-permute-done((bf16[160,1024]{1,0:T(8,128)(2,1)}, bf16[160,1024]{1,0:T(8,128)(2,1)S(1)}, u32[]{:S(2)}, u32[]{:S(2)}) %collective-permute-start.12) | collective-permute-done | bytes 327712 | tf_op jit(solution)/shard_map/ppermute | solution.py:61
  139.1 2.8 %shard_map.108 = bf16[160,1024]{1,0:T(8,128)(2,1)} custom-call(s32[3]{0:T(128)} %pad_add_fusion.3.refs_0_, bf16[1280,1024]{1,0:T(8,128)(2,1)} %get-tuple-element.49.refs_1_.refs_3_.refs_5_.refs_4_.refs_7_, bf16[1280,1024]{1,0:T(8,128)(2,1)} %collective-permute-done.8.refs_2_.refs_4_.refs_6_.refs_5_.refs_8_, bf16[160,1024]{1,0:T(8,128)(2,1)} %copy-done.6, ...), custom_call_target="tpu_custom_call" | custom-call | bytes 5898240 | tf_op jit(solution)/shard_map/pallas_call | solution.py:93
  142.5 4.8 %shard_map.105 = (bf16[8,144,128]{2,1,0:T(8,128)(2,1)}, bf16[144,1152]{1,0:T(8,128)(2,1)}) custom-call(s32[3]{0:T(128)} %pad_add_fusion.refs_0_, bf16[8,160,1024]{2,1,0:T(8,128)(2,1)} %all-to-all-done.1.refs_1_, bf16[1152,1024]{1,0:T(8,128)(2,1)} %divide_convert_fusion.refs_3_.refs_2_, f32[1,1024]{1,0:T(1,128)} %bitcast.48, bf16[1024,1152]{1,0:T(8,128)(2,1)} %bitcast.4.refs_4_), custom_call_target="tpu_custom_call" | custom-call | tf_op jit(solution)/shard_map/pallas_call | solution.py:93
  147.4 4.0 %all-to-all-start.2 = ((bf16[8,144,128]{2,1,0:T(8,128)(2,1)}), bf16[8,144,128]{2,1,0:T(8,128)(2,1)S(1)}, u32[]{:S(2)}, u32[]{:S(2)}) async-start(bf16[8,144,128]{2,1,0:T(8,128)(2,1)} %get-tuple-element.47), calls=%async_computation.2 | async-start | bytes 589824 | tf_op jit(solution)/shard_map/all_to_all | solution.py:65
  152.0 3.6 %collective-permute-start.16 = (bf16[144,1152]{1,0:T(8,128)(2,1)}, bf16[144,1152]{1,0:T(8,128)(2,1)S(1)}, u32[]{:S(2)}, u32[]{:S(2)}) collective-permute-start(bf16[144,1152]{1,0:T(8,128)(2,1)} %get-tuple-element.48.img), channel_id=1, source_target_pairs={{0,1},{1,0},{2,3},{3,2},{4,5},{5,4},{6,7},{7,6},{8,9},{9,8},{10,11... | collective-permute-start | bytes 995336 | tf_op jit(solution)/shard_map/ppermute | solution.py:61
  155.6 4.9 %shard_map.109 = (bf16[4,144,128]{2,1,0:T(8,128)(2,1)}, bf16[4,144,128]{2,1,0:T(8,128)(2,1)}, bf16[144,1152]{1,0:T(8,128)(2,1)}) custom-call(s32[3]{0:T(128)} %pad_add_fusion.2.refs_0_, bf16[1280,1024]{1,0:T(8,128)(2,1)} %get-tuple-element.49.refs_1_.refs_3_.refs_5_.refs_4_.refs_7_, ...), custom_call_target="tpu_custom_call" | custom-call | tf_op jit(solution)/shard_map/pallas_call | solution.py:93
  160.5 3.7 %collective-permute-start.18 = (bf16[4,144,128]{2,1,0:T(8,128)(2,1)}, bf16[4,144,128]{2,1,0:T(8,128)(2,1)}, u32[]{:S(2)}, u32[]{:S(2)}) collective-permute-start(bf16[4,144,128]{2,1,0:T(8,128)(2,1)} %get-tuple-element.66), channel_id=1, source_target_pairs={{0,24},{1,25},{2,26},{3,27},{4,28},{5,29},{6,30},{7,31},{8,16},{9,... | collective-permute-start | bytes 442376 | tf_op jit(solution)/shard_map/ppermute | solution.py:61
  166.7 3.7 %shard_map.110 = bf16[512,384]{1,0:T(8,128)(2,1)} custom-call(s32[1]{0:T(128)} %bitcast.13.at_ref, bf16[144,1152]{1,0:T(8,128)(2,1)} %get-tuple-element.48.img, bf16[144,1152]{1,0:T(8,128)(2,1)} %get-tuple-element.65.txt, bf16[144,1152]{1,0:T(8,128)(2,1)} %copy-done.5, bf16[144,1152]{1,0:T(8,128)(2,1)} %collective-permute-done.17.other_txt), custom_call_target="tpu_custom_call" | custom-call | tf_op jit(solution)/shard_map/pallas_call | solution.py:93
  174.4 7.8 %all-to-all-start.3 = ((bf16[64,8,384]{2,1,0:T(8,128)(2,1)}), bf16[64,8,384]{2,1,0:T(8,128)(2,1)S(1)}, u32[]{:S(2)}, u32[]{:S(2)}) async-start(bf16[64,8,384]{2,1,0:T(8,128)(2,1)} %bitcast.46), calls=%async_computation.3 | async-start | bytes 786432 | tf_op jit(solution)/shard_map/all_to_all | solution.py:65
  184.1 3.5 %fusion = f32[128,1152]{1,0:T(8,128)} fusion(bf16[1152,1152]{1,0:T(8,128)(2,1)} %param.10, bf16[2304,128]{1,0:T(8,128)(2,1)S(1)} %constant_dynamic-update-slice_fusion, s32[]{:T(128)S(6)} %select_n.154), kind=kOutput, calls=%fused_computation.13 | convolution fusion | flops 339738624 | bytes 3538948 | tf_op jit(solution)/shard_map/dot_general | solution.py:75
  187.7 4.4 %all-to-all-done.3.got = bf16[64,8,384]{2,1,0:T(8,128)(2,1)S(1)} async-done(((bf16[64,8,384]{2,1,0:T(8,128)(2,1)}), bf16[64,8,384]{2,1,0:T(8,128)(2,1)S(1)}, u32[]{:S(2)}, u32[]{:S(2)}) %all-to-all-start.3) | async-done | bytes 393248 | tf_op jit(solution)/shard_map/all_to_all | solution.py:65
  (89 shorter events, 27.4 us)
Async XLA Ops:
  0.6 52.1 %copy-start = (bf16[1152,1152]{1,0:T(8,128)(2,1)S(1)}, bf16[1152,1152]{1,0:T(8,128)(2,1)}, u32[]{:S(2)}) copy-start(bf16[1152,1152]{1,0:T(8,128)(2,1)} %param.9) | copy-start | bytes 7962628
  3.5 7.0 %copy-start.10 = (bf16[128,1152]{1,0:T(8,128)(2,1)S(1)}, bf16[128,1152]{1,0:T(8,128)(2,1)}, u32[]{:S(2)}) copy-start(bf16[128,1152]{1,0:T(8,128)(2,1)} %param.8) | copy-start | bytes 884740
  3.5 49.3 %all-to-all-start = ((bf16[8,128,1152]{2,1,0:T(8,128)(2,1)}), bf16[8,128,1152]{2,1,0:T(8,128)(2,1)}, u32[]{:S(2)}, u32[]{:S(2)}) async-start(bf16[8,128,1152]{2,1,0:T(8,128)(2,1)} %broadcast_in_dim.2), calls=%async_computation | async-start | bytes 4718592 | tf_op jit(solution)/shard_map/all_to_all | solution.py:65
  10.5 10.8 %copy-start.2 = (bf16[144,1152]{1,0:T(8,128)(2,1)}, bf16[144,1152]{1,0:T(8,128)(2,1)S(1)}, u32[]{:S(2)}) copy-start(bf16[144,1152]{1,0:T(8,128)(2,1)S(1)} %pad_maximum_fusion.refs_1_.refs_8_) | copy-start | bytes 995332
  10.5 10.8 %collective-permute-start = (bf16[144,1152]{1,0:T(8,128)(2,1)S(1)}, bf16[144,1152]{1,0:T(8,128)(2,1)S(1)}, u32[]{:S(2)}, u32[]{:S(2)}) collective-permute-start(bf16[144,1152]{1,0:T(8,128)(2,1)S(1)} %pad_maximum_fusion.refs_1_.refs_8_), channel_id=1, source_target_pairs={{0,24},{1,25},{2,26},{3,27},{4,28},{5,29},{6,30},{7,31},{8,16},{9,... | collective-permute-start | bytes 995336 | tf_op jit(solution)/shard_map/ppermute | solution.py:61
  13.3 9.2 %collective-permute-start.1 = (bf16[144,1152]{1,0:T(8,128)(2,1)S(1)}, bf16[144,1152]{1,0:T(8,128)(2,1)}, u32[]{:S(2)}, u32[]{:S(2)}) collective-permute-start(bf16[144,1152]{1,0:T(8,128)(2,1)S(1)} %pad_maximum_fusion.refs_1_.refs_8_), channel_id=1, source_target_pairs={{0,2},{1,3},{2,4},{3,5},{4,6},{5,7},{6,0},{7,1},{8,10},{9,11},{10,... | collective-permute-start | bytes 995336 | tf_op jit(solution)/shard_map/ppermute | solution.py:61
  14.6 7.9 %collective-permute-start.2 = (bf16[144,1152]{1,0:T(8,128)(2,1)S(1)}, bf16[144,1152]{1,0:T(8,128)(2,1)}, u32[]{:S(2)}, u32[]{:S(2)}) collective-permute-start(bf16[144,1152]{1,0:T(8,128)(2,1)S(1)} %pad_maximum_fusion.refs_1_.refs_8_), channel_id=1, source_target_pairs={{0,6},{1,7},{2,0},{3,1},{4,2},{5,3},{6,4},{7,5},{8,14},{9,15},{10,... | collective-permute-start | bytes 995336 | tf_op jit(solution)/shard_map/ppermute | solution.py:61
  21.3 18.4 %copy-start.3 = (bf16[144,1152]{1,0:T(8,128)(2,1)}, bf16[144,1152]{1,0:T(8,128)(2,1)S(1)}, u32[]{:S(2)}) copy-start(bf16[144,1152]{1,0:T(8,128)(2,1)S(1)} %collective-permute-done.refs_2_.refs_9_) | copy-start | bytes 995332
  22.6 7.0 %collective-permute-start.3 = (bf16[144,1152]{1,0:T(8,128)(2,1)S(1)}, bf16[144,1152]{1,0:T(8,128)(2,1)S(1)}, u32[]{:S(2)}, u32[]{:S(2)}) collective-permute-start(bf16[144,1152]{1,0:T(8,128)(2,1)S(1)} %collective-permute-done.refs_2_.refs_9_), channel_id=1, source_target_pairs={{0,6},{1,7},{2,0},{3,1},{4,2},{5,3},{6,4},{7,5},{8,14},{9,15},{10,... | collective-permute-start | bytes 995336 | tf_op jit(solution)/shard_map/ppermute | solution.py:61
  24.9 14.8 %collective-permute-start.6 = (bf16[144,1152]{1,0:T(8,128)(2,1)S(1)}, bf16[144,1152]{1,0:T(8,128)(2,1)}, u32[]{:S(2)}, u32[]{:S(2)}) collective-permute-start(bf16[144,1152]{1,0:T(8,128)(2,1)S(1)} %collective-permute-done.refs_2_.refs_9_), channel_id=1, source_target_pairs={{0,2},{1,3},{2,4},{3,5},{4,6},{5,7},{6,0},{7,1},{8,10},{9,11},{10,... | collective-permute-start | bytes 995336 | tf_op jit(solution)/shard_map/ppermute | solution.py:61
  24.9 14.8 %collective-permute-start.4 = (bf16[144,1152]{1,0:T(8,128)(2,1)}, bf16[144,1152]{1,0:T(8,128)(2,1)}, u32[]{:S(2)}, u32[]{:S(2)}) collective-permute-start(bf16[144,1152]{1,0:T(8,128)(2,1)} %collective-permute-done.1.refs_7_.refs_14_), channel_id=1, source_target_pairs={{0,2},{1,3},{2,4},{3,5},{4,6},{5,7},{6,0},{7,1},{8,10},{9,11},{10,... | collective-permute-start | bytes 995336 | tf_op jit(solution)/shard_map/ppermute | solution.py:61
  29.5 10.2 %copy-start.4 = (bf16[144,1152]{1,0:T(8,128)(2,1)}, bf16[144,1152]{1,0:T(8,128)(2,1)S(1)}, u32[]{:S(2)}) copy-start(bf16[144,1152]{1,0:T(8,128)(2,1)S(1)} %collective-permute-done.3.refs_4_.refs_11_) | copy-start | bytes 995332
  29.6 10.2 %collective-permute-start.5 = (bf16[144,1152]{1,0:T(8,128)(2,1)S(1)}, bf16[144,1152]{1,0:T(8,128)(2,1)}, u32[]{:S(2)}, u32[]{:S(2)}) collective-permute-start(bf16[144,1152]{1,0:T(8,128)(2,1)S(1)} %collective-permute-done.3.refs_4_.refs_11_), channel_id=1, source_target_pairs={{0,6},{1,7},{2,0},{3,1},{4,2},{5,3},{6,4},{7,5},{8,14},{9,15},{10,... | collective-permute-start | bytes 995336 | tf_op jit(solution)/shard_map/ppermute | solution.py:61
  48.9 18.3 %collective-permute-start.7 = (bf16[1168,1024]{1,0:T(8,128)(2,1)}, bf16[1168,1024]{1,0:T(8,128)(2,1)}, u32[]{:S(2)}, u32[]{:S(2)}) collective-permute-start(bf16[1168,1024]{1,0:T(8,128)(2,1)} %get-tuple-element.42.refs_4_.refs_6_), channel_id=1, source_target_pairs={{0,1},{1,0},{2,3},{3,2},{4,5},{5,4},{6,7},{7,6},{8,9},{9,8},{10,11... | collective-permute-start | bytes 7176200 | tf_op jit(solution)/shard_map/ppermute | solution.py:61
  82.2 27.3 %collective-permute-start.8 = (bf16[1280,1024]{1,0:T(8,128)(2,1)}, bf16[1280,1024]{1,0:T(8,128)(2,1)}, u32[]{:S(2)}, u32[]{:S(2)}) collective-permute-start(bf16[1280,1024]{1,0:T(8,128)(2,1)} %get-tuple-element.50), channel_id=1, source_target_pairs={{0,1},{1,0},{2,3},{3,2},{4,5},{5,4},{6,7},{7,6},{8,9},{9,8},{10,11... | collective-permute-start | bytes 7864328 | tf_op jit(solution)/shard_map/ppermute | solution.py:61
  104.4 38.1 %all-to-all-start.1 = ((bf16[8,160,1024]{2,1,0:T(8,128)(2,1)}), bf16[8,160,1024]{2,1,0:T(8,128)(2,1)}, u32[]{:S(2)}, u32[]{:S(2)}) async-start(bf16[8,160,1024]{2,1,0:T(8,128)(2,1)} %get-tuple-element.46), calls=%async_computation.1 | async-start | bytes 5242880 | tf_op jit(solution)/shard_map/all_to_all | solution.py:65
  112.6 10.3 %collective-permute-start.9 = (bf16[160,1024]{1,0:T(8,128)(2,1)}, bf16[160,1024]{1,0:T(8,128)(2,1)S(1)}, u32[]{:S(2)}, u32[]{:S(2)}) collective-permute-start(bf16[160,1024]{1,0:T(8,128)(2,1)} %get-tuple-element.51), channel_id=1, source_target_pairs={{0,2},{1,3},{2,4},{3,5},{4,6},{5,7},{6,0},{7,1},{8,10},{9,11},{10,... | collective-permute-start | bytes 983048 | tf_op jit(solution)/shard_map/ppermute | solution.py:61
  112.7 10.3 %collective-permute-start.10 = (bf16[160,1024]{1,0:T(8,128)(2,1)}, bf16[160,1024]{1,0:T(8,128)(2,1)S(1)}, u32[]{:S(2)}, u32[]{:S(2)}) collective-permute-start(bf16[160,1024]{1,0:T(8,128)(2,1)} %get-tuple-element.52), channel_id=1, source_target_pairs={{0,6},{1,7},{2,0},{3,1},{4,2},{5,3},{6,4},{7,5},{8,14},{9,15},{10,... | collective-permute-start | bytes 983048 | tf_op jit(solution)/shard_map/ppermute | solution.py:61
  123.8 9.5 %collective-permute-start.11 = (bf16[160,1024]{1,0:T(8,128)(2,1)}, bf16[160,1024]{1,0:T(8,128)(2,1)S(1)}, u32[]{:S(2)}, u32[]{:S(2)}) collective-permute-start(bf16[160,1024]{1,0:T(8,128)(2,1)} %get-tuple-element.54), channel_id=1, source_target_pairs={{0,2},{1,3},{2,4},{3,5},{4,6},{5,7},{6,0},{7,1},{8,10},{9,11},{10,... | collective-permute-start | bytes 983048 | tf_op jit(solution)/shard_map/ppermute | solution.py:61
  127.2 8.5 %collective-permute-start.12 = (bf16[160,1024]{1,0:T(8,128)(2,1)}, bf16[160,1024]{1,0:T(8,128)(2,1)S(1)}, u32[]{:S(2)}, u32[]{:S(2)}) collective-permute-start(bf16[160,1024]{1,0:T(8,128)(2,1)} %get-tuple-element.57), channel_id=1, source_target_pairs={{0,6},{1,7},{2,0},{3,1},{4,2},{5,3},{6,4},{7,5},{8,14},{9,15},{10,... | collective-permute-start | bytes 983048 | tf_op jit(solution)/shard_map/ppermute | solution.py:61
  135.7 19.9 %collective-permute-start.13 = (bf16[160,1024]{1,0:T(8,128)(2,1)}, bf16[160,1024]{1,0:T(8,128)(2,1)}, u32[]{:S(2)}, u32[]{:S(2)}) collective-permute-start(bf16[160,1024]{1,0:T(8,128)(2,1)} %get-tuple-element.60), channel_id=1, source_target_pairs={{0,2},{1,3},{2,4},{3,5},{4,6},{5,7},{6,0},{7,1},{8,10},{9,11},{10,... | collective-permute-start | bytes 983048 | tf_op jit(solution)/shard_map/ppermute | solution.py:61
  136.8 18.8 %collective-permute-start.14 = (bf16[160,1024]{1,0:T(8,128)(2,1)}, bf16[160,1024]{1,0:T(8,128)(2,1)}, u32[]{:S(2)}, u32[]{:S(2)}) collective-permute-start(bf16[160,1024]{1,0:T(8,128)(2,1)} %get-tuple-element.61), channel_id=1, source_target_pairs={{0,6},{1,7},{2,0},{3,1},{4,2},{5,3},{6,4},{7,5},{8,14},{9,15},{10,... | collective-permute-start | bytes 983048 | tf_op jit(solution)/shard_map/ppermute | solution.py:61
  141.9 13.7 %collective-permute-start.15 = (bf16[160,1024]{1,0:T(8,128)(2,1)}, bf16[160,1024]{1,0:T(8,128)(2,1)}, u32[]{:S(2)}, u32[]{:S(2)}) collective-permute-start(bf16[160,1024]{1,0:T(8,128)(2,1)} %shard_map.108), channel_id=1, source_target_pairs={{0,24},{1,25},{2,26},{3,27},{4,28},{5,29},{6,30},{7,31},{8,16},{9,... | collective-permute-start | bytes 983048 | tf_op jit(solution)/shard_map/ppermute | solution.py:61
  147.4 16.9 %all-to-all-start.2 = ((bf16[8,144,128]{2,1,0:T(8,128)(2,1)}), bf16[8,144,128]{2,1,0:T(8,128)(2,1)S(1)}, u32[]{:S(2)}, u32[]{:S(2)}) async-start(bf16[8,144,128]{2,1,0:T(8,128)(2,1)} %get-tuple-element.47), calls=%async_computation.2 | async-start | bytes 589824 | tf_op jit(solution)/shard_map/all_to_all | solution.py:65
  152.0 14.0 %collective-permute-start.16 = (bf16[144,1152]{1,0:T(8,128)(2,1)}, bf16[144,1152]{1,0:T(8,128)(2,1)S(1)}, u32[]{:S(2)}, u32[]{:S(2)}) collective-permute-start(bf16[144,1152]{1,0:T(8,128)(2,1)} %get-tuple-element.48.img), channel_id=1, source_target_pairs={{0,1},{1,0},{2,3},{3,2},{4,5},{5,4},{6,7},{7,6},{8,9},{9,8},{10,11... | collective-permute-start | bytes 995336 | tf_op jit(solution)/shard_map/ppermute | solution.py:61
  160.5 5.5 %collective-permute-start.17 = (bf16[144,1152]{1,0:T(8,128)(2,1)}, bf16[144,1152]{1,0:T(8,128)(2,1)}, u32[]{:S(2)}, u32[]{:S(2)}) collective-permute-start(bf16[144,1152]{1,0:T(8,128)(2,1)} %get-tuple-element.65.txt), channel_id=1, source_target_pairs={{0,1},{1,0},{2,3},{3,2},{4,5},{5,4},{6,7},{7,6},{8,9},{9,8},{10,11... | collective-permute-start | bytes 995336 | tf_op jit(solution)/shard_map/ppermute | solution.py:61
  160.5 9.9 %copy-start.11 = (bf16[4,144,128]{2,1,0:T(8,128)(2,1)S(1)}, bf16[4,144,128]{2,1,0:T(8,128)(2,1)}, u32[]{:S(2)}) copy-start(bf16[4,144,128]{2,1,0:T(8,128)(2,1)} %get-tuple-element.68) | copy-start | bytes 442372
  160.5 9.9 %collective-permute-start.18 = (bf16[4,144,128]{2,1,0:T(8,128)(2,1)}, bf16[4,144,128]{2,1,0:T(8,128)(2,1)}, u32[]{:S(2)}, u32[]{:S(2)}) collective-permute-start(bf16[4,144,128]{2,1,0:T(8,128)(2,1)} %get-tuple-element.66), channel_id=1, source_target_pairs={{0,24},{1,25},{2,26},{3,27},{4,28},{5,29},{6,30},{7,31},{8,16},{9,... | collective-permute-start | bytes 442376 | tf_op jit(solution)/shard_map/ppermute | solution.py:61
  172.1 10.1 %collective-permute-start.19 = (bf16[288,128]{1,0:T(8,128)(2,1)}, bf16[288,128]{1,0:T(8,128)(2,1)S(1)}, u32[]{:S(2)}, u32[]{:S(2)}) collective-permute-start(bf16[288,128]{1,0:T(8,128)(2,1)} %get-tuple-element.73), channel_id=1, source_target_pairs={{0,6},{1,7},{2,0},{3,1},{4,2},{5,3},{6,4},{7,5},{8,14},{9,15},{10,... | collective-permute-start | bytes 221192 | tf_op jit(solution)/shard_map/ppermute | solution.py:61
  173.8 8.4 %collective-permute-start.20 = (bf16[288,128]{1,0:T(8,128)(2,1)}, bf16[288,128]{1,0:T(8,128)(2,1)S(1)}, u32[]{:S(2)}, u32[]{:S(2)}) collective-permute-start(bf16[288,128]{1,0:T(8,128)(2,1)} %get-tuple-element.74), channel_id=1, source_target_pairs={{0,4},{1,5},{2,6},{3,7},{4,0},{5,1},{6,2},{7,3},{8,12},{9,13},{10,... | collective-permute-start | bytes 221192 | tf_op jit(solution)/shard_map/ppermute | solution.py:61
  173.8 8.4 %collective-permute-start.21 = (bf16[288,128]{1,0:T(8,128)(2,1)}, bf16[288,128]{1,0:T(8,128)(2,1)}, u32[]{:S(2)}, u32[]{:S(2)}) collective-permute-start(bf16[288,128]{1,0:T(8,128)(2,1)} %get-tuple-element.72), channel_id=1, source_target_pairs={{0,2},{1,3},{2,4},{3,5},{4,6},{5,7},{6,0},{7,1},{8,10},{9,11},{10,... | collective-permute-start | bytes 221192 | tf_op jit(solution)/shard_map/ppermute | solution.py:61
  174.4 17.7 %all-to-all-start.3 = ((bf16[64,8,384]{2,1,0:T(8,128)(2,1)}), bf16[64,8,384]{2,1,0:T(8,128)(2,1)S(1)}, u32[]{:S(2)}, u32[]{:S(2)}) async-start(bf16[64,8,384]{2,1,0:T(8,128)(2,1)} %bitcast.46), calls=%async_computation.3 | async-start | bytes 786432 | tf_op jit(solution)/shard_map/all_to_all | solution.py:65
  (9 other events, 28.3 us)

commit v6 on v4

--- a/solution.py
+++ b/solution.py
@@ -75,7 +75,7 @@
     return lax.dot_general(a, b, dims, preferred_element_type=f32)
 
 
-def call(body, out_shape, scalars, arrays, in_specs=None, out_specs=None, grid=(), scratch=(), cost=0, aliases=None, weight=1):
+def call(body, out_shape, places, arrays, in_specs=None, out_specs=None, grid=(), scratch=(), cost=0, aliases=None, weight=1):
     whole = pl.BlockSpec(memory_space=pltpu.VMEM)
     many = isinstance(out_shape, (list, tuple))
     if in_specs is None:
@@ -97,7 +97,7 @@
         input_output_aliases=aliases or {},
         compiler_params=pltpu.CompilerParams(vmem_limit_bytes=60 * 2**20),
         cost_estimate=pl.CostEstimate(flops=weight * cost, bytes_accessed=moved, transcendentals=0),
-    )(jnp.stack(scalars).astype(jnp.int32), *arrays)
+    )(places, *arrays)
 
 
 def aligned(index, size):
@@ -156,7 +156,7 @@
     put_units(feats, turned_head, proj, turned, norm)
 
 
-def units(blocks, turned_head, ring, second, rows):
+def units(blocks, turned_head, places, rows):
     width = turned_head.shape[0]
     tile = 2 * rows
     whole = lambda a: pl.BlockSpec(a.shape, lambda i, at: (0, 0))
@@ -166,7 +166,7 @@
             jax.ShapeDtypeStruct((width + PAD, 8 * rows), b16),
             jax.ShapeDtypeStruct((1, 8 * rows), f32),
         ],
-        [ring, second],
+        places,
         [*blocks, turned_head],
         in_specs=[whole(a) for a in [*blocks, turned_head]],
         out_specs=[
@@ -185,13 +185,11 @@
     return (projected / norm).astype(b16), norm
 
 
-def unit_rows(feats, head):
-    projected = dot(feats, head, NN)
-    norm = jnp.sqrt(jnp.sum(projected * projected, axis=1, keepdims=True) + epsilon)
-    return (projected / norm).astype(b16)
-
-
-def tile_slopes(rows, groups, place, bias_ref, img, txt, slopes, by_img):
+def unit_rows(feats, head, norm):
+    return (dot(feats, head, NN) / norm.reshape(-1, 1)).astype(b16)
+
+
+def tile_slopes(rows, groups, place, bias_ref, img, txt, slopes, by_img, use):
     width = img.shape[1]
     tile = 2 * rows
     lang = txt[width : width + PAD].astype(f32)
@@ -203,11 +201,11 @@
     bias = bias * -log2e
     down = jnp.zeros((1, tile), f32)
     high = 4 * rows
-    for m in range(img.shape[0] // high):
-        span = slice(m * high, (m + 1) * high)
+    spans = [slice(m * high, (m + 1) * high) for m in range(img.shape[0] // high)]
+    cosines = dot(img[spans[0]], txt[:width], NN)
+    for m, span in enumerate(spans):
         index = m * high + lax.broadcasted_iota(jnp.int32, (high, 1), 0)
         ids = ((index // rows * 16 + place) * rows + index % rows).astype(f32)
-        cosines = dot(img[span], txt[:width], NN)
         below = 1.0 + jnp.exp2(cosines * (-log2e * logit_scale) + bias)
         gate = pl.reciprocal(below, approx=True)
         gate = gate * (2.0 - below * gate)
@@ -219,13 +217,15 @@
         for k in range(0, tile, by_img.shape[1]):
             side = side + weighted[:, k : k + by_img.shape[1]]
         by_img[span] = side
+        if m + 1 < len(spans):
+            cosines = dot(img[spans[m + 1]], txt[:width], NN)
+        use(span)
     return logit_scale * down
 
 
-def put_text_terms(up, turned, slopes, down):
-    slab = turned.shape[0] // 8
+def put_text_terms(up, part, down):
+    slab = part.shape[0] // 8
     figures = split_rows(down, up.shape[1])
-    part = dot(turned[...], slopes, NN)
     for e in range(8):
         at = e * (slab + PAD)
         up[at : at + slab] = part[e * slab : (e + 1) * slab].astype(b16)
@@ -239,15 +239,20 @@
     def _():
         by_img[...] = jnp.zeros(by_img.shape, f32)
 
-    down = tile_slopes(rows, groups, at_ref[0], bias_ref, img, txt, slopes.at[0], by_img)
-    put_text_terms(up, turned, slopes[0], down)
+    parts = []
+
+    def use(span):
+        parts.append(dot(turned[:, span], slopes[0, span], NN))
+
+    down = tile_slopes(rows, groups, at_ref[5], bias_ref, img, txt, slopes.at[0], by_img, use)
+    put_text_terms(up, sum(parts[1:], parts[0]), down)
 
     @pl.when(step == 3)
     def _():
         img_sum[...] = logit_scale * jnp.sum(by_img[...].T, axis=0, keepdims=True)
 
 
-def other_tile(img, turned, txt, group_bias, place, rows):
+def other_tile(img, turned, txt, group_bias, places, rows):
     count, width = img.shape
     tile = 2 * rows
     height = width + 8 * PAD
@@ -259,7 +264,7 @@
             jax.ShapeDtypeStruct((1, count), f32),
             jax.ShapeDtypeStruct((height, count), b16),
         ],
-        [place],
+        places,
         [group_bias, img, turned, txt],
         in_specs=[
             pl.BlockSpec(memory_space=pltpu.SMEM),
@@ -292,9 +297,14 @@
     both[:, tile:] = other[:width]
     held[:, tile:] = other_slopes[0]
     both[:, :tile] = txt[:width]
-    down = tile_slopes(rows, groups, at_ref[0], bias_ref, img, txt, held, by_img)
-    put_text_terms(up, turned, held[:, :tile], down)
-    total[...] += dot(both[...], held[...], NT)
+    parts = []
+
+    def use(span):
+        parts.append(dot(turned[:, span], held[span, :tile], NN))
+        total[:, span] += dot(both[...], held[span], NT)
+
+    down = tile_slopes(rows, groups, at_ref[5], bias_ref, img, txt, held, by_img, use)
+    put_text_terms(up, sum(parts[1:], parts[0]), down)
 
     @pl.when(step == 3)
     def _():
@@ -307,7 +317,7 @@
 
 
 def own_tile(
-    img, turned, txt, other, other_slopes, other_sum, group_bias, place, rows
+    img, turned, txt, other, other_slopes, other_sum, group_bias, places, rows
 ):
     count, width = img.shape
     tile = 2 * rows
@@ -319,7 +329,7 @@
     return call(
         lambda *refs: own_kernel(rows, group_bias.shape[0], *refs),
         [jax.ShapeDtypeStruct((height, count), b16), pieces],
-        [place],
+        places,
         [group_bias, img, turned, txt, other, other_slopes, other_sum],
         in_specs=[
             pl.BlockSpec(memory_space=pltpu.SMEM),
@@ -358,32 +368,27 @@
         start += size
 
 
-def sums(groups, rows):
-    flat_terms = [term for group in groups for term in group]
-    arrays, specs, places = [], [], [jnp.int32(0)]
-    height = None
-    for term in flat_terms:
+def sums(groups, places, rows):
+    arrays, specs = [], []
+    lanes = 4 * rows
+    for term in [term for group in groups for term in group]:
         if isinstance(term, tuple):
             arrays.append(term[0])
             height = term[0].shape[0] // 8
-            specs.append(
-                pl.BlockSpec((height, 4 * rows), lambda i, at, n=len(places): (at[n], i))
-            )
-            places.append(term[1])
+            specs.append(pl.BlockSpec((height, lanes), lambda i, at, n=term[1]: (at[n], i)))
         else:
             arrays.append(term)
             height = term.shape[0]
-            specs.append(pl.BlockSpec((height, 4 * rows), lambda i, at: (0, i)))
+            specs.append(pl.BlockSpec((height, lanes), lambda i, at: (0, i)))
     count = arrays[0].shape[1]
-    spec = pl.BlockSpec((height, 4 * rows), lambda i, at: (0, i))
     return call(
         lambda *refs: sum_kernel([len(group) for group in groups], *refs),
         [jax.ShapeDtypeStruct((height, count), b16)] * len(groups),
         places,
         arrays,
         in_specs=specs,
-        out_specs=[spec] * len(groups),
-        grid=(count // (4 * rows),),
+        out_specs=[pl.BlockSpec((height, lanes), lambda i, at: (0, i))] * len(groups),
+        grid=(count // lanes,),
     )
 
 
@@ -416,23 +421,23 @@
         give[ring] = jnp.where(at_ref[1] == 0, high, low)
     total = None
     for d in range(4):
-        cols = grad[:, aligned((at_ref[2] + d) % 4, 2 * rows)]
+        cols = grad[:, aligned((at_ref[0] + d) % 4, 2 * rows)]
         term = dot(cols, in_pair(blocks[2 * d], blocks[2 * d + 1], at_ref[1], rows), NN)
         total = term if total is None else total + term
     part[...] = total.astype(b16)
 
 
-def gradient(kernel, place, second, ring, terms, unit, norm, feats, halves, rows):
+def gradient(kernel, own, terms, unit, norm, feats, halves, places, rows):
     width = feats[0].shape[1]
     slab, count = width // 8, 8 * rows
     whole = lambda a: pl.BlockSpec(a.shape, lambda i, at: (0,) * len(a.shape))
-    mine = lambda height: pl.BlockSpec((height, count), lambda i, at: (at[0], 0))
+    mine = lambda height: pl.BlockSpec((height, count), lambda i, at: (at[own], 0))
     block = jax.ShapeDtypeStruct((8 // halves, slab, rows), b16)
     part = jax.ShapeDtypeStruct((slab, width), b16)
     return call(
         lambda *refs: kernel(rows, *refs),
         [block] * halves + [part],
-        [place, second, ring],
+        places,
         [term[0] if isinstance(term, tuple) else term for term in terms] + [unit, norm, *feats],
         in_specs=[mine(slab + PAD) if isinstance(term, tuple) else whole(term) for term in terms]
         + [mine(slab), whole(norm)]
@@ -455,7 +460,7 @@
     part = jnp.concatenate([img, txt], axis=0).astype(b16)
     slot = lax.broadcasted_iota(jnp.int32, (slots, 1), 0)
     feature = lax.broadcasted_iota(jnp.int32, (slots, width), 1)
-    base = (slot // 8 * 2 + at_ref[0]) * own
+    base = (slot // 8 * 2 + at_ref[4]) * own
     chosen = jnp.where(feature == base + slot % 8, 1.0, 0.0).astype(b16)
     out[:, : 3 * third] = dot(chosen, part, NT).astype(b16)
     chosen = jnp.where(feature == base + 8, 1.0, 0.0).astype(b16)
@@ -466,12 +471,12 @@
     out[:, 3 * third :] = rest.astype(b16)
 
 
-def picked(core, parts):
+def picked(parts, places):
     slab, width = parts[0].shape
     return call(
         pick_kernel,
         jax.ShapeDtypeStruct((64 * 8, slab * 8 // 3), b16),
-        [core],
+        places,
         parts,
         cost=8 * 512 * width * slab,
         weight=0,
@@ -525,6 +530,9 @@
     place = lax.axis_index(DEV)
     z, lo, hi, y, core = place // 32, place // 16 % 2, place // 8 % 2, place // 2 % 4, place % 2
 
+    slots = [(y + d) % 4 * 2 + (hi + e) % 2 for d in range(4) for e in range(2)]
+    places = [y, hi, z, lo, core, place % 16, z * 2 + lo, y * 2 + hi, *slots]
+    (places,) = together([jnp.stack(places).astype(jnp.int32)])
     figures = jnp.stack([text_lang, partner // 128, partner % 128]).astype(b16)
     figures = jnp.pad(figures, ((0, PAD - 3), (0, width - rows)))
     text_rows = jnp.concatenate([text_feat, figures], axis=0)
@@ -533,44 +541,42 @@
     across = send(text_rows, txt_move(0, 1))
     before = send(text_rows, txt_move(1, 0))
     after = send(text_rows, txt_move(3, 0))
+    across, turned_txt = together([across, text_head.T])
     across_after = send(across, txt_move(3, 0))
     across_before = send(across, txt_move(1, 0))
-    across_after, before, after, across, turned_txt = together(
-        [across_after, before, after, across, text_head.T]
-    )
+    across_after, before, after, across = together([across_after, before, after, across])
     far = send(before, txt_move(1, 0))
     across_far = send(across_after, txt_move(3, 0))
     txt_blocks = [
         text_rows, across, after, across_after, far, across_far, before, across_before
     ]
-    unit_txt, norm_txt = units(txt_blocks, turned_txt, y, hi, rows)
+    unit_txt, norm_txt = units(txt_blocks, turned_txt, places, rows)
     other_txt = send(unit_txt, core_move)
     turned_units, norm_img = unit_columns(img_feats, image_head)
-    unit_img = unit_rows(together([img_feats, unit_txt])[0], image_head)
+    unit_img = unit_rows(together([img_feats, unit_txt])[0], image_head, norm_img)
 
     other_slopes, other_sum, other_up = other_tile(
-        unit_img, turned_units, other_txt, group_bias, place % 16, rows
+        unit_img, turned_units, other_txt, group_bias, places, rows
     )
     back = send(other_up, core_move)
     text_up, img_terms = own_tile(
         unit_img, turned_units, unit_txt, other_txt, other_slopes, other_sum, group_bias,
-        place % 16, rows,
+        places, rows,
     )
     img_terms = exchange(img_terms, IMG_GROUPS)
 
     def slab_terms(d, e):
-        at = (y + d) % 4 * 2 + (hi + e) % 2
-        return [(text_up, at), (back, at)]
+        return [(text_up, 8 + 2 * d + e), (back, 8 + 2 * d + e)]
 
     far, across_far, across_after = sums(
-        [slab_terms(2, 0), slab_terms(2, 1), slab_terms(1, 1)], rows
+        [slab_terms(2, 0), slab_terms(2, 1), slab_terms(1, 1)], places, rows
     )
     far = send(far, txt_move(1, 0))
     across_far = send(across_far, txt_move(3, 0))
     far, across_far, across_after = together([far, across_far, across_after])
     across_before = send(across_after, txt_move(1, 0))
     across_after, before, after = sums(
-        [slab_terms(3, 1) + [across_far], slab_terms(1, 0) + [far], slab_terms(3, 0)], rows
+        [slab_terms(3, 1) + [across_far], slab_terms(1, 0) + [far], slab_terms(3, 0)], places, rows
     )
     across_after = send(across_after, txt_move(3, 0))
     across_before, across_after, before, after = together(
@@ -578,24 +584,24 @@
     )
     before = send(before, txt_move(1, 0))
     after = send(after, txt_move(3, 0))
-    (across,) = sums([slab_terms(0, 1) + [across_before, across_after]], rows)
+    (across,) = sums([slab_terms(0, 1) + [across_before, across_after]], places, rows)
     across = send(across, txt_move(0, 1))
 
     img_blocks, img_part = gradient(
-        img_grad_kernel, z * 2 + lo, lo, z, [img_terms], turned_units, norm_img, [img_feats], 1, rows
+        img_grad_kernel, 6, [img_terms], turned_units, norm_img, [img_feats], 1, places, rows
     )
     grad_img = exchange(img_blocks, IMG_GROUPS).reshape(width, rows)
     txt_own, txt_give, txt_part = gradient(
-        txt_grad_kernel, y * 2 + hi, hi, y, slab_terms(0, 0) + [before, after, across],
-        unit_txt, norm_txt, txt_blocks, 2, rows,
+        txt_grad_kernel, 7, slab_terms(0, 0) + [before, after, across], unit_txt, norm_txt,
+        txt_blocks, 2, places, rows,
     )
     img_theirs = send(img_part, core_move)
     txt_theirs = send(txt_part, core_move)
     txt_got = send(txt_give, txt_move(0, 1))
-    heads, txt_got = together([picked(core, [img_part, txt_part, img_theirs, txt_theirs]), txt_got])
+    heads, txt_got = together([picked([img_part, txt_part, img_theirs, txt_theirs], places), txt_got])
     heads = exchange(heads.reshape(64, 8, -1), CHIP_GROUPS)
     head_shape = jax.ShapeDtypeStruct((width // 128, width), f32)
-    image_head_grad, text_head_grad = call(head_kernel, [head_shape] * 2, [core], [heads])
+    image_head_grad, text_head_grad = call(head_kernel, [head_shape] * 2, places, [heads])
 
     image_grad = dot(grad_img, image_head, (((0,), (1,)), ((), ())))
     grad_txt = whole_columns(pair_lines(txt_own, txt_got, hi), txt_move, y)

time: 196 us -> 189 us (0.964)
  other arithmetic: 8.17 us -> 3.29 us
  Pallas kernels: 64.3 us -> 67.1 us
  local copies, waits for them, and re-layouts: 14.3 us -> 11.9 us
    all_to_all x4, waiting for transfers between devices: 4.37 us -> 0.01 us  [exchange(): lax.all_to_all(blocks, DEV, 0, 0, axis_index_groups=groups, tiled=True)]
    ppermute x22, waiting for transfers between devices: 28.9 us -> 31.8 us  [send(): lax.ppermute(block, DEV, [(flat(*p), flat(*move(*p))) for p in PLACES])]
    ppermute x22, starting transfers between devices: 32.8 us -> 35.6 us  [send(): lax.ppermute(block, DEV, [(flat(*p), flat(*move(*p))) for p in PLACES])]
    pallas_call x10, Pallas kernels: 64.3 us -> 67.1 us  [call(): pl.pallas_call(body, out_shape=out_shape, grid_spec=spec, input_output_al...]
    another operation x4 -> x0, other arithmetic: 2.36 us -> none  [call(): jnp.stack(scalars).astype(jnp.int32)]
    convert_element_type x1 -> x0, other arithmetic: 1.96 us -> none  [unit_rows(): return (projected / norm).astype(b16)]
    unnamed x36 -> x38, local copies, waits for them, and re-layouts: 9.29 us -> 8.34 us
  transfers between devices with their start and end apart: 26 -> 26, of which waited for: 8 -> 9; matrix products, arithmetic and copies ran while one was open for 16% -> 13% of each run, Pallas kernels for 26% -> 28%
where the time goes in v6:
time: 189 us; the launch traced here: 188 us
  Pallas kernels  67.1 us (36%)
  starting transfers between devices  57.9 us (31%)
  waiting for transfers between devices  31.8 us (17%)
  matrix products  15 us (8%)
  local copies, waits for them, and re-layouts  11.9 us (6%)
  other arithmetic  3.29 us (2%)
    pallas_call x10, Pallas kernels, call(): pl.pallas_call(body, out_shape=out_shape, grid_spec=spec, input_output_al...  67.1 us
    ppermute x22, starting transfers between devices, send(): lax.ppermute(block, DEV, [(flat(*p), flat(*move(*p))) for p in PLACES])  35.6 us
    ppermute x22, waiting for transfers between devices, send(): lax.ppermute(block, DEV, [(flat(*p), flat(*move(*p))) for p in PLACES])  31.8 us
    all_to_all x4, starting transfers between devices, exchange(): lax.all_to_all(blocks, DEV, 0, 0, axis_index_groups=groups, tiled=True)  22.3 us
    dot_general x4, matrix products, dot(): return lax.dot_general(a, b, dims, preferred_element_type=f32)  15 us
    unnamed x38, local copies, waits for them, and re-layouts  8.34 us
  transfers between devices with their start and end apart: 26, of which 9 were waited for; matrix products, arithmetic and copies ran while one was open for 13% of the time, Pallas kernels for 28%

profile of v6, /device:TPU:1, one launch (start us, length us, event | category | flops | bytes accessed | tf_op | source)
XLA Modules:
  0.0 187.9 jit_solution(17120376511826712377)
XLA Ops:
  0.6 2.8 %broadcast_in_dim.2 = bf16[8,128,1152]{2,1,0:T(8,128)(2,1)} broadcast(bf16[128,1152]{1,0:T(8,128)(2,1)} %param.7), dimensions={1,2} | broadcast | bytes 2654208 | tf_op jit(solution)/shard_map/broadcast_in_dim | solution.py:539
  3.5 6.9 %all-to-all-start = ((bf16[8,128,1152]{2,1,0:T(8,128)(2,1)}), bf16[8,128,1152]{2,1,0:T(8,128)(2,1)}, u32[]{:S(2)}, u32[]{:S(2)}) async-start(bf16[8,128,1152]{2,1,0:T(8,128)(2,1)} %broadcast_in_dim.2), calls=%async_computation | async-start | bytes 4718592 | tf_op jit(solution)/shard_map/all_to_all | solution.py:65
  10.5 2.8 %collective-permute-start = (bf16[144,1152]{1,0:T(8,128)(2,1)S(1)}, bf16[144,1152]{1,0:T(8,128)(2,1)S(1)}, u32[]{:S(2)}, u32[]{:S(2)}) collective-permute-start(bf16[144,1152]{1,0:T(8,128)(2,1)S(1)} %pad_maximum_fusion.refs_1_.refs_8_), channel_id=1, source_target_pairs={{0,24},{1,25},{2,26},{3,27},{4,28},{5,29},{6,30},{7,31},{8,16},{9,... | collective-permute-start | bytes 995336 | tf_op jit(solution)/shard_map/ppermute | solution.py:61
  13.3 2.7 %collective-permute-start.3 = (bf16[144,1152]{1,0:T(8,128)(2,1)S(1)}, bf16[144,1152]{1,0:T(8,128)(2,1)}, u32[]{:S(2)}, u32[]{:S(2)}) collective-permute-start(bf16[144,1152]{1,0:T(8,128)(2,1)S(1)} %pad_maximum_fusion.refs_1_.refs_8_), channel_id=1, source_target_pairs={{0,6},{1,7},{2,0},{3,1},{4,2},{5,3},{6,4},{7,5},{8,14},{9,15},{10,... | collective-permute-start | bytes 995336 | tf_op jit(solution)/shard_map/ppermute | solution.py:61
  16.1 5.2 %copy.11 = bf16[1152,1152]{0,1:T(8,128)(2,1)} copy(bf16[1152,1152]{1,0:T(8,128)(2,1)} %param.10) | data formatting | bytes 5308416 | tf_op args[3]
  21.3 2.7 %collective-permute-start.1 = (bf16[144,1152]{1,0:T(8,128)(2,1)S(1)}, bf16[144,1152]{1,0:T(8,128)(2,1)}, u32[]{:S(2)}, u32[]{:S(2)}) collective-permute-start(bf16[144,1152]{1,0:T(8,128)(2,1)S(1)} %collective-permute-done.refs_2_.refs_9_), channel_id=1, source_target_pairs={{0,6},{1,7},{2,0},{3,1},{4,2},{5,3},{6,4},{7,5},{8,14},{9,15},{10,... | collective-permute-start | bytes 995336 | tf_op jit(solution)/shard_map/ppermute | solution.py:61
  24.9 4.2 %collective-permute-done.1.refs_4_.refs_11_ = bf16[144,1152]{1,0:T(8,128)(2,1)} collective-permute-done((bf16[144,1152]{1,0:T(8,128)(2,1)S(1)}, bf16[144,1152]{1,0:T(8,128)(2,1)}, u32[]{:S(2)}, u32[]{:S(2)}) %collective-permute-start.1) | collective-permute-done | bytes 331808 | tf_op jit(solution)/shard_map/ppermute | solution.py:61
  29.0 3.5 %collective-permute-start.5 = (bf16[144,1152]{1,0:T(8,128)(2,1)}, bf16[144,1152]{1,0:T(8,128)(2,1)S(1)}, u32[]{:S(2)}, u32[]{:S(2)}) collective-permute-start(bf16[144,1152]{1,0:T(8,128)(2,1)} %collective-permute-done.1.refs_4_.refs_11_), channel_id=1, source_target_pairs={{0,6},{1,7},{2,0},{3,1},{4,2},{5,3},{6,4},{7,5},{8,14},{9,15},{10,... | collective-permute-start | bytes 995336 | tf_op jit(solution)/shard_map/ppermute | solution.py:61
  33.3 3.7 %collective-permute-done.5.refs_6_.refs_13_ = bf16[144,1152]{1,0:T(8,128)(2,1)S(1)} collective-permute-done((bf16[144,1152]{1,0:T(8,128)(2,1)}, bf16[144,1152]{1,0:T(8,128)(2,1)S(1)}, u32[]{:S(2)}, u32[]{:S(2)}) %collective-permute-start.5) | collective-permute-done | bytes 331808 | tf_op jit(solution)/shard_map/ppermute | solution.py:61
  36.9 3.4 %collective-permute-done.4.refs_5_.refs_12_ = bf16[144,1152]{1,0:T(8,128)(2,1)} collective-permute-done((bf16[144,1152]{1,0:T(8,128)(2,1)}, bf16[144,1152]{1,0:T(8,128)(2,1)}, u32[]{:S(2)}, u32[]{:S(2)}) %collective-permute-start.4) | collective-permute-done | bytes 331808 | tf_op jit(solution)/shard_map/ppermute | solution.py:61
  40.4 9.1 %shard_map.102 = (bf16[1168,1024]{1,0:T(8,128)(2,1)}, f32[1,1024]{1,0:T(1,128)}) custom-call(s32[16]{0:T(128)} %stack.83.refs_0_.at_ref, bf16[144,1152]{1,0:T(8,128)(2,1)} %copy-done.3, bf16[144,1152]{1,0:T(8,128)(2,1)} %copy-done.4, bf16[144,1152]{1,0:T(8,128)(2,1)} %collective-permute-done.3.refs_3_.refs_10_, ...), custom_call_target="tpu_custom_call" | custom-call | flops 2717908992 | bytes 5308416 | tf_op jit(solution)/shard_map/pallas_call | solution.py:93
  49.5 4.1 %collective-permute-start.7 = (bf16[1168,1024]{1,0:T(8,128)(2,1)}, bf16[1168,1024]{1,0:T(8,128)(2,1)}, u32[]{:S(2)}, u32[]{:S(2)}) collective-permute-start(bf16[1168,1024]{1,0:T(8,128)(2,1)} %get-tuple-element.46.refs_4_.refs_6_), channel_id=1, source_target_pairs={{0,1},{1,0},{2,3},{3,2},{4,5},{5,4},{6,7},{7,6},{8,9},{9,8},{10,11... | collective-permute-start | bytes 7176200 | tf_op jit(solution)/shard_map/ppermute | solution.py:61
  53.6 5.0 %multiply_reduce_fusion = (f32[1024]{0:T(1024)S(1)}, f32[1152,1024]{1,0:T(8,128)S(1)}) fusion(bf16[1152,1152]{1,0:T(8,128)(2,1)S(1)} %copy-done, bf16[1024,1152]{1,0:T(8,128)(2,1)} %bitcast.16.refs_4_), kind=kOutput, calls=%fused_computation.2 | convolution fusion | flops 2720267264 | bytes 9736192 | tf_op jit(solution)/shard_map/dot_general | solution.py:75
  58.6 6.6 %divide_convert_fusion.1.refs_2_ = bf16[1024,1152]{1,0:T(8,128)(2,1)} fusion(bf16[1024,1152]{1,0:T(8,128)(2,1)} %bitcast.16.refs_4_, bf16[1152,1152]{1,0:T(8,128)(2,1)S(1)} %copy-done, f32[1024]{0:T(1024)S(1)} %add_sqrt_fusion), kind=kOutput, calls=%fused_computation.1 | convolution fusion | flops 2720268288 | bytes 7376896 | tf_op jit(solution)/shard_map/dot_general | solution.py:75
  67.3 12.8 %shard_map.103 = (bf16[4,1024,256]{2,1,0:T(8,128)(2,1)}, f32[1,1024]{1,0:T(1,128)}, bf16[1280,1024]{1,0:T(8,128)(2,1)}) custom-call(s32[16]{0:T(128)} %stack.83.refs_0_.at_ref, f32[32]{0:T(128)} %refs_1_.3, bf16[1024,1152]{1,0:T(8,128)(2,1)} %divide_convert_fusion.1.refs_2_, bf16[1152,1024]{1,0:T(8,128)(2,1)} %divide_convert_fusion.refs_3_.refs_2_, ...), custom_call_target="tpu_custom_call" | custom-call | flops 4831838208 | bytes 7110784 | tf_op jit(solution)/shard_map/pallas_call | solution.py:93
  80.1 19.3 %shard_map.104 = (bf16[1280,1024]{1,0:T(8,128)(2,1)}, bf16[8,160,1024]{2,1,0:T(8,128)(2,1)}) custom-call(s32[16]{0:T(128)} %stack.83.refs_0_.at_ref, f32[32]{0:T(128)} %refs_1_.3, bf16[1024,1152]{1,0:T(8,128)(2,1)} %divide_convert_fusion.1.refs_2_, bf16[1152,1024]{1,0:T(8,128)(2,1)} %divide_convert_fusion.refs_3_.refs_2_, ...), custom_call_target="tpu_custom_call" | custom-call | flops 9663676416 | bytes 11604096 | tf_op jit(solution)/shard_map/pallas_call | solution.py:93
  99.4 4.6 %all-to-all-start.1 = ((bf16[8,160,1024]{2,1,0:T(8,128)(2,1)}), bf16[8,160,1024]{2,1,0:T(8,128)(2,1)}, u32[]{:S(2)}, u32[]{:S(2)}) async-start(bf16[8,160,1024]{2,1,0:T(8,128)(2,1)} %get-tuple-element.50), calls=%async_computation.1 | async-start | bytes 5242880 | tf_op jit(solution)/shard_map/all_to_all | solution.py:65
  104.0 3.1 %shard_map.106 = (bf16[160,1024]{1,0:T(8,128)(2,1)}, bf16[160,1024]{1,0:T(8,128)(2,1)}, bf16[160,1024]{1,0:T(8,128)(2,1)}) custom-call(s32[16]{0:T(128)} %stack.83.refs_0_.at_ref, bf16[1280,1024]{1,0:T(8,128)(2,1)} %get-tuple-element.53.refs_1_.refs_3_.refs_5_.refs_4_.refs_7_, ...), custom_call_target="tpu_custom_call" | custom-call | bytes 15728640 | tf_op jit(solution)/shard_map/pallas_call | solution.py:93
  109.9 7.6 %collective-permute-done.9.refs_6_ = bf16[160,1024]{1,0:T(8,128)(2,1)S(1)} collective-permute-done((bf16[160,1024]{1,0:T(8,128)(2,1)}, bf16[160,1024]{1,0:T(8,128)(2,1)S(1)}, u32[]{:S(2)}, u32[]{:S(2)}) %collective-permute-start.9) | collective-permute-done | bytes 327712 | tf_op jit(solution)/shard_map/ppermute | solution.py:61
  118.4 3.4 %shard_map.107 = (bf16[160,1024]{1,0:T(8,128)(2,1)}, bf16[160,1024]{1,0:T(8,128)(2,1)}, bf16[160,1024]{1,0:T(8,128)(2,1)}) custom-call(s32[16]{0:T(128)} %stack.83.refs_0_.at_ref, bf16[1280,1024]{1,0:T(8,128)(2,1)} %get-tuple-element.53.refs_1_.refs_3_.refs_5_.refs_4_.refs_7_, ...), custom_call_target="tpu_custom_call" | custom-call | bytes 16384000 | tf_op jit(solution)/shard_map/pallas_call | solution.py:93
  124.1 3.0 %collective-permute-done.11.refs_3_ = bf16[160,1024]{1,0:T(8,128)(2,1)S(1)} collective-permute-done((bf16[160,1024]{1,0:T(8,128)(2,1)}, bf16[160,1024]{1,0:T(8,128)(2,1)S(1)}, u32[]{:S(2)}, u32[]{:S(2)}) %collective-permute-start.11) | collective-permute-done | bytes 327712 | tf_op jit(solution)/shard_map/ppermute | solution.py:61
  127.1 2.9 %collective-permute-done.12.refs_4_ = bf16[160,1024]{1,0:T(8,128)(2,1)S(1)} collective-permute-done((bf16[160,1024]{1,0:T(8,128)(2,1)}, bf16[160,1024]{1,0:T(8,128)(2,1)S(1)}, u32[]{:S(2)}, u32[]{:S(2)}) %collective-permute-start.12) | collective-permute-done | bytes 327712 | tf_op jit(solution)/shard_map/ppermute | solution.py:61
  130.7 2.8 %shard_map.108 = bf16[160,1024]{1,0:T(8,128)(2,1)} custom-call(s32[16]{0:T(128)} %stack.83.refs_0_.at_ref, bf16[1280,1024]{1,0:T(8,128)(2,1)} %get-tuple-element.53.refs_1_.refs_3_.refs_5_.refs_4_.refs_7_, bf16[1280,1024]{1,0:T(8,128)(2,1)} %collective-permute-done.8.refs_2_.refs_4_.refs_6_.refs_5_.refs_8_, bf16[160,1024]{1,0:T(8,128)(2,1)} %copy-done.7, ...), custom_call_target="tpu_custom_call" | custom-call | bytes 5898240 | tf_op jit(solution)/shard_map/pallas_call | solution.py:93
  137.5 4.8 %shard_map.105 = (bf16[8,144,128]{2,1,0:T(8,128)(2,1)}, bf16[144,1152]{1,0:T(8,128)(2,1)}) custom-call(s32[16]{0:T(128)} %stack.83.refs_0_.at_ref, bf16[8,160,1024]{2,1,0:T(8,128)(2,1)} %all-to-all-done.1.refs_1_, bf16[1152,1024]{1,0:T(8,128)(2,1)} %divide_convert_fusion.refs_3_.refs_2_, f32[1,1024]{1,0:T(1,128)} %bitcast.49, bf16[1024,1152]{1,0:T(8,128)(2,1)} %bitcast.16.refs_4_), custom_call_target="tpu_custom_call" | custom-call | tf_op jit(solution)/shard_map/pallas_call | solution.py:93
  142.3 3.7 %all-to-all-start.2 = ((bf16[8,144,128]{2,1,0:T(8,128)(2,1)}), bf16[8,144,128]{2,1,0:T(8,128)(2,1)S(1)}, u32[]{:S(2)}, u32[]{:S(2)}) async-start(bf16[8,144,128]{2,1,0:T(8,128)(2,1)} %get-tuple-element.51), calls=%async_computation.2 | async-start | bytes 589824 | tf_op jit(solution)/shard_map/all_to_all | solution.py:65
  146.0 4.0 %collective-permute-start.16 = (bf16[144,1152]{1,0:T(8,128)(2,1)}, bf16[144,1152]{1,0:T(8,128)(2,1)S(1)}, u32[]{:S(2)}, u32[]{:S(2)}) collective-permute-start(bf16[144,1152]{1,0:T(8,128)(2,1)} %get-tuple-element.52.img), channel_id=1, source_target_pairs={{0,1},{1,0},{2,3},{3,2},{4,5},{5,4},{6,7},{7,6},{8,9},{9,8},{10,11... | collective-permute-start | bytes 995336 | tf_op jit(solution)/shard_map/ppermute | solution.py:61
  150.0 4.8 %shard_map.109 = (bf16[4,144,128]{2,1,0:T(8,128)(2,1)}, bf16[4,144,128]{2,1,0:T(8,128)(2,1)}, bf16[144,1152]{1,0:T(8,128)(2,1)}) custom-call(s32[16]{0:T(128)} %stack.83.refs_0_.at_ref, bf16[1280,1024]{1,0:T(8,128)(2,1)} %get-tuple-element.53.refs_1_.refs_3_.refs_5_.refs_4_.refs_7_, ...), custom_call_target="tpu_custom_call" | custom-call | tf_op jit(solution)/shard_map/pallas_call | solution.py:93
  154.8 2.7 %collective-permute-start.18 = (bf16[4,144,128]{2,1,0:T(8,128)(2,1)}, bf16[4,144,128]{2,1,0:T(8,128)(2,1)}, u32[]{:S(2)}, u32[]{:S(2)}) collective-permute-start(bf16[4,144,128]{2,1,0:T(8,128)(2,1)} %get-tuple-element.70), channel_id=1, source_target_pairs={{0,24},{1,25},{2,26},{3,27},{4,28},{5,29},{6,30},{7,31},{8,16},{9,... | collective-permute-start | bytes 442376 | tf_op jit(solution)/shard_map/ppermute | solution.py:61
  160.0 4.4 %shard_map.110 = bf16[512,384]{1,0:T(8,128)(2,1)} custom-call(s32[16]{0:T(128)} %stack.83.refs_0_.at_ref, bf16[144,1152]{1,0:T(8,128)(2,1)} %get-tuple-element.52.img, bf16[144,1152]{1,0:T(8,128)(2,1)} %get-tuple-element.69.txt, bf16[144,1152]{1,0:T(8,128)(2,1)} %copy-done.6, bf16[144,1152]{1,0:T(8,128)(2,1)} %collective-permute-done.17.other_txt), custom_call_target="tpu_custom_call" | custom-call | tf_op jit(solution)/shard_map/pallas_call | solution.py:93
  164.4 7.1 %all-to-all-start.3 = ((bf16[64,8,384]{2,1,0:T(8,128)(2,1)}), bf16[64,8,384]{2,1,0:T(8,128)(2,1)S(1)}, u32[]{:S(2)}, u32[]{:S(2)}) async-start(bf16[64,8,384]{2,1,0:T(8,128)(2,1)} %bitcast.47), calls=%async_computation.3 | async-start | bytes 786432 | tf_op jit(solution)/shard_map/all_to_all | solution.py:65
  176.7 2.8 %collective-permute-done.19 = bf16[288,128]{1,0:T(8,128)(2,1)S(1)} collective-permute-done((bf16[288,128]{1,0:T(8,128)(2,1)S(1)}, bf16[288,128]{1,0:T(8,128)(2,1)S(1)}, u32[]{:S(2)}, u32[]{:S(2)}) %collective-permute-start.19) | collective-permute-done | bytes 73760 | tf_op jit(solution)/shard_map/ppermute | solution.py:61
  179.4 3.3 %collective-permute-done.20 = bf16[288,128]{1,0:T(8,128)(2,1)S(1)} collective-permute-done((bf16[288,128]{1,0:T(8,128)(2,1)S(1)}, bf16[288,128]{1,0:T(8,128)(2,1)S(1)}, u32[]{:S(2)}, u32[]{:S(2)}) %collective-permute-start.20) | collective-permute-done | bytes 73760 | tf_op jit(solution)/shard_map/ppermute | solution.py:61
  (84 shorter events, 27.0 us)
Async XLA Ops:
  0.6 53.0 %copy-start = (bf16[1152,1152]{1,0:T(8,128)(2,1)S(1)}, bf16[1152,1152]{1,0:T(8,128)(2,1)}, u32[]{:S(2)}) copy-start(bf16[1152,1152]{1,0:T(8,128)(2,1)} %param.9) | copy-start | bytes 7962628
  3.5 7.0 %copy-start.11 = (bf16[128,1152]{1,0:T(8,128)(2,1)S(1)}, bf16[128,1152]{1,0:T(8,128)(2,1)}, u32[]{:S(2)}) copy-start(bf16[128,1152]{1,0:T(8,128)(2,1)} %param.8) | copy-start | bytes 884740
  3.5 50.2 %all-to-all-start = ((bf16[8,128,1152]{2,1,0:T(8,128)(2,1)}), bf16[8,128,1152]{2,1,0:T(8,128)(2,1)}, u32[]{:S(2)}, u32[]{:S(2)}) async-start(bf16[8,128,1152]{2,1,0:T(8,128)(2,1)} %broadcast_in_dim.2), calls=%async_computation | async-start | bytes 4718592 | tf_op jit(solution)/shard_map/all_to_all | solution.py:65
  10.5 10.8 %copy-start.3 = (bf16[144,1152]{1,0:T(8,128)(2,1)}, bf16[144,1152]{1,0:T(8,128)(2,1)S(1)}, u32[]{:S(2)}) copy-start(bf16[144,1152]{1,0:T(8,128)(2,1)S(1)} %pad_maximum_fusion.refs_1_.refs_8_) | copy-start | bytes 995332
  10.5 10.8 %collective-permute-start = (bf16[144,1152]{1,0:T(8,128)(2,1)S(1)}, bf16[144,1152]{1,0:T(8,128)(2,1)S(1)}, u32[]{:S(2)}, u32[]{:S(2)}) collective-permute-start(bf16[144,1152]{1,0:T(8,128)(2,1)S(1)} %pad_maximum_fusion.refs_1_.refs_8_), channel_id=1, source_target_pairs={{0,24},{1,25},{2,26},{3,27},{4,28},{5,29},{6,30},{7,31},{8,16},{9,... | collective-permute-start | bytes 995336 | tf_op jit(solution)/shard_map/ppermute | solution.py:61
  13.3 10.7 %collective-permute-start.3 = (bf16[144,1152]{1,0:T(8,128)(2,1)S(1)}, bf16[144,1152]{1,0:T(8,128)(2,1)}, u32[]{:S(2)}, u32[]{:S(2)}) collective-permute-start(bf16[144,1152]{1,0:T(8,128)(2,1)S(1)} %pad_maximum_fusion.refs_1_.refs_8_), channel_id=1, source_target_pairs={{0,6},{1,7},{2,0},{3,1},{4,2},{5,3},{6,4},{7,5},{8,14},{9,15},{10,... | collective-permute-start | bytes 995336 | tf_op jit(solution)/shard_map/ppermute | solution.py:61
  16.0 8.8 %collective-permute-start.2 = (bf16[144,1152]{1,0:T(8,128)(2,1)S(1)}, bf16[144,1152]{1,0:T(8,128)(2,1)}, u32[]{:S(2)}, u32[]{:S(2)}) collective-permute-start(bf16[144,1152]{1,0:T(8,128)(2,1)S(1)} %pad_maximum_fusion.refs_1_.refs_8_), channel_id=1, source_target_pairs={{0,2},{1,3},{2,4},{3,5},{4,6},{5,7},{6,0},{7,1},{8,10},{9,11},{10,... | collective-permute-start | bytes 995336 | tf_op jit(solution)/shard_map/ppermute | solution.py:61
  21.3 19.1 %copy-start.4 = (bf16[144,1152]{1,0:T(8,128)(2,1)}, bf16[144,1152]{1,0:T(8,128)(2,1)S(1)}, u32[]{:S(2)}) copy-start(bf16[144,1152]{1,0:T(8,128)(2,1)S(1)} %collective-permute-done.refs_2_.refs_9_) | copy-start | bytes 995332
  21.3 7.8 %collective-permute-start.1 = (bf16[144,1152]{1,0:T(8,128)(2,1)S(1)}, bf16[144,1152]{1,0:T(8,128)(2,1)}, u32[]{:S(2)}, u32[]{:S(2)}) collective-permute-start(bf16[144,1152]{1,0:T(8,128)(2,1)S(1)} %collective-permute-done.refs_2_.refs_9_), channel_id=1, source_target_pairs={{0,6},{1,7},{2,0},{3,1},{4,2},{5,3},{6,4},{7,5},{8,14},{9,15},{10,... | collective-permute-start | bytes 995336 | tf_op jit(solution)/shard_map/ppermute | solution.py:61
  24.0 9.2 %collective-permute-start.6 = (bf16[144,1152]{1,0:T(8,128)(2,1)S(1)}, bf16[144,1152]{1,0:T(8,128)(2,1)}, u32[]{:S(2)}, u32[]{:S(2)}) collective-permute-start(bf16[144,1152]{1,0:T(8,128)(2,1)S(1)} %collective-permute-done.refs_2_.refs_9_), channel_id=1, source_target_pairs={{0,2},{1,3},{2,4},{3,5},{4,6},{5,7},{6,0},{7,1},{8,10},{9,11},{10,... | collective-permute-start | bytes 995336 | tf_op jit(solution)/shard_map/ppermute | solution.py:61
  29.0 7.9 %collective-permute-start.5 = (bf16[144,1152]{1,0:T(8,128)(2,1)}, bf16[144,1152]{1,0:T(8,128)(2,1)S(1)}, u32[]{:S(2)}, u32[]{:S(2)}) collective-permute-start(bf16[144,1152]{1,0:T(8,128)(2,1)} %collective-permute-done.1.refs_4_.refs_11_), channel_id=1, source_target_pairs={{0,6},{1,7},{2,0},{3,1},{4,2},{5,3},{6,4},{7,5},{8,14},{9,15},{10,... | collective-permute-start | bytes 995336 | tf_op jit(solution)/shard_map/ppermute | solution.py:61
  32.6 7.8 %collective-permute-start.4 = (bf16[144,1152]{1,0:T(8,128)(2,1)}, bf16[144,1152]{1,0:T(8,128)(2,1)}, u32[]{:S(2)}, u32[]{:S(2)}) collective-permute-start(bf16[144,1152]{1,0:T(8,128)(2,1)} %collective-permute-done.2.refs_7_.refs_14_), channel_id=1, source_target_pairs={{0,2},{1,3},{2,4},{3,5},{4,6},{5,7},{6,0},{7,1},{8,10},{9,11},{10,... | collective-permute-start | bytes 995336 | tf_op jit(solution)/shard_map/ppermute | solution.py:61
  49.5 17.8 %collective-permute-start.7 = (bf16[1168,1024]{1,0:T(8,128)(2,1)}, bf16[1168,1024]{1,0:T(8,128)(2,1)}, u32[]{:S(2)}, u32[]{:S(2)}) collective-permute-start(bf16[1168,1024]{1,0:T(8,128)(2,1)} %get-tuple-element.46.refs_4_.refs_6_), channel_id=1, source_target_pairs={{0,1},{1,0},{2,3},{3,2},{4,5},{5,4},{6,7},{7,6},{8,9},{9,8},{10,11... | collective-permute-start | bytes 7176200 | tf_op jit(solution)/shard_map/ppermute | solution.py:61
  80.1 23.9 %collective-permute-start.8 = (bf16[1280,1024]{1,0:T(8,128)(2,1)}, bf16[1280,1024]{1,0:T(8,128)(2,1)}, u32[]{:S(2)}, u32[]{:S(2)}) collective-permute-start(bf16[1280,1024]{1,0:T(8,128)(2,1)} %get-tuple-element.54), channel_id=1, source_target_pairs={{0,1},{1,0},{2,3},{3,2},{4,5},{5,4},{6,7},{7,6},{8,9},{9,8},{10,11... | collective-permute-start | bytes 7864328 | tf_op jit(solution)/shard_map/ppermute | solution.py:61
  99.4 38.0 %all-to-all-start.1 = ((bf16[8,160,1024]{2,1,0:T(8,128)(2,1)}), bf16[8,160,1024]{2,1,0:T(8,128)(2,1)}, u32[]{:S(2)}, u32[]{:S(2)}) async-start(bf16[8,160,1024]{2,1,0:T(8,128)(2,1)} %get-tuple-element.50), calls=%async_computation.1 | async-start | bytes 5242880 | tf_op jit(solution)/shard_map/all_to_all | solution.py:65
  107.2 10.3 %collective-permute-start.9 = (bf16[160,1024]{1,0:T(8,128)(2,1)}, bf16[160,1024]{1,0:T(8,128)(2,1)S(1)}, u32[]{:S(2)}, u32[]{:S(2)}) collective-permute-start(bf16[160,1024]{1,0:T(8,128)(2,1)} %get-tuple-element.55), channel_id=1, source_target_pairs={{0,2},{1,3},{2,4},{3,5},{4,6},{5,7},{6,0},{7,1},{8,10},{9,11},{10,... | collective-permute-start | bytes 983048 | tf_op jit(solution)/shard_map/ppermute | solution.py:61
  107.2 10.3 %collective-permute-start.10 = (bf16[160,1024]{1,0:T(8,128)(2,1)}, bf16[160,1024]{1,0:T(8,128)(2,1)S(1)}, u32[]{:S(2)}, u32[]{:S(2)}) collective-permute-start(bf16[160,1024]{1,0:T(8,128)(2,1)} %get-tuple-element.56), channel_id=1, source_target_pairs={{0,6},{1,7},{2,0},{3,1},{4,2},{5,3},{6,4},{7,5},{8,14},{9,15},{10,... | collective-permute-start | bytes 983048 | tf_op jit(solution)/shard_map/ppermute | solution.py:61
  117.5 9.6 %collective-permute-start.11 = (bf16[160,1024]{1,0:T(8,128)(2,1)}, bf16[160,1024]{1,0:T(8,128)(2,1)S(1)}, u32[]{:S(2)}, u32[]{:S(2)}) collective-permute-start(bf16[160,1024]{1,0:T(8,128)(2,1)} %get-tuple-element.58), channel_id=1, source_target_pairs={{0,2},{1,3},{2,4},{3,5},{4,6},{5,7},{6,0},{7,1},{8,10},{9,11},{10,... | collective-permute-start | bytes 983048 | tf_op jit(solution)/shard_map/ppermute | solution.py:61
  121.8 8.2 %collective-permute-start.12 = (bf16[160,1024]{1,0:T(8,128)(2,1)}, bf16[160,1024]{1,0:T(8,128)(2,1)S(1)}, u32[]{:S(2)}, u32[]{:S(2)}) collective-permute-start(bf16[160,1024]{1,0:T(8,128)(2,1)} %get-tuple-element.61), channel_id=1, source_target_pairs={{0,6},{1,7},{2,0},{3,1},{4,2},{5,3},{6,4},{7,5},{8,14},{9,15},{10,... | collective-permute-start | bytes 983048 | tf_op jit(solution)/shard_map/ppermute | solution.py:61
  133.6 16.4 %collective-permute-start.15 = (bf16[160,1024]{1,0:T(8,128)(2,1)}, bf16[160,1024]{1,0:T(8,128)(2,1)}, u32[]{:S(2)}, u32[]{:S(2)}) collective-permute-start(bf16[160,1024]{1,0:T(8,128)(2,1)} %shard_map.108), channel_id=1, source_target_pairs={{0,24},{1,25},{2,26},{3,27},{4,28},{5,29},{6,30},{7,31},{8,16},{9,... | collective-permute-start | bytes 983048 | tf_op jit(solution)/shard_map/ppermute | solution.py:61
  134.3 15.7 %collective-permute-start.13 = (bf16[160,1024]{1,0:T(8,128)(2,1)}, bf16[160,1024]{1,0:T(8,128)(2,1)}, u32[]{:S(2)}, u32[]{:S(2)}) collective-permute-start(bf16[160,1024]{1,0:T(8,128)(2,1)} %get-tuple-element.64), channel_id=1, source_target_pairs={{0,2},{1,3},{2,4},{3,5},{4,6},{5,7},{6,0},{7,1},{8,10},{9,11},{10,... | collective-permute-start | bytes 983048 | tf_op jit(solution)/shard_map/ppermute | solution.py:61
  134.9 15.1 %collective-permute-start.14 = (bf16[160,1024]{1,0:T(8,128)(2,1)}, bf16[160,1024]{1,0:T(8,128)(2,1)}, u32[]{:S(2)}, u32[]{:S(2)}) collective-permute-start(bf16[160,1024]{1,0:T(8,128)(2,1)} %get-tuple-element.65), channel_id=1, source_target_pairs={{0,6},{1,7},{2,0},{3,1},{4,2},{5,3},{6,4},{7,5},{8,14},{9,15},{10,... | collective-permute-start | bytes 983048 | tf_op jit(solution)/shard_map/ppermute | solution.py:61
  142.3 15.2 %all-to-all-start.2 = ((bf16[8,144,128]{2,1,0:T(8,128)(2,1)}), bf16[8,144,128]{2,1,0:T(8,128)(2,1)S(1)}, u32[]{:S(2)}, u32[]{:S(2)}) async-start(bf16[8,144,128]{2,1,0:T(8,128)(2,1)} %get-tuple-element.51), calls=%async_computation.2 | async-start | bytes 589824 | tf_op jit(solution)/shard_map/all_to_all | solution.py:65
  146.0 13.3 %collective-permute-start.16 = (bf16[144,1152]{1,0:T(8,128)(2,1)}, bf16[144,1152]{1,0:T(8,128)(2,1)S(1)}, u32[]{:S(2)}, u32[]{:S(2)}) collective-permute-start(bf16[144,1152]{1,0:T(8,128)(2,1)} %get-tuple-element.52.img), channel_id=1, source_target_pairs={{0,1},{1,0},{2,3},{3,2},{4,5},{5,4},{6,7},{7,6},{8,9},{9,8},{10,11... | collective-permute-start | bytes 995336 | tf_op jit(solution)/shard_map/ppermute | solution.py:61
  154.8 4.5 %collective-permute-start.17 = (bf16[144,1152]{1,0:T(8,128)(2,1)}, bf16[144,1152]{1,0:T(8,128)(2,1)}, u32[]{:S(2)}, u32[]{:S(2)}) collective-permute-start(bf16[144,1152]{1,0:T(8,128)(2,1)} %get-tuple-element.69.txt), channel_id=1, source_target_pairs={{0,1},{1,0},{2,3},{3,2},{4,5},{5,4},{6,7},{7,6},{8,9},{9,8},{10,11... | collective-permute-start | bytes 995336 | tf_op jit(solution)/shard_map/ppermute | solution.py:61
  154.8 9.5 %collective-permute-start.18 = (bf16[4,144,128]{2,1,0:T(8,128)(2,1)}, bf16[4,144,128]{2,1,0:T(8,128)(2,1)}, u32[]{:S(2)}, u32[]{:S(2)}) collective-permute-start(bf16[4,144,128]{2,1,0:T(8,128)(2,1)} %get-tuple-element.70), channel_id=1, source_target_pairs={{0,24},{1,25},{2,26},{3,27},{4,28},{5,29},{6,30},{7,31},{8,16},{9,... | collective-permute-start | bytes 442376 | tf_op jit(solution)/shard_map/ppermute | solution.py:61
  157.5 13.9 %copy-start.12 = (bf16[4,144,128]{2,1,0:T(8,128)(2,1)S(1)}, bf16[4,144,128]{2,1,0:T(8,128)(2,1)}, u32[]{:S(2)}) copy-start(bf16[4,144,128]{2,1,0:T(8,128)(2,1)} %get-tuple-element.72) | copy-start | bytes 442372
  164.4 20.3 %all-to-all-start.3 = ((bf16[64,8,384]{2,1,0:T(8,128)(2,1)}), bf16[64,8,384]{2,1,0:T(8,128)(2,1)S(1)}, u32[]{:S(2)}, u32[]{:S(2)}) async-start(bf16[64,8,384]{2,1,0:T(8,128)(2,1)} %bitcast.47), calls=%async_computation.3 | async-start | bytes 786432 | tf_op jit(solution)/shard_map/all_to_all | solution.py:65
  171.4 11.5 %copy-start.1 = (bf16[1152,1152]{1,0:T(8,128)(2,1)S(1)}, bf16[1152,1152]{1,0:T(8,128)(2,1)}, u32[]{:S(2)}) copy-start(bf16[1152,1152]{1,0:T(8,128)(2,1)} %param.10) | copy-start | bytes 7962628
  172.6 10.2 %collective-permute-start.21 = (bf16[288,128]{1,0:T(8,128)(2,1)S(1)}, bf16[288,128]{1,0:T(8,128)(2,1)S(1)}, u32[]{:S(2)}, u32[]{:S(2)}) collective-permute-start(bf16[288,128]{1,0:T(8,128)(2,1)S(1)} %get-tuple-element.76), channel_id=1, source_target_pairs={{0,2},{1,3},{2,4},{3,5},{4,6},{5,7},{6,0},{7,1},{8,10},{9,11},{10,... | collective-permute-start | bytes 221192 | tf_op jit(solution)/shard_map/ppermute | solution.py:61
  173.7 5.8 %collective-permute-start.19 = (bf16[288,128]{1,0:T(8,128)(2,1)S(1)}, bf16[288,128]{1,0:T(8,128)(2,1)S(1)}, u32[]{:S(2)}, u32[]{:S(2)}) collective-permute-start(bf16[288,128]{1,0:T(8,128)(2,1)S(1)} %get-tuple-element.77), channel_id=1, source_target_pairs={{0,6},{1,7},{2,0},{3,1},{4,2},{5,3},{6,4},{7,5},{8,14},{9,15},{10,... | collective-permute-start | bytes 221192 | tf_op jit(solution)/shard_map/ppermute | solution.py:61
  175.3 7.4 %collective-permute-start.20 = (bf16[288,128]{1,0:T(8,128)(2,1)S(1)}, bf16[288,128]{1,0:T(8,128)(2,1)S(1)}, u32[]{:S(2)}, u32[]{:S(2)}) collective-permute-start(bf16[288,128]{1,0:T(8,128)(2,1)S(1)} %get-tuple-element.78), channel_id=1, source_target_pairs={{0,4},{1,5},{2,6},{3,7},{4,0},{5,1},{6,2},{7,3},{8,12},{9,13},{10,... | collective-permute-start | bytes 221192 | tf_op jit(solution)/shard_map/ppermute | solution.py:61
  (10 other events, 30.6 us)

commit v7 on v6

--- a/solution.py
+++ b/solution.py
@@ -137,15 +137,16 @@
         turned[span] = (proj[span] * inverse).astype(b16)
 
 
-def unit_kernel(rows, at_ref, *refs):
-    blocks, (turned_head, turned, norm, feats, proj) = refs[:8], refs[8:]
+def unit_kernel(rows, pairs, at_ref, *refs):
+    blocks, turned_head = refs[: 2 * pairs], refs[2 * pairs]
+    turned, norm, feats, proj = refs[-4:]
     width = turned_head.shape[0]
     second = at_ref[1]
     step = pl.program_id(0)
-    for d in range(4):
-        own, across = blocks[2 * d], blocks[2 * d + 1]
-
-        @pl.when(step == d)
+    for p in range(pairs):
+        own, across = blocks[2 * p], blocks[2 * p + 1]
+
+        @pl.when(step == p)
         def _():
             feats[...] = in_pair(own, across, second, rows)
             first = second == 0
@@ -156,26 +157,29 @@
     put_units(feats, turned_head, proj, turned, norm)
 
 
-def units(blocks, turned_head, places, rows):
+def units(pairs, distance, turned_head, carried, places, rows):
     width = turned_head.shape[0]
     tile = 2 * rows
     whole = lambda a: pl.BlockSpec(a.shape, lambda i, at: (0, 0))
+    blocks = [block for pair in pairs for block in pair]
     return call(
-        lambda *refs: unit_kernel(rows, *refs),
+        lambda *refs: unit_kernel(rows, len(pairs), *refs),
         [
             jax.ShapeDtypeStruct((width + PAD, 8 * rows), b16),
             jax.ShapeDtypeStruct((1, 8 * rows), f32),
         ],
         places,
-        [*blocks, turned_head],
-        in_specs=[whole(a) for a in [*blocks, turned_head]],
+        [*blocks, turned_head, *carried],
+        in_specs=[whole(a) for a in [*blocks, turned_head]]
+        + [pl.BlockSpec(memory_space=pl.ANY)] * len(carried),
         out_specs=[
-            pl.BlockSpec((width + PAD, tile), lambda i, at: (0, (at[0] + i) % 4)),
-            pl.BlockSpec((1, tile), lambda i, at: (0, (at[0] + i) % 4)),
+            pl.BlockSpec((width + PAD, tile), lambda i, at: (0, (at[0] + distance + i) % 4)),
+            pl.BlockSpec((1, tile), lambda i, at: (0, (at[0] + distance + i) % 4)),
         ],
-        grid=(4,),
+        grid=(len(pairs),),
         scratch=[pltpu.VMEM((tile, width), b16), pltpu.VMEM((width, tile), f32)],
-        cost=2 * 8 * rows * width * width,
+        cost=2 * tile * width * width * len(pairs),
+        aliases={len(blocks) + 2 + n: n for n in range(len(carried))},
     )
 
 
@@ -189,7 +193,7 @@
     return (dot(feats, head, NN) / norm.reshape(-1, 1)).astype(b16)
 
 
-def tile_slopes(rows, groups, place, bias_ref, img, txt, slopes, by_img, use):
+def tile_slopes(rows, groups, place, bias_ref, img, txt, slopes, by_img):
     width = img.shape[1]
     tile = 2 * rows
     lang = txt[width : width + PAD].astype(f32)
@@ -201,11 +205,11 @@
     bias = bias * -log2e
     down = jnp.zeros((1, tile), f32)
     high = 4 * rows
-    spans = [slice(m * high, (m + 1) * high) for m in range(img.shape[0] // high)]
-    cosines = dot(img[spans[0]], txt[:width], NN)
-    for m, span in enumerate(spans):
+    for m in range(img.shape[0] // high):
+        span = slice(m * high, (m + 1) * high)
         index = m * high + lax.broadcasted_iota(jnp.int32, (high, 1), 0)
         ids = ((index // rows * 16 + place) * rows + index % rows).astype(f32)
+        cosines = dot(img[span], txt[:width], NN)
         below = 1.0 + jnp.exp2(cosines * (-log2e * logit_scale) + bias)
         gate = pl.reciprocal(below, approx=True)
         gate = gate * (2.0 - below * gate)
@@ -217,15 +221,13 @@
         for k in range(0, tile, by_img.shape[1]):
             side = side + weighted[:, k : k + by_img.shape[1]]
         by_img[span] = side
-        if m + 1 < len(spans):
-            cosines = dot(img[spans[m + 1]], txt[:width], NN)
-        use(span)
     return logit_scale * down
 
 
-def put_text_terms(up, part, down):
-    slab = part.shape[0] // 8
+def put_text_terms(up, turned, slopes, down):
+    slab = turned.shape[0] // 8
     figures = split_rows(down, up.shape[1])
+    part = dot(turned[...], slopes, NN)
     for e in range(8):
         at = e * (slab + PAD)
         up[at : at + slab] = part[e * slab : (e + 1) * slab].astype(b16)
@@ -239,13 +241,8 @@
     def _():
         by_img[...] = jnp.zeros(by_img.shape, f32)
 
-    parts = []
-
-    def use(span):
-        parts.append(dot(turned[:, span], slopes[0, span], NN))
-
-    down = tile_slopes(rows, groups, at_ref[5], bias_ref, img, txt, slopes.at[0], by_img, use)
-    put_text_terms(up, sum(parts[1:], parts[0]), down)
+    down = tile_slopes(rows, groups, at_ref[5], bias_ref, img, txt, slopes.at[0], by_img)
+    put_text_terms(up, turned, slopes[0], down)
 
     @pl.when(step == 3)
     def _():
@@ -297,14 +294,9 @@
     both[:, tile:] = other[:width]
     held[:, tile:] = other_slopes[0]
     both[:, :tile] = txt[:width]
-    parts = []
-
-    def use(span):
-        parts.append(dot(turned[:, span], held[span, :tile], NN))
-        total[:, span] += dot(both[...], held[span], NT)
-
-    down = tile_slopes(rows, groups, at_ref[5], bias_ref, img, txt, held, by_img, use)
-    put_text_terms(up, sum(parts[1:], parts[0]), down)
+    down = tile_slopes(rows, groups, at_ref[5], bias_ref, img, txt, held, by_img)
+    put_text_terms(up, turned, held[:, :tile], down)
+    total[...] += dot(both[...], held[...], NT)
 
     @pl.when(step == 3)
     def _():
@@ -550,7 +542,9 @@
     txt_blocks = [
         text_rows, across, after, across_after, far, across_far, before, across_before
     ]
-    unit_txt, norm_txt = units(txt_blocks, turned_txt, places, rows)
+    pairs = [(before, across_before), (text_rows, across), (after, across_after)]
+    made = units(pairs, 3, turned_txt, (), places, rows)
+    unit_txt, norm_txt = units([(far, across_far)], 2, turned_txt, made, places, rows)
     other_txt = send(unit_txt, core_move)
     turned_units, norm_img = unit_columns(img_feats, image_head)
     unit_img = unit_rows(together([img_feats, unit_txt])[0], image_head, norm_img)

time: 189 us -> 185 us (0.979)
  waiting for transfers between devices: 31.8 us -> 25 us
  Pallas kernels: 67.1 us -> 70.2 us
    ppermute x22, waiting for transfers between devices: 31.8 us -> 25 us  [send(): lax.ppermute(block, DEV, [(flat(*p), flat(*move(*p))) for p in PLACES])]
    pallas_call x10 -> x11, Pallas kernels: 67.1 us -> 70.2 us  [call(): pl.pallas_call(body, out_shape=out_shape, grid_spec=spec, input_output_al...]
    unnamed x38 -> x40, local copies, waits for them, and re-layouts: 8.34 us -> 9.15 us
  transfers between devices with their start and end apart: 26 -> 26, of which waited for: 9 -> 7; matrix products, arithmetic and copies ran while one was open for 13% -> 13% of each run, Pallas kernels for 28% -> 30%
where the time goes in v7:
time: 185 us; the launch traced here: 184 us
  Pallas kernels  70.2 us (38%)
  starting transfers between devices  57 us (31%)
  waiting for transfers between devices  25 us (14%)
  matrix products  15.1 us (8%)
  local copies, waits for them, and re-layouts  12.7 us (7%)
  other arithmetic  3.3 us (2%)
    pallas_call x11, Pallas kernels, call(): pl.pallas_call(body, out_shape=out_shape, grid_spec=spec, input_output_al...  70.2 us
    ppermute x22, starting transfers between devices, send(): lax.ppermute(block, DEV, [(flat(*p), flat(*move(*p))) for p in PLACES])  34.6 us
    ppermute x22, waiting for transfers between devices, send(): lax.ppermute(block, DEV, [(flat(*p), flat(*move(*p))) for p in PLACES])  25 us
    all_to_all x4, starting transfers between devices, exchange(): lax.all_to_all(blocks, DEV, 0, 0, axis_index_groups=groups, tiled=True)  22.5 us
    dot_general x4, matrix products, dot(): return lax.dot_general(a, b, dims, preferred_element_type=f32)  15.1 us
    unnamed x40, local copies, waits for them, and re-layouts  9.15 us
  transfers between devices with their start and end apart: 26, of which 7 were waited for; matrix products, arithmetic and copies ran while one was open for 13% of the time, Pallas kernels for 30%

profile of v7, /device:TPU:1, one launch (start us, length us, event | category | flops | bytes accessed | tf_op | source)
XLA Modules:
  0.0 184.2 jit_solution(5036992925751663304)
XLA Ops:
  0.6 2.8 %broadcast_in_dim.2 = bf16[8,128,1152]{2,1,0:T(8,128)(2,1)} broadcast(bf16[128,1152]{1,0:T(8,128)(2,1)} %param.7), dimensions={1,2} | broadcast | bytes 2654208 | tf_op jit(solution)/shard_map/broadcast_in_dim | solution.py:531
  3.5 6.9 %all-to-all-start = ((bf16[8,128,1152]{2,1,0:T(8,128)(2,1)}), bf16[8,128,1152]{2,1,0:T(8,128)(2,1)}, u32[]{:S(2)}, u32[]{:S(2)}) async-start(bf16[8,128,1152]{2,1,0:T(8,128)(2,1)} %broadcast_in_dim.2), calls=%async_computation | async-start | bytes 4718592 | tf_op jit(solution)/shard_map/all_to_all | solution.py:65
  10.5 2.8 %collective-permute-start = (bf16[144,1152]{1,0:T(8,128)(2,1)S(1)}, bf16[144,1152]{1,0:T(8,128)(2,1)}, u32[]{:S(2)}, u32[]{:S(2)}) collective-permute-start(bf16[144,1152]{1,0:T(8,128)(2,1)S(1)} %pad_maximum_fusion.refs_3_.refs_8_), channel_id=1, source_target_pairs={{0,24},{1,25},{2,26},{3,27},{4,28},{5,29},{6,30},{7,31},{8,16},{9,... | collective-permute-start | bytes 995336 | tf_op jit(solution)/shard_map/ppermute | solution.py:61
  13.3 2.7 %collective-permute-start.3 = (bf16[144,1152]{1,0:T(8,128)(2,1)S(1)}, bf16[144,1152]{1,0:T(8,128)(2,1)S(1)}, u32[]{:S(2)}, u32[]{:S(2)}) collective-permute-start(bf16[144,1152]{1,0:T(8,128)(2,1)S(1)} %pad_maximum_fusion.refs_3_.refs_8_), channel_id=1, source_target_pairs={{0,6},{1,7},{2,0},{3,1},{4,2},{5,3},{6,4},{7,5},{8,14},{9,15},{10,... | collective-permute-start | bytes 995336 | tf_op jit(solution)/shard_map/ppermute | solution.py:61
  16.0 5.2 %copy.13 = bf16[1152,1152]{0,1:T(8,128)(2,1)} copy(bf16[1152,1152]{1,0:T(8,128)(2,1)} %param.10) | data formatting | bytes 5308416 | tf_op args[3]
  21.3 2.7 %collective-permute-start.1 = (bf16[144,1152]{1,0:T(8,128)(2,1)}, bf16[144,1152]{1,0:T(8,128)(2,1)}, u32[]{:S(2)}, u32[]{:S(2)}) collective-permute-start(bf16[144,1152]{1,0:T(8,128)(2,1)} %collective-permute-done.refs_4_.refs_9_), channel_id=1, source_target_pairs={{0,6},{1,7},{2,0},{3,1},{4,2},{5,3},{6,4},{7,5},{8,14},{9,15},{10,... | collective-permute-start | bytes 995336 | tf_op jit(solution)/shard_map/ppermute | solution.py:61
  24.8 4.4 %collective-permute-done.1.refs_6_.refs_11_ = bf16[144,1152]{1,0:T(8,128)(2,1)} collective-permute-done((bf16[144,1152]{1,0:T(8,128)(2,1)}, bf16[144,1152]{1,0:T(8,128)(2,1)}, u32[]{:S(2)}, u32[]{:S(2)}) %collective-permute-start.1) | collective-permute-done | bytes 331808 | tf_op jit(solution)/shard_map/ppermute | solution.py:61
  29.3 3.4 %collective-permute-start.5 = (bf16[144,1152]{1,0:T(8,128)(2,1)}, bf16[144,1152]{1,0:T(8,128)(2,1)S(1)}, u32[]{:S(2)}, u32[]{:S(2)}) collective-permute-start(bf16[144,1152]{1,0:T(8,128)(2,1)} %collective-permute-done.1.refs_6_.refs_11_), channel_id=1, source_target_pairs={{0,6},{1,7},{2,0},{3,1},{4,2},{5,3},{6,4},{7,5},{8,14},{9,15},{10,... | collective-permute-start | bytes 995336 | tf_op jit(solution)/shard_map/ppermute | solution.py:61
  33.4 7.6 %shard_map.102 = (bf16[1168,1024]{1,0:T(8,128)(2,1)}, f32[1,1024]{1,0:T(1,128)}) custom-call(s32[16]{0:T(128)} %stack.83.refs_0_.at_ref, bf16[144,1152]{1,0:T(8,128)(2,1)} %collective-permute-done.2.refs_1_.refs_14_, bf16[144,1152]{1,0:T(8,128)(2,1)} %collective-permute-done.6.refs_2_.refs_15_, bf16[144,1152]{1,0:T(8,128)(2,1)} %copy-done.5, ...), custom_call_target="tpu_custom_call" | custom-call | flops 2038431744 | bytes 4644864 | tf_op jit(solution)/shard_map/pallas_call | solution.py:93
  41.9 4.7 %shard_map.103 = (bf16[1168,1024]{1,0:T(8,128)(2,1)}, f32[1,1024]{1,0:T(1,128)}) custom-call(s32[16]{0:T(128)} %stack.83.refs_0_.at_ref, bf16[144,1152]{1,0:T(8,128)(2,1)} %copy-done.3, bf16[144,1152]{1,0:T(8,128)(2,1)} %copy-done.4, bf16[1152,1152]{1,0:T(8,128)(2,1)} %bitcast.47, ...), custom_call_target="tpu_custom_call", output_to_operand_aliasing={{0}: (4, {}), {1}: (5, {})} | custom-call | flops 679477248 | bytes 5713920 | tf_op jit(solution)/shard_map/pallas_call | solution.py:93
  46.5 3.3 %collective-permute-start.7 = (bf16[1168,1024]{1,0:T(8,128)(2,1)}, bf16[1168,1024]{1,0:T(8,128)(2,1)}, u32[]{:S(2)}, u32[]{:S(2)}) collective-permute-start(bf16[1168,1024]{1,0:T(8,128)(2,1)} %get-tuple-element.50.refs_4_.refs_6_), channel_id=1, source_target_pairs={{0,1},{1,0},{2,3},{3,2},{4,5},{5,4},{6,7},{7,6},{8,9},{9,8},{10,11... | collective-permute-start | bytes 7176200 | tf_op jit(solution)/shard_map/ppermute | solution.py:61
  49.8 5.0 %multiply_reduce_fusion = (f32[1024]{0:T(1024)S(1)}, f32[1152,1024]{1,0:T(8,128)S(1)}) fusion(bf16[1152,1152]{1,0:T(8,128)(2,1)S(1)} %copy-done, bf16[1024,1152]{1,0:T(8,128)(2,1)} %bitcast.16.refs_4_), kind=kOutput, calls=%fused_computation.2 | convolution fusion | flops 2720267264 | bytes 9736192 | tf_op jit(solution)/shard_map/dot_general | solution.py:75
  54.8 6.6 %divide_convert_fusion.1.refs_2_ = bf16[1024,1152]{1,0:T(8,128)(2,1)} fusion(bf16[1024,1152]{1,0:T(8,128)(2,1)} %bitcast.16.refs_4_, bf16[1152,1152]{1,0:T(8,128)(2,1)S(1)} %copy-done, f32[1024]{0:T(1024)S(1)} %add_sqrt_fusion), kind=kOutput, calls=%fused_computation.1 | convolution fusion | flops 2720268288 | bytes 7376896 | tf_op jit(solution)/shard_map/dot_general | solution.py:75
  63.5 12.8 %shard_map.104 = (bf16[4,1024,256]{2,1,0:T(8,128)(2,1)}, f32[1,1024]{1,0:T(1,128)}, bf16[1280,1024]{1,0:T(8,128)(2,1)}) custom-call(s32[16]{0:T(128)} %stack.83.refs_0_.at_ref, f32[32]{0:T(128)} %refs_1_.3, bf16[1024,1152]{1,0:T(8,128)(2,1)} %divide_convert_fusion.1.refs_2_, bf16[1152,1024]{1,0:T(8,128)(2,1)} %divide_convert_fusion.refs_3_.refs_2_, ...), custom_call_target="tpu_custom_call" | custom-call | flops 4831838208 | bytes 7110784 | tf_op jit(solution)/shard_map/pallas_call | solution.py:93
  76.3 19.2 %shard_map.105 = (bf16[1280,1024]{1,0:T(8,128)(2,1)}, bf16[8,160,1024]{2,1,0:T(8,128)(2,1)}) custom-call(s32[16]{0:T(128)} %stack.83.refs_0_.at_ref, f32[32]{0:T(128)} %refs_1_.3, bf16[1024,1152]{1,0:T(8,128)(2,1)} %divide_convert_fusion.1.refs_2_, bf16[1152,1024]{1,0:T(8,128)(2,1)} %divide_convert_fusion.refs_3_.refs_2_, ...), custom_call_target="tpu_custom_call" | custom-call | flops 9663676416 | bytes 11604096 | tf_op jit(solution)/shard_map/pallas_call | solution.py:93
  95.5 4.6 %all-to-all-start.1 = ((bf16[8,160,1024]{2,1,0:T(8,128)(2,1)}), bf16[8,160,1024]{2,1,0:T(8,128)(2,1)}, u32[]{:S(2)}, u32[]{:S(2)}) async-start(bf16[8,160,1024]{2,1,0:T(8,128)(2,1)} %get-tuple-element.54), calls=%async_computation.1 | async-start | bytes 5242880 | tf_op jit(solution)/shard_map/all_to_all | solution.py:65
  100.1 3.1 %shard_map.107 = (bf16[160,1024]{1,0:T(8,128)(2,1)}, bf16[160,1024]{1,0:T(8,128)(2,1)}, bf16[160,1024]{1,0:T(8,128)(2,1)}) custom-call(s32[16]{0:T(128)} %stack.83.refs_0_.at_ref, bf16[1280,1024]{1,0:T(8,128)(2,1)} %get-tuple-element.57.refs_1_.refs_3_.refs_5_.refs_4_.refs_7_, ...), custom_call_target="tpu_custom_call" | custom-call | bytes 15728640 | tf_op jit(solution)/shard_map/pallas_call | solution.py:93
  103.3 2.7 %collective-permute-start.10 = (bf16[160,1024]{1,0:T(8,128)(2,1)}, bf16[160,1024]{1,0:T(8,128)(2,1)S(1)}, u32[]{:S(2)}, u32[]{:S(2)}) collective-permute-start(bf16[160,1024]{1,0:T(8,128)(2,1)} %get-tuple-element.60), channel_id=1, source_target_pairs={{0,6},{1,7},{2,0},{3,1},{4,2},{5,3},{6,4},{7,5},{8,14},{9,15},{10,... | collective-permute-start | bytes 983048 | tf_op jit(solution)/shard_map/ppermute | solution.py:61
  105.9 7.6 %collective-permute-done.9.refs_6_ = bf16[160,1024]{1,0:T(8,128)(2,1)S(1)} collective-permute-done((bf16[160,1024]{1,0:T(8,128)(2,1)}, bf16[160,1024]{1,0:T(8,128)(2,1)S(1)}, u32[]{:S(2)}, u32[]{:S(2)}) %collective-permute-start.9) | collective-permute-done | bytes 327712 | tf_op jit(solution)/shard_map/ppermute | solution.py:61
  114.4 3.4 %shard_map.108 = (bf16[160,1024]{1,0:T(8,128)(2,1)}, bf16[160,1024]{1,0:T(8,128)(2,1)}, bf16[160,1024]{1,0:T(8,128)(2,1)}) custom-call(s32[16]{0:T(128)} %stack.83.refs_0_.at_ref, bf16[1280,1024]{1,0:T(8,128)(2,1)} %get-tuple-element.57.refs_1_.refs_3_.refs_5_.refs_4_.refs_7_, ...), custom_call_target="tpu_custom_call" | custom-call | bytes 16384000 | tf_op jit(solution)/shard_map/pallas_call | solution.py:93
  120.1 3.0 %collective-permute-done.11.refs_3_ = bf16[160,1024]{1,0:T(8,128)(2,1)S(1)} collective-permute-done((bf16[160,1024]{1,0:T(8,128)(2,1)}, bf16[160,1024]{1,0:T(8,128)(2,1)S(1)}, u32[]{:S(2)}, u32[]{:S(2)}) %collective-permute-start.11) | collective-permute-done | bytes 327712 | tf_op jit(solution)/shard_map/ppermute | solution.py:61
  123.1 2.9 %collective-permute-done.12.refs_4_ = bf16[160,1024]{1,0:T(8,128)(2,1)S(1)} collective-permute-done((bf16[160,1024]{1,0:T(8,128)(2,1)}, bf16[160,1024]{1,0:T(8,128)(2,1)S(1)}, u32[]{:S(2)}, u32[]{:S(2)}) %collective-permute-start.12) | collective-permute-done | bytes 327712 | tf_op jit(solution)/shard_map/ppermute | solution.py:61
  126.8 2.8 %shard_map.109 = bf16[160,1024]{1,0:T(8,128)(2,1)} custom-call(s32[16]{0:T(128)} %stack.83.refs_0_.at_ref, bf16[1280,1024]{1,0:T(8,128)(2,1)} %get-tuple-element.57.refs_1_.refs_3_.refs_5_.refs_4_.refs_7_, bf16[1280,1024]{1,0:T(8,128)(2,1)} %collective-permute-done.8.refs_2_.refs_4_.refs_6_.refs_5_.refs_8_, bf16[160,1024]{1,0:T(8,128)(2,1)} %copy-done.8, ...), custom_call_target="tpu_custom_call" | custom-call | bytes 5898240 | tf_op jit(solution)/shard_map/pallas_call | solution.py:93
  131.1 2.6 %collective-permute-start.14 = (bf16[160,1024]{1,0:T(8,128)(2,1)}, bf16[160,1024]{1,0:T(8,128)(2,1)}, u32[]{:S(2)}, u32[]{:S(2)}) collective-permute-start(bf16[160,1024]{1,0:T(8,128)(2,1)} %get-tuple-element.69), channel_id=1, source_target_pairs={{0,6},{1,7},{2,0},{3,1},{4,2},{5,3},{6,4},{7,5},{8,14},{9,15},{10,... | collective-permute-start | bytes 983048 | tf_op jit(solution)/shard_map/ppermute | solution.py:61
  133.7 4.8 %shard_map.106 = (bf16[8,144,128]{2,1,0:T(8,128)(2,1)}, bf16[144,1152]{1,0:T(8,128)(2,1)}) custom-call(s32[16]{0:T(128)} %stack.83.refs_0_.at_ref, bf16[8,160,1024]{2,1,0:T(8,128)(2,1)} %all-to-all-done.1.refs_1_, bf16[1152,1024]{1,0:T(8,128)(2,1)} %divide_convert_fusion.refs_3_.refs_2_, f32[1,1024]{1,0:T(1,128)} %bitcast.50, bf16[1024,1152]{1,0:T(8,128)(2,1)} %bitcast.16.refs_4_), custom_call_target="tpu_custom_call" | custom-call | tf_op jit(solution)/shard_map/pallas_call | solution.py:93
  138.5 3.7 %all-to-all-start.2 = ((bf16[8,144,128]{2,1,0:T(8,128)(2,1)}), bf16[8,144,128]{2,1,0:T(8,128)(2,1)S(1)}, u32[]{:S(2)}, u32[]{:S(2)}) async-start(bf16[8,144,128]{2,1,0:T(8,128)(2,1)} %get-tuple-element.55), calls=%async_computation.2 | async-start | bytes 589824 | tf_op jit(solution)/shard_map/all_to_all | solution.py:65
  142.2 4.0 %collective-permute-start.16 = (bf16[144,1152]{1,0:T(8,128)(2,1)}, bf16[144,1152]{1,0:T(8,128)(2,1)S(1)}, u32[]{:S(2)}, u32[]{:S(2)}) collective-permute-start(bf16[144,1152]{1,0:T(8,128)(2,1)} %get-tuple-element.56.img), channel_id=1, source_target_pairs={{0,1},{1,0},{2,3},{3,2},{4,5},{5,4},{6,7},{7,6},{8,9},{9,8},{10,11... | collective-permute-start | bytes 995336 | tf_op jit(solution)/shard_map/ppermute | solution.py:61
  146.2 4.8 %shard_map.110 = (bf16[4,144,128]{2,1,0:T(8,128)(2,1)}, bf16[4,144,128]{2,1,0:T(8,128)(2,1)}, bf16[144,1152]{1,0:T(8,128)(2,1)}) custom-call(s32[16]{0:T(128)} %stack.83.refs_0_.at_ref, bf16[1280,1024]{1,0:T(8,128)(2,1)} %get-tuple-element.57.refs_1_.refs_3_.refs_5_.refs_4_.refs_7_, ...), custom_call_target="tpu_custom_call" | custom-call | tf_op jit(solution)/shard_map/pallas_call | solution.py:93
  156.1 4.4 %shard_map.111 = bf16[512,384]{1,0:T(8,128)(2,1)} custom-call(s32[16]{0:T(128)} %stack.83.refs_0_.at_ref, bf16[144,1152]{1,0:T(8,128)(2,1)} %get-tuple-element.56.img, bf16[144,1152]{1,0:T(8,128)(2,1)} %get-tuple-element.73.txt, bf16[144,1152]{1,0:T(8,128)(2,1)} %copy-done.7, bf16[144,1152]{1,0:T(8,128)(2,1)} %collective-permute-done.17.other_txt), custom_call_target="tpu_custom_call" | custom-call | tf_op jit(solution)/shard_map/pallas_call | solution.py:93
  160.4 7.2 %all-to-all-start.3 = ((bf16[64,8,384]{2,1,0:T(8,128)(2,1)}), bf16[64,8,384]{2,1,0:T(8,128)(2,1)S(1)}, u32[]{:S(2)}, u32[]{:S(2)}) async-start(bf16[64,8,384]{2,1,0:T(8,128)(2,1)} %bitcast.48), calls=%async_computation.3 | async-start | bytes 786432 | tf_op jit(solution)/shard_map/all_to_all | solution.py:65
  172.9 2.8 %collective-permute-done.19 = bf16[288,128]{1,0:T(8,128)(2,1)S(1)} collective-permute-done((bf16[288,128]{1,0:T(8,128)(2,1)S(1)}, bf16[288,128]{1,0:T(8,128)(2,1)S(1)}, u32[]{:S(2)}, u32[]{:S(2)}) %collective-permute-start.19) | collective-permute-done | bytes 73760 | tf_op jit(solution)/shard_map/ppermute | solution.py:61
  175.7 3.3 %collective-permute-done.20 = bf16[288,128]{1,0:T(8,128)(2,1)S(1)} collective-permute-done((bf16[288,128]{1,0:T(8,128)(2,1)S(1)}, bf16[288,128]{1,0:T(8,128)(2,1)S(1)}, u32[]{:S(2)}, u32[]{:S(2)}) %collective-permute-start.20) | collective-permute-done | bytes 73760 | tf_op jit(solution)/shard_map/ppermute | solution.py:61
  (87 shorter events, 25.3 us)
Async XLA Ops:
  0.6 49.2 %copy-start = (bf16[1152,1152]{1,0:T(8,128)(2,1)S(1)}, bf16[1152,1152]{1,0:T(8,128)(2,1)}, u32[]{:S(2)}) copy-start(bf16[1152,1152]{1,0:T(8,128)(2,1)} %param.9) | copy-start | bytes 7962628
  3.5 6.9 %copy-start.16 = (s32[128]{0:T(128)S(1)}, s32[128]{0:T(128)}, u32[]{:S(2)}) copy-start(s32[128]{0:T(128)} %param.12) | copy-start | bytes 1540
  3.5 7.0 %copy-start.12 = (bf16[128,1152]{1,0:T(8,128)(2,1)S(1)}, bf16[128,1152]{1,0:T(8,128)(2,1)}, u32[]{:S(2)}) copy-start(bf16[128,1152]{1,0:T(8,128)(2,1)} %param.8) | copy-start | bytes 884740
  3.5 46.3 %all-to-all-start = ((bf16[8,128,1152]{2,1,0:T(8,128)(2,1)}), bf16[8,128,1152]{2,1,0:T(8,128)(2,1)}, u32[]{:S(2)}, u32[]{:S(2)}) async-start(bf16[8,128,1152]{2,1,0:T(8,128)(2,1)} %broadcast_in_dim.2), calls=%async_computation | async-start | bytes 4718592 | tf_op jit(solution)/shard_map/all_to_all | solution.py:65
  10.5 10.8 %copy-start.5 = (bf16[144,1152]{1,0:T(8,128)(2,1)}, bf16[144,1152]{1,0:T(8,128)(2,1)S(1)}, u32[]{:S(2)}) copy-start(bf16[144,1152]{1,0:T(8,128)(2,1)S(1)} %pad_maximum_fusion.refs_3_.refs_8_) | copy-start | bytes 995332
  10.5 10.8 %collective-permute-start = (bf16[144,1152]{1,0:T(8,128)(2,1)S(1)}, bf16[144,1152]{1,0:T(8,128)(2,1)}, u32[]{:S(2)}, u32[]{:S(2)}) collective-permute-start(bf16[144,1152]{1,0:T(8,128)(2,1)S(1)} %pad_maximum_fusion.refs_3_.refs_8_), channel_id=1, source_target_pairs={{0,24},{1,25},{2,26},{3,27},{4,28},{5,29},{6,30},{7,31},{8,16},{9,... | collective-permute-start | bytes 995336 | tf_op jit(solution)/shard_map/ppermute | solution.py:61
  13.3 10.7 %collective-permute-start.3 = (bf16[144,1152]{1,0:T(8,128)(2,1)S(1)}, bf16[144,1152]{1,0:T(8,128)(2,1)S(1)}, u32[]{:S(2)}, u32[]{:S(2)}) collective-permute-start(bf16[144,1152]{1,0:T(8,128)(2,1)S(1)} %pad_maximum_fusion.refs_3_.refs_8_), channel_id=1, source_target_pairs={{0,6},{1,7},{2,0},{3,1},{4,2},{5,3},{6,4},{7,5},{8,14},{9,15},{10,... | collective-permute-start | bytes 995336 | tf_op jit(solution)/shard_map/ppermute | solution.py:61
  16.0 8.8 %collective-permute-start.2 = (bf16[144,1152]{1,0:T(8,128)(2,1)S(1)}, bf16[144,1152]{1,0:T(8,128)(2,1)}, u32[]{:S(2)}, u32[]{:S(2)}) collective-permute-start(bf16[144,1152]{1,0:T(8,128)(2,1)S(1)} %pad_maximum_fusion.refs_3_.refs_8_), channel_id=1, source_target_pairs={{0,2},{1,3},{2,4},{3,5},{4,6},{5,7},{6,0},{7,1},{8,10},{9,11},{10,... | collective-permute-start | bytes 995336 | tf_op jit(solution)/shard_map/ppermute | solution.py:61
  21.3 8.0 %collective-permute-start.1 = (bf16[144,1152]{1,0:T(8,128)(2,1)}, bf16[144,1152]{1,0:T(8,128)(2,1)}, u32[]{:S(2)}, u32[]{:S(2)}) collective-permute-start(bf16[144,1152]{1,0:T(8,128)(2,1)} %collective-permute-done.refs_4_.refs_9_), channel_id=1, source_target_pairs={{0,6},{1,7},{2,0},{3,1},{4,2},{5,3},{6,4},{7,5},{8,14},{9,15},{10,... | collective-permute-start | bytes 995336 | tf_op jit(solution)/shard_map/ppermute | solution.py:61
  24.0 9.4 %collective-permute-start.6 = (bf16[144,1152]{1,0:T(8,128)(2,1)}, bf16[144,1152]{1,0:T(8,128)(2,1)}, u32[]{:S(2)}, u32[]{:S(2)}) collective-permute-start(bf16[144,1152]{1,0:T(8,128)(2,1)} %collective-permute-done.refs_4_.refs_9_), channel_id=1, source_target_pairs={{0,2},{1,3},{2,4},{3,5},{4,6},{5,7},{6,0},{7,1},{8,10},{9,11},{10,... | collective-permute-start | bytes 995336 | tf_op jit(solution)/shard_map/ppermute | solution.py:61
  29.3 11.7 %collective-permute-start.4 = (bf16[144,1152]{1,0:T(8,128)(2,1)}, bf16[144,1152]{1,0:T(8,128)(2,1)S(1)}, u32[]{:S(2)}, u32[]{:S(2)}) collective-permute-start(bf16[144,1152]{1,0:T(8,128)(2,1)} %collective-permute-done.2.refs_1_.refs_14_), channel_id=1, source_target_pairs={{0,2},{1,3},{2,4},{3,5},{4,6},{5,7},{6,0},{7,1},{8,10},{9,11},{10,... | collective-permute-start | bytes 995336 | tf_op jit(solution)/shard_map/ppermute | solution.py:61
  29.3 11.7 %collective-permute-start.5 = (bf16[144,1152]{1,0:T(8,128)(2,1)}, bf16[144,1152]{1,0:T(8,128)(2,1)S(1)}, u32[]{:S(2)}, u32[]{:S(2)}) collective-permute-start(bf16[144,1152]{1,0:T(8,128)(2,1)} %collective-permute-done.1.refs_6_.refs_11_), channel_id=1, source_target_pairs={{0,6},{1,7},{2,0},{3,1},{4,2},{5,3},{6,4},{7,5},{8,14},{9,15},{10,... | collective-permute-start | bytes 995336 | tf_op jit(solution)/shard_map/ppermute | solution.py:61
  46.5 16.9 %collective-permute-start.7 = (bf16[1168,1024]{1,0:T(8,128)(2,1)}, bf16[1168,1024]{1,0:T(8,128)(2,1)}, u32[]{:S(2)}, u32[]{:S(2)}) collective-permute-start(bf16[1168,1024]{1,0:T(8,128)(2,1)} %get-tuple-element.50.refs_4_.refs_6_), channel_id=1, source_target_pairs={{0,1},{1,0},{2,3},{3,2},{4,5},{5,4},{6,7},{7,6},{8,9},{9,8},{10,11... | collective-permute-start | bytes 7176200 | tf_op jit(solution)/shard_map/ppermute | solution.py:61
  76.3 23.8 %collective-permute-start.8 = (bf16[1280,1024]{1,0:T(8,128)(2,1)}, bf16[1280,1024]{1,0:T(8,128)(2,1)}, u32[]{:S(2)}, u32[]{:S(2)}) collective-permute-start(bf16[1280,1024]{1,0:T(8,128)(2,1)} %get-tuple-element.58), channel_id=1, source_target_pairs={{0,1},{1,0},{2,3},{3,2},{4,5},{5,4},{6,7},{7,6},{8,9},{9,8},{10,11... | collective-permute-start | bytes 7864328 | tf_op jit(solution)/shard_map/ppermute | solution.py:61
  95.5 38.2 %all-to-all-start.1 = ((bf16[8,160,1024]{2,1,0:T(8,128)(2,1)}), bf16[8,160,1024]{2,1,0:T(8,128)(2,1)}, u32[]{:S(2)}, u32[]{:S(2)}) async-start(bf16[8,160,1024]{2,1,0:T(8,128)(2,1)} %get-tuple-element.54), calls=%async_computation.1 | async-start | bytes 5242880 | tf_op jit(solution)/shard_map/all_to_all | solution.py:65
  103.2 10.3 %collective-permute-start.9 = (bf16[160,1024]{1,0:T(8,128)(2,1)}, bf16[160,1024]{1,0:T(8,128)(2,1)S(1)}, u32[]{:S(2)}, u32[]{:S(2)}) collective-permute-start(bf16[160,1024]{1,0:T(8,128)(2,1)} %get-tuple-element.59), channel_id=1, source_target_pairs={{0,2},{1,3},{2,4},{3,5},{4,6},{5,7},{6,0},{7,1},{8,10},{9,11},{10,... | collective-permute-start | bytes 983048 | tf_op jit(solution)/shard_map/ppermute | solution.py:61
  103.3 10.3 %collective-permute-start.10 = (bf16[160,1024]{1,0:T(8,128)(2,1)}, bf16[160,1024]{1,0:T(8,128)(2,1)S(1)}, u32[]{:S(2)}, u32[]{:S(2)}) collective-permute-start(bf16[160,1024]{1,0:T(8,128)(2,1)} %get-tuple-element.60), channel_id=1, source_target_pairs={{0,6},{1,7},{2,0},{3,1},{4,2},{5,3},{6,4},{7,5},{8,14},{9,15},{10,... | collective-permute-start | bytes 983048 | tf_op jit(solution)/shard_map/ppermute | solution.py:61
  113.6 9.6 %collective-permute-start.11 = (bf16[160,1024]{1,0:T(8,128)(2,1)}, bf16[160,1024]{1,0:T(8,128)(2,1)S(1)}, u32[]{:S(2)}, u32[]{:S(2)}) collective-permute-start(bf16[160,1024]{1,0:T(8,128)(2,1)} %get-tuple-element.62), channel_id=1, source_target_pairs={{0,2},{1,3},{2,4},{3,5},{4,6},{5,7},{6,0},{7,1},{8,10},{9,11},{10,... | collective-permute-start | bytes 983048 | tf_op jit(solution)/shard_map/ppermute | solution.py:61
  117.9 8.2 %collective-permute-start.12 = (bf16[160,1024]{1,0:T(8,128)(2,1)}, bf16[160,1024]{1,0:T(8,128)(2,1)S(1)}, u32[]{:S(2)}, u32[]{:S(2)}) collective-permute-start(bf16[160,1024]{1,0:T(8,128)(2,1)} %get-tuple-element.65), channel_id=1, source_target_pairs={{0,6},{1,7},{2,0},{3,1},{4,2},{5,3},{6,4},{7,5},{8,14},{9,15},{10,... | collective-permute-start | bytes 983048 | tf_op jit(solution)/shard_map/ppermute | solution.py:61
  129.6 16.6 %collective-permute-start.15 = (bf16[160,1024]{1,0:T(8,128)(2,1)}, bf16[160,1024]{1,0:T(8,128)(2,1)}, u32[]{:S(2)}, u32[]{:S(2)}) collective-permute-start(bf16[160,1024]{1,0:T(8,128)(2,1)} %shard_map.109), channel_id=1, source_target_pairs={{0,24},{1,25},{2,26},{3,27},{4,28},{5,29},{6,30},{7,31},{8,16},{9,... | collective-permute-start | bytes 983048 | tf_op jit(solution)/shard_map/ppermute | solution.py:61
  130.5 15.7 %collective-permute-start.13 = (bf16[160,1024]{1,0:T(8,128)(2,1)}, bf16[160,1024]{1,0:T(8,128)(2,1)}, u32[]{:S(2)}, u32[]{:S(2)}) collective-permute-start(bf16[160,1024]{1,0:T(8,128)(2,1)} %get-tuple-element.68), channel_id=1, source_target_pairs={{0,2},{1,3},{2,4},{3,5},{4,6},{5,7},{6,0},{7,1},{8,10},{9,11},{10,... | collective-permute-start | bytes 983048 | tf_op jit(solution)/shard_map/ppermute | solution.py:61
  131.1 15.1 %collective-permute-start.14 = (bf16[160,1024]{1,0:T(8,128)(2,1)}, bf16[160,1024]{1,0:T(8,128)(2,1)}, u32[]{:S(2)}, u32[]{:S(2)}) collective-permute-start(bf16[160,1024]{1,0:T(8,128)(2,1)} %get-tuple-element.69), channel_id=1, source_target_pairs={{0,6},{1,7},{2,0},{3,1},{4,2},{5,3},{6,4},{7,5},{8,14},{9,15},{10,... | collective-permute-start | bytes 983048 | tf_op jit(solution)/shard_map/ppermute | solution.py:61
  138.5 15.1 %all-to-all-start.2 = ((bf16[8,144,128]{2,1,0:T(8,128)(2,1)}), bf16[8,144,128]{2,1,0:T(8,128)(2,1)S(1)}, u32[]{:S(2)}, u32[]{:S(2)}) async-start(bf16[8,144,128]{2,1,0:T(8,128)(2,1)} %get-tuple-element.55), calls=%async_computation.2 | async-start | bytes 589824 | tf_op jit(solution)/shard_map/all_to_all | solution.py:65
  142.2 13.1 %collective-permute-start.16 = (bf16[144,1152]{1,0:T(8,128)(2,1)}, bf16[144,1152]{1,0:T(8,128)(2,1)S(1)}, u32[]{:S(2)}, u32[]{:S(2)}) collective-permute-start(bf16[144,1152]{1,0:T(8,128)(2,1)} %get-tuple-element.56.img), channel_id=1, source_target_pairs={{0,1},{1,0},{2,3},{3,2},{4,5},{5,4},{6,7},{7,6},{8,9},{9,8},{10,11... | collective-permute-start | bytes 995336 | tf_op jit(solution)/shard_map/ppermute | solution.py:61
  151.1 4.3 %collective-permute-start.17 = (bf16[144,1152]{1,0:T(8,128)(2,1)}, bf16[144,1152]{1,0:T(8,128)(2,1)}, u32[]{:S(2)}, u32[]{:S(2)}) collective-permute-start(bf16[144,1152]{1,0:T(8,128)(2,1)} %get-tuple-element.73.txt), channel_id=1, source_target_pairs={{0,1},{1,0},{2,3},{3,2},{4,5},{5,4},{6,7},{7,6},{8,9},{9,8},{10,11... | collective-permute-start | bytes 995336 | tf_op jit(solution)/shard_map/ppermute | solution.py:61
  151.1 9.3 %collective-permute-start.18 = (bf16[4,144,128]{2,1,0:T(8,128)(2,1)}, bf16[4,144,128]{2,1,0:T(8,128)(2,1)}, u32[]{:S(2)}, u32[]{:S(2)}) collective-permute-start(bf16[4,144,128]{2,1,0:T(8,128)(2,1)} %get-tuple-element.74), channel_id=1, source_target_pairs={{0,24},{1,25},{2,26},{3,27},{4,28},{5,29},{6,30},{7,31},{8,16},{9,... | collective-permute-start | bytes 442376 | tf_op jit(solution)/shard_map/ppermute | solution.py:61
  153.6 14.1 %copy-start.13 = (bf16[4,144,128]{2,1,0:T(8,128)(2,1)S(1)}, bf16[4,144,128]{2,1,0:T(8,128)(2,1)}, u32[]{:S(2)}) copy-start(bf16[4,144,128]{2,1,0:T(8,128)(2,1)} %get-tuple-element.76) | copy-start | bytes 442372
  160.4 20.5 %all-to-all-start.3 = ((bf16[64,8,384]{2,1,0:T(8,128)(2,1)}), bf16[64,8,384]{2,1,0:T(8,128)(2,1)S(1)}, u32[]{:S(2)}, u32[]{:S(2)}) async-start(bf16[64,8,384]{2,1,0:T(8,128)(2,1)} %bitcast.48), calls=%async_computation.3 | async-start | bytes 786432 | tf_op jit(solution)/shard_map/all_to_all | solution.py:65
  167.7 11.5 %copy-start.1 = (bf16[1152,1152]{1,0:T(8,128)(2,1)S(1)}, bf16[1152,1152]{1,0:T(8,128)(2,1)}, u32[]{:S(2)}) copy-start(bf16[1152,1152]{1,0:T(8,128)(2,1)} %param.10) | copy-start | bytes 7962628
  168.9 10.2 %collective-permute-start.21 = (bf16[288,128]{1,0:T(8,128)(2,1)S(1)}, bf16[288,128]{1,0:T(8,128)(2,1)S(1)}, u32[]{:S(2)}, u32[]{:S(2)}) collective-permute-start(bf16[288,128]{1,0:T(8,128)(2,1)S(1)} %get-tuple-element.80), channel_id=1, source_target_pairs={{0,2},{1,3},{2,4},{3,5},{4,6},{5,7},{6,0},{7,1},{8,10},{9,11},{10,... | collective-permute-start | bytes 221192 | tf_op jit(solution)/shard_map/ppermute | solution.py:61
  169.9 5.8 %collective-permute-start.19 = (bf16[288,128]{1,0:T(8,128)(2,1)S(1)}, bf16[288,128]{1,0:T(8,128)(2,1)S(1)}, u32[]{:S(2)}, u32[]{:S(2)}) collective-permute-start(bf16[288,128]{1,0:T(8,128)(2,1)S(1)} %get-tuple-element.81), channel_id=1, source_target_pairs={{0,6},{1,7},{2,0},{3,1},{4,2},{5,3},{6,4},{7,5},{8,14},{9,15},{10,... | collective-permute-start | bytes 221192 | tf_op jit(solution)/shard_map/ppermute | solution.py:61
  171.6 7.4 %collective-permute-start.20 = (bf16[288,128]{1,0:T(8,128)(2,1)S(1)}, bf16[288,128]{1,0:T(8,128)(2,1)S(1)}, u32[]{:S(2)}, u32[]{:S(2)}) collective-permute-start(bf16[288,128]{1,0:T(8,128)(2,1)S(1)} %get-tuple-element.82), channel_id=1, source_target_pairs={{0,4},{1,5},{2,6},{3,7},{4,0},{5,1},{6,2},{7,3},{8,12},{9,13},{10,... | collective-permute-start | bytes 221192 | tf_op jit(solution)/shard_map/ppermute | solution.py:61
  (11 other events, 27.1 us)

commit v8 on v7

--- a/solution.py
+++ b/solution.py
@@ -83,7 +83,7 @@
     if out_specs is None:
         out_specs = [whole] * len(out_shape) if many else whole
     spec = pltpu.PrefetchScalarGridSpec(
-        num_scalar_prefetch=1,
+        num_scalar_prefetch=0 if places is None else 1,
         grid=grid,
         in_specs=in_specs,
         out_specs=out_specs,
@@ -97,7 +97,7 @@
         input_output_aliases=aliases or {},
         compiler_params=pltpu.CompilerParams(vmem_limit_bytes=60 * 2**20),
         cost_estimate=pl.CostEstimate(flops=weight * cost, bytes_accessed=moved, transcendentals=0),
-    )(places, *arrays)
+    )(*([] if places is None else [places]), *arrays)
 
 
 def aligned(index, size):
@@ -234,14 +234,14 @@
         up[at + slab : at + slab + PAD] = figures
 
 
-def other_kernel(rows, groups, at_ref, bias_ref, img, turned, txt, slopes, img_sum, up, by_img):
+def other_kernel(rows, groups, bias_ref, img, turned, txt, slopes, img_sum, up, by_img):
     step = pl.program_id(0)
 
     @pl.when(step == 0)
     def _():
         by_img[...] = jnp.zeros(by_img.shape, f32)
 
-    down = tile_slopes(rows, groups, at_ref[5], bias_ref, img, txt, slopes.at[0], by_img)
+    down = tile_slopes(rows, groups, bias_ref[groups].astype(jnp.int32), bias_ref, img, txt, slopes.at[0], by_img)
     put_text_terms(up, turned, slopes[0], down)
 
     @pl.when(step == 3)
@@ -249,30 +249,30 @@
         img_sum[...] = logit_scale * jnp.sum(by_img[...].T, axis=0, keepdims=True)
 
 
-def other_tile(img, turned, txt, group_bias, places, rows):
+def other_tile(img, turned, txt, group_bias, rows):
     count, width = img.shape
     tile = 2 * rows
     height = width + 8 * PAD
-    whole = lambda a: pl.BlockSpec(a.shape, lambda i, at: (0, 0))
+    whole = lambda a: pl.BlockSpec(a.shape, lambda i: (0, 0))
     return call(
-        lambda *refs: other_kernel(rows, group_bias.shape[0], *refs),
+        lambda *refs: other_kernel(rows, group_bias.shape[0] - 1, *refs),
         [
             jax.ShapeDtypeStruct((4, count, tile), b16),
             jax.ShapeDtypeStruct((1, count), f32),
             jax.ShapeDtypeStruct((height, count), b16),
         ],
-        places,
+        None,
         [group_bias, img, turned, txt],
         in_specs=[
             pl.BlockSpec(memory_space=pltpu.SMEM),
             whole(img),
             whole(turned),
-            pl.BlockSpec((width + PAD, tile), lambda i, at: (0, i)),
+            pl.BlockSpec((width + PAD, tile), lambda i: (0, i)),
         ],
         out_specs=[
-            pl.BlockSpec((1, count, tile), lambda i, at: (i, 0, 0)),
-            pl.BlockSpec((1, count), lambda i, at: (0, 0)),
-            pl.BlockSpec((height, tile), lambda i, at: (0, i)),
+            pl.BlockSpec((1, count, tile), lambda i: (i, 0, 0)),
+            pl.BlockSpec((1, count), lambda i: (0, 0)),
+            pl.BlockSpec((height, tile), lambda i: (0, i)),
         ],
         grid=(4,),
         scratch=[pltpu.VMEM((count, min(128, tile)), f32)],
@@ -280,7 +280,7 @@
     )
 
 
-def own_kernel(rows, groups, at_ref, bias_ref, img, turned, txt, other, *refs):
+def own_kernel(rows, groups, bias_ref, img, turned, txt, other, *refs):
     other_slopes, other_sum, up, out, by_img, held, both, total = refs
     step = pl.program_id(0)
     width = img.shape[1]
@@ -294,7 +294,7 @@
     both[:, tile:] = other[:width]
     held[:, tile:] = other_slopes[0]
     both[:, :tile] = txt[:width]
-    down = tile_slopes(rows, groups, at_ref[5], bias_ref, img, txt, held, by_img)
+    down = tile_slopes(rows, groups, bias_ref[groups].astype(jnp.int32), bias_ref, img, txt, held, by_img)
     put_text_terms(up, turned, held[:, :tile], down)
     total[...] += dot(both[...], held[...], NT)
 
@@ -309,30 +309,30 @@
 
 
 def own_tile(
-    img, turned, txt, other, other_slopes, other_sum, group_bias, places, rows
+    img, turned, txt, other, other_slopes, other_sum, group_bias, rows
 ):
     count, width = img.shape
     tile = 2 * rows
     height = width + 8 * PAD
     slab = width // 8
-    whole = lambda a: pl.BlockSpec(a.shape, lambda i, at: (0, 0))
-    stack = lambda a: pl.BlockSpec(a.shape, lambda i, at: (0, 0, 0))
+    whole = lambda a: pl.BlockSpec(a.shape, lambda i: (0, 0))
+    stack = lambda a: pl.BlockSpec(a.shape, lambda i: (0, 0, 0))
     pieces = jax.ShapeDtypeStruct((8, slab + PAD, count), b16)
     return call(
-        lambda *refs: own_kernel(rows, group_bias.shape[0], *refs),
+        lambda *refs: own_kernel(rows, group_bias.shape[0] - 1, *refs),
         [jax.ShapeDtypeStruct((height, count), b16), pieces],
-        places,
+        None,
         [group_bias, img, turned, txt, other, other_slopes, other_sum],
         in_specs=[
             pl.BlockSpec(memory_space=pltpu.SMEM),
             whole(img),
             whole(turned),
-            pl.BlockSpec((width + PAD, tile), lambda i, at: (0, i)),
-            pl.BlockSpec((width + PAD, tile), lambda i, at: (0, i)),
-            pl.BlockSpec((1, count, tile), lambda i, at: (i, 0, 0)),
+            pl.BlockSpec((width + PAD, tile), lambda i: (0, i)),
+            pl.BlockSpec((width + PAD, tile), lambda i: (0, i)),
+            pl.BlockSpec((1, count, tile), lambda i: (i, 0, 0)),
             whole(other_sum),
         ],
-        out_specs=[pl.BlockSpec((height, tile), lambda i, at: (0, i)), stack(pieces)],
+        out_specs=[pl.BlockSpec((height, tile), lambda i: (0, i)), stack(pieces)],
         grid=(4,),
         scratch=[
             pltpu.VMEM((count, min(128, tile)), f32),
@@ -384,7 +384,9 @@
     )
 
 
-def img_grad_kernel(rows, at_ref, got, unit, norm, feats, blocks, part, grad):
+def img_grad_kernel(rows, at_ref, got, unit, norm, feats_from, blocks, part, grad, feats, sem):
+    copy = pltpu.make_async_copy(feats_from, feats, sem.at[0])
+    copy.start()
     slab = unit.shape[0]
     up, inner = got[0, :slab].astype(f32), joined(got[0, slab:])
     for n in range(1, 8):
@@ -393,13 +395,18 @@
     grad[...] = (up * (1.0 / norm[...])).astype(b16)
     for n in range(8):
         blocks[n] = grad[:, n * rows : (n + 1) * rows]
+    copy.wait()
     part[...] = dot(grad[...], feats[...], NN).astype(b16)
 
 
 def txt_grad_kernel(rows, at_ref, *refs):
-    terms, unit, norm, blocks, (own, give, part, grad) = (
+    terms, unit, norm, sources, (own, give, part, grad, feats, sem) = (
         refs[:5], refs[5], refs[6], refs[7:15], refs[15:]
     )
+    blocks = [feats.at[n] for n in range(8)]
+    copies = [pltpu.make_async_copy(sources[n], blocks[n], sem.at[n]) for n in range(8)]
+    for copy in copies:
+        copy.start()
     slab = unit.shape[0]
     up, inner = terms[0][:slab].astype(f32), joined(terms[0][slab:])
     for term in terms[1:]:
@@ -411,6 +418,8 @@
         high = grad[:, (2 * ring + 1) * rows : (2 * ring + 2) * rows]
         own[ring] = jnp.where(at_ref[1] == 0, low, high)
         give[ring] = jnp.where(at_ref[1] == 0, high, low)
+    for copy in copies:
+        copy.wait()
     total = None
     for d in range(4):
         cols = grad[:, aligned((at_ref[0] + d) % 4, 2 * rows)]
@@ -433,16 +442,20 @@
         [term[0] if isinstance(term, tuple) else term for term in terms] + [unit, norm, *feats],
         in_specs=[mine(slab + PAD) if isinstance(term, tuple) else whole(term) for term in terms]
         + [mine(slab), whole(norm)]
-        + [whole(a) for a in feats],
+        + [pl.BlockSpec(memory_space=pl.ANY)] * len(feats),
         out_specs=[whole(block)] * halves + [whole(part)],
         grid=(1,),
-        scratch=[pltpu.VMEM((slab, count), b16)],
+        scratch=[
+            pltpu.VMEM((slab, count), b16),
+            pltpu.VMEM(((len(feats),) if len(feats) > 1 else ()) + feats[0].shape, b16),
+            pltpu.SemaphoreType.DMA((len(feats),)),
+        ],
         cost=2 * slab * count * width,
         weight=0,
     )
 
 
-def pick_kernel(at_ref, img, txt, other_img, other_txt, out):
+def pick_kernel(core, img, txt, other_img, other_txt, out):
     width = img.shape[1]
     slots = out.shape[0]
     own = width // 128
@@ -452,7 +465,7 @@
     part = jnp.concatenate([img, txt], axis=0).astype(b16)
     slot = lax.broadcasted_iota(jnp.int32, (slots, 1), 0)
     feature = lax.broadcasted_iota(jnp.int32, (slots, width), 1)
-    base = (slot // 8 * 2 + at_ref[4]) * own
+    base = (slot // 8 * 2 + core[0]) * own
     chosen = jnp.where(feature == base + slot % 8, 1.0, 0.0).astype(b16)
     out[:, : 3 * third] = dot(chosen, part, NT).astype(b16)
     chosen = jnp.where(feature == base + 8, 1.0, 0.0).astype(b16)
@@ -463,19 +476,21 @@
     out[:, 3 * third :] = rest.astype(b16)
 
 
-def picked(parts, places):
+def picked(core, parts):
     slab, width = parts[0].shape
     return call(
         pick_kernel,
         jax.ShapeDtypeStruct((64 * 8, slab * 8 // 3), b16),
-        places,
-        parts,
+        None,
+        [core, *parts],
+        in_specs=[pl.BlockSpec(memory_space=pltpu.SMEM)]
+        + [pl.BlockSpec(memory_space=pltpu.VMEM)] * len(parts),
         cost=8 * 512 * width * slab,
         weight=0,
     )
 
 
-def head_kernel(at_ref, got, img_out, txt_out):
+def head_kernel(got, img_out, txt_out):
     slab = img_out.shape[1] // 8
     third = slab * 2 // 3
     half = third // 2
@@ -524,7 +539,10 @@
 
     slots = [(y + d) % 4 * 2 + (hi + e) % 2 for d in range(4) for e in range(2)]
     places = [y, hi, z, lo, core, place % 16, z * 2 + lo, y * 2 + hi, *slots]
-    (places,) = together([jnp.stack(places).astype(jnp.int32)])
+    biases = jnp.append(group_bias, (place % 16).astype(f32))
+    places, biases, alone = together(
+        [jnp.stack(places).astype(jnp.int32), biases, core.astype(jnp.int32).reshape(1)]
+    )
     figures = jnp.stack([text_lang, partner // 128, partner % 128]).astype(b16)
     figures = jnp.pad(figures, ((0, PAD - 3), (0, width - rows)))
     text_rows = jnp.concatenate([text_feat, figures], axis=0)
@@ -533,10 +551,12 @@
     across = send(text_rows, txt_move(0, 1))
     before = send(text_rows, txt_move(1, 0))
     after = send(text_rows, txt_move(3, 0))
-    across, turned_txt = together([across, text_head.T])
+    turned_txt = together([text_head, before])[0].T
     across_after = send(across, txt_move(3, 0))
     across_before = send(across, txt_move(1, 0))
-    across_after, before, after, across = together([across_after, before, after, across])
+    across_after, before, after, across, turned_txt = together(
+        [across_after, before, after, across, turned_txt]
+    )
     far = send(before, txt_move(1, 0))
     across_far = send(across_after, txt_move(3, 0))
     txt_blocks = [
@@ -550,12 +570,11 @@
     unit_img = unit_rows(together([img_feats, unit_txt])[0], image_head, norm_img)
 
     other_slopes, other_sum, other_up = other_tile(
-        unit_img, turned_units, other_txt, group_bias, places, rows
+        unit_img, turned_units, other_txt, biases, rows
     )
     back = send(other_up, core_move)
     text_up, img_terms = own_tile(
-        unit_img, turned_units, unit_txt, other_txt, other_slopes, other_sum, group_bias,
-        places, rows,
+        unit_img, turned_units, unit_txt, other_txt, other_slopes, other_sum, biases, rows
     )
     img_terms = exchange(img_terms, IMG_GROUPS)
 
@@ -592,10 +611,10 @@
     img_theirs = send(img_part, core_move)
     txt_theirs = send(txt_part, core_move)
     txt_got = send(txt_give, txt_move(0, 1))
-    heads, txt_got = together([picked([img_part, txt_part, img_theirs, txt_theirs], places), txt_got])
+    heads, txt_got = together([picked(alone, [img_part, txt_part, img_theirs, txt_theirs]), txt_got])
     heads = exchange(heads.reshape(64, 8, -1), CHIP_GROUPS)
     head_shape = jax.ShapeDtypeStruct((width // 128, width), f32)
-    image_head_grad, text_head_grad = call(head_kernel, [head_shape] * 2, places, [heads])
+    image_head_grad, text_head_grad = call(head_kernel, [head_shape] * 2, None, [heads])
 
     image_grad = dot(grad_img, image_head, (((0,), (1,)), ((), ())))
     grad_txt = whole_columns(pair_lines(txt_own, txt_got, hi), txt_move, y)

time: 185 us -> 184 us (level)
    optimization_barrier x0 -> x1, local copies, waits for them, and re-layouts: none -> 5.23 us  [together(): return lax.optimization_barrier(list(arrays))]
    unnamed x40 -> x41, local copies, waits for them, and re-layouts: 9.15 us -> 3.93 us
  transfers between devices with their start and end apart: 26 -> 26, of which waited for: 7 -> 7; matrix products, arithmetic and copies ran while one was open for 13% -> 14% of each run, Pallas kernels for 30% -> 30%
where the time goes in v8:
time: 184 us; the launch traced here: 183 us
  Pallas kernels  68.4 us (37%)
  starting transfers between devices  56 us (30%)
  waiting for transfers between devices  26.2 us (14%)
  matrix products  15.1 us (8%)
  local copies, waits for them, and re-layouts  12.6 us (7%)
  other arithmetic  3.96 us (2%)
    pallas_call x11, Pallas kernels, call(): pl.pallas_call(body, out_shape=out_shape, grid_spec=spec, input_output_al...  68.4 us
    ppermute x22, starting transfers between devices, send(): lax.ppermute(block, DEV, [(flat(*p), flat(*move(*p))) for p in PLACES])  32.8 us
    ppermute x22, waiting for transfers between devices, send(): lax.ppermute(block, DEV, [(flat(*p), flat(*move(*p))) for p in PLACES])  26.2 us
    all_to_all x4, starting transfers between devices, exchange(): lax.all_to_all(blocks, DEV, 0, 0, axis_index_groups=groups, tiled=True)  23.1 us
    dot_general x4, matrix products, dot(): return lax.dot_general(a, b, dims, preferred_element_type=f32)  15.1 us
    optimization_barrier x1, local copies, waits for them, and re-layouts, together(): return lax.optimization_barrier(list(arrays))  5.23 us
    unnamed x41, local copies, waits for them, and re-layouts  3.93 us
  transfers between devices with their start and end apart: 26, of which 7 were waited for; matrix products, arithmetic and copies ran while one was open for 14% of the time, Pallas kernels for 30%

profile of v8, /device:TPU:1, one launch (start us, length us, event | category | flops | bytes accessed | tf_op | source)
XLA Modules:
  0.0 183.2 jit_solution(10837954624857389199)
XLA Ops:
  0.6 2.8 %broadcast_in_dim.2 = bf16[8,128,1152]{2,1,0:T(8,128)(2,1)} broadcast(bf16[128,1152]{1,0:T(8,128)(2,1)} %param.7), dimensions={1,2} | broadcast | bytes 2654208 | tf_op jit(solution)/shard_map/broadcast_in_dim | solution.py:549
  3.5 6.9 %all-to-all-start = ((bf16[8,128,1152]{2,1,0:T(8,128)(2,1)}), bf16[8,128,1152]{2,1,0:T(8,128)(2,1)}, u32[]{:S(2)}, u32[]{:S(2)}) async-start(bf16[8,128,1152]{2,1,0:T(8,128)(2,1)} %broadcast_in_dim.2), calls=%async_computation | async-start | bytes 4718592 | tf_op jit(solution)/shard_map/all_to_all | solution.py:65
  10.5 2.8 %collective-permute-start = (bf16[144,1152]{1,0:T(8,128)(2,1)S(1)}, bf16[144,1152]{1,0:T(8,128)(2,1)}, u32[]{:S(2)}, u32[]{:S(2)}) collective-permute-start(bf16[144,1152]{1,0:T(8,128)(2,1)S(1)} %pad_maximum_fusion.refs_3_.refs_8_), channel_id=1, source_target_pairs={{0,24},{1,25},{2,26},{3,27},{4,28},{5,29},{6,30},{7,31},{8,16},{9,... | collective-permute-start | bytes 995336 | tf_op jit(solution)/shard_map/ppermute | solution.py:61
  16.0 4.3 %collective-permute-done.refs_4_.refs_9_ = bf16[144,1152]{1,0:T(8,128)(2,1)} collective-permute-done((bf16[144,1152]{1,0:T(8,128)(2,1)S(1)}, bf16[144,1152]{1,0:T(8,128)(2,1)}, u32[]{:S(2)}, u32[]{:S(2)}) %collective-permute-start) | collective-permute-done | bytes 331808 | tf_op jit(solution)/shard_map/ppermute | solution.py:61
  20.3 2.7 %collective-permute-start.1 = (bf16[144,1152]{1,0:T(8,128)(2,1)}, bf16[144,1152]{1,0:T(8,128)(2,1)}, u32[]{:S(2)}, u32[]{:S(2)}) collective-permute-start(bf16[144,1152]{1,0:T(8,128)(2,1)} %collective-permute-done.refs_4_.refs_9_), channel_id=1, source_target_pairs={{0,6},{1,7},{2,0},{3,1},{4,2},{5,3},{6,4},{7,5},{8,14},{9,15},{10,... | collective-permute-start | bytes 995336 | tf_op jit(solution)/shard_map/ppermute | solution.py:61
  23.0 5.2 %copy.13 = bf16[1152,1152]{0,1:T(8,128)(2,1)} copy(bf16[1152,1152]{1,0:T(8,128)(2,1)} %param.10) | data formatting | bytes 5308416 | tf_op jit(solution)/shard_map/optimization_barrier | solution.py:517
  28.3 2.2 %collective-permute-done.1.refs_6_.refs_11_ = bf16[144,1152]{1,0:T(8,128)(2,1)} collective-permute-done((bf16[144,1152]{1,0:T(8,128)(2,1)}, bf16[144,1152]{1,0:T(8,128)(2,1)}, u32[]{:S(2)}, u32[]{:S(2)}) %collective-permute-start.1) | collective-permute-done | bytes 331808 | tf_op jit(solution)/shard_map/ppermute | solution.py:61
  34.5 7.6 %shard_map.102 = (bf16[1168,1024]{1,0:T(8,128)(2,1)}, f32[1,1024]{1,0:T(1,128)}) custom-call(s32[16]{0:T(128)} %stack.83.refs_0_, bf16[144,1152]{1,0:T(8,128)(2,1)} %collective-permute-done.2.refs_1_.refs_14_, bf16[144,1152]{1,0:T(8,128)(2,1)} %collective-permute-done.6.refs_2_.refs_15_, bf16[144,1152]{1,0:T(8,128)(2,1)} %copy-done.5, ...), custom_call_target="tpu_custom_call" | custom-call | flops 2038431744 | bytes 4644864 | tf_op jit(solution)/shard_map/pallas_call | solution.py:93
  42.9 4.7 %shard_map.103 = (bf16[1168,1024]{1,0:T(8,128)(2,1)}, f32[1,1024]{1,0:T(1,128)}) custom-call(s32[16]{0:T(128)} %stack.83.refs_0_, bf16[144,1152]{1,0:T(8,128)(2,1)} %copy-done.3, bf16[144,1152]{1,0:T(8,128)(2,1)} %copy-done.4, bf16[1152,1152]{1,0:T(8,128)(2,1)} %bitcast.48, ...), custom_call_target="tpu_custom_call", output_to_operand_aliasing={{0}: (4, {}), {1}: (5, {})} | custom-call | flops 679477248 | bytes 5713920 | tf_op jit(solution)/shard_map/pallas_call | solution.py:93
  47.6 2.1 %collective-permute-start.7 = (bf16[1168,1024]{1,0:T(8,128)(2,1)}, bf16[1168,1024]{1,0:T(8,128)(2,1)}, u32[]{:S(2)}, u32[]{:S(2)}) collective-permute-start(bf16[1168,1024]{1,0:T(8,128)(2,1)} %get-tuple-element.55.refs_3_.refs_6_), channel_id=1, source_target_pairs={{0,1},{1,0},{2,3},{3,2},{4,5},{5,4},{6,7},{7,6},{8,9},{9,8},{10,11... | collective-permute-start | bytes 7176200 | tf_op jit(solution)/shard_map/ppermute | solution.py:61
  49.7 5.0 %multiply_reduce_fusion = (f32[1024]{0:T(1024)S(1)}, f32[1152,1024]{1,0:T(8,128)S(1)}) fusion(bf16[1152,1152]{1,0:T(8,128)(2,1)S(1)} %copy-done, bf16[1024,1152]{1,0:T(8,128)(2,1)} %bitcast.17.refs_4_), kind=kOutput, calls=%fused_computation.2 | convolution fusion | flops 2720267264 | bytes 9736192 | tf_op jit(solution)/shard_map/dot_general | solution.py:75
  54.7 6.6 %divide_convert_fusion.1.refs_1_ = bf16[1024,1152]{1,0:T(8,128)(2,1)} fusion(bf16[1024,1152]{1,0:T(8,128)(2,1)} %bitcast.17.refs_4_, bf16[1152,1152]{1,0:T(8,128)(2,1)S(1)} %copy-done, f32[1024]{0:T(1024)S(1)} %add_sqrt_fusion), kind=kOutput, calls=%fused_computation.1 | convolution fusion | flops 2720268288 | bytes 7376896 | tf_op jit(solution)/shard_map/dot_general | solution.py:75
  63.4 12.2 %shard_map.104 = (bf16[4,1024,256]{2,1,0:T(8,128)(2,1)}, f32[1,1024]{1,0:T(1,128)}, bf16[1280,1024]{1,0:T(8,128)(2,1)}) custom-call(f32[33]{0:T(128)} %pad_maximum_fusion.1.refs_0_, bf16[1024,1152]{1,0:T(8,128)(2,1)} %divide_convert_fusion.1.refs_1_, bf16[1152,1024]{1,0:T(8,128)(2,1)} %divide_convert_fusion.refs_2_, ...), custom_call_target="tpu_custom_call" | custom-call | flops 4831838208 | bytes 7110788 | tf_op jit(solution)/shard_map/pallas_call | solution.py:93
  75.5 18.5 %shard_map.105 = (bf16[1280,1024]{1,0:T(8,128)(2,1)}, bf16[8,160,1024]{2,1,0:T(8,128)(2,1)}) custom-call(f32[33]{0:T(128)} %pad_maximum_fusion.1.refs_0_, bf16[1024,1152]{1,0:T(8,128)(2,1)} %divide_convert_fusion.1.refs_1_, bf16[1152,1024]{1,0:T(8,128)(2,1)} %divide_convert_fusion.refs_2_, bf16[1168,1024]{1,0:T(8,128)(2,1)} %get-tuple-element.55.refs_3_.refs_6_, ...), custom_call_target="tpu_custom_call" | custom-call | flops 9663676416 | bytes 11604100 | tf_op jit(solution)/shard_map/pallas_call | solution.py:93
  94.1 4.6 %all-to-all-start.1 = ((bf16[8,160,1024]{2,1,0:T(8,128)(2,1)}), bf16[8,160,1024]{2,1,0:T(8,128)(2,1)}, u32[]{:S(2)}, u32[]{:S(2)}) async-start(bf16[8,160,1024]{2,1,0:T(8,128)(2,1)} %get-tuple-element.59), calls=%async_computation.1 | async-start | bytes 5242880 | tf_op jit(solution)/shard_map/all_to_all | solution.py:65
  98.7 3.1 %shard_map.107 = (bf16[160,1024]{1,0:T(8,128)(2,1)}, bf16[160,1024]{1,0:T(8,128)(2,1)}, bf16[160,1024]{1,0:T(8,128)(2,1)}) custom-call(s32[16]{0:T(128)} %stack.83.refs_0_, bf16[1280,1024]{1,0:T(8,128)(2,1)} %get-tuple-element.63.refs_1_.refs_3_.refs_5_.refs_4_.refs_7_, bf16[1280,1024]{1,0:T(8,128)(2,1)} %collective-permute-done.8.refs_2_.refs_4_.refs_6_.refs_5_.refs_8_, ...), custom_call_target="tpu_custom_call" | custom-call | bytes 15728640 | tf_op jit(solution)/shard_map/pallas_call | solution.py:93
  102.0 2.6 %collective-permute-start.10 = (bf16[160,1024]{1,0:T(8,128)(2,1)}, bf16[160,1024]{1,0:T(8,128)(2,1)S(1)}, u32[]{:S(2)}, u32[]{:S(2)}) collective-permute-start(bf16[160,1024]{1,0:T(8,128)(2,1)} %get-tuple-element.66), channel_id=1, source_target_pairs={{0,6},{1,7},{2,0},{3,1},{4,2},{5,3},{6,4},{7,5},{8,14},{9,15},{10,... | collective-permute-start | bytes 983048 | tf_op jit(solution)/shard_map/ppermute | solution.py:61
  104.5 7.6 %collective-permute-done.9.refs_6_ = bf16[160,1024]{1,0:T(8,128)(2,1)S(1)} collective-permute-done((bf16[160,1024]{1,0:T(8,128)(2,1)}, bf16[160,1024]{1,0:T(8,128)(2,1)S(1)}, u32[]{:S(2)}, u32[]{:S(2)}) %collective-permute-start.9) | collective-permute-done | bytes 327712 | tf_op jit(solution)/shard_map/ppermute | solution.py:61
  113.1 3.4 %shard_map.108 = (bf16[160,1024]{1,0:T(8,128)(2,1)}, bf16[160,1024]{1,0:T(8,128)(2,1)}, bf16[160,1024]{1,0:T(8,128)(2,1)}) custom-call(s32[16]{0:T(128)} %stack.83.refs_0_, bf16[1280,1024]{1,0:T(8,128)(2,1)} %get-tuple-element.63.refs_1_.refs_3_.refs_5_.refs_4_.refs_7_, bf16[1280,1024]{1,0:T(8,128)(2,1)} %collective-permute-done.8.refs_2_.refs_4_.refs_6_.refs_5_.refs_8_, ...), custom_call_target="tpu_custom_call" | custom-call | bytes 16384000 | tf_op jit(solution)/shard_map/pallas_call | solution.py:93
  116.5 2.3 %collective-permute-start.12 = (bf16[160,1024]{1,0:T(8,128)(2,1)}, bf16[160,1024]{1,0:T(8,128)(2,1)S(1)}, u32[]{:S(2)}, u32[]{:S(2)}) collective-permute-start(bf16[160,1024]{1,0:T(8,128)(2,1)} %get-tuple-element.71), channel_id=1, source_target_pairs={{0,6},{1,7},{2,0},{3,1},{4,2},{5,3},{6,4},{7,5},{8,14},{9,15},{10,... | collective-permute-start | bytes 983048 | tf_op jit(solution)/shard_map/ppermute | solution.py:61
  118.7 3.0 %collective-permute-done.11.refs_3_ = bf16[160,1024]{1,0:T(8,128)(2,1)S(1)} collective-permute-done((bf16[160,1024]{1,0:T(8,128)(2,1)}, bf16[160,1024]{1,0:T(8,128)(2,1)S(1)}, u32[]{:S(2)}, u32[]{:S(2)}) %collective-permute-start.11) | collective-permute-done | bytes 327712 | tf_op jit(solution)/shard_map/ppermute | solution.py:61
  121.8 2.9 %collective-permute-done.12.refs_4_ = bf16[160,1024]{1,0:T(8,128)(2,1)S(1)} collective-permute-done((bf16[160,1024]{1,0:T(8,128)(2,1)}, bf16[160,1024]{1,0:T(8,128)(2,1)S(1)}, u32[]{:S(2)}, u32[]{:S(2)}) %collective-permute-start.12) | collective-permute-done | bytes 327712 | tf_op jit(solution)/shard_map/ppermute | solution.py:61
  125.4 2.8 %shard_map.109 = bf16[160,1024]{1,0:T(8,128)(2,1)} custom-call(s32[16]{0:T(128)} %stack.83.refs_0_, bf16[1280,1024]{1,0:T(8,128)(2,1)} %get-tuple-element.63.refs_1_.refs_3_.refs_5_.refs_4_.refs_7_, bf16[1280,1024]{1,0:T(8,128)(2,1)} %collective-permute-done.8.refs_2_.refs_4_.refs_6_.refs_5_.refs_8_, bf16[160,1024]{1,0:T(8,128)(2,1)} %copy-done.8, ...), custom_call_target="tpu_custom_call" | custom-call | bytes 5898240 | tf_op jit(solution)/shard_map/pallas_call | solution.py:93
  130.4 2.6 %collective-permute-start.14 = (bf16[160,1024]{1,0:T(8,128)(2,1)}, bf16[160,1024]{1,0:T(8,128)(2,1)}, u32[]{:S(2)}, u32[]{:S(2)}) collective-permute-start(bf16[160,1024]{1,0:T(8,128)(2,1)} %get-tuple-element.75), channel_id=1, source_target_pairs={{0,6},{1,7},{2,0},{3,1},{4,2},{5,3},{6,4},{7,5},{8,14},{9,15},{10,... | collective-permute-start | bytes 983048 | tf_op jit(solution)/shard_map/ppermute | solution.py:61
  133.0 5.4 %shard_map.106 = (bf16[8,144,128]{2,1,0:T(8,128)(2,1)}, bf16[144,1152]{1,0:T(8,128)(2,1)}) custom-call(s32[16]{0:T(128)} %stack.83.refs_0_, bf16[8,160,1024]{2,1,0:T(8,128)(2,1)} %all-to-all-done.1.refs_1_, bf16[1152,1024]{1,0:T(8,128)(2,1)} %divide_convert_fusion.refs_2_, f32[1,1024]{1,0:T(1,128)} %bitcast.51, bf16[1024,1152]{1,0:T(8,128)(2,1)} %bitcast.17.refs_4_), custom_call_target="tpu_custom_call" | custom-call | tf_op jit(solution)/shard_map/pallas_call | solution.py:93
  138.3 3.7 %all-to-all-start.2 = ((bf16[8,144,128]{2,1,0:T(8,128)(2,1)}), bf16[8,144,128]{2,1,0:T(8,128)(2,1)S(1)}, u32[]{:S(2)}, u32[]{:S(2)}) async-start(bf16[8,144,128]{2,1,0:T(8,128)(2,1)} %get-tuple-element.60), calls=%async_computation.2 | async-start | bytes 589824 | tf_op jit(solution)/shard_map/all_to_all | solution.py:65
  142.0 4.0 %collective-permute-start.16 = (bf16[144,1152]{1,0:T(8,128)(2,1)}, bf16[144,1152]{1,0:T(8,128)(2,1)S(1)}, u32[]{:S(2)}, u32[]{:S(2)}) collective-permute-start(bf16[144,1152]{1,0:T(8,128)(2,1)} %get-tuple-element.62.img), channel_id=1, source_target_pairs={{0,1},{1,0},{2,3},{3,2},{4,5},{5,4},{6,7},{7,6},{8,9},{9,8},{10,11... | collective-permute-start | bytes 995336 | tf_op jit(solution)/shard_map/ppermute | solution.py:61
  146.0 5.2 %shard_map.110 = (bf16[4,144,128]{2,1,0:T(8,128)(2,1)}, bf16[4,144,128]{2,1,0:T(8,128)(2,1)}, bf16[144,1152]{1,0:T(8,128)(2,1)}) custom-call(s32[16]{0:T(128)} %stack.83.refs_0_, bf16[1280,1024]{1,0:T(8,128)(2,1)} %get-tuple-element.63.refs_1_.refs_3_.refs_5_.refs_4_.refs_7_, ...), custom_call_target="tpu_custom_call" | custom-call | tf_op jit(solution)/shard_map/pallas_call | solution.py:93
  155.7 3.7 %shard_map.111 = bf16[512,384]{1,0:T(8,128)(2,1)} custom-call(s32[1]{0:T(128)} %bitcast.4.core, bf16[144,1152]{1,0:T(8,128)(2,1)} %get-tuple-element.62.img, bf16[144,1152]{1,0:T(8,128)(2,1)} %get-tuple-element.79.txt, bf16[144,1152]{1,0:T(8,128)(2,1)} %copy-done.7, bf16[144,1152]{1,0:T(8,128)(2,1)} %collective-permute-done.17.other_txt), custom_call_target="tpu_custom_call" | custom-call | tf_op jit(solution)/shard_map/pallas_call | solution.py:93
  159.4 7.9 %all-to-all-start.3 = ((bf16[64,8,384]{2,1,0:T(8,128)(2,1)}), bf16[64,8,384]{2,1,0:T(8,128)(2,1)S(1)}, u32[]{:S(2)}, u32[]{:S(2)}) async-start(bf16[64,8,384]{2,1,0:T(8,128)(2,1)} %bitcast.49), calls=%async_computation.3 | async-start | bytes 786432 | tf_op jit(solution)/shard_map/all_to_all | solution.py:65
  172.6 2.6 %collective-permute-done.19 = bf16[288,128]{1,0:T(8,128)(2,1)S(1)} collective-permute-done((bf16[288,128]{1,0:T(8,128)(2,1)S(1)}, bf16[288,128]{1,0:T(8,128)(2,1)S(1)}, u32[]{:S(2)}, u32[]{:S(2)}) %collective-permute-start.19) | collective-permute-done | bytes 73760 | tf_op jit(solution)/shard_map/ppermute | solution.py:61
  175.2 3.5 %collective-permute-done.20 = bf16[288,128]{1,0:T(8,128)(2,1)S(1)} collective-permute-done((bf16[288,128]{1,0:T(8,128)(2,1)S(1)}, bf16[288,128]{1,0:T(8,128)(2,1)S(1)}, u32[]{:S(2)}, u32[]{:S(2)}) %collective-permute-start.20) | collective-permute-done | bytes 73760 | tf_op jit(solution)/shard_map/ppermute | solution.py:61
  (90 shorter events, 27.7 us)
Async XLA Ops:
  0.6 49.1 %copy-start = (bf16[1152,1152]{1,0:T(8,128)(2,1)S(1)}, bf16[1152,1152]{1,0:T(8,128)(2,1)}, u32[]{:S(2)}) copy-start(bf16[1152,1152]{1,0:T(8,128)(2,1)} %param.9) | copy-start | bytes 7962628
  3.5 7.0 %copy-start.12 = (bf16[128,1152]{1,0:T(8,128)(2,1)S(1)}, bf16[128,1152]{1,0:T(8,128)(2,1)}, u32[]{:S(2)}) copy-start(bf16[128,1152]{1,0:T(8,128)(2,1)} %param.8) | copy-start | bytes 884740
  3.5 46.2 %all-to-all-start = ((bf16[8,128,1152]{2,1,0:T(8,128)(2,1)}), bf16[8,128,1152]{2,1,0:T(8,128)(2,1)}, u32[]{:S(2)}, u32[]{:S(2)}) async-start(bf16[8,128,1152]{2,1,0:T(8,128)(2,1)} %broadcast_in_dim.2), calls=%async_computation | async-start | bytes 4718592 | tf_op jit(solution)/shard_map/all_to_all | solution.py:65
  10.5 17.8 %copy-start.5 = (bf16[144,1152]{1,0:T(8,128)(2,1)}, bf16[144,1152]{1,0:T(8,128)(2,1)S(1)}, u32[]{:S(2)}) copy-start(bf16[144,1152]{1,0:T(8,128)(2,1)S(1)} %pad_maximum_fusion.refs_3_.refs_8_) | copy-start | bytes 995332
  10.5 23.3 %copy-start.17 = (f32[32]{0:T(128)S(1)}, f32[32]{0:T(128)}, u32[]{:S(2)}) copy-start(f32[32]{0:T(128)} %param.11) | copy-start | bytes 388
  10.5 9.8 %collective-permute-start = (bf16[144,1152]{1,0:T(8,128)(2,1)S(1)}, bf16[144,1152]{1,0:T(8,128)(2,1)}, u32[]{:S(2)}, u32[]{:S(2)}) collective-permute-start(bf16[144,1152]{1,0:T(8,128)(2,1)S(1)} %pad_maximum_fusion.refs_3_.refs_8_), channel_id=1, source_target_pairs={{0,24},{1,25},{2,26},{3,27},{4,28},{5,29},{6,30},{7,31},{8,16},{9,... | collective-permute-start | bytes 995336 | tf_op jit(solution)/shard_map/ppermute | solution.py:61
  13.3 9.7 %collective-permute-start.2 = (bf16[144,1152]{1,0:T(8,128)(2,1)S(1)}, bf16[144,1152]{1,0:T(8,128)(2,1)}, u32[]{:S(2)}, u32[]{:S(2)}) collective-permute-start(bf16[144,1152]{1,0:T(8,128)(2,1)S(1)} %pad_maximum_fusion.refs_3_.refs_8_), channel_id=1, source_target_pairs={{0,2},{1,3},{2,4},{3,5},{4,6},{5,7},{6,0},{7,1},{8,10},{9,11},{10,... | collective-permute-start | bytes 995336 | tf_op jit(solution)/shard_map/ppermute | solution.py:61
  14.6 13.7 %collective-permute-start.3 = (bf16[144,1152]{1,0:T(8,128)(2,1)S(1)}, bf16[144,1152]{1,0:T(8,128)(2,1)S(1)}, u32[]{:S(2)}, u32[]{:S(2)}) collective-permute-start(bf16[144,1152]{1,0:T(8,128)(2,1)S(1)} %pad_maximum_fusion.refs_3_.refs_8_), channel_id=1, source_target_pairs={{0,6},{1,7},{2,0},{3,1},{4,2},{5,3},{6,4},{7,5},{8,14},{9,15},{10,... | collective-permute-start | bytes 995336 | tf_op jit(solution)/shard_map/ppermute | solution.py:61
  20.3 10.2 %collective-permute-start.1 = (bf16[144,1152]{1,0:T(8,128)(2,1)}, bf16[144,1152]{1,0:T(8,128)(2,1)}, u32[]{:S(2)}, u32[]{:S(2)}) collective-permute-start(bf16[144,1152]{1,0:T(8,128)(2,1)} %collective-permute-done.refs_4_.refs_9_), channel_id=1, source_target_pairs={{0,6},{1,7},{2,0},{3,1},{4,2},{5,3},{6,4},{7,5},{8,14},{9,15},{10,... | collective-permute-start | bytes 995336 | tf_op jit(solution)/shard_map/ppermute | solution.py:61
  23.0 11.4 %collective-permute-start.6 = (bf16[144,1152]{1,0:T(8,128)(2,1)}, bf16[144,1152]{1,0:T(8,128)(2,1)}, u32[]{:S(2)}, u32[]{:S(2)}) collective-permute-start(bf16[144,1152]{1,0:T(8,128)(2,1)} %collective-permute-done.refs_4_.refs_9_), channel_id=1, source_target_pairs={{0,2},{1,3},{2,4},{3,5},{4,6},{5,7},{6,0},{7,1},{8,10},{9,11},{10,... | collective-permute-start | bytes 995336 | tf_op jit(solution)/shard_map/ppermute | solution.py:61
  30.5 11.6 %collective-permute-start.4 = (bf16[144,1152]{1,0:T(8,128)(2,1)}, bf16[144,1152]{1,0:T(8,128)(2,1)S(1)}, u32[]{:S(2)}, u32[]{:S(2)}) collective-permute-start(bf16[144,1152]{1,0:T(8,128)(2,1)} %collective-permute-done.2.refs_1_.refs_14_), channel_id=1, source_target_pairs={{0,2},{1,3},{2,4},{3,5},{4,6},{5,7},{6,0},{7,1},{8,10},{9,11},{10,... | collective-permute-start | bytes 995336 | tf_op jit(solution)/shard_map/ppermute | solution.py:61
  31.8 10.3 %collective-permute-start.5 = (bf16[144,1152]{1,0:T(8,128)(2,1)}, bf16[144,1152]{1,0:T(8,128)(2,1)S(1)}, u32[]{:S(2)}, u32[]{:S(2)}) collective-permute-start(bf16[144,1152]{1,0:T(8,128)(2,1)} %collective-permute-done.1.refs_6_.refs_11_), channel_id=1, source_target_pairs={{0,6},{1,7},{2,0},{3,1},{4,2},{5,3},{6,4},{7,5},{8,14},{9,15},{10,... | collective-permute-start | bytes 995336 | tf_op jit(solution)/shard_map/ppermute | solution.py:61
  47.6 15.8 %collective-permute-start.7 = (bf16[1168,1024]{1,0:T(8,128)(2,1)}, bf16[1168,1024]{1,0:T(8,128)(2,1)}, u32[]{:S(2)}, u32[]{:S(2)}) collective-permute-start(bf16[1168,1024]{1,0:T(8,128)(2,1)} %get-tuple-element.55.refs_3_.refs_6_), channel_id=1, source_target_pairs={{0,1},{1,0},{2,3},{3,2},{4,5},{5,4},{6,7},{7,6},{8,9},{9,8},{10,11... | collective-permute-start | bytes 7176200 | tf_op jit(solution)/shard_map/ppermute | solution.py:61
  75.5 23.2 %collective-permute-start.8 = (bf16[1280,1024]{1,0:T(8,128)(2,1)}, bf16[1280,1024]{1,0:T(8,128)(2,1)}, u32[]{:S(2)}, u32[]{:S(2)}) collective-permute-start(bf16[1280,1024]{1,0:T(8,128)(2,1)} %get-tuple-element.64), channel_id=1, source_target_pairs={{0,1},{1,0},{2,3},{3,2},{4,5},{5,4},{6,7},{7,6},{8,9},{9,8},{10,11... | collective-permute-start | bytes 7864328 | tf_op jit(solution)/shard_map/ppermute | solution.py:61
  94.1 38.9 %all-to-all-start.1 = ((bf16[8,160,1024]{2,1,0:T(8,128)(2,1)}), bf16[8,160,1024]{2,1,0:T(8,128)(2,1)}, u32[]{:S(2)}, u32[]{:S(2)}) async-start(bf16[8,160,1024]{2,1,0:T(8,128)(2,1)} %get-tuple-element.59), calls=%async_computation.1 | async-start | bytes 5242880 | tf_op jit(solution)/shard_map/all_to_all | solution.py:65
  101.8 10.3 %collective-permute-start.9 = (bf16[160,1024]{1,0:T(8,128)(2,1)}, bf16[160,1024]{1,0:T(8,128)(2,1)S(1)}, u32[]{:S(2)}, u32[]{:S(2)}) collective-permute-start(bf16[160,1024]{1,0:T(8,128)(2,1)} %get-tuple-element.65), channel_id=1, source_target_pairs={{0,2},{1,3},{2,4},{3,5},{4,6},{5,7},{6,0},{7,1},{8,10},{9,11},{10,... | collective-permute-start | bytes 983048 | tf_op jit(solution)/shard_map/ppermute | solution.py:61
  102.0 10.2 %collective-permute-start.10 = (bf16[160,1024]{1,0:T(8,128)(2,1)}, bf16[160,1024]{1,0:T(8,128)(2,1)S(1)}, u32[]{:S(2)}, u32[]{:S(2)}) collective-permute-start(bf16[160,1024]{1,0:T(8,128)(2,1)} %get-tuple-element.66), channel_id=1, source_target_pairs={{0,6},{1,7},{2,0},{3,1},{4,2},{5,3},{6,4},{7,5},{8,14},{9,15},{10,... | collective-permute-start | bytes 983048 | tf_op jit(solution)/shard_map/ppermute | solution.py:61
  112.2 9.6 %collective-permute-start.11 = (bf16[160,1024]{1,0:T(8,128)(2,1)}, bf16[160,1024]{1,0:T(8,128)(2,1)S(1)}, u32[]{:S(2)}, u32[]{:S(2)}) collective-permute-start(bf16[160,1024]{1,0:T(8,128)(2,1)} %get-tuple-element.68), channel_id=1, source_target_pairs={{0,2},{1,3},{2,4},{3,5},{4,6},{5,7},{6,0},{7,1},{8,10},{9,11},{10,... | collective-permute-start | bytes 983048 | tf_op jit(solution)/shard_map/ppermute | solution.py:61
  116.5 8.2 %collective-permute-start.12 = (bf16[160,1024]{1,0:T(8,128)(2,1)}, bf16[160,1024]{1,0:T(8,128)(2,1)S(1)}, u32[]{:S(2)}, u32[]{:S(2)}) collective-permute-start(bf16[160,1024]{1,0:T(8,128)(2,1)} %get-tuple-element.71), channel_id=1, source_target_pairs={{0,6},{1,7},{2,0},{3,1},{4,2},{5,3},{6,4},{7,5},{8,14},{9,15},{10,... | collective-permute-start | bytes 983048 | tf_op jit(solution)/shard_map/ppermute | solution.py:61
  128.2 17.8 %collective-permute-start.15 = (bf16[160,1024]{1,0:T(8,128)(2,1)}, bf16[160,1024]{1,0:T(8,128)(2,1)}, u32[]{:S(2)}, u32[]{:S(2)}) collective-permute-start(bf16[160,1024]{1,0:T(8,128)(2,1)} %shard_map.109), channel_id=1, source_target_pairs={{0,24},{1,25},{2,26},{3,27},{4,28},{5,29},{6,30},{7,31},{8,16},{9,... | collective-permute-start | bytes 983048 | tf_op jit(solution)/shard_map/ppermute | solution.py:61
  129.7 16.3 %collective-permute-start.13 = (bf16[160,1024]{1,0:T(8,128)(2,1)}, bf16[160,1024]{1,0:T(8,128)(2,1)}, u32[]{:S(2)}, u32[]{:S(2)}) collective-permute-start(bf16[160,1024]{1,0:T(8,128)(2,1)} %get-tuple-element.74), channel_id=1, source_target_pairs={{0,2},{1,3},{2,4},{3,5},{4,6},{5,7},{6,0},{7,1},{8,10},{9,11},{10,... | collective-permute-start | bytes 983048 | tf_op jit(solution)/shard_map/ppermute | solution.py:61
  130.4 15.6 %collective-permute-start.14 = (bf16[160,1024]{1,0:T(8,128)(2,1)}, bf16[160,1024]{1,0:T(8,128)(2,1)}, u32[]{:S(2)}, u32[]{:S(2)}) collective-permute-start(bf16[160,1024]{1,0:T(8,128)(2,1)} %get-tuple-element.75), channel_id=1, source_target_pairs={{0,6},{1,7},{2,0},{3,1},{4,2},{5,3},{6,4},{7,5},{8,14},{9,15},{10,... | collective-permute-start | bytes 983048 | tf_op jit(solution)/shard_map/ppermute | solution.py:61
  138.3 14.9 %all-to-all-start.2 = ((bf16[8,144,128]{2,1,0:T(8,128)(2,1)}), bf16[8,144,128]{2,1,0:T(8,128)(2,1)S(1)}, u32[]{:S(2)}, u32[]{:S(2)}) async-start(bf16[8,144,128]{2,1,0:T(8,128)(2,1)} %get-tuple-element.60), calls=%async_computation.2 | async-start | bytes 589824 | tf_op jit(solution)/shard_map/all_to_all | solution.py:65
  142.0 13.0 %collective-permute-start.16 = (bf16[144,1152]{1,0:T(8,128)(2,1)}, bf16[144,1152]{1,0:T(8,128)(2,1)S(1)}, u32[]{:S(2)}, u32[]{:S(2)}) collective-permute-start(bf16[144,1152]{1,0:T(8,128)(2,1)} %get-tuple-element.62.img), channel_id=1, source_target_pairs={{0,1},{1,0},{2,3},{3,2},{4,5},{5,4},{6,7},{7,6},{8,9},{9,8},{10,11... | collective-permute-start | bytes 995336 | tf_op jit(solution)/shard_map/ppermute | solution.py:61
  151.2 3.8 %collective-permute-start.17 = (bf16[144,1152]{1,0:T(8,128)(2,1)}, bf16[144,1152]{1,0:T(8,128)(2,1)}, u32[]{:S(2)}, u32[]{:S(2)}) collective-permute-start(bf16[144,1152]{1,0:T(8,128)(2,1)} %get-tuple-element.79.txt), channel_id=1, source_target_pairs={{0,1},{1,0},{2,3},{3,2},{4,5},{5,4},{6,7},{7,6},{8,9},{9,8},{10,11... | collective-permute-start | bytes 995336 | tf_op jit(solution)/shard_map/ppermute | solution.py:61
  151.4 8.0 %collective-permute-start.18 = (bf16[4,144,128]{2,1,0:T(8,128)(2,1)}, bf16[4,144,128]{2,1,0:T(8,128)(2,1)}, u32[]{:S(2)}, u32[]{:S(2)}) collective-permute-start(bf16[4,144,128]{2,1,0:T(8,128)(2,1)} %get-tuple-element.80), channel_id=1, source_target_pairs={{0,24},{1,25},{2,26},{3,27},{4,28},{5,29},{6,30},{7,31},{8,16},{9,... | collective-permute-start | bytes 442376 | tf_op jit(solution)/shard_map/ppermute | solution.py:61
  153.3 14.1 %copy-start.13 = (bf16[4,144,128]{2,1,0:T(8,128)(2,1)S(1)}, bf16[4,144,128]{2,1,0:T(8,128)(2,1)}, u32[]{:S(2)}) copy-start(bf16[4,144,128]{2,1,0:T(8,128)(2,1)} %get-tuple-element.82) | copy-start | bytes 442372
  159.4 21.2 %all-to-all-start.3 = ((bf16[64,8,384]{2,1,0:T(8,128)(2,1)}), bf16[64,8,384]{2,1,0:T(8,128)(2,1)S(1)}, u32[]{:S(2)}, u32[]{:S(2)}) async-start(bf16[64,8,384]{2,1,0:T(8,128)(2,1)} %bitcast.49), calls=%async_computation.3 | async-start | bytes 786432 | tf_op jit(solution)/shard_map/all_to_all | solution.py:65
  167.4 11.5 %copy-start.1 = (bf16[1152,1152]{1,0:T(8,128)(2,1)S(1)}, bf16[1152,1152]{1,0:T(8,128)(2,1)}, u32[]{:S(2)}) copy-start(bf16[1152,1152]{1,0:T(8,128)(2,1)} %param.10) | copy-start | bytes 7962628
  168.5 10.2 %collective-permute-start.21 = (bf16[288,128]{1,0:T(8,128)(2,1)S(1)}, bf16[288,128]{1,0:T(8,128)(2,1)S(1)}, u32[]{:S(2)}, u32[]{:S(2)}) collective-permute-start(bf16[288,128]{1,0:T(8,128)(2,1)S(1)} %get-tuple-element.86), channel_id=1, source_target_pairs={{0,2},{1,3},{2,4},{3,5},{4,6},{5,7},{6,0},{7,1},{8,10},{9,11},{10,... | collective-permute-start | bytes 221192 | tf_op jit(solution)/shard_map/ppermute | solution.py:61
  169.6 5.6 %collective-permute-start.19 = (bf16[288,128]{1,0:T(8,128)(2,1)S(1)}, bf16[288,128]{1,0:T(8,128)(2,1)S(1)}, u32[]{:S(2)}, u32[]{:S(2)}) collective-permute-start(bf16[288,128]{1,0:T(8,128)(2,1)S(1)} %get-tuple-element.87), channel_id=1, source_target_pairs={{0,6},{1,7},{2,0},{3,1},{4,2},{5,3},{6,4},{7,5},{8,14},{9,15},{10,... | collective-permute-start | bytes 221192 | tf_op jit(solution)/shard_map/ppermute | solution.py:61
  171.3 7.4 %collective-permute-start.20 = (bf16[288,128]{1,0:T(8,128)(2,1)S(1)}, bf16[288,128]{1,0:T(8,128)(2,1)S(1)}, u32[]{:S(2)}, u32[]{:S(2)}) collective-permute-start(bf16[288,128]{1,0:T(8,128)(2,1)S(1)} %get-tuple-element.88), channel_id=1, source_target_pairs={{0,4},{1,5},{2,6},{3,7},{4,0},{5,1},{6,2},{7,3},{8,12},{9,13},{10,... | collective-permute-start | bytes 221192 | tf_op jit(solution)/shard_map/ppermute | solution.py:61
  (12 other events, 30.9 us)

commit v9 on v8

--- a/solution.py
+++ b/solution.py
@@ -186,11 +186,11 @@
 def unit_columns(feats, head):
     projected = dot(head, feats, (((0,), (1,)), ((), ())))
     norm = jnp.sqrt(jnp.sum(projected * projected, axis=0, keepdims=True) + epsilon)
-    return (projected / norm).astype(b16), norm
+    return (projected * (1.0 / norm)).astype(b16), norm
 
 
 def unit_rows(feats, head, norm):
-    return (dot(feats, head, NN) / norm.reshape(-1, 1)).astype(b16)
+    return (dot(feats, head, NN) * (1.0 / norm).reshape(-1, 1)).astype(b16)
 
 
 def tile_slopes(rows, groups, place, bias_ref, img, txt, slopes, by_img):
@@ -362,7 +362,7 @@
 
 def sums(groups, places, rows):
     arrays, specs = [], []
-    lanes = 4 * rows
+    lanes = 8 * rows
     for term in [term for group in groups for term in group]:
         if isinstance(term, tuple):
             arrays.append(term[0])
@@ -384,9 +384,7 @@
     )
 
 
-def img_grad_kernel(rows, at_ref, got, unit, norm, feats_from, blocks, part, grad, feats, sem):
-    copy = pltpu.make_async_copy(feats_from, feats, sem.at[0])
-    copy.start()
+def img_grad_kernel(rows, at_ref, got, unit, norm, feats, blocks, part, grad):
     slab = unit.shape[0]
     up, inner = got[0, :slab].astype(f32), joined(got[0, slab:])
     for n in range(1, 8):
@@ -395,18 +393,13 @@
     grad[...] = (up * (1.0 / norm[...])).astype(b16)
     for n in range(8):
         blocks[n] = grad[:, n * rows : (n + 1) * rows]
-    copy.wait()
     part[...] = dot(grad[...], feats[...], NN).astype(b16)
 
 
 def txt_grad_kernel(rows, at_ref, *refs):
-    terms, unit, norm, sources, (own, give, part, grad, feats, sem) = (
+    terms, unit, norm, blocks, (own, give, part, grad) = (
         refs[:5], refs[5], refs[6], refs[7:15], refs[15:]
     )
-    blocks = [feats.at[n] for n in range(8)]
-    copies = [pltpu.make_async_copy(sources[n], blocks[n], sem.at[n]) for n in range(8)]
-    for copy in copies:
-        copy.start()
     slab = unit.shape[0]
     up, inner = terms[0][:slab].astype(f32), joined(terms[0][slab:])
     for term in terms[1:]:
@@ -418,8 +411,6 @@
         high = grad[:, (2 * ring + 1) * rows : (2 * ring + 2) * rows]
         own[ring] = jnp.where(at_ref[1] == 0, low, high)
         give[ring] = jnp.where(at_ref[1] == 0, high, low)
-    for copy in copies:
-        copy.wait()
     total = None
     for d in range(4):
         cols = grad[:, aligned((at_ref[0] + d) % 4, 2 * rows)]
@@ -442,14 +433,10 @@
         [term[0] if isinstance(term, tuple) else term for term in terms] + [unit, norm, *feats],
         in_specs=[mine(slab + PAD) if isinstance(term, tuple) else whole(term) for term in terms]
         + [mine(slab), whole(norm)]
-        + [pl.BlockSpec(memory_space=pl.ANY)] * len(feats),
+        + [whole(a) for a in feats],
         out_specs=[whole(block)] * halves + [whole(part)],
         grid=(1,),
-        scratch=[
-            pltpu.VMEM((slab, count), b16),
-            pltpu.VMEM(((len(feats),) if len(feats) > 1 else ()) + feats[0].shape, b16),
-            pltpu.SemaphoreType.DMA((len(feats),)),
-        ],
+        scratch=[pltpu.VMEM((slab, count), b16)],
         cost=2 * slab * count * width,
         weight=0,
     )
@@ -576,7 +563,6 @@
     text_up, img_terms = own_tile(
         unit_img, turned_units, unit_txt, other_txt, other_slopes, other_sum, biases, rows
     )
-    img_terms = exchange(img_terms, IMG_GROUPS)
 
     def slab_terms(d, e):
         return [(text_up, 8 + 2 * d + e), (back, 8 + 2 * d + e)]
@@ -584,6 +570,8 @@
     far, across_far, across_after = sums(
         [slab_terms(2, 0), slab_terms(2, 1), slab_terms(1, 1)], places, rows
     )
+    far, across_far, across_after, img_terms = together([far, across_far, across_after, img_terms])
+    img_terms = exchange(img_terms, IMG_GROUPS)
     far = send(far, txt_move(1, 0))
     across_far = send(across_far, txt_move(3, 0))
     far, across_far, across_after = together([far, across_far, across_after])

time: 184 us -> 184 us (level)
    unnamed x41 -> x43, local copies, waits for them, and re-layouts: 3.93 us -> 3.9 us
  transfers between devices with their start and end apart: 26 -> 26, of which waited for: 7 -> 8; matrix products, arithmetic and copies ran while one was open for 14% -> 14% of each run, Pallas kernels for 30% -> 28%
where the time goes in v9:
time: 184 us; the launch traced here: 183 us
  Pallas kernels  67.9 us (37%)
  starting transfers between devices  54.9 us (30%)
  waiting for transfers between devices  27.2 us (15%)
  matrix products  15.1 us (8%)
  local copies, waits for them, and re-layouts  12.6 us (7%)
  other arithmetic  4.48 us (2%)
    pallas_call x11, Pallas kernels, call(): pl.pallas_call(body, out_shape=out_shape, grid_spec=spec, input_output_al...  67.9 us
    ppermute x22, starting transfers between devices, send(): lax.ppermute(block, DEV, [(flat(*p), flat(*move(*p))) for p in PLACES])  32.2 us
    ppermute x22, waiting for transfers between devices, send(): lax.ppermute(block, DEV, [(flat(*p), flat(*move(*p))) for p in PLACES])  26.3 us
    all_to_all x4, starting transfers between devices, exchange(): lax.all_to_all(blocks, DEV, 0, 0, axis_index_groups=groups, tiled=True)  22.8 us
    dot_general x4, matrix products, dot(): return lax.dot_general(a, b, dims, preferred_element_type=f32)  15.1 us
    optimization_barrier x1, local copies, waits for them, and re-layouts, together(): return lax.optimization_barrier(list(arrays))  5.22 us
    unnamed x43, local copies, waits for them, and re-layouts  3.9 us
  transfers between devices with their start and end apart: 26, of which 8 were waited for; matrix products, arithmetic and copies ran while one was open for 14% of the time, Pallas kernels for 28%

profile of v9, /device:TPU:1, one launch (start us, length us, event | category | flops | bytes accessed | tf_op | source)
XLA Modules:
  0.0 183.1 jit_solution(17365234618707572813)
XLA Ops:
  0.6 2.8 %broadcast_in_dim.2 = bf16[8,128,1152]{2,1,0:T(8,128)(2,1)} broadcast(bf16[128,1152]{1,0:T(8,128)(2,1)} %param.7), dimensions={1,2} | broadcast | bytes 2654208 | tf_op jit(solution)/shard_map/broadcast_in_dim | solution.py:536
  3.5 6.9 %all-to-all-start = ((bf16[8,128,1152]{2,1,0:T(8,128)(2,1)}), bf16[8,128,1152]{2,1,0:T(8,128)(2,1)}, u32[]{:S(2)}, u32[]{:S(2)}) async-start(bf16[8,128,1152]{2,1,0:T(8,128)(2,1)} %broadcast_in_dim.2), calls=%async_computation | async-start | bytes 4718592 | tf_op jit(solution)/shard_map/all_to_all | solution.py:65
  10.5 2.8 %collective-permute-start = (bf16[144,1152]{1,0:T(8,128)(2,1)S(1)}, bf16[144,1152]{1,0:T(8,128)(2,1)}, u32[]{:S(2)}, u32[]{:S(2)}) collective-permute-start(bf16[144,1152]{1,0:T(8,128)(2,1)S(1)} %pad_maximum_fusion.refs_3_.refs_8_), channel_id=1, source_target_pairs={{0,24},{1,25},{2,26},{3,27},{4,28},{5,29},{6,30},{7,31},{8,16},{9,... | collective-permute-start | bytes 995336 | tf_op jit(solution)/shard_map/ppermute | solution.py:61
  16.1 4.3 %collective-permute-done.refs_4_.refs_9_ = bf16[144,1152]{1,0:T(8,128)(2,1)} collective-permute-done((bf16[144,1152]{1,0:T(8,128)(2,1)S(1)}, bf16[144,1152]{1,0:T(8,128)(2,1)}, u32[]{:S(2)}, u32[]{:S(2)}) %collective-permute-start) | collective-permute-done | bytes 331808 | tf_op jit(solution)/shard_map/ppermute | solution.py:61
  20.3 2.7 %collective-permute-start.1 = (bf16[144,1152]{1,0:T(8,128)(2,1)}, bf16[144,1152]{1,0:T(8,128)(2,1)}, u32[]{:S(2)}, u32[]{:S(2)}) collective-permute-start(bf16[144,1152]{1,0:T(8,128)(2,1)} %collective-permute-done.refs_4_.refs_9_), channel_id=1, source_target_pairs={{0,6},{1,7},{2,0},{3,1},{4,2},{5,3},{6,4},{7,5},{8,14},{9,15},{10,... | collective-permute-start | bytes 995336 | tf_op jit(solution)/shard_map/ppermute | solution.py:61
  23.1 5.2 %copy.13 = bf16[1152,1152]{0,1:T(8,128)(2,1)} copy(bf16[1152,1152]{1,0:T(8,128)(2,1)} %param.10) | data formatting | bytes 5308416 | tf_op jit(solution)/shard_map/optimization_barrier | solution.py:504
  28.3 2.2 %collective-permute-done.1.refs_6_.refs_11_ = bf16[144,1152]{1,0:T(8,128)(2,1)} collective-permute-done((bf16[144,1152]{1,0:T(8,128)(2,1)}, bf16[144,1152]{1,0:T(8,128)(2,1)}, u32[]{:S(2)}, u32[]{:S(2)}) %collective-permute-start.1) | collective-permute-done | bytes 331808 | tf_op jit(solution)/shard_map/ppermute | solution.py:61
  34.4 7.6 %shard_map.102 = (bf16[1168,1024]{1,0:T(8,128)(2,1)}, f32[1,1024]{1,0:T(1,128)}) custom-call(s32[16]{0:T(128)} %stack.83.refs_0_, bf16[144,1152]{1,0:T(8,128)(2,1)} %collective-permute-done.2.refs_1_.refs_14_, bf16[144,1152]{1,0:T(8,128)(2,1)} %collective-permute-done.6.refs_2_.refs_15_, bf16[144,1152]{1,0:T(8,128)(2,1)} %copy-done.5, ...), custom_call_target="tpu_custom_call" | custom-call | flops 2038431744 | bytes 4644864 | tf_op jit(solution)/shard_map/pallas_call | solution.py:93
  42.9 4.7 %shard_map.103 = (bf16[1168,1024]{1,0:T(8,128)(2,1)}, f32[1,1024]{1,0:T(1,128)}) custom-call(s32[16]{0:T(128)} %stack.83.refs_0_, bf16[144,1152]{1,0:T(8,128)(2,1)} %copy-done.3, bf16[144,1152]{1,0:T(8,128)(2,1)} %copy-done.4, bf16[1152,1152]{1,0:T(8,128)(2,1)} %bitcast.48, ...), custom_call_target="tpu_custom_call", output_to_operand_aliasing={{0}: (4, {}), {1}: (5, {})} | custom-call | flops 679477248 | bytes 5713920 | tf_op jit(solution)/shard_map/pallas_call | solution.py:93
  47.6 2.1 %collective-permute-start.7 = (bf16[1168,1024]{1,0:T(8,128)(2,1)}, bf16[1168,1024]{1,0:T(8,128)(2,1)}, u32[]{:S(2)}, u32[]{:S(2)}) collective-permute-start(bf16[1168,1024]{1,0:T(8,128)(2,1)} %get-tuple-element.59.refs_3_.refs_6_), channel_id=1, source_target_pairs={{0,1},{1,0},{2,3},{3,2},{4,5},{5,4},{6,7},{7,6},{8,9},{9,8},{10,11... | collective-permute-start | bytes 7176200 | tf_op jit(solution)/shard_map/ppermute | solution.py:61
  49.7 5.0 %multiply_reduce_fusion = (f32[1024]{0:T(1024)S(1)}, f32[1152,1024]{1,0:T(8,128)S(1)}) fusion(bf16[1152,1152]{1,0:T(8,128)(2,1)S(1)} %copy-done, bf16[1024,1152]{1,0:T(8,128)(2,1)} %bitcast.17.refs_4_), kind=kOutput, calls=%fused_computation.2 | convolution fusion | flops 2720267264 | bytes 9736192 | tf_op jit(solution)/shard_map/dot_general | solution.py:75
  55.3 6.6 %fusion.refs_1_ = bf16[1024,1152]{1,0:T(8,128)(2,1)} fusion(bf16[1024,1152]{1,0:T(8,128)(2,1)} %bitcast.17.refs_4_, bf16[1152,1152]{1,0:T(8,128)(2,1)S(1)} %copy-done, f32[1024]{0:T(1024)S(1)} %get-tuple-element.100), kind=kOutput, calls=%fused_computation.3 | convolution fusion | flops 2720268288 | bytes 7376896 | tf_op jit(solution)/shard_map/dot_general | solution.py:75
  63.9 12.3 %shard_map.104 = (bf16[4,1024,256]{2,1,0:T(8,128)(2,1)}, f32[1,1024]{1,0:T(1,128)}, bf16[1280,1024]{1,0:T(8,128)(2,1)}) custom-call(f32[33]{0:T(128)} %pad_maximum_fusion.1.refs_0_, bf16[1024,1152]{1,0:T(8,128)(2,1)} %fusion.refs_1_, bf16[1152,1024]{1,0:T(8,128)(2,1)} %multiply_convert_fusion.refs_2_, bf16[1168,1024]{1,0:T(8,128)(2,1)} %collective-permute-done.7.refs_3_.refs_4_), custom_call_target="tpu_custom_call" | custom-call | flops 4831838208 | bytes 7110788 | tf_op jit(solution)/shard_map/pallas_call | solution.py:93
  76.2 18.5 %shard_map.105 = (bf16[1280,1024]{1,0:T(8,128)(2,1)}, bf16[8,160,1024]{2,1,0:T(8,128)(2,1)}) custom-call(f32[33]{0:T(128)} %pad_maximum_fusion.1.refs_0_, bf16[1024,1152]{1,0:T(8,128)(2,1)} %fusion.refs_1_, bf16[1152,1024]{1,0:T(8,128)(2,1)} %multiply_convert_fusion.refs_2_, bf16[1168,1024]{1,0:T(8,128)(2,1)} %get-tuple-element.59.refs_3_.refs_6_, ...), custom_call_target="tpu_custom_call" | custom-call | flops 9663676416 | bytes 11604100 | tf_op jit(solution)/shard_map/pallas_call | solution.py:93
  94.7 3.2 %shard_map.106 = (bf16[160,1024]{1,0:T(8,128)(2,1)}, bf16[160,1024]{1,0:T(8,128)(2,1)}, bf16[160,1024]{1,0:T(8,128)(2,1)}) custom-call(s32[16]{0:T(128)} %stack.83.refs_0_, bf16[1280,1024]{1,0:T(8,128)(2,1)} %get-tuple-element.63.refs_1_.refs_3_.refs_5_.refs_4_.refs_7_, bf16[1280,1024]{1,0:T(8,128)(2,1)} %collective-permute-done.8.refs_2_.refs_4_.refs_6_.refs_5_.refs_8_, ...), custom_call_target="tpu_custom_call" | custom-call | bytes 15728640 | tf_op jit(solution)/shard_map/pallas_call | solution.py:93
  97.9 4.6 %all-to-all-start.1 = ((bf16[8,160,1024]{2,1,0:T(8,128)(2,1)}), bf16[8,160,1024]{2,1,0:T(8,128)(2,1)}, u32[]{:S(2)}, u32[]{:S(2)}) async-start(bf16[8,160,1024]{2,1,0:T(8,128)(2,1)} %get-tuple-element.69), calls=%async_computation.1 | async-start | bytes 5242880 | tf_op jit(solution)/shard_map/all_to_all | solution.py:65
  102.7 2.5 %collective-permute-start.10 = (bf16[160,1024]{1,0:T(8,128)(2,1)}, bf16[160,1024]{1,0:T(8,128)(2,1)S(1)}, u32[]{:S(2)}, u32[]{:S(2)}) collective-permute-start(bf16[160,1024]{1,0:T(8,128)(2,1)} %get-tuple-element.74), channel_id=1, source_target_pairs={{0,6},{1,7},{2,0},{3,1},{4,2},{5,3},{6,4},{7,5},{8,14},{9,15},{10,... | collective-permute-start | bytes 983048 | tf_op jit(solution)/shard_map/ppermute | solution.py:61
  105.2 7.7 %collective-permute-done.9.refs_6_ = bf16[160,1024]{1,0:T(8,128)(2,1)S(1)} collective-permute-done((bf16[160,1024]{1,0:T(8,128)(2,1)}, bf16[160,1024]{1,0:T(8,128)(2,1)S(1)}, u32[]{:S(2)}, u32[]{:S(2)}) %collective-permute-start.9) | collective-permute-done | bytes 327712 | tf_op jit(solution)/shard_map/ppermute | solution.py:61
  113.7 3.4 %shard_map.108 = (bf16[160,1024]{1,0:T(8,128)(2,1)}, bf16[160,1024]{1,0:T(8,128)(2,1)}, bf16[160,1024]{1,0:T(8,128)(2,1)}) custom-call(s32[16]{0:T(128)} %stack.83.refs_0_, bf16[1280,1024]{1,0:T(8,128)(2,1)} %get-tuple-element.63.refs_1_.refs_3_.refs_5_.refs_4_.refs_7_, bf16[1280,1024]{1,0:T(8,128)(2,1)} %collective-permute-done.8.refs_2_.refs_4_.refs_6_.refs_5_.refs_8_, ...), custom_call_target="tpu_custom_call" | custom-call | bytes 16384000 | tf_op jit(solution)/shard_map/pallas_call | solution.py:93
  117.1 2.3 %collective-permute-start.12 = (bf16[160,1024]{1,0:T(8,128)(2,1)}, bf16[160,1024]{1,0:T(8,128)(2,1)S(1)}, u32[]{:S(2)}, u32[]{:S(2)}) collective-permute-start(bf16[160,1024]{1,0:T(8,128)(2,1)} %get-tuple-element.79), channel_id=1, source_target_pairs={{0,6},{1,7},{2,0},{3,1},{4,2},{5,3},{6,4},{7,5},{8,14},{9,15},{10,... | collective-permute-start | bytes 983048 | tf_op jit(solution)/shard_map/ppermute | solution.py:61
  119.4 2.9 %collective-permute-done.11.refs_3_ = bf16[160,1024]{1,0:T(8,128)(2,1)S(1)} collective-permute-done((bf16[160,1024]{1,0:T(8,128)(2,1)S(1)}, bf16[160,1024]{1,0:T(8,128)(2,1)S(1)}, u32[]{:S(2)}, u32[]{:S(2)}) %collective-permute-start.11) | collective-permute-done | bytes 327712 | tf_op jit(solution)/shard_map/ppermute | solution.py:61
  122.3 3.2 %collective-permute-done.12.refs_4_ = bf16[160,1024]{1,0:T(8,128)(2,1)S(1)} collective-permute-done((bf16[160,1024]{1,0:T(8,128)(2,1)}, bf16[160,1024]{1,0:T(8,128)(2,1)S(1)}, u32[]{:S(2)}, u32[]{:S(2)}) %collective-permute-start.12) | collective-permute-done | bytes 327712 | tf_op jit(solution)/shard_map/ppermute | solution.py:61
  126.2 2.9 %shard_map.109 = bf16[160,1024]{1,0:T(8,128)(2,1)} custom-call(s32[16]{0:T(128)} %stack.83.refs_0_, bf16[1280,1024]{1,0:T(8,128)(2,1)} %get-tuple-element.63.refs_1_.refs_3_.refs_5_.refs_4_.refs_7_, bf16[1280,1024]{1,0:T(8,128)(2,1)} %collective-permute-done.8.refs_2_.refs_4_.refs_6_.refs_5_.refs_8_, bf16[160,1024]{1,0:T(8,128)(2,1)} %copy-done.8, ...), custom_call_target="tpu_custom_call" | custom-call | bytes 5898240 | tf_op jit(solution)/shard_map/pallas_call | solution.py:93
  131.3 2.5 %collective-permute-start.14 = (bf16[160,1024]{1,0:T(8,128)(2,1)}, bf16[160,1024]{1,0:T(8,128)(2,1)}, u32[]{:S(2)}, u32[]{:S(2)}) collective-permute-start(bf16[160,1024]{1,0:T(8,128)(2,1)} %get-tuple-element.83), channel_id=1, source_target_pairs={{0,6},{1,7},{2,0},{3,1},{4,2},{5,3},{6,4},{7,5},{8,14},{9,15},{10,... | collective-permute-start | bytes 983048 | tf_op jit(solution)/shard_map/ppermute | solution.py:61
  134.7 4.9 %shard_map.107 = (bf16[8,144,128]{2,1,0:T(8,128)(2,1)}, bf16[144,1152]{1,0:T(8,128)(2,1)}) custom-call(s32[16]{0:T(128)} %stack.83.refs_0_, bf16[8,160,1024]{2,1,0:T(8,128)(2,1)} %all-to-all-done.1.refs_1_, bf16[1152,1024]{1,0:T(8,128)(2,1)} %multiply_convert_fusion.refs_2_, f32[1,1024]{1,0:T(1,128)} %bitcast.51, bf16[1024,1152]{1,0:T(8,128)(2,1)} %bitcast.17.refs_4_), custom_call_target="tpu_custom_call" | custom-call | tf_op jit(solution)/shard_map/pallas_call | solution.py:93
  139.6 3.4 %all-to-all-start.2 = ((bf16[8,144,128]{2,1,0:T(8,128)(2,1)}), bf16[8,144,128]{2,1,0:T(8,128)(2,1)S(1)}, u32[]{:S(2)}, u32[]{:S(2)}) async-start(bf16[8,144,128]{2,1,0:T(8,128)(2,1)} %get-tuple-element.70), calls=%async_computation.2 | async-start | bytes 589824 | tf_op jit(solution)/shard_map/all_to_all | solution.py:65
  143.8 5.0 %shard_map.110 = (bf16[4,144,128]{2,1,0:T(8,128)(2,1)}, bf16[4,144,128]{2,1,0:T(8,128)(2,1)}, bf16[144,1152]{1,0:T(8,128)(2,1)}) custom-call(s32[16]{0:T(128)} %stack.83.refs_0_, bf16[1280,1024]{1,0:T(8,128)(2,1)} %get-tuple-element.63.refs_1_.refs_3_.refs_5_.refs_4_.refs_7_, ...), custom_call_target="tpu_custom_call" | custom-call | tf_op jit(solution)/shard_map/pallas_call | solution.py:93
  148.8 3.3 %collective-permute-start.17 = (bf16[144,1152]{1,0:T(8,128)(2,1)}, bf16[144,1152]{1,0:T(8,128)(2,1)}, u32[]{:S(2)}, u32[]{:S(2)}) collective-permute-start(bf16[144,1152]{1,0:T(8,128)(2,1)} %get-tuple-element.87.txt), channel_id=1, source_target_pairs={{0,1},{1,0},{2,3},{3,2},{4,5},{5,4},{6,7},{7,6},{8,9},{9,8},{10,11... | collective-permute-start | bytes 995336 | tf_op jit(solution)/shard_map/ppermute | solution.py:61
  155.7 3.7 %shard_map.111 = bf16[512,384]{1,0:T(8,128)(2,1)} custom-call(s32[1]{0:T(128)} %bitcast.4.core, bf16[144,1152]{1,0:T(8,128)(2,1)} %get-tuple-element.72.img, bf16[144,1152]{1,0:T(8,128)(2,1)} %get-tuple-element.87.txt, bf16[144,1152]{1,0:T(8,128)(2,1)} %collective-permute-done.16.other_img, bf16[144,1152]{1,0:T(8,128)(2,1)} %collective-permute-done.17.other_txt), custom_call_target="tpu_custom_call" | custom-call | tf_op jit(solution)/shard_map/pallas_call | solution.py:93
  159.4 7.8 %all-to-all-start.3 = ((bf16[64,8,384]{2,1,0:T(8,128)(2,1)}), bf16[64,8,384]{2,1,0:T(8,128)(2,1)S(1)}, u32[]{:S(2)}, u32[]{:S(2)}) async-start(bf16[64,8,384]{2,1,0:T(8,128)(2,1)} %bitcast.49), calls=%async_computation.3 | async-start | bytes 786432 | tf_op jit(solution)/shard_map/all_to_all | solution.py:65
  172.5 2.8 %collective-permute-done.19 = bf16[288,128]{1,0:T(8,128)(2,1)S(1)} collective-permute-done((bf16[288,128]{1,0:T(8,128)(2,1)S(1)}, bf16[288,128]{1,0:T(8,128)(2,1)S(1)}, u32[]{:S(2)}, u32[]{:S(2)}) %collective-permute-start.19) | collective-permute-done | bytes 73760 | tf_op jit(solution)/shard_map/ppermute | solution.py:61
  175.3 3.3 %collective-permute-done.20 = bf16[288,128]{1,0:T(8,128)(2,1)S(1)} collective-permute-done((bf16[288,128]{1,0:T(8,128)(2,1)S(1)}, bf16[288,128]{1,0:T(8,128)(2,1)S(1)}, u32[]{:S(2)}, u32[]{:S(2)}) %collective-permute-start.20) | collective-permute-done | bytes 73760 | tf_op jit(solution)/shard_map/ppermute | solution.py:61
  (92 shorter events, 29.2 us)
Async XLA Ops:
  0.6 49.1 %copy-start = (bf16[1152,1152]{1,0:T(8,128)(2,1)S(1)}, bf16[1152,1152]{1,0:T(8,128)(2,1)}, u32[]{:S(2)}) copy-start(bf16[1152,1152]{1,0:T(8,128)(2,1)} %param.9) | copy-start | bytes 7962628
  3.5 46.2 %all-to-all-start = ((bf16[8,128,1152]{2,1,0:T(8,128)(2,1)}), bf16[8,128,1152]{2,1,0:T(8,128)(2,1)}, u32[]{:S(2)}, u32[]{:S(2)}) async-start(bf16[8,128,1152]{2,1,0:T(8,128)(2,1)} %broadcast_in_dim.2), calls=%async_computation | async-start | bytes 4718592 | tf_op jit(solution)/shard_map/all_to_all | solution.py:65
  10.5 17.8 %copy-start.5 = (bf16[144,1152]{1,0:T(8,128)(2,1)}, bf16[144,1152]{1,0:T(8,128)(2,1)S(1)}, u32[]{:S(2)}) copy-start(bf16[144,1152]{1,0:T(8,128)(2,1)S(1)} %pad_maximum_fusion.refs_3_.refs_8_) | copy-start | bytes 995332
  10.5 23.3 %copy-start.18 = (f32[32]{0:T(128)S(1)}, f32[32]{0:T(128)}, u32[]{:S(2)}) copy-start(f32[32]{0:T(128)} %param.11) | copy-start | bytes 388
  10.5 9.8 %collective-permute-start = (bf16[144,1152]{1,0:T(8,128)(2,1)S(1)}, bf16[144,1152]{1,0:T(8,128)(2,1)}, u32[]{:S(2)}, u32[]{:S(2)}) collective-permute-start(bf16[144,1152]{1,0:T(8,128)(2,1)S(1)} %pad_maximum_fusion.refs_3_.refs_8_), channel_id=1, source_target_pairs={{0,24},{1,25},{2,26},{3,27},{4,28},{5,29},{6,30},{7,31},{8,16},{9,... | collective-permute-start | bytes 995336 | tf_op jit(solution)/shard_map/ppermute | solution.py:61
  13.3 9.7 %collective-permute-start.2 = (bf16[144,1152]{1,0:T(8,128)(2,1)S(1)}, bf16[144,1152]{1,0:T(8,128)(2,1)}, u32[]{:S(2)}, u32[]{:S(2)}) collective-permute-start(bf16[144,1152]{1,0:T(8,128)(2,1)S(1)} %pad_maximum_fusion.refs_3_.refs_8_), channel_id=1, source_target_pairs={{0,2},{1,3},{2,4},{3,5},{4,6},{5,7},{6,0},{7,1},{8,10},{9,11},{10,... | collective-permute-start | bytes 995336 | tf_op jit(solution)/shard_map/ppermute | solution.py:61
  14.6 13.7 %collective-permute-start.3 = (bf16[144,1152]{1,0:T(8,128)(2,1)S(1)}, bf16[144,1152]{1,0:T(8,128)(2,1)S(1)}, u32[]{:S(2)}, u32[]{:S(2)}) collective-permute-start(bf16[144,1152]{1,0:T(8,128)(2,1)S(1)} %pad_maximum_fusion.refs_3_.refs_8_), channel_id=1, source_target_pairs={{0,6},{1,7},{2,0},{3,1},{4,2},{5,3},{6,4},{7,5},{8,14},{9,15},{10,... | collective-permute-start | bytes 995336 | tf_op jit(solution)/shard_map/ppermute | solution.py:61
  20.3 10.2 %collective-permute-start.1 = (bf16[144,1152]{1,0:T(8,128)(2,1)}, bf16[144,1152]{1,0:T(8,128)(2,1)}, u32[]{:S(2)}, u32[]{:S(2)}) collective-permute-start(bf16[144,1152]{1,0:T(8,128)(2,1)} %collective-permute-done.refs_4_.refs_9_), channel_id=1, source_target_pairs={{0,6},{1,7},{2,0},{3,1},{4,2},{5,3},{6,4},{7,5},{8,14},{9,15},{10,... | collective-permute-start | bytes 995336 | tf_op jit(solution)/shard_map/ppermute | solution.py:61
  23.1 11.4 %collective-permute-start.6 = (bf16[144,1152]{1,0:T(8,128)(2,1)}, bf16[144,1152]{1,0:T(8,128)(2,1)}, u32[]{:S(2)}, u32[]{:S(2)}) collective-permute-start(bf16[144,1152]{1,0:T(8,128)(2,1)} %collective-permute-done.refs_4_.refs_9_), channel_id=1, source_target_pairs={{0,2},{1,3},{2,4},{3,5},{4,6},{5,7},{6,0},{7,1},{8,10},{9,11},{10,... | collective-permute-start | bytes 995336 | tf_op jit(solution)/shard_map/ppermute | solution.py:61
  30.5 11.6 %collective-permute-start.4 = (bf16[144,1152]{1,0:T(8,128)(2,1)}, bf16[144,1152]{1,0:T(8,128)(2,1)S(1)}, u32[]{:S(2)}, u32[]{:S(2)}) collective-permute-start(bf16[144,1152]{1,0:T(8,128)(2,1)} %collective-permute-done.2.refs_1_.refs_14_), channel_id=1, source_target_pairs={{0,2},{1,3},{2,4},{3,5},{4,6},{5,7},{6,0},{7,1},{8,10},{9,11},{10,... | collective-permute-start | bytes 995336 | tf_op jit(solution)/shard_map/ppermute | solution.py:61
  31.8 10.3 %collective-permute-start.5 = (bf16[144,1152]{1,0:T(8,128)(2,1)}, bf16[144,1152]{1,0:T(8,128)(2,1)S(1)}, u32[]{:S(2)}, u32[]{:S(2)}) collective-permute-start(bf16[144,1152]{1,0:T(8,128)(2,1)} %collective-permute-done.1.refs_6_.refs_11_), channel_id=1, source_target_pairs={{0,6},{1,7},{2,0},{3,1},{4,2},{5,3},{6,4},{7,5},{8,14},{9,15},{10,... | collective-permute-start | bytes 995336 | tf_op jit(solution)/shard_map/ppermute | solution.py:61
  47.6 16.3 %collective-permute-start.7 = (bf16[1168,1024]{1,0:T(8,128)(2,1)}, bf16[1168,1024]{1,0:T(8,128)(2,1)}, u32[]{:S(2)}, u32[]{:S(2)}) collective-permute-start(bf16[1168,1024]{1,0:T(8,128)(2,1)} %get-tuple-element.59.refs_3_.refs_6_), channel_id=1, source_target_pairs={{0,1},{1,0},{2,3},{3,2},{4,5},{5,4},{6,7},{7,6},{8,9},{9,8},{10,11... | collective-permute-start | bytes 7176200 | tf_op jit(solution)/shard_map/ppermute | solution.py:61
  76.2 18.5 %collective-permute-start.8 = (bf16[1280,1024]{1,0:T(8,128)(2,1)}, bf16[1280,1024]{1,0:T(8,128)(2,1)}, u32[]{:S(2)}, u32[]{:S(2)}) collective-permute-start(bf16[1280,1024]{1,0:T(8,128)(2,1)} %get-tuple-element.64), channel_id=1, source_target_pairs={{0,1},{1,0},{2,3},{3,2},{4,5},{5,4},{6,7},{7,6},{8,9},{9,8},{10,11... | collective-permute-start | bytes 7864328 | tf_op jit(solution)/shard_map/ppermute | solution.py:61
  97.9 15.0 %copy-start.17 = (bf16[160,1024]{1,0:T(8,128)(2,1)S(1)}, bf16[160,1024]{1,0:T(8,128)(2,1)}, u32[]{:S(2)}) copy-start(bf16[160,1024]{1,0:T(8,128)(2,1)} %get-tuple-element.76) | copy-start | bytes 983044
  97.9 36.8 %all-to-all-start.1 = ((bf16[8,160,1024]{2,1,0:T(8,128)(2,1)}), bf16[8,160,1024]{2,1,0:T(8,128)(2,1)}, u32[]{:S(2)}, u32[]{:S(2)}) async-start(bf16[8,160,1024]{2,1,0:T(8,128)(2,1)} %get-tuple-element.69), calls=%async_computation.1 | async-start | bytes 5242880 | tf_op jit(solution)/shard_map/all_to_all | solution.py:65
  102.5 10.4 %collective-permute-start.9 = (bf16[160,1024]{1,0:T(8,128)(2,1)}, bf16[160,1024]{1,0:T(8,128)(2,1)S(1)}, u32[]{:S(2)}, u32[]{:S(2)}) collective-permute-start(bf16[160,1024]{1,0:T(8,128)(2,1)} %get-tuple-element.73), channel_id=1, source_target_pairs={{0,2},{1,3},{2,4},{3,5},{4,6},{5,7},{6,0},{7,1},{8,10},{9,11},{10,... | collective-permute-start | bytes 983048 | tf_op jit(solution)/shard_map/ppermute | solution.py:61
  102.7 10.2 %collective-permute-start.10 = (bf16[160,1024]{1,0:T(8,128)(2,1)}, bf16[160,1024]{1,0:T(8,128)(2,1)S(1)}, u32[]{:S(2)}, u32[]{:S(2)}) collective-permute-start(bf16[160,1024]{1,0:T(8,128)(2,1)} %get-tuple-element.74), channel_id=1, source_target_pairs={{0,6},{1,7},{2,0},{3,1},{4,2},{5,3},{6,4},{7,5},{8,14},{9,15},{10,... | collective-permute-start | bytes 983048 | tf_op jit(solution)/shard_map/ppermute | solution.py:61
  112.9 9.4 %collective-permute-start.11 = (bf16[160,1024]{1,0:T(8,128)(2,1)S(1)}, bf16[160,1024]{1,0:T(8,128)(2,1)S(1)}, u32[]{:S(2)}, u32[]{:S(2)}) collective-permute-start(bf16[160,1024]{1,0:T(8,128)(2,1)S(1)} %copy-done.17), channel_id=1, source_target_pairs={{0,2},{1,3},{2,4},{3,5},{4,6},{5,7},{6,0},{7,1},{8,10},{9,11},{10,... | collective-permute-start | bytes 983048 | tf_op jit(solution)/shard_map/ppermute | solution.py:61
  117.1 8.3 %collective-permute-start.12 = (bf16[160,1024]{1,0:T(8,128)(2,1)}, bf16[160,1024]{1,0:T(8,128)(2,1)S(1)}, u32[]{:S(2)}, u32[]{:S(2)}) collective-permute-start(bf16[160,1024]{1,0:T(8,128)(2,1)} %get-tuple-element.79), channel_id=1, source_target_pairs={{0,6},{1,7},{2,0},{3,1},{4,2},{5,3},{6,4},{7,5},{8,14},{9,15},{10,... | collective-permute-start | bytes 983048 | tf_op jit(solution)/shard_map/ppermute | solution.py:61
  129.1 13.9 %collective-permute-start.15 = (bf16[160,1024]{1,0:T(8,128)(2,1)}, bf16[160,1024]{1,0:T(8,128)(2,1)S(1)}, u32[]{:S(2)}, u32[]{:S(2)}) collective-permute-start(bf16[160,1024]{1,0:T(8,128)(2,1)} %shard_map.109), channel_id=1, source_target_pairs={{0,24},{1,25},{2,26},{3,27},{4,28},{5,29},{6,30},{7,31},{8,16},{9,... | collective-permute-start | bytes 983048 | tf_op jit(solution)/shard_map/ppermute | solution.py:61
  130.6 12.4 %collective-permute-start.13 = (bf16[160,1024]{1,0:T(8,128)(2,1)}, bf16[160,1024]{1,0:T(8,128)(2,1)}, u32[]{:S(2)}, u32[]{:S(2)}) collective-permute-start(bf16[160,1024]{1,0:T(8,128)(2,1)} %get-tuple-element.82), channel_id=1, source_target_pairs={{0,2},{1,3},{2,4},{3,5},{4,6},{5,7},{6,0},{7,1},{8,10},{9,11},{10,... | collective-permute-start | bytes 983048 | tf_op jit(solution)/shard_map/ppermute | solution.py:61
  131.3 11.8 %collective-permute-start.14 = (bf16[160,1024]{1,0:T(8,128)(2,1)}, bf16[160,1024]{1,0:T(8,128)(2,1)}, u32[]{:S(2)}, u32[]{:S(2)}) collective-permute-start(bf16[160,1024]{1,0:T(8,128)(2,1)} %get-tuple-element.83), channel_id=1, source_target_pairs={{0,6},{1,7},{2,0},{3,1},{4,2},{5,3},{6,4},{7,5},{8,14},{9,15},{10,... | collective-permute-start | bytes 983048 | tf_op jit(solution)/shard_map/ppermute | solution.py:61
  139.6 14.4 %all-to-all-start.2 = ((bf16[8,144,128]{2,1,0:T(8,128)(2,1)}), bf16[8,144,128]{2,1,0:T(8,128)(2,1)S(1)}, u32[]{:S(2)}, u32[]{:S(2)}) async-start(bf16[8,144,128]{2,1,0:T(8,128)(2,1)} %get-tuple-element.70), calls=%async_computation.2 | async-start | bytes 589824 | tf_op jit(solution)/shard_map/all_to_all | solution.py:65
  148.8 7.0 %collective-permute-start.17 = (bf16[144,1152]{1,0:T(8,128)(2,1)}, bf16[144,1152]{1,0:T(8,128)(2,1)}, u32[]{:S(2)}, u32[]{:S(2)}) collective-permute-start(bf16[144,1152]{1,0:T(8,128)(2,1)} %get-tuple-element.87.txt), channel_id=1, source_target_pairs={{0,1},{1,0},{2,3},{3,2},{4,5},{5,4},{6,7},{7,6},{8,9},{9,8},{10,11... | collective-permute-start | bytes 995336 | tf_op jit(solution)/shard_map/ppermute | solution.py:61
  152.1 3.7 %collective-permute-start.16 = (bf16[144,1152]{1,0:T(8,128)(2,1)S(1)}, bf16[144,1152]{1,0:T(8,128)(2,1)}, u32[]{:S(2)}, u32[]{:S(2)}) collective-permute-start(bf16[144,1152]{1,0:T(8,128)(2,1)S(1)} %copy-done.7), channel_id=1, source_target_pairs={{0,1},{1,0},{2,3},{3,2},{4,5},{5,4},{6,7},{7,6},{8,9},{9,8},{10,11... | collective-permute-start | bytes 995336 | tf_op jit(solution)/shard_map/ppermute | solution.py:61
  152.1 7.3 %collective-permute-start.18 = (bf16[4,144,128]{2,1,0:T(8,128)(2,1)}, bf16[4,144,128]{2,1,0:T(8,128)(2,1)}, u32[]{:S(2)}, u32[]{:S(2)}) collective-permute-start(bf16[4,144,128]{2,1,0:T(8,128)(2,1)} %get-tuple-element.88), channel_id=1, source_target_pairs={{0,24},{1,25},{2,26},{3,27},{4,28},{5,29},{6,30},{7,31},{8,16},{9,... | collective-permute-start | bytes 442376 | tf_op jit(solution)/shard_map/ppermute | solution.py:61
  154.0 13.3 %copy-start.14 = (bf16[4,144,128]{2,1,0:T(8,128)(2,1)S(1)}, bf16[4,144,128]{2,1,0:T(8,128)(2,1)}, u32[]{:S(2)}) copy-start(bf16[4,144,128]{2,1,0:T(8,128)(2,1)} %get-tuple-element.90) | copy-start | bytes 442372
  159.4 21.1 %all-to-all-start.3 = ((bf16[64,8,384]{2,1,0:T(8,128)(2,1)}), bf16[64,8,384]{2,1,0:T(8,128)(2,1)S(1)}, u32[]{:S(2)}, u32[]{:S(2)}) async-start(bf16[64,8,384]{2,1,0:T(8,128)(2,1)} %bitcast.49), calls=%async_computation.3 | async-start | bytes 786432 | tf_op jit(solution)/shard_map/all_to_all | solution.py:65
  167.3 11.5 %copy-start.1 = (bf16[1152,1152]{1,0:T(8,128)(2,1)S(1)}, bf16[1152,1152]{1,0:T(8,128)(2,1)}, u32[]{:S(2)}) copy-start(bf16[1152,1152]{1,0:T(8,128)(2,1)} %param.10) | copy-start | bytes 7962628
  168.4 10.2 %collective-permute-start.21 = (bf16[288,128]{1,0:T(8,128)(2,1)S(1)}, bf16[288,128]{1,0:T(8,128)(2,1)S(1)}, u32[]{:S(2)}, u32[]{:S(2)}) collective-permute-start(bf16[288,128]{1,0:T(8,128)(2,1)S(1)} %get-tuple-element.94), channel_id=1, source_target_pairs={{0,2},{1,3},{2,4},{3,5},{4,6},{5,7},{6,0},{7,1},{8,10},{9,11},{10,... | collective-permute-start | bytes 221192 | tf_op jit(solution)/shard_map/ppermute | solution.py:61
  169.5 5.8 %collective-permute-start.19 = (bf16[288,128]{1,0:T(8,128)(2,1)S(1)}, bf16[288,128]{1,0:T(8,128)(2,1)S(1)}, u32[]{:S(2)}, u32[]{:S(2)}) collective-permute-start(bf16[288,128]{1,0:T(8,128)(2,1)S(1)} %get-tuple-element.95), channel_id=1, source_target_pairs={{0,6},{1,7},{2,0},{3,1},{4,2},{5,3},{6,4},{7,5},{8,14},{9,15},{10,... | collective-permute-start | bytes 221192 | tf_op jit(solution)/shard_map/ppermute | solution.py:61
  171.2 7.4 %collective-permute-start.20 = (bf16[288,128]{1,0:T(8,128)(2,1)S(1)}, bf16[288,128]{1,0:T(8,128)(2,1)S(1)}, u32[]{:S(2)}, u32[]{:S(2)}) collective-permute-start(bf16[288,128]{1,0:T(8,128)(2,1)S(1)} %get-tuple-element.96), channel_id=1, source_target_pairs={{0,4},{1,5},{2,6},{3,7},{4,0},{5,1},{6,2},{7,3},{8,12},{9,13},{10,... | collective-permute-start | bytes 221192 | tf_op jit(solution)/shard_map/ppermute | solution.py:61
  (13 other events, 39.9 us)

commit v10 on v9

--- a/solution.py
+++ b/solution.py
@@ -455,11 +455,16 @@
     base = (slot // 8 * 2 + core[0]) * own
     chosen = jnp.where(feature == base + slot % 8, 1.0, 0.0).astype(b16)
     out[:, : 3 * third] = dot(chosen, part, NT).astype(b16)
-    chosen = jnp.where(feature == base + 8, 1.0, 0.0).astype(b16)
+    chips = slots // 8
+    chip = lax.broadcasted_iota(jnp.int32, (chips, 1), 0)
+    feature = lax.broadcasted_iota(jnp.int32, (chips, width), 1)
+    chosen = jnp.where(feature == (chip * 2 + core[0]) * own + 8, 1.0, 0.0).astype(b16)
     ninth = dot(chosen, part, NT)
-    pick = slot % 8
-    rest = jnp.where(pick == 1, ninth[:, third : 2 * third], ninth[:, :third])
-    rest = jnp.where(pick == 2, ninth[:, 2 * third :], rest)
+    chip = lax.broadcasted_iota(jnp.int32, (slots, chips), 1)
+    rest = jnp.zeros((slots, third), f32)
+    for n in range(3):
+        spread = jnp.where(slot == chip * 8 + n, 1.0, 0.0).astype(b16)
+        rest = rest + dot(spread, ninth[:, n * third : (n + 1) * third].astype(b16), NN)
     out[:, 3 * third :] = rest.astype(b16)
 
 
@@ -576,10 +581,10 @@
     across_far = send(across_far, txt_move(3, 0))
     far, across_far, across_after = together([far, across_far, across_after])
     across_before = send(across_after, txt_move(1, 0))
-    across_after, before, after = sums(
-        [slab_terms(3, 1) + [across_far], slab_terms(1, 0) + [far], slab_terms(3, 0)], places, rows
-    )
+    (across_after,) = sums([slab_terms(3, 1) + [across_far]], places, rows)
     across_after = send(across_after, txt_move(3, 0))
+    far, across_before = together([far, across_before])
+    before, after = sums([slab_terms(1, 0) + [far], slab_terms(3, 0)], places, rows)
     across_before, across_after, before, after = together(
         [across_before, across_after, before, after]
     )

time: 184 us -> 184 us (level)
  Pallas kernels: 67.9 us -> 69.9 us
    ppermute x22, waiting for transfers between devices: 26.3 us -> 24.3 us  [send(): lax.ppermute(block, DEV, [(flat(*p), flat(*move(*p))) for p in PLACES])]
    pallas_call x11 -> x12, Pallas kernels: 67.9 us -> 69.9 us  [call(): pl.pallas_call(body, out_shape=out_shape, grid_spec=spec, input_output_al...]
  transfers between devices with their start and end apart: 26 -> 26, of which waited for: 8 -> 7; matrix products, arithmetic and copies ran while one was open for 14% -> 14% of each run, Pallas kernels for 28% -> 29%
where the time goes in v10:
time: 184 us; the launch traced here: 183 us
  Pallas kernels  69.9 us (38%)
  starting transfers between devices  54 us (29%)
  waiting for transfers between devices  25.9 us (14%)
  matrix products  15 us (8%)
  local copies, waits for them, and re-layouts  12.5 us (7%)
  other arithmetic  4.48 us (2%)
    pallas_call x12, Pallas kernels, call(): pl.pallas_call(body, out_shape=out_shape, grid_spec=spec, input_output_al...  69.9 us
    ppermute x22, starting transfers between devices, send(): lax.ppermute(block, DEV, [(flat(*p), flat(*move(*p))) for p in PLACES])  31 us
    ppermute x22, waiting for transfers between devices, send(): lax.ppermute(block, DEV, [(flat(*p), flat(*move(*p))) for p in PLACES])  24.3 us
    all_to_all x4, starting transfers between devices, exchange(): lax.all_to_all(blocks, DEV, 0, 0, axis_index_groups=groups, tiled=True)  23 us
    dot_general x4, matrix products, dot(): return lax.dot_general(a, b, dims, preferred_element_type=f32)  15 us
    optimization_barrier x1, local copies, waits for them, and re-layouts, together(): return lax.optimization_barrier(list(arrays))  5.22 us
    unnamed x43, local copies, waits for them, and re-layouts  3.84 us
  transfers between devices with their start and end apart: 26, of which 7 were waited for; matrix products, arithmetic and copies ran while one was open for 14% of the time, Pallas kernels for 29%

profile of v10, /device:TPU:1, one launch (start us, length us, event | category | flops | bytes accessed | tf_op | source)
XLA Modules:
  0.0 182.8 jit_solution(17314183994244563738)
XLA Ops:
  0.6 2.8 %broadcast_in_dim.2 = bf16[8,128,1152]{2,1,0:T(8,128)(2,1)} broadcast(bf16[128,1152]{1,0:T(8,128)(2,1)} %param.7), dimensions={1,2} | broadcast | bytes 2654208 | tf_op jit(solution)/shard_map/broadcast_in_dim | solution.py:541
  3.5 6.9 %all-to-all-start = ((bf16[8,128,1152]{2,1,0:T(8,128)(2,1)}), bf16[8,128,1152]{2,1,0:T(8,128)(2,1)}, u32[]{:S(2)}, u32[]{:S(2)}) async-start(bf16[8,128,1152]{2,1,0:T(8,128)(2,1)} %broadcast_in_dim.2), calls=%async_computation | async-start | bytes 4718592 | tf_op jit(solution)/shard_map/all_to_all | solution.py:65
  10.5 2.8 %collective-permute-start = (bf16[144,1152]{1,0:T(8,128)(2,1)S(1)}, bf16[144,1152]{1,0:T(8,128)(2,1)}, u32[]{:S(2)}, u32[]{:S(2)}) collective-permute-start(bf16[144,1152]{1,0:T(8,128)(2,1)S(1)} %pad_maximum_fusion.refs_3_.refs_8_), channel_id=1, source_target_pairs={{0,24},{1,25},{2,26},{3,27},{4,28},{5,29},{6,30},{7,31},{8,16},{9,... | collective-permute-start | bytes 995336 | tf_op jit(solution)/shard_map/ppermute | solution.py:61
  16.1 4.3 %collective-permute-done.refs_4_.refs_9_ = bf16[144,1152]{1,0:T(8,128)(2,1)} collective-permute-done((bf16[144,1152]{1,0:T(8,128)(2,1)S(1)}, bf16[144,1152]{1,0:T(8,128)(2,1)}, u32[]{:S(2)}, u32[]{:S(2)}) %collective-permute-start) | collective-permute-done | bytes 331808 | tf_op jit(solution)/shard_map/ppermute | solution.py:61
  20.3 2.7 %collective-permute-start.1 = (bf16[144,1152]{1,0:T(8,128)(2,1)}, bf16[144,1152]{1,0:T(8,128)(2,1)}, u32[]{:S(2)}, u32[]{:S(2)}) collective-permute-start(bf16[144,1152]{1,0:T(8,128)(2,1)} %collective-permute-done.refs_4_.refs_9_), channel_id=1, source_target_pairs={{0,6},{1,7},{2,0},{3,1},{4,2},{5,3},{6,4},{7,5},{8,14},{9,15},{10,... | collective-permute-start | bytes 995336 | tf_op jit(solution)/shard_map/ppermute | solution.py:61
  23.1 5.2 %copy.13 = bf16[1152,1152]{0,1:T(8,128)(2,1)} copy(bf16[1152,1152]{1,0:T(8,128)(2,1)} %param.10) | data formatting | bytes 5308416 | tf_op jit(solution)/shard_map/optimization_barrier | solution.py:509
  28.3 2.2 %collective-permute-done.1.refs_6_.refs_11_ = bf16[144,1152]{1,0:T(8,128)(2,1)} collective-permute-done((bf16[144,1152]{1,0:T(8,128)(2,1)}, bf16[144,1152]{1,0:T(8,128)(2,1)}, u32[]{:S(2)}, u32[]{:S(2)}) %collective-permute-start.1) | collective-permute-done | bytes 331808 | tf_op jit(solution)/shard_map/ppermute | solution.py:61
  34.4 7.6 %shard_map.102 = (bf16[1168,1024]{1,0:T(8,128)(2,1)}, f32[1,1024]{1,0:T(1,128)}) custom-call(s32[16]{0:T(128)} %stack.83.refs_0_, bf16[144,1152]{1,0:T(8,128)(2,1)} %collective-permute-done.2.refs_1_.refs_14_, bf16[144,1152]{1,0:T(8,128)(2,1)} %collective-permute-done.6.refs_2_.refs_15_, bf16[144,1152]{1,0:T(8,128)(2,1)} %copy-done.5, ...), custom_call_target="tpu_custom_call" | custom-call | flops 2038431744 | bytes 4644864 | tf_op jit(solution)/shard_map/pallas_call | solution.py:93
  42.9 4.7 %shard_map.103 = (bf16[1168,1024]{1,0:T(8,128)(2,1)}, f32[1,1024]{1,0:T(1,128)}) custom-call(s32[16]{0:T(128)} %stack.83.refs_0_, bf16[144,1152]{1,0:T(8,128)(2,1)} %copy-done.3, bf16[144,1152]{1,0:T(8,128)(2,1)} %copy-done.4, bf16[1152,1152]{1,0:T(8,128)(2,1)} %bitcast.48, ...), custom_call_target="tpu_custom_call", output_to_operand_aliasing={{0}: (4, {}), {1}: (5, {})} | custom-call | flops 679477248 | bytes 5713920 | tf_op jit(solution)/shard_map/pallas_call | solution.py:93
  47.6 2.1 %collective-permute-start.7 = (bf16[1168,1024]{1,0:T(8,128)(2,1)}, bf16[1168,1024]{1,0:T(8,128)(2,1)}, u32[]{:S(2)}, u32[]{:S(2)}) collective-permute-start(bf16[1168,1024]{1,0:T(8,128)(2,1)} %get-tuple-element.60.refs_3_.refs_6_), channel_id=1, source_target_pairs={{0,1},{1,0},{2,3},{3,2},{4,5},{5,4},{6,7},{7,6},{8,9},{9,8},{10,11... | collective-permute-start | bytes 7176200 | tf_op jit(solution)/shard_map/ppermute | solution.py:61
  49.7 5.0 %multiply_reduce_fusion = (f32[1024]{0:T(1024)S(1)}, f32[1152,1024]{1,0:T(8,128)S(1)}) fusion(bf16[1152,1152]{1,0:T(8,128)(2,1)S(1)} %copy-done, bf16[1024,1152]{1,0:T(8,128)(2,1)} %bitcast.17.refs_4_), kind=kOutput, calls=%fused_computation.2 | convolution fusion | flops 2720267264 | bytes 9736192 | tf_op jit(solution)/shard_map/dot_general | solution.py:75
  55.3 6.6 %fusion.refs_1_ = bf16[1024,1152]{1,0:T(8,128)(2,1)} fusion(bf16[1024,1152]{1,0:T(8,128)(2,1)} %bitcast.17.refs_4_, bf16[1152,1152]{1,0:T(8,128)(2,1)S(1)} %copy-done, f32[1024]{0:T(1024)S(1)} %get-tuple-element.102), kind=kOutput, calls=%fused_computation.3 | convolution fusion | flops 2720268288 | bytes 7376896 | tf_op jit(solution)/shard_map/dot_general | solution.py:75
  63.9 12.3 %shard_map.104 = (bf16[4,1024,256]{2,1,0:T(8,128)(2,1)}, f32[1,1024]{1,0:T(1,128)}, bf16[1280,1024]{1,0:T(8,128)(2,1)}) custom-call(f32[33]{0:T(128)} %pad_maximum_fusion.1.refs_0_, bf16[1024,1152]{1,0:T(8,128)(2,1)} %fusion.refs_1_, bf16[1152,1024]{1,0:T(8,128)(2,1)} %multiply_convert_fusion.refs_2_, bf16[1168,1024]{1,0:T(8,128)(2,1)} %collective-permute-done.7.refs_3_.refs_4_), custom_call_target="tpu_custom_call" | custom-call | flops 4831838208 | bytes 7110788 | tf_op jit(solution)/shard_map/pallas_call | solution.py:93
  76.2 18.5 %shard_map.105 = (bf16[1280,1024]{1,0:T(8,128)(2,1)}, bf16[8,160,1024]{2,1,0:T(8,128)(2,1)}) custom-call(f32[33]{0:T(128)} %pad_maximum_fusion.1.refs_0_, bf16[1024,1152]{1,0:T(8,128)(2,1)} %fusion.refs_1_, bf16[1152,1024]{1,0:T(8,128)(2,1)} %multiply_convert_fusion.refs_2_, bf16[1168,1024]{1,0:T(8,128)(2,1)} %get-tuple-element.60.refs_3_.refs_6_, ...), custom_call_target="tpu_custom_call" | custom-call | flops 9663676416 | bytes 11604100 | tf_op jit(solution)/shard_map/pallas_call | solution.py:93
  94.7 3.2 %shard_map.106 = (bf16[160,1024]{1,0:T(8,128)(2,1)}, bf16[160,1024]{1,0:T(8,128)(2,1)}, bf16[160,1024]{1,0:T(8,128)(2,1)}) custom-call(s32[16]{0:T(128)} %stack.83.refs_0_, bf16[1280,1024]{1,0:T(8,128)(2,1)} %get-tuple-element.64.refs_1_.refs_3_.refs_5_.refs_4_, bf16[1280,1024]{1,0:T(8,128)(2,1)} %collective-permute-done.8.refs_2_.refs_4_.refs_6_.refs_5_, ...), custom_call_target="tpu_custom_call" | custom-call | bytes 15728640 | tf_op jit(solution)/shard_map/pallas_call | solution.py:93
  97.9 4.6 %all-to-all-start.1 = ((bf16[8,160,1024]{2,1,0:T(8,128)(2,1)}), bf16[8,160,1024]{2,1,0:T(8,128)(2,1)}, u32[]{:S(2)}, u32[]{:S(2)}) async-start(bf16[8,160,1024]{2,1,0:T(8,128)(2,1)} %get-tuple-element.70), calls=%async_computation.1 | async-start | bytes 5242880 | tf_op jit(solution)/shard_map/all_to_all | solution.py:65
  102.7 2.5 %collective-permute-start.10 = (bf16[160,1024]{1,0:T(8,128)(2,1)}, bf16[160,1024]{1,0:T(8,128)(2,1)S(1)}, u32[]{:S(2)}, u32[]{:S(2)}) collective-permute-start(bf16[160,1024]{1,0:T(8,128)(2,1)} %get-tuple-element.75), channel_id=1, source_target_pairs={{0,6},{1,7},{2,0},{3,1},{4,2},{5,3},{6,4},{7,5},{8,14},{9,15},{10,... | collective-permute-start | bytes 983048 | tf_op jit(solution)/shard_map/ppermute | solution.py:61
  105.2 7.7 %collective-permute-done.9.refs_3_ = bf16[160,1024]{1,0:T(8,128)(2,1)S(1)} collective-permute-done((bf16[160,1024]{1,0:T(8,128)(2,1)}, bf16[160,1024]{1,0:T(8,128)(2,1)S(1)}, u32[]{:S(2)}, u32[]{:S(2)}) %collective-permute-start.9) | collective-permute-done | bytes 327712 | tf_op jit(solution)/shard_map/ppermute | solution.py:61
  113.7 2.7 %shard_map.108 = bf16[160,1024]{1,0:T(8,128)(2,1)} custom-call(s32[16]{0:T(128)} %stack.83.refs_0_, bf16[1280,1024]{1,0:T(8,128)(2,1)} %get-tuple-element.64.refs_1_.refs_3_.refs_5_.refs_4_, bf16[1280,1024]{1,0:T(8,128)(2,1)} %collective-permute-done.8.refs_2_.refs_4_.refs_6_.refs_5_, bf16[160,1024]{1,0:T(8,128)(2,1)} %copy-done.11), custom_call_target="tpu_custom_call" | custom-call | bytes 5570560 | tf_op jit(solution)/shard_map/pallas_call | solution.py:93
  116.4 2.3 %collective-permute-start.12 = (bf16[160,1024]{1,0:T(8,128)(2,1)}, bf16[160,1024]{1,0:T(8,128)(2,1)S(1)}, u32[]{:S(2)}, u32[]{:S(2)}) collective-permute-start(bf16[160,1024]{1,0:T(8,128)(2,1)} %shard_map.108), channel_id=1, source_target_pairs={{0,6},{1,7},{2,0},{3,1},{4,2},{5,3},{6,4},{7,5},{8,14},{9,15},{10,... | collective-permute-start | bytes 983048 | tf_op jit(solution)/shard_map/ppermute | solution.py:61
  118.7 3.6 %collective-permute-done.11.refs_3_ = bf16[160,1024]{1,0:T(8,128)(2,1)S(1)} collective-permute-done((bf16[160,1024]{1,0:T(8,128)(2,1)S(1)}, bf16[160,1024]{1,0:T(8,128)(2,1)S(1)}, u32[]{:S(2)}, u32[]{:S(2)}) %collective-permute-start.11) | collective-permute-done | bytes 327712 | tf_op jit(solution)/shard_map/ppermute | solution.py:61
  122.3 3.0 %shard_map.109 = (bf16[160,1024]{1,0:T(8,128)(2,1)}, bf16[160,1024]{1,0:T(8,128)(2,1)}) custom-call(s32[16]{0:T(128)} %stack.83.refs_0_, bf16[1280,1024]{1,0:T(8,128)(2,1)} %get-tuple-element.64.refs_1_.refs_3_.refs_5_.refs_4_, bf16[1280,1024]{1,0:T(8,128)(2,1)} %collective-permute-done.8.refs_2_.refs_4_.refs_6_.refs_5_, bf16[160,1024]{1,0:T(8,128)(2,1)} %copy-done.8, ...), custom_call_target="tpu_custom_call" | custom-call | bytes 10813440 | tf_op jit(solution)/shard_map/pallas_call | solution.py:93
  126.0 2.9 %shard_map.110 = bf16[160,1024]{1,0:T(8,128)(2,1)} custom-call(s32[16]{0:T(128)} %stack.83.refs_0_, bf16[1280,1024]{1,0:T(8,128)(2,1)} %get-tuple-element.64.refs_1_.refs_3_.refs_5_.refs_4_, bf16[1280,1024]{1,0:T(8,128)(2,1)} %collective-permute-done.8.refs_2_.refs_4_.refs_6_.refs_5_, bf16[160,1024]{1,0:T(8,128)(2,1)} %copy-done.9, bf16[160,1024]{1,0:T(8,128)(2,1)} %copy-done.10), custom_call_target="tpu_custom_call" | custom-call | bytes 5898240 | tf_op jit(solution)/shard_map/pallas_call | solution.py:93
  130.6 2.6 %collective-permute-start.14 = (bf16[160,1024]{1,0:T(8,128)(2,1)}, bf16[160,1024]{1,0:T(8,128)(2,1)}, u32[]{:S(2)}, u32[]{:S(2)}) collective-permute-start(bf16[160,1024]{1,0:T(8,128)(2,1)} %get-tuple-element.85), channel_id=1, source_target_pairs={{0,6},{1,7},{2,0},{3,1},{4,2},{5,3},{6,4},{7,5},{8,14},{9,15},{10,... | collective-permute-start | bytes 983048 | tf_op jit(solution)/shard_map/ppermute | solution.py:61
  134.7 4.9 %shard_map.107 = (bf16[8,144,128]{2,1,0:T(8,128)(2,1)}, bf16[144,1152]{1,0:T(8,128)(2,1)}) custom-call(s32[16]{0:T(128)} %stack.83.refs_0_, bf16[8,160,1024]{2,1,0:T(8,128)(2,1)} %all-to-all-done.1.refs_1_, bf16[1152,1024]{1,0:T(8,128)(2,1)} %multiply_convert_fusion.refs_2_, f32[1,1024]{1,0:T(1,128)} %bitcast.51, bf16[1024,1152]{1,0:T(8,128)(2,1)} %bitcast.17.refs_4_), custom_call_target="tpu_custom_call" | custom-call | tf_op jit(solution)/shard_map/pallas_call | solution.py:93
  139.6 3.4 %all-to-all-start.2 = ((bf16[8,144,128]{2,1,0:T(8,128)(2,1)}), bf16[8,144,128]{2,1,0:T(8,128)(2,1)S(1)}, u32[]{:S(2)}, u32[]{:S(2)}) async-start(bf16[8,144,128]{2,1,0:T(8,128)(2,1)} %get-tuple-element.71), calls=%async_computation.2 | async-start | bytes 589824 | tf_op jit(solution)/shard_map/all_to_all | solution.py:65
  143.8 5.0 %shard_map.111 = (bf16[4,144,128]{2,1,0:T(8,128)(2,1)}, bf16[4,144,128]{2,1,0:T(8,128)(2,1)}, bf16[144,1152]{1,0:T(8,128)(2,1)}) custom-call(s32[16]{0:T(128)} %stack.83.refs_0_, bf16[1280,1024]{1,0:T(8,128)(2,1)} %get-tuple-element.64.refs_1_.refs_3_.refs_5_.refs_4_, bf16[1280,1024]{1,0:T(8,128)(2,1)} %collective-permute-done.8.refs_2_.refs_4_.refs_6_.refs_5_, ...), custom_call_target="tpu_custom_call" | custom-call | tf_op jit(solution)/shard_map/pallas_call | solution.py:93
  148.8 2.6 %collective-permute-start.17 = (bf16[144,1152]{1,0:T(8,128)(2,1)}, bf16[144,1152]{1,0:T(8,128)(2,1)}, u32[]{:S(2)}, u32[]{:S(2)}) collective-permute-start(bf16[144,1152]{1,0:T(8,128)(2,1)} %get-tuple-element.89.txt), channel_id=1, source_target_pairs={{0,1},{1,0},{2,3},{3,2},{4,5},{5,4},{6,7},{7,6},{8,9},{9,8},{10,11... | collective-permute-start | bytes 995336 | tf_op jit(solution)/shard_map/ppermute | solution.py:61
  155.0 3.4 %shard_map.112 = bf16[512,384]{1,0:T(8,128)(2,1)} custom-call(s32[1]{0:T(128)} %bitcast.4.core, bf16[144,1152]{1,0:T(8,128)(2,1)} %get-tuple-element.73.img, bf16[144,1152]{1,0:T(8,128)(2,1)} %get-tuple-element.89.txt, bf16[144,1152]{1,0:T(8,128)(2,1)} %collective-permute-done.16.other_img, bf16[144,1152]{1,0:T(8,128)(2,1)} %collective-permute-done.17.other_txt), custom_call_target="tpu_custom_call" | custom-call | tf_op jit(solution)/shard_map/pallas_call | solution.py:93
  158.4 8.1 %all-to-all-start.3 = ((bf16[64,8,384]{2,1,0:T(8,128)(2,1)}), bf16[64,8,384]{2,1,0:T(8,128)(2,1)S(1)}, u32[]{:S(2)}, u32[]{:S(2)}) async-start(bf16[64,8,384]{2,1,0:T(8,128)(2,1)} %bitcast.49), calls=%async_computation.3 | async-start | bytes 786432 | tf_op jit(solution)/shard_map/all_to_all | solution.py:65
  171.8 2.5 %collective-permute-done.19 = bf16[288,128]{1,0:T(8,128)(2,1)S(1)} collective-permute-done((bf16[288,128]{1,0:T(8,128)(2,1)S(1)}, bf16[288,128]{1,0:T(8,128)(2,1)S(1)}, u32[]{:S(2)}, u32[]{:S(2)}) %collective-permute-start.19) | collective-permute-done | bytes 73760 | tf_op jit(solution)/shard_map/ppermute | solution.py:61
  174.3 4.0 %collective-permute-done.20 = bf16[288,128]{1,0:T(8,128)(2,1)S(1)} collective-permute-done((bf16[288,128]{1,0:T(8,128)(2,1)S(1)}, bf16[288,128]{1,0:T(8,128)(2,1)S(1)}, u32[]{:S(2)}, u32[]{:S(2)}) %collective-permute-start.20) | collective-permute-done | bytes 73760 | tf_op jit(solution)/shard_map/ppermute | solution.py:61
  (93 shorter events, 29.3 us)
Async XLA Ops:
  0.6 49.1 %copy-start = (bf16[1152,1152]{1,0:T(8,128)(2,1)S(1)}, bf16[1152,1152]{1,0:T(8,128)(2,1)}, u32[]{:S(2)}) copy-start(bf16[1152,1152]{1,0:T(8,128)(2,1)} %param.9) | copy-start | bytes 7962628
  3.5 46.2 %all-to-all-start = ((bf16[8,128,1152]{2,1,0:T(8,128)(2,1)}), bf16[8,128,1152]{2,1,0:T(8,128)(2,1)}, u32[]{:S(2)}, u32[]{:S(2)}) async-start(bf16[8,128,1152]{2,1,0:T(8,128)(2,1)} %broadcast_in_dim.2), calls=%async_computation | async-start | bytes 4718592 | tf_op jit(solution)/shard_map/all_to_all | solution.py:65
  10.5 17.8 %copy-start.5 = (bf16[144,1152]{1,0:T(8,128)(2,1)}, bf16[144,1152]{1,0:T(8,128)(2,1)S(1)}, u32[]{:S(2)}) copy-start(bf16[144,1152]{1,0:T(8,128)(2,1)S(1)} %pad_maximum_fusion.refs_3_.refs_8_) | copy-start | bytes 995332
  10.5 23.3 %copy-start.18 = (f32[32]{0:T(128)S(1)}, f32[32]{0:T(128)}, u32[]{:S(2)}) copy-start(f32[32]{0:T(128)} %param.11) | copy-start | bytes 388
  10.5 9.8 %collective-permute-start = (bf16[144,1152]{1,0:T(8,128)(2,1)S(1)}, bf16[144,1152]{1,0:T(8,128)(2,1)}, u32[]{:S(2)}, u32[]{:S(2)}) collective-permute-start(bf16[144,1152]{1,0:T(8,128)(2,1)S(1)} %pad_maximum_fusion.refs_3_.refs_8_), channel_id=1, source_target_pairs={{0,24},{1,25},{2,26},{3,27},{4,28},{5,29},{6,30},{7,31},{8,16},{9,... | collective-permute-start | bytes 995336 | tf_op jit(solution)/shard_map/ppermute | solution.py:61
  13.3 9.7 %collective-permute-start.2 = (bf16[144,1152]{1,0:T(8,128)(2,1)S(1)}, bf16[144,1152]{1,0:T(8,128)(2,1)}, u32[]{:S(2)}, u32[]{:S(2)}) collective-permute-start(bf16[144,1152]{1,0:T(8,128)(2,1)S(1)} %pad_maximum_fusion.refs_3_.refs_8_), channel_id=1, source_target_pairs={{0,2},{1,3},{2,4},{3,5},{4,6},{5,7},{6,0},{7,1},{8,10},{9,11},{10,... | collective-permute-start | bytes 995336 | tf_op jit(solution)/shard_map/ppermute | solution.py:61
  14.6 13.7 %collective-permute-start.3 = (bf16[144,1152]{1,0:T(8,128)(2,1)S(1)}, bf16[144,1152]{1,0:T(8,128)(2,1)S(1)}, u32[]{:S(2)}, u32[]{:S(2)}) collective-permute-start(bf16[144,1152]{1,0:T(8,128)(2,1)S(1)} %pad_maximum_fusion.refs_3_.refs_8_), channel_id=1, source_target_pairs={{0,6},{1,7},{2,0},{3,1},{4,2},{5,3},{6,4},{7,5},{8,14},{9,15},{10,... | collective-permute-start | bytes 995336 | tf_op jit(solution)/shard_map/ppermute | solution.py:61
  20.3 10.2 %collective-permute-start.1 = (bf16[144,1152]{1,0:T(8,128)(2,1)}, bf16[144,1152]{1,0:T(8,128)(2,1)}, u32[]{:S(2)}, u32[]{:S(2)}) collective-permute-start(bf16[144,1152]{1,0:T(8,128)(2,1)} %collective-permute-done.refs_4_.refs_9_), channel_id=1, source_target_pairs={{0,6},{1,7},{2,0},{3,1},{4,2},{5,3},{6,4},{7,5},{8,14},{9,15},{10,... | collective-permute-start | bytes 995336 | tf_op jit(solution)/shard_map/ppermute | solution.py:61
  23.1 11.4 %collective-permute-start.6 = (bf16[144,1152]{1,0:T(8,128)(2,1)}, bf16[144,1152]{1,0:T(8,128)(2,1)}, u32[]{:S(2)}, u32[]{:S(2)}) collective-permute-start(bf16[144,1152]{1,0:T(8,128)(2,1)} %collective-permute-done.refs_4_.refs_9_), channel_id=1, source_target_pairs={{0,2},{1,3},{2,4},{3,5},{4,6},{5,7},{6,0},{7,1},{8,10},{9,11},{10,... | collective-permute-start | bytes 995336 | tf_op jit(solution)/shard_map/ppermute | solution.py:61
  30.5 11.6 %collective-permute-start.4 = (bf16[144,1152]{1,0:T(8,128)(2,1)}, bf16[144,1152]{1,0:T(8,128)(2,1)S(1)}, u32[]{:S(2)}, u32[]{:S(2)}) collective-permute-start(bf16[144,1152]{1,0:T(8,128)(2,1)} %collective-permute-done.2.refs_1_.refs_14_), channel_id=1, source_target_pairs={{0,2},{1,3},{2,4},{3,5},{4,6},{5,7},{6,0},{7,1},{8,10},{9,11},{10,... | collective-permute-start | bytes 995336 | tf_op jit(solution)/shard_map/ppermute | solution.py:61
  31.8 10.3 %collective-permute-start.5 = (bf16[144,1152]{1,0:T(8,128)(2,1)}, bf16[144,1152]{1,0:T(8,128)(2,1)S(1)}, u32[]{:S(2)}, u32[]{:S(2)}) collective-permute-start(bf16[144,1152]{1,0:T(8,128)(2,1)} %collective-permute-done.1.refs_6_.refs_11_), channel_id=1, source_target_pairs={{0,6},{1,7},{2,0},{3,1},{4,2},{5,3},{6,4},{7,5},{8,14},{9,15},{10,... | collective-permute-start | bytes 995336 | tf_op jit(solution)/shard_map/ppermute | solution.py:61
  47.6 16.3 %collective-permute-start.7 = (bf16[1168,1024]{1,0:T(8,128)(2,1)}, bf16[1168,1024]{1,0:T(8,128)(2,1)}, u32[]{:S(2)}, u32[]{:S(2)}) collective-permute-start(bf16[1168,1024]{1,0:T(8,128)(2,1)} %get-tuple-element.60.refs_3_.refs_6_), channel_id=1, source_target_pairs={{0,1},{1,0},{2,3},{3,2},{4,5},{5,4},{6,7},{7,6},{8,9},{9,8},{10,11... | collective-permute-start | bytes 7176200 | tf_op jit(solution)/shard_map/ppermute | solution.py:61
  76.2 18.5 %collective-permute-start.8 = (bf16[1280,1024]{1,0:T(8,128)(2,1)}, bf16[1280,1024]{1,0:T(8,128)(2,1)}, u32[]{:S(2)}, u32[]{:S(2)}) collective-permute-start(bf16[1280,1024]{1,0:T(8,128)(2,1)} %get-tuple-element.65), channel_id=1, source_target_pairs={{0,1},{1,0},{2,3},{3,2},{4,5},{5,4},{6,7},{7,6},{8,9},{9,8},{10,11... | collective-permute-start | bytes 7864328 | tf_op jit(solution)/shard_map/ppermute | solution.py:61
  97.9 15.0 %copy-start.17 = (bf16[160,1024]{1,0:T(8,128)(2,1)S(1)}, bf16[160,1024]{1,0:T(8,128)(2,1)}, u32[]{:S(2)}) copy-start(bf16[160,1024]{1,0:T(8,128)(2,1)} %get-tuple-element.78) | copy-start | bytes 983044
  97.9 36.8 %all-to-all-start.1 = ((bf16[8,160,1024]{2,1,0:T(8,128)(2,1)}), bf16[8,160,1024]{2,1,0:T(8,128)(2,1)}, u32[]{:S(2)}, u32[]{:S(2)}) async-start(bf16[8,160,1024]{2,1,0:T(8,128)(2,1)} %get-tuple-element.70), calls=%async_computation.1 | async-start | bytes 5242880 | tf_op jit(solution)/shard_map/all_to_all | solution.py:65
  102.5 10.4 %collective-permute-start.9 = (bf16[160,1024]{1,0:T(8,128)(2,1)}, bf16[160,1024]{1,0:T(8,128)(2,1)S(1)}, u32[]{:S(2)}, u32[]{:S(2)}) collective-permute-start(bf16[160,1024]{1,0:T(8,128)(2,1)} %get-tuple-element.74), channel_id=1, source_target_pairs={{0,2},{1,3},{2,4},{3,5},{4,6},{5,7},{6,0},{7,1},{8,10},{9,11},{10,... | collective-permute-start | bytes 983048 | tf_op jit(solution)/shard_map/ppermute | solution.py:61
  102.7 10.2 %collective-permute-start.10 = (bf16[160,1024]{1,0:T(8,128)(2,1)}, bf16[160,1024]{1,0:T(8,128)(2,1)S(1)}, u32[]{:S(2)}, u32[]{:S(2)}) collective-permute-start(bf16[160,1024]{1,0:T(8,128)(2,1)} %get-tuple-element.75), channel_id=1, source_target_pairs={{0,6},{1,7},{2,0},{3,1},{4,2},{5,3},{6,4},{7,5},{8,14},{9,15},{10,... | collective-permute-start | bytes 983048 | tf_op jit(solution)/shard_map/ppermute | solution.py:61
  112.9 9.4 %collective-permute-start.11 = (bf16[160,1024]{1,0:T(8,128)(2,1)S(1)}, bf16[160,1024]{1,0:T(8,128)(2,1)S(1)}, u32[]{:S(2)}, u32[]{:S(2)}) collective-permute-start(bf16[160,1024]{1,0:T(8,128)(2,1)S(1)} %copy-done.17), channel_id=1, source_target_pairs={{0,2},{1,3},{2,4},{3,5},{4,6},{5,7},{6,0},{7,1},{8,10},{9,11},{10,... | collective-permute-start | bytes 983048 | tf_op jit(solution)/shard_map/ppermute | solution.py:61
  116.4 8.9 %collective-permute-start.12 = (bf16[160,1024]{1,0:T(8,128)(2,1)}, bf16[160,1024]{1,0:T(8,128)(2,1)S(1)}, u32[]{:S(2)}, u32[]{:S(2)}) collective-permute-start(bf16[160,1024]{1,0:T(8,128)(2,1)} %shard_map.108), channel_id=1, source_target_pairs={{0,6},{1,7},{2,0},{3,1},{4,2},{5,3},{6,4},{7,5},{8,14},{9,15},{10,... | collective-permute-start | bytes 983048 | tf_op jit(solution)/shard_map/ppermute | solution.py:61
  128.9 14.1 %collective-permute-start.15 = (bf16[160,1024]{1,0:T(8,128)(2,1)}, bf16[160,1024]{1,0:T(8,128)(2,1)S(1)}, u32[]{:S(2)}, u32[]{:S(2)}) collective-permute-start(bf16[160,1024]{1,0:T(8,128)(2,1)} %shard_map.110), channel_id=1, source_target_pairs={{0,24},{1,25},{2,26},{3,27},{4,28},{5,29},{6,30},{7,31},{8,16},{9,... | collective-permute-start | bytes 983048 | tf_op jit(solution)/shard_map/ppermute | solution.py:61
  130.4 12.6 %collective-permute-start.13 = (bf16[160,1024]{1,0:T(8,128)(2,1)}, bf16[160,1024]{1,0:T(8,128)(2,1)}, u32[]{:S(2)}, u32[]{:S(2)}) collective-permute-start(bf16[160,1024]{1,0:T(8,128)(2,1)} %get-tuple-element.84), channel_id=1, source_target_pairs={{0,2},{1,3},{2,4},{3,5},{4,6},{5,7},{6,0},{7,1},{8,10},{9,11},{10,... | collective-permute-start | bytes 983048 | tf_op jit(solution)/shard_map/ppermute | solution.py:61
  130.6 12.5 %collective-permute-start.14 = (bf16[160,1024]{1,0:T(8,128)(2,1)}, bf16[160,1024]{1,0:T(8,128)(2,1)}, u32[]{:S(2)}, u32[]{:S(2)}) collective-permute-start(bf16[160,1024]{1,0:T(8,128)(2,1)} %get-tuple-element.85), channel_id=1, source_target_pairs={{0,6},{1,7},{2,0},{3,1},{4,2},{5,3},{6,4},{7,5},{8,14},{9,15},{10,... | collective-permute-start | bytes 983048 | tf_op jit(solution)/shard_map/ppermute | solution.py:61
  139.6 13.7 %all-to-all-start.2 = ((bf16[8,144,128]{2,1,0:T(8,128)(2,1)}), bf16[8,144,128]{2,1,0:T(8,128)(2,1)S(1)}, u32[]{:S(2)}, u32[]{:S(2)}) async-start(bf16[8,144,128]{2,1,0:T(8,128)(2,1)} %get-tuple-element.71), calls=%async_computation.2 | async-start | bytes 589824 | tf_op jit(solution)/shard_map/all_to_all | solution.py:65
  148.8 6.3 %collective-permute-start.17 = (bf16[144,1152]{1,0:T(8,128)(2,1)}, bf16[144,1152]{1,0:T(8,128)(2,1)}, u32[]{:S(2)}, u32[]{:S(2)}) collective-permute-start(bf16[144,1152]{1,0:T(8,128)(2,1)} %get-tuple-element.89.txt), channel_id=1, source_target_pairs={{0,1},{1,0},{2,3},{3,2},{4,5},{5,4},{6,7},{7,6},{8,9},{9,8},{10,11... | collective-permute-start | bytes 995336 | tf_op jit(solution)/shard_map/ppermute | solution.py:61
  151.4 3.7 %collective-permute-start.16 = (bf16[144,1152]{1,0:T(8,128)(2,1)S(1)}, bf16[144,1152]{1,0:T(8,128)(2,1)}, u32[]{:S(2)}, u32[]{:S(2)}) collective-permute-start(bf16[144,1152]{1,0:T(8,128)(2,1)S(1)} %copy-done.7), channel_id=1, source_target_pairs={{0,1},{1,0},{2,3},{3,2},{4,5},{5,4},{6,7},{7,6},{8,9},{9,8},{10,11... | collective-permute-start | bytes 995336 | tf_op jit(solution)/shard_map/ppermute | solution.py:61
  151.4 7.0 %collective-permute-start.18 = (bf16[4,144,128]{2,1,0:T(8,128)(2,1)}, bf16[4,144,128]{2,1,0:T(8,128)(2,1)}, u32[]{:S(2)}, u32[]{:S(2)}) collective-permute-start(bf16[4,144,128]{2,1,0:T(8,128)(2,1)} %get-tuple-element.90), channel_id=1, source_target_pairs={{0,24},{1,25},{2,26},{3,27},{4,28},{5,29},{6,30},{7,31},{8,16},{9,... | collective-permute-start | bytes 442376 | tf_op jit(solution)/shard_map/ppermute | solution.py:61
  153.3 13.3 %copy-start.14 = (bf16[4,144,128]{2,1,0:T(8,128)(2,1)S(1)}, bf16[4,144,128]{2,1,0:T(8,128)(2,1)}, u32[]{:S(2)}) copy-start(bf16[4,144,128]{2,1,0:T(8,128)(2,1)} %get-tuple-element.92) | copy-start | bytes 442372
  158.4 21.8 %all-to-all-start.3 = ((bf16[64,8,384]{2,1,0:T(8,128)(2,1)}), bf16[64,8,384]{2,1,0:T(8,128)(2,1)S(1)}, u32[]{:S(2)}, u32[]{:S(2)}) async-start(bf16[64,8,384]{2,1,0:T(8,128)(2,1)} %bitcast.49), calls=%async_computation.3 | async-start | bytes 786432 | tf_op jit(solution)/shard_map/all_to_all | solution.py:65
  166.6 11.9 %copy-start.1 = (bf16[1152,1152]{1,0:T(8,128)(2,1)S(1)}, bf16[1152,1152]{1,0:T(8,128)(2,1)}, u32[]{:S(2)}) copy-start(bf16[1152,1152]{1,0:T(8,128)(2,1)} %param.10) | copy-start | bytes 7962628
  167.7 10.6 %collective-permute-start.21 = (bf16[288,128]{1,0:T(8,128)(2,1)S(1)}, bf16[288,128]{1,0:T(8,128)(2,1)S(1)}, u32[]{:S(2)}, u32[]{:S(2)}) collective-permute-start(bf16[288,128]{1,0:T(8,128)(2,1)S(1)} %get-tuple-element.96), channel_id=1, source_target_pairs={{0,2},{1,3},{2,4},{3,5},{4,6},{5,7},{6,0},{7,1},{8,10},{9,11},{10,... | collective-permute-start | bytes 221192 | tf_op jit(solution)/shard_map/ppermute | solution.py:61
  168.8 5.5 %collective-permute-start.19 = (bf16[288,128]{1,0:T(8,128)(2,1)S(1)}, bf16[288,128]{1,0:T(8,128)(2,1)S(1)}, u32[]{:S(2)}, u32[]{:S(2)}) collective-permute-start(bf16[288,128]{1,0:T(8,128)(2,1)S(1)} %get-tuple-element.97), channel_id=1, source_target_pairs={{0,6},{1,7},{2,0},{3,1},{4,2},{5,3},{6,4},{7,5},{8,14},{9,15},{10,... | collective-permute-start | bytes 221192 | tf_op jit(solution)/shard_map/ppermute | solution.py:61
  170.5 7.9 %collective-permute-start.20 = (bf16[288,128]{1,0:T(8,128)(2,1)S(1)}, bf16[288,128]{1,0:T(8,128)(2,1)S(1)}, u32[]{:S(2)}, u32[]{:S(2)}) collective-permute-start(bf16[288,128]{1,0:T(8,128)(2,1)S(1)} %get-tuple-element.98), channel_id=1, source_target_pairs={{0,4},{1,5},{2,6},{3,7},{4,0},{5,1},{6,2},{7,3},{8,12},{9,13},{10,... | collective-permute-start | bytes 221192 | tf_op jit(solution)/shard_map/ppermute | solution.py:61
  (13 other events, 41.7 us)

commit v11 on v10

--- a/solution.py
+++ b/solution.py
@@ -538,11 +538,11 @@
     figures = jnp.stack([text_lang, partner // 128, partner % 128]).astype(b16)
     figures = jnp.pad(figures, ((0, PAD - 3), (0, width - rows)))
     text_rows = jnp.concatenate([text_feat, figures], axis=0)
-    img_feats = exchange(jnp.broadcast_to(image_feat[None], (8, rows, width)), IMG_GROUPS)
-    img_feats = img_feats.reshape(8 * rows, width)
     across = send(text_rows, txt_move(0, 1))
     before = send(text_rows, txt_move(1, 0))
     after = send(text_rows, txt_move(3, 0))
+    img_feats = jnp.broadcast_to(together([image_feat, text_rows])[0][None], (8, rows, width))
+    img_feats = exchange(img_feats, IMG_GROUPS).reshape(8 * rows, width)
     turned_txt = together([text_head, before])[0].T
     across_after = send(across, txt_move(3, 0))
     across_before = send(across, txt_move(1, 0))

time: 184 us -> 200 us (1.087)
  local copies, waits for them, and re-layouts: 12.5 us -> 22.9 us
  other arithmetic: 4.48 us -> 8.63 us
  matrix products: 15 us -> 17.2 us
    dot_general x0 -> x1, local copies, waits for them, and re-layouts: none -> 6.09 us  [dot(): return lax.dot_general(a, b, dims, preferred_element_type=f32)]
    convert_element_type x0 -> x1, local copies, waits for them, and re-layouts: none -> 4.29 us  [unit_rows(): return (dot(feats, head, NN) * (1.0 / norm).reshape(-1, 1)).astype(b16)]
    convert_element_type x1, other arithmetic: 2.05 us -> 4.39 us  [unit_columns(): return ((projected * (1.0 / norm)).astype(b16), norm)]
    dot_general x4, matrix products: 15 us -> 17.2 us  [dot(): return lax.dot_general(a, b, dims, preferred_element_type=f32)]
  transfers between devices with their start and end apart: 26 -> 26, of which waited for: 7 -> 7; matrix products, arithmetic and copies ran while one was open for 14% -> 20% of each run, Pallas kernels for 29% -> 26%
where the time goes in v11:
time: 200 us; the launch traced here: 199 us
  Pallas kernels  69.8 us (35%)
  starting transfers between devices  53.9 us (27%)
  waiting for transfers between devices  25.8 us (13%)
  local copies, waits for them, and re-layouts  22.9 us (11%)
  matrix products  17.2 us (9%)
  other arithmetic  8.63 us (4%)
    pallas_call x12, Pallas kernels, call(): pl.pallas_call(body, out_shape=out_shape, grid_spec=spec, input_output_al...  69.8 us
    ppermute x22, starting transfers between devices, send(): lax.ppermute(block, DEV, [(flat(*p), flat(*move(*p))) for p in PLACES])  31.1 us
    ppermute x22, waiting for transfers between devices, send(): lax.ppermute(block, DEV, [(flat(*p), flat(*move(*p))) for p in PLACES])  24.2 us
    all_to_all x4, starting transfers between devices, exchange(): lax.all_to_all(blocks, DEV, 0, 0, axis_index_groups=groups, tiled=True)  22.8 us
    dot_general x4, matrix products, dot(): return lax.dot_general(a, b, dims, preferred_element_type=f32)  17.2 us
    dot_general x1, local copies, waits for them, and re-layouts, dot(): return lax.dot_general(a, b, dims, preferred_element_type=f32)  6.09 us
    optimization_barrier x1, local copies, waits for them, and re-layouts, together(): return lax.optimization_barrier(list(arrays))  5.24 us
    convert_element_type x1, other arithmetic, unit_columns(): return ((projected * (1.0 / norm)).astype(b16), norm)  4.39 us
  transfers between devices with their start and end apart: 26, of which 7 were waited for; matrix products, arithmetic and copies ran while one was open for 20% of the time, Pallas kernels for 26%

profile of v11, /device:TPU:1, one launch (start us, length us, event | category | flops | bytes accessed | tf_op | source)
XLA Modules:
  0.0 199.1 jit_solution(8920560025404623661)
XLA Ops:
  2.5 2.8 %broadcast_in_dim.2 = bf16[8,128,1152]{2,1,0:T(8,128)(2,1)} broadcast(bf16[128,1152]{1,0:T(8,128)(2,1)} %param.7), dimensions={1,2} | broadcast | bytes 2654208 | tf_op jit(solution)/shard_map/broadcast_in_dim | solution.py:544
  5.3 6.8 %all-to-all-start = ((bf16[8,128,1152]{2,1,0:T(8,128)(2,1)}), bf16[8,128,1152]{2,1,0:T(8,128)(2,1)}, u32[]{:S(2)}, u32[]{:S(2)}) async-start(bf16[8,128,1152]{2,1,0:T(8,128)(2,1)} %broadcast_in_dim.2), calls=%async_computation | async-start | bytes 4718592 | tf_op jit(solution)/shard_map/all_to_all | solution.py:65
  12.1 2.7 %collective-permute-start = (bf16[144,1152]{1,0:T(8,128)(2,1)S(1)}, bf16[144,1152]{1,0:T(8,128)(2,1)}, u32[]{:S(2)}, u32[]{:S(2)}) collective-permute-start(bf16[144,1152]{1,0:T(8,128)(2,1)S(1)} %pad_maximum_fusion.refs_3_.refs_8_), channel_id=1, source_target_pairs={{0,24},{1,25},{2,26},{3,27},{4,28},{5,29},{6,30},{7,31},{8,16},{9,... | collective-permute-start | bytes 995336 | tf_op jit(solution)/shard_map/ppermute | solution.py:61
  17.6 4.3 %collective-permute-done.refs_4_.refs_9_ = bf16[144,1152]{1,0:T(8,128)(2,1)} collective-permute-done((bf16[144,1152]{1,0:T(8,128)(2,1)S(1)}, bf16[144,1152]{1,0:T(8,128)(2,1)}, u32[]{:S(2)}, u32[]{:S(2)}) %collective-permute-start) | collective-permute-done | bytes 331808 | tf_op jit(solution)/shard_map/ppermute | solution.py:61
  21.8 2.7 %collective-permute-start.1 = (bf16[144,1152]{1,0:T(8,128)(2,1)}, bf16[144,1152]{1,0:T(8,128)(2,1)}, u32[]{:S(2)}, u32[]{:S(2)}) collective-permute-start(bf16[144,1152]{1,0:T(8,128)(2,1)} %collective-permute-done.refs_4_.refs_9_), channel_id=1, source_target_pairs={{0,6},{1,7},{2,0},{3,1},{4,2},{5,3},{6,4},{7,5},{8,14},{9,15},{10,... | collective-permute-start | bytes 995336 | tf_op jit(solution)/shard_map/ppermute | solution.py:61
  24.6 5.2 %copy.13 = bf16[1152,1152]{0,1:T(8,128)(2,1)} copy(bf16[1152,1152]{1,0:T(8,128)(2,1)} %param.10) | data formatting | bytes 5308416 | tf_op jit(solution)/shard_map/optimization_barrier | solution.py:509
  35.9 7.6 %shard_map.102 = (bf16[1168,1024]{1,0:T(8,128)(2,1)}, f32[1,1024]{1,0:T(1,128)}) custom-call(s32[16]{0:T(128)} %stack.83.refs_0_, bf16[144,1152]{1,0:T(8,128)(2,1)} %collective-permute-done.2.refs_1_.refs_14_, bf16[144,1152]{1,0:T(8,128)(2,1)} %collective-permute-done.6.refs_2_.refs_15_, bf16[144,1152]{1,0:T(8,128)(2,1)} %copy-done.5, ...), custom_call_target="tpu_custom_call" | custom-call | flops 2038431744 | bytes 4644864 | tf_op jit(solution)/shard_map/pallas_call | solution.py:93
  44.4 4.7 %shard_map.103 = (bf16[1168,1024]{1,0:T(8,128)(2,1)}, f32[1,1024]{1,0:T(1,128)}) custom-call(s32[16]{0:T(128)} %stack.83.refs_0_, bf16[144,1152]{1,0:T(8,128)(2,1)} %copy-done.3, bf16[144,1152]{1,0:T(8,128)(2,1)} %copy-done.4, bf16[1152,1152]{1,0:T(8,128)(2,1)} %bitcast.50, ...), custom_call_target="tpu_custom_call", output_to_operand_aliasing={{0}: (4, {}), {1}: (5, {})} | custom-call | flops 679477248 | bytes 5713920 | tf_op jit(solution)/shard_map/pallas_call | solution.py:93
  51.3 7.4 %multiply_reduce_fusion = (f32[1024]{0:T(1024)S(1)}, f32[1024,1152]{1,0:T(8,128)}) fusion(bf16[1024,1152]{1,0:T(8,128)(2,1)} %bitcast.20.refs_4_, bf16[1152,1152]{1,0:T(8,128)(2,1)S(1)} %copy-done), kind=kOutput, calls=%fused_computation.2 | convolution fusion | flops 2720267264 | bytes 9736192 | tf_op jit(solution)/shard_map/dot_general | solution.py:75
  59.2 6.3 %fusion = bf16[1024,1152]{0,1:T(8,128)(2,1)} fusion(bf16[1024,1152]{1,0:T(8,128)(2,1)} %bitcast.20.refs_4_, bf16[1152,1152]{1,0:T(8,128)(2,1)S(1)} %copy-done, f32[1024]{0:T(1024)S(1)} %get-tuple-element.104), kind=kOutput, calls=%fused_computation.3 | convolution fusion | flops 2720268288 | bytes 7376896 | tf_op jit(solution)/shard_map/dot_general | solution.py:75
  65.5 4.3 %copy.17.refs_1_ = bf16[1024,1152]{1,0:T(8,128)(2,1)} copy(bf16[1024,1152]{0,1:T(8,128)(2,1)} %fusion) | data formatting | bytes 4718592 | tf_op jit(solution)/shard_map/convert_element_type | solution.py:193
  69.8 6.1 %copy.15 = f32[1024,1152]{0,1:T(8,128)} copy(f32[1024,1152]{1,0:T(8,128)} %get-tuple-element.108) | data formatting | bytes 9437184 | tf_op jit(solution)/shard_map/dot_general | solution.py:75
  75.9 4.4 %fusion.1.refs_2_ = bf16[1152,1024]{1,0:T(8,128)(2,1)} fusion(f32[1024,1152]{0,1:T(8,128)} %copy.15, f32[1024]{0:T(1024)S(1)} %get-tuple-element.104), kind=kLoop, calls=%fused_computation.4 | loop fusion | flops 2359296 | bytes 7081984 | tf_op jit(solution)/shard_map/convert_element_type | solution.py:189
  80.3 12.2 %shard_map.104 = (bf16[4,1024,256]{2,1,0:T(8,128)(2,1)}, f32[1,1024]{1,0:T(1,128)}, bf16[1280,1024]{1,0:T(8,128)(2,1)}) custom-call(f32[33]{0:T(128)} %pad_maximum_fusion.1.refs_0_, bf16[1024,1152]{1,0:T(8,128)(2,1)} %copy.17.refs_1_, bf16[1152,1024]{1,0:T(8,128)(2,1)} %fusion.1.refs_2_, bf16[1168,1024]{1,0:T(8,128)(2,1)} %collective-permute-done.7.refs_3_.refs_4_), custom_call_target="tpu_custom_call" | custom-call | flops 4831838208 | bytes 7110788 | tf_op jit(solution)/shard_map/pallas_call | solution.py:93
  92.5 18.4 %shard_map.105 = (bf16[1280,1024]{1,0:T(8,128)(2,1)}, bf16[8,160,1024]{2,1,0:T(8,128)(2,1)}) custom-call(f32[33]{0:T(128)} %pad_maximum_fusion.1.refs_0_, bf16[1024,1152]{1,0:T(8,128)(2,1)} %copy.17.refs_1_, bf16[1152,1024]{1,0:T(8,128)(2,1)} %fusion.1.refs_2_, bf16[1168,1024]{1,0:T(8,128)(2,1)} %get-tuple-element.62.refs_3_.refs_6_, ...), custom_call_target="tpu_custom_call" | custom-call | flops 9663676416 | bytes 11604100 | tf_op jit(solution)/shard_map/pallas_call | solution.py:93
  111.0 3.2 %shard_map.106 = (bf16[160,1024]{1,0:T(8,128)(2,1)}, bf16[160,1024]{1,0:T(8,128)(2,1)}, bf16[160,1024]{1,0:T(8,128)(2,1)}) custom-call(s32[16]{0:T(128)} %stack.83.refs_0_, bf16[1280,1024]{1,0:T(8,128)(2,1)} %get-tuple-element.66.refs_1_.refs_3_.refs_5_.refs_4_, bf16[1280,1024]{1,0:T(8,128)(2,1)} %collective-permute-done.8.refs_2_.refs_4_.refs_6_.refs_5_, ...), custom_call_target="tpu_custom_call" | custom-call | bytes 15728640 | tf_op jit(solution)/shard_map/pallas_call | solution.py:93
  114.2 4.6 %all-to-all-start.1 = ((bf16[8,160,1024]{2,1,0:T(8,128)(2,1)}), bf16[8,160,1024]{2,1,0:T(8,128)(2,1)}, u32[]{:S(2)}, u32[]{:S(2)}) async-start(bf16[8,160,1024]{2,1,0:T(8,128)(2,1)} %get-tuple-element.72), calls=%async_computation.1 | async-start | bytes 5242880 | tf_op jit(solution)/shard_map/all_to_all | solution.py:65
  118.9 2.5 %collective-permute-start.10 = (bf16[160,1024]{1,0:T(8,128)(2,1)}, bf16[160,1024]{1,0:T(8,128)(2,1)S(1)}, u32[]{:S(2)}, u32[]{:S(2)}) collective-permute-start(bf16[160,1024]{1,0:T(8,128)(2,1)} %get-tuple-element.77), channel_id=1, source_target_pairs={{0,6},{1,7},{2,0},{3,1},{4,2},{5,3},{6,4},{7,5},{8,14},{9,15},{10,... | collective-permute-start | bytes 983048 | tf_op jit(solution)/shard_map/ppermute | solution.py:61
  121.5 7.7 %collective-permute-done.9.refs_3_ = bf16[160,1024]{1,0:T(8,128)(2,1)S(1)} collective-permute-done((bf16[160,1024]{1,0:T(8,128)(2,1)}, bf16[160,1024]{1,0:T(8,128)(2,1)S(1)}, u32[]{:S(2)}, u32[]{:S(2)}) %collective-permute-start.9) | collective-permute-done | bytes 327712 | tf_op jit(solution)/shard_map/ppermute | solution.py:61
  129.9 2.7 %shard_map.108 = bf16[160,1024]{1,0:T(8,128)(2,1)} custom-call(s32[16]{0:T(128)} %stack.83.refs_0_, bf16[1280,1024]{1,0:T(8,128)(2,1)} %get-tuple-element.66.refs_1_.refs_3_.refs_5_.refs_4_, bf16[1280,1024]{1,0:T(8,128)(2,1)} %collective-permute-done.8.refs_2_.refs_4_.refs_6_.refs_5_, bf16[160,1024]{1,0:T(8,128)(2,1)} %copy-done.11), custom_call_target="tpu_custom_call" | custom-call | bytes 5570560 | tf_op jit(solution)/shard_map/pallas_call | solution.py:93
  135.0 3.6 %collective-permute-done.11.refs_3_ = bf16[160,1024]{1,0:T(8,128)(2,1)S(1)} collective-permute-done((bf16[160,1024]{1,0:T(8,128)(2,1)S(1)}, bf16[160,1024]{1,0:T(8,128)(2,1)S(1)}, u32[]{:S(2)}, u32[]{:S(2)}) %collective-permute-start.11) | collective-permute-done | bytes 327712 | tf_op jit(solution)/shard_map/ppermute | solution.py:61
  138.5 3.0 %shard_map.109 = (bf16[160,1024]{1,0:T(8,128)(2,1)}, bf16[160,1024]{1,0:T(8,128)(2,1)}) custom-call(s32[16]{0:T(128)} %stack.83.refs_0_, bf16[1280,1024]{1,0:T(8,128)(2,1)} %get-tuple-element.66.refs_1_.refs_3_.refs_5_.refs_4_, bf16[1280,1024]{1,0:T(8,128)(2,1)} %collective-permute-done.8.refs_2_.refs_4_.refs_6_.refs_5_, bf16[160,1024]{1,0:T(8,128)(2,1)} %copy-done.8, ...), custom_call_target="tpu_custom_call" | custom-call | bytes 10813440 | tf_op jit(solution)/shard_map/pallas_call | solution.py:93
  142.3 2.9 %shard_map.110 = bf16[160,1024]{1,0:T(8,128)(2,1)} custom-call(s32[16]{0:T(128)} %stack.83.refs_0_, bf16[1280,1024]{1,0:T(8,128)(2,1)} %get-tuple-element.66.refs_1_.refs_3_.refs_5_.refs_4_, bf16[1280,1024]{1,0:T(8,128)(2,1)} %collective-permute-done.8.refs_2_.refs_4_.refs_6_.refs_5_, bf16[160,1024]{1,0:T(8,128)(2,1)} %copy-done.9, bf16[160,1024]{1,0:T(8,128)(2,1)} %copy-done.10), custom_call_target="tpu_custom_call" | custom-call | bytes 5898240 | tf_op jit(solution)/shard_map/pallas_call | solution.py:93
  146.8 2.6 %collective-permute-start.14 = (bf16[160,1024]{1,0:T(8,128)(2,1)}, bf16[160,1024]{1,0:T(8,128)(2,1)}, u32[]{:S(2)}, u32[]{:S(2)}) collective-permute-start(bf16[160,1024]{1,0:T(8,128)(2,1)} %get-tuple-element.87), channel_id=1, source_target_pairs={{0,6},{1,7},{2,0},{3,1},{4,2},{5,3},{6,4},{7,5},{8,14},{9,15},{10,... | collective-permute-start | bytes 983048 | tf_op jit(solution)/shard_map/ppermute | solution.py:61
  151.0 4.9 %shard_map.107 = (bf16[8,144,128]{2,1,0:T(8,128)(2,1)}, bf16[144,1152]{1,0:T(8,128)(2,1)}) custom-call(s32[16]{0:T(128)} %stack.83.refs_0_, bf16[8,160,1024]{2,1,0:T(8,128)(2,1)} %all-to-all-done.1.refs_1_, bf16[1152,1024]{1,0:T(8,128)(2,1)} %fusion.1.refs_2_, f32[1,1024]{1,0:T(1,128)} %bitcast.53, bf16[1024,1152]{1,0:T(8,128)(2,1)} %bitcast.20.refs_4_), custom_call_target="tpu_custom_call" | custom-call | tf_op jit(solution)/shard_map/pallas_call | solution.py:93
  155.8 3.4 %all-to-all-start.2 = ((bf16[8,144,128]{2,1,0:T(8,128)(2,1)}), bf16[8,144,128]{2,1,0:T(8,128)(2,1)S(1)}, u32[]{:S(2)}, u32[]{:S(2)}) async-start(bf16[8,144,128]{2,1,0:T(8,128)(2,1)} %get-tuple-element.73), calls=%async_computation.2 | async-start | bytes 589824 | tf_op jit(solution)/shard_map/all_to_all | solution.py:65
  160.0 5.0 %shard_map.111 = (bf16[4,144,128]{2,1,0:T(8,128)(2,1)}, bf16[4,144,128]{2,1,0:T(8,128)(2,1)}, bf16[144,1152]{1,0:T(8,128)(2,1)}) custom-call(s32[16]{0:T(128)} %stack.83.refs_0_, bf16[1280,1024]{1,0:T(8,128)(2,1)} %get-tuple-element.66.refs_1_.refs_3_.refs_5_.refs_4_, bf16[1280,1024]{1,0:T(8,128)(2,1)} %collective-permute-done.8.refs_2_.refs_4_.refs_6_.refs_5_, ...), custom_call_target="tpu_custom_call" | custom-call | tf_op jit(solution)/shard_map/pallas_call | solution.py:93
  165.0 2.6 %collective-permute-start.17 = (bf16[144,1152]{1,0:T(8,128)(2,1)}, bf16[144,1152]{1,0:T(8,128)(2,1)}, u32[]{:S(2)}, u32[]{:S(2)}) collective-permute-start(bf16[144,1152]{1,0:T(8,128)(2,1)} %get-tuple-element.91.txt), channel_id=1, source_target_pairs={{0,1},{1,0},{2,3},{3,2},{4,5},{5,4},{6,7},{7,6},{8,9},{9,8},{10,11... | collective-permute-start | bytes 995336 | tf_op jit(solution)/shard_map/ppermute | solution.py:61
  171.3 3.4 %shard_map.112 = bf16[512,384]{1,0:T(8,128)(2,1)} custom-call(s32[1]{0:T(128)} %bitcast.4.core, bf16[144,1152]{1,0:T(8,128)(2,1)} %get-tuple-element.75.img, bf16[144,1152]{1,0:T(8,128)(2,1)} %get-tuple-element.91.txt, bf16[144,1152]{1,0:T(8,128)(2,1)} %collective-permute-done.16.other_img, bf16[144,1152]{1,0:T(8,128)(2,1)} %collective-permute-done.17.other_txt), custom_call_target="tpu_custom_call" | custom-call | tf_op jit(solution)/shard_map/pallas_call | solution.py:93
  174.8 8.1 %all-to-all-start.3 = ((bf16[64,8,384]{2,1,0:T(8,128)(2,1)}), bf16[64,8,384]{2,1,0:T(8,128)(2,1)S(1)}, u32[]{:S(2)}, u32[]{:S(2)}) async-start(bf16[64,8,384]{2,1,0:T(8,128)(2,1)} %bitcast.51), calls=%async_computation.3 | async-start | bytes 786432 | tf_op jit(solution)/shard_map/all_to_all | solution.py:65
  188.1 2.5 %collective-permute-done.19 = bf16[288,128]{1,0:T(8,128)(2,1)S(1)} collective-permute-done((bf16[288,128]{1,0:T(8,128)(2,1)S(1)}, bf16[288,128]{1,0:T(8,128)(2,1)S(1)}, u32[]{:S(2)}, u32[]{:S(2)}) %collective-permute-start.19) | collective-permute-done | bytes 73760 | tf_op jit(solution)/shard_map/ppermute | solution.py:61
  190.6 4.0 %collective-permute-done.20 = bf16[288,128]{1,0:T(8,128)(2,1)S(1)} collective-permute-done((bf16[288,128]{1,0:T(8,128)(2,1)S(1)}, bf16[288,128]{1,0:T(8,128)(2,1)S(1)}, u32[]{:S(2)}, u32[]{:S(2)}) %collective-permute-start.20) | collective-permute-done | bytes 73760 | tf_op jit(solution)/shard_map/ppermute | solution.py:61
  (89 shorter events, 35.7 us)
Async XLA Ops:
  0.6 50.6 %copy-start = (bf16[1152,1152]{1,0:T(8,128)(2,1)S(1)}, bf16[1152,1152]{1,0:T(8,128)(2,1)}, u32[]{:S(2)}) copy-start(bf16[1152,1152]{1,0:T(8,128)(2,1)} %param.9) | copy-start | bytes 7962628
  2.5 13.6 %copy-start.5 = (bf16[144,1152]{1,0:T(8,128)(2,1)}, bf16[144,1152]{1,0:T(8,128)(2,1)S(1)}, u32[]{:S(2)}) copy-start(bf16[144,1152]{1,0:T(8,128)(2,1)S(1)} %pad_maximum_fusion.refs_3_.refs_8_) | copy-start | bytes 995332
  5.3 46.0 %all-to-all-start = ((bf16[8,128,1152]{2,1,0:T(8,128)(2,1)}), bf16[8,128,1152]{2,1,0:T(8,128)(2,1)}, u32[]{:S(2)}, u32[]{:S(2)}) async-start(bf16[8,128,1152]{2,1,0:T(8,128)(2,1)} %broadcast_in_dim.2), calls=%async_computation | async-start | bytes 4718592 | tf_op jit(solution)/shard_map/all_to_all | solution.py:65
  12.1 23.2 %copy-start.15 = (f32[32]{0:T(128)S(1)}, f32[32]{0:T(128)}, u32[]{:S(2)}) copy-start(f32[32]{0:T(128)} %param.11) | copy-start | bytes 388
  12.1 9.7 %collective-permute-start = (bf16[144,1152]{1,0:T(8,128)(2,1)S(1)}, bf16[144,1152]{1,0:T(8,128)(2,1)}, u32[]{:S(2)}, u32[]{:S(2)}) collective-permute-start(bf16[144,1152]{1,0:T(8,128)(2,1)S(1)} %pad_maximum_fusion.refs_3_.refs_8_), channel_id=1, source_target_pairs={{0,24},{1,25},{2,26},{3,27},{4,28},{5,29},{6,30},{7,31},{8,16},{9,... | collective-permute-start | bytes 995336 | tf_op jit(solution)/shard_map/ppermute | solution.py:61
  14.8 9.8 %collective-permute-start.2 = (bf16[144,1152]{1,0:T(8,128)(2,1)S(1)}, bf16[144,1152]{1,0:T(8,128)(2,1)}, u32[]{:S(2)}, u32[]{:S(2)}) collective-permute-start(bf16[144,1152]{1,0:T(8,128)(2,1)S(1)} %pad_maximum_fusion.refs_3_.refs_8_), channel_id=1, source_target_pairs={{0,2},{1,3},{2,4},{3,5},{4,6},{5,7},{6,0},{7,1},{8,10},{9,11},{10,... | collective-permute-start | bytes 995336 | tf_op jit(solution)/shard_map/ppermute | solution.py:61
  16.1 13.7 %collective-permute-start.3 = (bf16[144,1152]{1,0:T(8,128)(2,1)S(1)}, bf16[144,1152]{1,0:T(8,128)(2,1)S(1)}, u32[]{:S(2)}, u32[]{:S(2)}) collective-permute-start(bf16[144,1152]{1,0:T(8,128)(2,1)S(1)} %pad_maximum_fusion.refs_3_.refs_8_), channel_id=1, source_target_pairs={{0,6},{1,7},{2,0},{3,1},{4,2},{5,3},{6,4},{7,5},{8,14},{9,15},{10,... | collective-permute-start | bytes 995336 | tf_op jit(solution)/shard_map/ppermute | solution.py:61
  21.8 10.1 %collective-permute-start.1 = (bf16[144,1152]{1,0:T(8,128)(2,1)}, bf16[144,1152]{1,0:T(8,128)(2,1)}, u32[]{:S(2)}, u32[]{:S(2)}) collective-permute-start(bf16[144,1152]{1,0:T(8,128)(2,1)} %collective-permute-done.refs_4_.refs_9_), channel_id=1, source_target_pairs={{0,6},{1,7},{2,0},{3,1},{4,2},{5,3},{6,4},{7,5},{8,14},{9,15},{10,... | collective-permute-start | bytes 995336 | tf_op jit(solution)/shard_map/ppermute | solution.py:61
  24.6 11.4 %collective-permute-start.6 = (bf16[144,1152]{1,0:T(8,128)(2,1)}, bf16[144,1152]{1,0:T(8,128)(2,1)}, u32[]{:S(2)}, u32[]{:S(2)}) collective-permute-start(bf16[144,1152]{1,0:T(8,128)(2,1)} %collective-permute-done.refs_4_.refs_9_), channel_id=1, source_target_pairs={{0,2},{1,3},{2,4},{3,5},{4,6},{5,7},{6,0},{7,1},{8,10},{9,11},{10,... | collective-permute-start | bytes 995336 | tf_op jit(solution)/shard_map/ppermute | solution.py:61
  31.9 11.6 %collective-permute-start.4 = (bf16[144,1152]{1,0:T(8,128)(2,1)}, bf16[144,1152]{1,0:T(8,128)(2,1)S(1)}, u32[]{:S(2)}, u32[]{:S(2)}) collective-permute-start(bf16[144,1152]{1,0:T(8,128)(2,1)} %collective-permute-done.2.refs_1_.refs_14_), channel_id=1, source_target_pairs={{0,2},{1,3},{2,4},{3,5},{4,6},{5,7},{6,0},{7,1},{8,10},{9,11},{10,... | collective-permute-start | bytes 995336 | tf_op jit(solution)/shard_map/ppermute | solution.py:61
  33.2 10.3 %collective-permute-start.5 = (bf16[144,1152]{1,0:T(8,128)(2,1)}, bf16[144,1152]{1,0:T(8,128)(2,1)S(1)}, u32[]{:S(2)}, u32[]{:S(2)}) collective-permute-start(bf16[144,1152]{1,0:T(8,128)(2,1)} %collective-permute-done.1.refs_6_.refs_11_), channel_id=1, source_target_pairs={{0,6},{1,7},{2,0},{3,1},{4,2},{5,3},{6,4},{7,5},{8,14},{9,15},{10,... | collective-permute-start | bytes 995336 | tf_op jit(solution)/shard_map/ppermute | solution.py:61
  49.1 31.2 %collective-permute-start.7 = (bf16[1168,1024]{1,0:T(8,128)(2,1)}, bf16[1168,1024]{1,0:T(8,128)(2,1)}, u32[]{:S(2)}, u32[]{:S(2)}) collective-permute-start(bf16[1168,1024]{1,0:T(8,128)(2,1)} %get-tuple-element.62.refs_3_.refs_6_), channel_id=1, source_target_pairs={{0,1},{1,0},{2,3},{3,2},{4,5},{5,4},{6,7},{7,6},{8,9},{9,8},{10,11... | collective-permute-start | bytes 7176200 | tf_op jit(solution)/shard_map/ppermute | solution.py:61
  92.5 18.5 %collective-permute-start.8 = (bf16[1280,1024]{1,0:T(8,128)(2,1)}, bf16[1280,1024]{1,0:T(8,128)(2,1)}, u32[]{:S(2)}, u32[]{:S(2)}) collective-permute-start(bf16[1280,1024]{1,0:T(8,128)(2,1)} %get-tuple-element.67), channel_id=1, source_target_pairs={{0,1},{1,0},{2,3},{3,2},{4,5},{5,4},{6,7},{7,6},{8,9},{9,8},{10,11... | collective-permute-start | bytes 7864328 | tf_op jit(solution)/shard_map/ppermute | solution.py:61
  114.2 15.0 %copy-start.14 = (bf16[160,1024]{1,0:T(8,128)(2,1)S(1)}, bf16[160,1024]{1,0:T(8,128)(2,1)}, u32[]{:S(2)}) copy-start(bf16[160,1024]{1,0:T(8,128)(2,1)} %get-tuple-element.80) | copy-start | bytes 983044
  114.2 36.8 %all-to-all-start.1 = ((bf16[8,160,1024]{2,1,0:T(8,128)(2,1)}), bf16[8,160,1024]{2,1,0:T(8,128)(2,1)}, u32[]{:S(2)}, u32[]{:S(2)}) async-start(bf16[8,160,1024]{2,1,0:T(8,128)(2,1)} %get-tuple-element.72), calls=%async_computation.1 | async-start | bytes 5242880 | tf_op jit(solution)/shard_map/all_to_all | solution.py:65
  118.7 10.4 %collective-permute-start.9 = (bf16[160,1024]{1,0:T(8,128)(2,1)}, bf16[160,1024]{1,0:T(8,128)(2,1)S(1)}, u32[]{:S(2)}, u32[]{:S(2)}) collective-permute-start(bf16[160,1024]{1,0:T(8,128)(2,1)} %get-tuple-element.76), channel_id=1, source_target_pairs={{0,2},{1,3},{2,4},{3,5},{4,6},{5,7},{6,0},{7,1},{8,10},{9,11},{10,... | collective-permute-start | bytes 983048 | tf_op jit(solution)/shard_map/ppermute | solution.py:61
  118.9 10.2 %collective-permute-start.10 = (bf16[160,1024]{1,0:T(8,128)(2,1)}, bf16[160,1024]{1,0:T(8,128)(2,1)S(1)}, u32[]{:S(2)}, u32[]{:S(2)}) collective-permute-start(bf16[160,1024]{1,0:T(8,128)(2,1)} %get-tuple-element.77), channel_id=1, source_target_pairs={{0,6},{1,7},{2,0},{3,1},{4,2},{5,3},{6,4},{7,5},{8,14},{9,15},{10,... | collective-permute-start | bytes 983048 | tf_op jit(solution)/shard_map/ppermute | solution.py:61
  129.2 9.4 %collective-permute-start.11 = (bf16[160,1024]{1,0:T(8,128)(2,1)S(1)}, bf16[160,1024]{1,0:T(8,128)(2,1)S(1)}, u32[]{:S(2)}, u32[]{:S(2)}) collective-permute-start(bf16[160,1024]{1,0:T(8,128)(2,1)S(1)} %copy-done.14), channel_id=1, source_target_pairs={{0,2},{1,3},{2,4},{3,5},{4,6},{5,7},{6,0},{7,1},{8,10},{9,11},{10,... | collective-permute-start | bytes 983048 | tf_op jit(solution)/shard_map/ppermute | solution.py:61
  132.6 8.9 %collective-permute-start.12 = (bf16[160,1024]{1,0:T(8,128)(2,1)}, bf16[160,1024]{1,0:T(8,128)(2,1)S(1)}, u32[]{:S(2)}, u32[]{:S(2)}) collective-permute-start(bf16[160,1024]{1,0:T(8,128)(2,1)} %shard_map.108), channel_id=1, source_target_pairs={{0,6},{1,7},{2,0},{3,1},{4,2},{5,3},{6,4},{7,5},{8,14},{9,15},{10,... | collective-permute-start | bytes 983048 | tf_op jit(solution)/shard_map/ppermute | solution.py:61
  145.1 14.1 %collective-permute-start.15 = (bf16[160,1024]{1,0:T(8,128)(2,1)}, bf16[160,1024]{1,0:T(8,128)(2,1)S(1)}, u32[]{:S(2)}, u32[]{:S(2)}) collective-permute-start(bf16[160,1024]{1,0:T(8,128)(2,1)} %shard_map.110), channel_id=1, source_target_pairs={{0,24},{1,25},{2,26},{3,27},{4,28},{5,29},{6,30},{7,31},{8,16},{9,... | collective-permute-start | bytes 983048 | tf_op jit(solution)/shard_map/ppermute | solution.py:61
  146.7 12.6 %collective-permute-start.13 = (bf16[160,1024]{1,0:T(8,128)(2,1)}, bf16[160,1024]{1,0:T(8,128)(2,1)}, u32[]{:S(2)}, u32[]{:S(2)}) collective-permute-start(bf16[160,1024]{1,0:T(8,128)(2,1)} %get-tuple-element.86), channel_id=1, source_target_pairs={{0,2},{1,3},{2,4},{3,5},{4,6},{5,7},{6,0},{7,1},{8,10},{9,11},{10,... | collective-permute-start | bytes 983048 | tf_op jit(solution)/shard_map/ppermute | solution.py:61
  146.8 12.5 %collective-permute-start.14 = (bf16[160,1024]{1,0:T(8,128)(2,1)}, bf16[160,1024]{1,0:T(8,128)(2,1)}, u32[]{:S(2)}, u32[]{:S(2)}) collective-permute-start(bf16[160,1024]{1,0:T(8,128)(2,1)} %get-tuple-element.87), channel_id=1, source_target_pairs={{0,6},{1,7},{2,0},{3,1},{4,2},{5,3},{6,4},{7,5},{8,14},{9,15},{10,... | collective-permute-start | bytes 983048 | tf_op jit(solution)/shard_map/ppermute | solution.py:61
  155.8 13.8 %all-to-all-start.2 = ((bf16[8,144,128]{2,1,0:T(8,128)(2,1)}), bf16[8,144,128]{2,1,0:T(8,128)(2,1)S(1)}, u32[]{:S(2)}, u32[]{:S(2)}) async-start(bf16[8,144,128]{2,1,0:T(8,128)(2,1)} %get-tuple-element.73), calls=%async_computation.2 | async-start | bytes 589824 | tf_op jit(solution)/shard_map/all_to_all | solution.py:65
  165.0 6.3 %collective-permute-start.17 = (bf16[144,1152]{1,0:T(8,128)(2,1)}, bf16[144,1152]{1,0:T(8,128)(2,1)}, u32[]{:S(2)}, u32[]{:S(2)}) collective-permute-start(bf16[144,1152]{1,0:T(8,128)(2,1)} %get-tuple-element.91.txt), channel_id=1, source_target_pairs={{0,1},{1,0},{2,3},{3,2},{4,5},{5,4},{6,7},{7,6},{8,9},{9,8},{10,11... | collective-permute-start | bytes 995336 | tf_op jit(solution)/shard_map/ppermute | solution.py:61
  167.6 3.7 %collective-permute-start.16 = (bf16[144,1152]{1,0:T(8,128)(2,1)S(1)}, bf16[144,1152]{1,0:T(8,128)(2,1)}, u32[]{:S(2)}, u32[]{:S(2)}) collective-permute-start(bf16[144,1152]{1,0:T(8,128)(2,1)S(1)} %copy-done.7), channel_id=1, source_target_pairs={{0,1},{1,0},{2,3},{3,2},{4,5},{5,4},{6,7},{7,6},{8,9},{9,8},{10,11... | collective-permute-start | bytes 995336 | tf_op jit(solution)/shard_map/ppermute | solution.py:61
  167.7 7.0 %collective-permute-start.18 = (bf16[4,144,128]{2,1,0:T(8,128)(2,1)}, bf16[4,144,128]{2,1,0:T(8,128)(2,1)}, u32[]{:S(2)}, u32[]{:S(2)}) collective-permute-start(bf16[4,144,128]{2,1,0:T(8,128)(2,1)} %get-tuple-element.92), channel_id=1, source_target_pairs={{0,24},{1,25},{2,26},{3,27},{4,28},{5,29},{6,30},{7,31},{8,16},{9,... | collective-permute-start | bytes 442376 | tf_op jit(solution)/shard_map/ppermute | solution.py:61
  169.6 13.3 %copy-start.13 = (bf16[4,144,128]{2,1,0:T(8,128)(2,1)S(1)}, bf16[4,144,128]{2,1,0:T(8,128)(2,1)}, u32[]{:S(2)}) copy-start(bf16[4,144,128]{2,1,0:T(8,128)(2,1)} %get-tuple-element.94) | copy-start | bytes 442372
  174.8 21.8 %all-to-all-start.3 = ((bf16[64,8,384]{2,1,0:T(8,128)(2,1)}), bf16[64,8,384]{2,1,0:T(8,128)(2,1)S(1)}, u32[]{:S(2)}, u32[]{:S(2)}) async-start(bf16[64,8,384]{2,1,0:T(8,128)(2,1)} %bitcast.51), calls=%async_computation.3 | async-start | bytes 786432 | tf_op jit(solution)/shard_map/all_to_all | solution.py:65
  182.8 11.9 %copy-start.1 = (bf16[1152,1152]{1,0:T(8,128)(2,1)S(1)}, bf16[1152,1152]{1,0:T(8,128)(2,1)}, u32[]{:S(2)}) copy-start(bf16[1152,1152]{1,0:T(8,128)(2,1)} %param.10) | copy-start | bytes 7962628
  184.0 10.6 %collective-permute-start.21 = (bf16[288,128]{1,0:T(8,128)(2,1)S(1)}, bf16[288,128]{1,0:T(8,128)(2,1)S(1)}, u32[]{:S(2)}, u32[]{:S(2)}) collective-permute-start(bf16[288,128]{1,0:T(8,128)(2,1)S(1)} %get-tuple-element.98), channel_id=1, source_target_pairs={{0,2},{1,3},{2,4},{3,5},{4,6},{5,7},{6,0},{7,1},{8,10},{9,11},{10,... | collective-permute-start | bytes 221192 | tf_op jit(solution)/shard_map/ppermute | solution.py:61
  185.1 5.5 %collective-permute-start.19 = (bf16[288,128]{1,0:T(8,128)(2,1)S(1)}, bf16[288,128]{1,0:T(8,128)(2,1)S(1)}, u32[]{:S(2)}, u32[]{:S(2)}) collective-permute-start(bf16[288,128]{1,0:T(8,128)(2,1)S(1)} %get-tuple-element.99), channel_id=1, source_target_pairs={{0,6},{1,7},{2,0},{3,1},{4,2},{5,3},{6,4},{7,5},{8,14},{9,15},{10,... | collective-permute-start | bytes 221192 | tf_op jit(solution)/shard_map/ppermute | solution.py:61
  186.7 7.9 %collective-permute-start.20 = (bf16[288,128]{1,0:T(8,128)(2,1)S(1)}, bf16[288,128]{1,0:T(8,128)(2,1)S(1)}, u32[]{:S(2)}, u32[]{:S(2)}) collective-permute-start(bf16[288,128]{1,0:T(8,128)(2,1)S(1)} %get-tuple-element.100), channel_id=1, source_target_pairs={{0,4},{1,5},{2,6},{3,7},{4,0},{5,1},{6,2},{7,3},{8,12},{9,13},{10,... | collective-permute-start | bytes 221192 | tf_op jit(solution)/shard_map/ppermute | solution.py:61
  (10 other events, 20.9 us)

commit v12 on v10

--- a/solution.py
+++ b/solution.py
@@ -204,7 +204,7 @@
         bias = jnp.where(lang == g, bias_ref[g], bias)
     bias = bias * -log2e
     down = jnp.zeros((1, tile), f32)
-    high = 4 * rows
+    high = 2 * rows
     for m in range(img.shape[0] // high):
         span = slice(m * high, (m + 1) * high)
         index = m * high + lax.broadcasted_iota(jnp.int32, (high, 1), 0)

time: 184 us -> 183 us (level)
  transfers between devices with their start and end apart: 26 -> 26, of which waited for: 7 -> 7; matrix products, arithmetic and copies ran while one was open for 14% -> 14% of each run, Pallas kernels for 29% -> 28%
where the time goes in v12:
time: 183 us; the launch traced here: 182 us
  Pallas kernels  68.8 us (38%)
  starting transfers between devices  54 us (30%)
  waiting for transfers between devices  25.9 us (14%)
  matrix products  15.1 us (8%)
  local copies, waits for them, and re-layouts  12.5 us (7%)
  other arithmetic  4.48 us (2%)
    pallas_call x12, Pallas kernels, call(): pl.pallas_call(body, out_shape=out_shape, grid_spec=spec, input_output_al...  68.8 us
    ppermute x22, starting transfers between devices, send(): lax.ppermute(block, DEV, [(flat(*p), flat(*move(*p))) for p in PLACES])  31 us
    ppermute x22, waiting for transfers between devices, send(): lax.ppermute(block, DEV, [(flat(*p), flat(*move(*p))) for p in PLACES])  24.3 us
    all_to_all x4, starting transfers between devices, exchange(): lax.all_to_all(blocks, DEV, 0, 0, axis_index_groups=groups, tiled=True)  23 us
    dot_general x4, matrix products, dot(): return lax.dot_general(a, b, dims, preferred_element_type=f32)  15.1 us
    optimization_barrier x1, local copies, waits for them, and re-layouts, together(): return lax.optimization_barrier(list(arrays))  5.22 us
    unnamed x43, local copies, waits for them, and re-layouts  3.84 us
  transfers between devices with their start and end apart: 26, of which 7 were waited for; matrix products, arithmetic and copies ran while one was open for 14% of the time, Pallas kernels for 28%

profile of v12, /device:TPU:1, one launch (start us, length us, event | category | flops | bytes accessed | tf_op | source)
XLA Modules:
  0.0 181.7 jit_solution(15408171742027627193)
XLA Ops:
  0.6 2.8 %broadcast_in_dim.2 = bf16[8,128,1152]{2,1,0:T(8,128)(2,1)} broadcast(bf16[128,1152]{1,0:T(8,128)(2,1)} %param.7), dimensions={1,2} | broadcast | bytes 2654208 | tf_op jit(solution)/shard_map/broadcast_in_dim | solution.py:541
  3.5 6.9 %all-to-all-start = ((bf16[8,128,1152]{2,1,0:T(8,128)(2,1)}), bf16[8,128,1152]{2,1,0:T(8,128)(2,1)}, u32[]{:S(2)}, u32[]{:S(2)}) async-start(bf16[8,128,1152]{2,1,0:T(8,128)(2,1)} %broadcast_in_dim.2), calls=%async_computation | async-start | bytes 4718592 | tf_op jit(solution)/shard_map/all_to_all | solution.py:65
  10.5 2.8 %collective-permute-start = (bf16[144,1152]{1,0:T(8,128)(2,1)S(1)}, bf16[144,1152]{1,0:T(8,128)(2,1)}, u32[]{:S(2)}, u32[]{:S(2)}) collective-permute-start(bf16[144,1152]{1,0:T(8,128)(2,1)S(1)} %pad_maximum_fusion.refs_3_.refs_8_), channel_id=1, source_target_pairs={{0,24},{1,25},{2,26},{3,27},{4,28},{5,29},{6,30},{7,31},{8,16},{9,... | collective-permute-start | bytes 995336 | tf_op jit(solution)/shard_map/ppermute | solution.py:61
  16.1 4.3 %collective-permute-done.refs_4_.refs_9_ = bf16[144,1152]{1,0:T(8,128)(2,1)} collective-permute-done((bf16[144,1152]{1,0:T(8,128)(2,1)S(1)}, bf16[144,1152]{1,0:T(8,128)(2,1)}, u32[]{:S(2)}, u32[]{:S(2)}) %collective-permute-start) | collective-permute-done | bytes 331808 | tf_op jit(solution)/shard_map/ppermute | solution.py:61
  20.3 2.7 %collective-permute-start.1 = (bf16[144,1152]{1,0:T(8,128)(2,1)}, bf16[144,1152]{1,0:T(8,128)(2,1)}, u32[]{:S(2)}, u32[]{:S(2)}) collective-permute-start(bf16[144,1152]{1,0:T(8,128)(2,1)} %collective-permute-done.refs_4_.refs_9_), channel_id=1, source_target_pairs={{0,6},{1,7},{2,0},{3,1},{4,2},{5,3},{6,4},{7,5},{8,14},{9,15},{10,... | collective-permute-start | bytes 995336 | tf_op jit(solution)/shard_map/ppermute | solution.py:61
  23.1 5.2 %copy.13 = bf16[1152,1152]{0,1:T(8,128)(2,1)} copy(bf16[1152,1152]{1,0:T(8,128)(2,1)} %param.10) | data formatting | bytes 5308416 | tf_op jit(solution)/shard_map/optimization_barrier | solution.py:509
  28.3 2.2 %collective-permute-done.1.refs_6_.refs_11_ = bf16[144,1152]{1,0:T(8,128)(2,1)} collective-permute-done((bf16[144,1152]{1,0:T(8,128)(2,1)}, bf16[144,1152]{1,0:T(8,128)(2,1)}, u32[]{:S(2)}, u32[]{:S(2)}) %collective-permute-start.1) | collective-permute-done | bytes 331808 | tf_op jit(solution)/shard_map/ppermute | solution.py:61
  34.4 7.6 %shard_map.102 = (bf16[1168,1024]{1,0:T(8,128)(2,1)}, f32[1,1024]{1,0:T(1,128)}) custom-call(s32[16]{0:T(128)} %stack.83.refs_0_, bf16[144,1152]{1,0:T(8,128)(2,1)} %collective-permute-done.2.refs_1_.refs_14_, bf16[144,1152]{1,0:T(8,128)(2,1)} %collective-permute-done.6.refs_2_.refs_15_, bf16[144,1152]{1,0:T(8,128)(2,1)} %copy-done.5, ...), custom_call_target="tpu_custom_call" | custom-call | flops 2038431744 | bytes 4644864 | tf_op jit(solution)/shard_map/pallas_call | solution.py:93
  42.9 4.7 %shard_map.103 = (bf16[1168,1024]{1,0:T(8,128)(2,1)}, f32[1,1024]{1,0:T(1,128)}) custom-call(s32[16]{0:T(128)} %stack.83.refs_0_, bf16[144,1152]{1,0:T(8,128)(2,1)} %copy-done.3, bf16[144,1152]{1,0:T(8,128)(2,1)} %copy-done.4, bf16[1152,1152]{1,0:T(8,128)(2,1)} %bitcast.48, ...), custom_call_target="tpu_custom_call", output_to_operand_aliasing={{0}: (4, {}), {1}: (5, {})} | custom-call | flops 679477248 | bytes 5713920 | tf_op jit(solution)/shard_map/pallas_call | solution.py:93
  47.6 2.1 %collective-permute-start.7 = (bf16[1168,1024]{1,0:T(8,128)(2,1)}, bf16[1168,1024]{1,0:T(8,128)(2,1)}, u32[]{:S(2)}, u32[]{:S(2)}) collective-permute-start(bf16[1168,1024]{1,0:T(8,128)(2,1)} %get-tuple-element.60.refs_3_.refs_6_), channel_id=1, source_target_pairs={{0,1},{1,0},{2,3},{3,2},{4,5},{5,4},{6,7},{7,6},{8,9},{9,8},{10,11... | collective-permute-start | bytes 7176200 | tf_op jit(solution)/shard_map/ppermute | solution.py:61
  49.7 5.0 %multiply_reduce_fusion = (f32[1024]{0:T(1024)S(1)}, f32[1152,1024]{1,0:T(8,128)S(1)}) fusion(bf16[1152,1152]{1,0:T(8,128)(2,1)S(1)} %copy-done, bf16[1024,1152]{1,0:T(8,128)(2,1)} %bitcast.17.refs_4_), kind=kOutput, calls=%fused_computation.2 | convolution fusion | flops 2720267264 | bytes 9736192 | tf_op jit(solution)/shard_map/dot_general | solution.py:75
  55.3 6.6 %fusion.refs_1_ = bf16[1024,1152]{1,0:T(8,128)(2,1)} fusion(bf16[1024,1152]{1,0:T(8,128)(2,1)} %bitcast.17.refs_4_, bf16[1152,1152]{1,0:T(8,128)(2,1)S(1)} %copy-done, f32[1024]{0:T(1024)S(1)} %get-tuple-element.102), kind=kOutput, calls=%fused_computation.3 | convolution fusion | flops 2720268288 | bytes 7376896 | tf_op jit(solution)/shard_map/dot_general | solution.py:75
  63.9 12.3 %shard_map.104 = (bf16[4,1024,256]{2,1,0:T(8,128)(2,1)}, f32[1,1024]{1,0:T(1,128)}, bf16[1280,1024]{1,0:T(8,128)(2,1)}) custom-call(f32[33]{0:T(128)} %pad_maximum_fusion.1.refs_0_, bf16[1024,1152]{1,0:T(8,128)(2,1)} %fusion.refs_1_, bf16[1152,1024]{1,0:T(8,128)(2,1)} %multiply_convert_fusion.refs_2_, bf16[1168,1024]{1,0:T(8,128)(2,1)} %collective-permute-done.7.refs_3_.refs_4_), custom_call_target="tpu_custom_call" | custom-call | flops 4831838208 | bytes 7110788 | tf_op jit(solution)/shard_map/pallas_call | solution.py:93
  76.2 17.4 %shard_map.105 = (bf16[1280,1024]{1,0:T(8,128)(2,1)}, bf16[8,160,1024]{2,1,0:T(8,128)(2,1)}) custom-call(f32[33]{0:T(128)} %pad_maximum_fusion.1.refs_0_, bf16[1024,1152]{1,0:T(8,128)(2,1)} %fusion.refs_1_, bf16[1152,1024]{1,0:T(8,128)(2,1)} %multiply_convert_fusion.refs_2_, bf16[1168,1024]{1,0:T(8,128)(2,1)} %get-tuple-element.60.refs_3_.refs_6_, ...), custom_call_target="tpu_custom_call" | custom-call | flops 9663676416 | bytes 11604100 | tf_op jit(solution)/shard_map/pallas_call | solution.py:93
  93.6 3.2 %shard_map.106 = (bf16[160,1024]{1,0:T(8,128)(2,1)}, bf16[160,1024]{1,0:T(8,128)(2,1)}, bf16[160,1024]{1,0:T(8,128)(2,1)}) custom-call(s32[16]{0:T(128)} %stack.83.refs_0_, bf16[1280,1024]{1,0:T(8,128)(2,1)} %get-tuple-element.64.refs_1_.refs_3_.refs_5_.refs_4_, bf16[1280,1024]{1,0:T(8,128)(2,1)} %collective-permute-done.8.refs_2_.refs_4_.refs_6_.refs_5_, ...), custom_call_target="tpu_custom_call" | custom-call | bytes 15728640 | tf_op jit(solution)/shard_map/pallas_call | solution.py:93
  96.8 4.6 %all-to-all-start.1 = ((bf16[8,160,1024]{2,1,0:T(8,128)(2,1)}), bf16[8,160,1024]{2,1,0:T(8,128)(2,1)}, u32[]{:S(2)}, u32[]{:S(2)}) async-start(bf16[8,160,1024]{2,1,0:T(8,128)(2,1)} %get-tuple-element.70), calls=%async_computation.1 | async-start | bytes 5242880 | tf_op jit(solution)/shard_map/all_to_all | solution.py:65
  101.6 2.5 %collective-permute-start.10 = (bf16[160,1024]{1,0:T(8,128)(2,1)}, bf16[160,1024]{1,0:T(8,128)(2,1)S(1)}, u32[]{:S(2)}, u32[]{:S(2)}) collective-permute-start(bf16[160,1024]{1,0:T(8,128)(2,1)} %get-tuple-element.75), channel_id=1, source_target_pairs={{0,6},{1,7},{2,0},{3,1},{4,2},{5,3},{6,4},{7,5},{8,14},{9,15},{10,... | collective-permute-start | bytes 983048 | tf_op jit(solution)/shard_map/ppermute | solution.py:61
  104.1 7.7 %collective-permute-done.9.refs_3_ = bf16[160,1024]{1,0:T(8,128)(2,1)S(1)} collective-permute-done((bf16[160,1024]{1,0:T(8,128)(2,1)}, bf16[160,1024]{1,0:T(8,128)(2,1)S(1)}, u32[]{:S(2)}, u32[]{:S(2)}) %collective-permute-start.9) | collective-permute-done | bytes 327712 | tf_op jit(solution)/shard_map/ppermute | solution.py:61
  112.5 2.7 %shard_map.108 = bf16[160,1024]{1,0:T(8,128)(2,1)} custom-call(s32[16]{0:T(128)} %stack.83.refs_0_, bf16[1280,1024]{1,0:T(8,128)(2,1)} %get-tuple-element.64.refs_1_.refs_3_.refs_5_.refs_4_, bf16[1280,1024]{1,0:T(8,128)(2,1)} %collective-permute-done.8.refs_2_.refs_4_.refs_6_.refs_5_, bf16[160,1024]{1,0:T(8,128)(2,1)} %copy-done.11), custom_call_target="tpu_custom_call" | custom-call | bytes 5570560 | tf_op jit(solution)/shard_map/pallas_call | solution.py:93
  115.3 2.3 %collective-permute-start.12 = (bf16[160,1024]{1,0:T(8,128)(2,1)}, bf16[160,1024]{1,0:T(8,128)(2,1)S(1)}, u32[]{:S(2)}, u32[]{:S(2)}) collective-permute-start(bf16[160,1024]{1,0:T(8,128)(2,1)} %shard_map.108), channel_id=1, source_target_pairs={{0,6},{1,7},{2,0},{3,1},{4,2},{5,3},{6,4},{7,5},{8,14},{9,15},{10,... | collective-permute-start | bytes 983048 | tf_op jit(solution)/shard_map/ppermute | solution.py:61
  117.6 3.6 %collective-permute-done.11.refs_3_ = bf16[160,1024]{1,0:T(8,128)(2,1)S(1)} collective-permute-done((bf16[160,1024]{1,0:T(8,128)(2,1)S(1)}, bf16[160,1024]{1,0:T(8,128)(2,1)S(1)}, u32[]{:S(2)}, u32[]{:S(2)}) %collective-permute-start.11) | collective-permute-done | bytes 327712 | tf_op jit(solution)/shard_map/ppermute | solution.py:61
  121.2 3.0 %shard_map.109 = (bf16[160,1024]{1,0:T(8,128)(2,1)}, bf16[160,1024]{1,0:T(8,128)(2,1)}) custom-call(s32[16]{0:T(128)} %stack.83.refs_0_, bf16[1280,1024]{1,0:T(8,128)(2,1)} %get-tuple-element.64.refs_1_.refs_3_.refs_5_.refs_4_, bf16[1280,1024]{1,0:T(8,128)(2,1)} %collective-permute-done.8.refs_2_.refs_4_.refs_6_.refs_5_, bf16[160,1024]{1,0:T(8,128)(2,1)} %copy-done.8, ...), custom_call_target="tpu_custom_call" | custom-call | bytes 10813440 | tf_op jit(solution)/shard_map/pallas_call | solution.py:93
  124.9 2.9 %shard_map.110 = bf16[160,1024]{1,0:T(8,128)(2,1)} custom-call(s32[16]{0:T(128)} %stack.83.refs_0_, bf16[1280,1024]{1,0:T(8,128)(2,1)} %get-tuple-element.64.refs_1_.refs_3_.refs_5_.refs_4_, bf16[1280,1024]{1,0:T(8,128)(2,1)} %collective-permute-done.8.refs_2_.refs_4_.refs_6_.refs_5_, bf16[160,1024]{1,0:T(8,128)(2,1)} %copy-done.9, bf16[160,1024]{1,0:T(8,128)(2,1)} %copy-done.10), custom_call_target="tpu_custom_call" | custom-call | bytes 5898240 | tf_op jit(solution)/shard_map/pallas_call | solution.py:93
  129.5 2.6 %collective-permute-start.14 = (bf16[160,1024]{1,0:T(8,128)(2,1)}, bf16[160,1024]{1,0:T(8,128)(2,1)}, u32[]{:S(2)}, u32[]{:S(2)}) collective-permute-start(bf16[160,1024]{1,0:T(8,128)(2,1)} %get-tuple-element.85), channel_id=1, source_target_pairs={{0,6},{1,7},{2,0},{3,1},{4,2},{5,3},{6,4},{7,5},{8,14},{9,15},{10,... | collective-permute-start | bytes 983048 | tf_op jit(solution)/shard_map/ppermute | solution.py:61
  133.6 4.9 %shard_map.107 = (bf16[8,144,128]{2,1,0:T(8,128)(2,1)}, bf16[144,1152]{1,0:T(8,128)(2,1)}) custom-call(s32[16]{0:T(128)} %stack.83.refs_0_, bf16[8,160,1024]{2,1,0:T(8,128)(2,1)} %all-to-all-done.1.refs_1_, bf16[1152,1024]{1,0:T(8,128)(2,1)} %multiply_convert_fusion.refs_2_, f32[1,1024]{1,0:T(1,128)} %bitcast.51, bf16[1024,1152]{1,0:T(8,128)(2,1)} %bitcast.17.refs_4_), custom_call_target="tpu_custom_call" | custom-call | tf_op jit(solution)/shard_map/pallas_call | solution.py:93
  138.5 3.4 %all-to-all-start.2 = ((bf16[8,144,128]{2,1,0:T(8,128)(2,1)}), bf16[8,144,128]{2,1,0:T(8,128)(2,1)S(1)}, u32[]{:S(2)}, u32[]{:S(2)}) async-start(bf16[8,144,128]{2,1,0:T(8,128)(2,1)} %get-tuple-element.71), calls=%async_computation.2 | async-start | bytes 589824 | tf_op jit(solution)/shard_map/all_to_all | solution.py:65
  142.7 5.0 %shard_map.111 = (bf16[4,144,128]{2,1,0:T(8,128)(2,1)}, bf16[4,144,128]{2,1,0:T(8,128)(2,1)}, bf16[144,1152]{1,0:T(8,128)(2,1)}) custom-call(s32[16]{0:T(128)} %stack.83.refs_0_, bf16[1280,1024]{1,0:T(8,128)(2,1)} %get-tuple-element.64.refs_1_.refs_3_.refs_5_.refs_4_, bf16[1280,1024]{1,0:T(8,128)(2,1)} %collective-permute-done.8.refs_2_.refs_4_.refs_6_.refs_5_, ...), custom_call_target="tpu_custom_call" | custom-call | tf_op jit(solution)/shard_map/pallas_call | solution.py:93
  147.6 2.6 %collective-permute-start.17 = (bf16[144,1152]{1,0:T(8,128)(2,1)}, bf16[144,1152]{1,0:T(8,128)(2,1)}, u32[]{:S(2)}, u32[]{:S(2)}) collective-permute-start(bf16[144,1152]{1,0:T(8,128)(2,1)} %get-tuple-element.89.txt), channel_id=1, source_target_pairs={{0,1},{1,0},{2,3},{3,2},{4,5},{5,4},{6,7},{7,6},{8,9},{9,8},{10,11... | collective-permute-start | bytes 995336 | tf_op jit(solution)/shard_map/ppermute | solution.py:61
  153.9 3.4 %shard_map.112 = bf16[512,384]{1,0:T(8,128)(2,1)} custom-call(s32[1]{0:T(128)} %bitcast.4.core, bf16[144,1152]{1,0:T(8,128)(2,1)} %get-tuple-element.73.img, bf16[144,1152]{1,0:T(8,128)(2,1)} %get-tuple-element.89.txt, bf16[144,1152]{1,0:T(8,128)(2,1)} %collective-permute-done.16.other_img, bf16[144,1152]{1,0:T(8,128)(2,1)} %collective-permute-done.17.other_txt), custom_call_target="tpu_custom_call" | custom-call | tf_op jit(solution)/shard_map/pallas_call | solution.py:93
  157.3 8.1 %all-to-all-start.3 = ((bf16[64,8,384]{2,1,0:T(8,128)(2,1)}), bf16[64,8,384]{2,1,0:T(8,128)(2,1)S(1)}, u32[]{:S(2)}, u32[]{:S(2)}) async-start(bf16[64,8,384]{2,1,0:T(8,128)(2,1)} %bitcast.49), calls=%async_computation.3 | async-start | bytes 786432 | tf_op jit(solution)/shard_map/all_to_all | solution.py:65
  170.7 2.5 %collective-permute-done.19 = bf16[288,128]{1,0:T(8,128)(2,1)S(1)} collective-permute-done((bf16[288,128]{1,0:T(8,128)(2,1)S(1)}, bf16[288,128]{1,0:T(8,128)(2,1)S(1)}, u32[]{:S(2)}, u32[]{:S(2)}) %collective-permute-start.19) | collective-permute-done | bytes 73760 | tf_op jit(solution)/shard_map/ppermute | solution.py:61
  173.2 4.0 %collective-permute-done.20 = bf16[288,128]{1,0:T(8,128)(2,1)S(1)} collective-permute-done((bf16[288,128]{1,0:T(8,128)(2,1)S(1)}, bf16[288,128]{1,0:T(8,128)(2,1)S(1)}, u32[]{:S(2)}, u32[]{:S(2)}) %collective-permute-start.20) | collective-permute-done | bytes 73760 | tf_op jit(solution)/shard_map/ppermute | solution.py:61
  (93 shorter events, 29.3 us)
Async XLA Ops:
  0.6 49.1 %copy-start = (bf16[1152,1152]{1,0:T(8,128)(2,1)S(1)}, bf16[1152,1152]{1,0:T(8,128)(2,1)}, u32[]{:S(2)}) copy-start(bf16[1152,1152]{1,0:T(8,128)(2,1)} %param.9) | copy-start | bytes 7962628
  3.5 46.2 %all-to-all-start = ((bf16[8,128,1152]{2,1,0:T(8,128)(2,1)}), bf16[8,128,1152]{2,1,0:T(8,128)(2,1)}, u32[]{:S(2)}, u32[]{:S(2)}) async-start(bf16[8,128,1152]{2,1,0:T(8,128)(2,1)} %broadcast_in_dim.2), calls=%async_computation | async-start | bytes 4718592 | tf_op jit(solution)/shard_map/all_to_all | solution.py:65
  10.5 17.8 %copy-start.5 = (bf16[144,1152]{1,0:T(8,128)(2,1)}, bf16[144,1152]{1,0:T(8,128)(2,1)S(1)}, u32[]{:S(2)}) copy-start(bf16[144,1152]{1,0:T(8,128)(2,1)S(1)} %pad_maximum_fusion.refs_3_.refs_8_) | copy-start | bytes 995332
  10.5 23.3 %copy-start.18 = (f32[32]{0:T(128)S(1)}, f32[32]{0:T(128)}, u32[]{:S(2)}) copy-start(f32[32]{0:T(128)} %param.11) | copy-start | bytes 388
  10.5 9.8 %collective-permute-start = (bf16[144,1152]{1,0:T(8,128)(2,1)S(1)}, bf16[144,1152]{1,0:T(8,128)(2,1)}, u32[]{:S(2)}, u32[]{:S(2)}) collective-permute-start(bf16[144,1152]{1,0:T(8,128)(2,1)S(1)} %pad_maximum_fusion.refs_3_.refs_8_), channel_id=1, source_target_pairs={{0,24},{1,25},{2,26},{3,27},{4,28},{5,29},{6,30},{7,31},{8,16},{9,... | collective-permute-start | bytes 995336 | tf_op jit(solution)/shard_map/ppermute | solution.py:61
  13.3 9.7 %collective-permute-start.2 = (bf16[144,1152]{1,0:T(8,128)(2,1)S(1)}, bf16[144,1152]{1,0:T(8,128)(2,1)}, u32[]{:S(2)}, u32[]{:S(2)}) collective-permute-start(bf16[144,1152]{1,0:T(8,128)(2,1)S(1)} %pad_maximum_fusion.refs_3_.refs_8_), channel_id=1, source_target_pairs={{0,2},{1,3},{2,4},{3,5},{4,6},{5,7},{6,0},{7,1},{8,10},{9,11},{10,... | collective-permute-start | bytes 995336 | tf_op jit(solution)/shard_map/ppermute | solution.py:61
  14.6 13.7 %collective-permute-start.3 = (bf16[144,1152]{1,0:T(8,128)(2,1)S(1)}, bf16[144,1152]{1,0:T(8,128)(2,1)S(1)}, u32[]{:S(2)}, u32[]{:S(2)}) collective-permute-start(bf16[144,1152]{1,0:T(8,128)(2,1)S(1)} %pad_maximum_fusion.refs_3_.refs_8_), channel_id=1, source_target_pairs={{0,6},{1,7},{2,0},{3,1},{4,2},{5,3},{6,4},{7,5},{8,14},{9,15},{10,... | collective-permute-start | bytes 995336 | tf_op jit(solution)/shard_map/ppermute | solution.py:61
  20.3 10.2 %collective-permute-start.1 = (bf16[144,1152]{1,0:T(8,128)(2,1)}, bf16[144,1152]{1,0:T(8,128)(2,1)}, u32[]{:S(2)}, u32[]{:S(2)}) collective-permute-start(bf16[144,1152]{1,0:T(8,128)(2,1)} %collective-permute-done.refs_4_.refs_9_), channel_id=1, source_target_pairs={{0,6},{1,7},{2,0},{3,1},{4,2},{5,3},{6,4},{7,5},{8,14},{9,15},{10,... | collective-permute-start | bytes 995336 | tf_op jit(solution)/shard_map/ppermute | solution.py:61
  23.1 11.4 %collective-permute-start.6 = (bf16[144,1152]{1,0:T(8,128)(2,1)}, bf16[144,1152]{1,0:T(8,128)(2,1)}, u32[]{:S(2)}, u32[]{:S(2)}) collective-permute-start(bf16[144,1152]{1,0:T(8,128)(2,1)} %collective-permute-done.refs_4_.refs_9_), channel_id=1, source_target_pairs={{0,2},{1,3},{2,4},{3,5},{4,6},{5,7},{6,0},{7,1},{8,10},{9,11},{10,... | collective-permute-start | bytes 995336 | tf_op jit(solution)/shard_map/ppermute | solution.py:61
  30.5 11.6 %collective-permute-start.4 = (bf16[144,1152]{1,0:T(8,128)(2,1)}, bf16[144,1152]{1,0:T(8,128)(2,1)S(1)}, u32[]{:S(2)}, u32[]{:S(2)}) collective-permute-start(bf16[144,1152]{1,0:T(8,128)(2,1)} %collective-permute-done.2.refs_1_.refs_14_), channel_id=1, source_target_pairs={{0,2},{1,3},{2,4},{3,5},{4,6},{5,7},{6,0},{7,1},{8,10},{9,11},{10,... | collective-permute-start | bytes 995336 | tf_op jit(solution)/shard_map/ppermute | solution.py:61
  31.8 10.3 %collective-permute-start.5 = (bf16[144,1152]{1,0:T(8,128)(2,1)}, bf16[144,1152]{1,0:T(8,128)(2,1)S(1)}, u32[]{:S(2)}, u32[]{:S(2)}) collective-permute-start(bf16[144,1152]{1,0:T(8,128)(2,1)} %collective-permute-done.1.refs_6_.refs_11_), channel_id=1, source_target_pairs={{0,6},{1,7},{2,0},{3,1},{4,2},{5,3},{6,4},{7,5},{8,14},{9,15},{10,... | collective-permute-start | bytes 995336 | tf_op jit(solution)/shard_map/ppermute | solution.py:61
  47.6 16.3 %collective-permute-start.7 = (bf16[1168,1024]{1,0:T(8,128)(2,1)}, bf16[1168,1024]{1,0:T(8,128)(2,1)}, u32[]{:S(2)}, u32[]{:S(2)}) collective-permute-start(bf16[1168,1024]{1,0:T(8,128)(2,1)} %get-tuple-element.60.refs_3_.refs_6_), channel_id=1, source_target_pairs={{0,1},{1,0},{2,3},{3,2},{4,5},{5,4},{6,7},{7,6},{8,9},{9,8},{10,11... | collective-permute-start | bytes 7176200 | tf_op jit(solution)/shard_map/ppermute | solution.py:61
  76.2 17.4 %collective-permute-start.8 = (bf16[1280,1024]{1,0:T(8,128)(2,1)}, bf16[1280,1024]{1,0:T(8,128)(2,1)}, u32[]{:S(2)}, u32[]{:S(2)}) collective-permute-start(bf16[1280,1024]{1,0:T(8,128)(2,1)} %get-tuple-element.65), channel_id=1, source_target_pairs={{0,1},{1,0},{2,3},{3,2},{4,5},{5,4},{6,7},{7,6},{8,9},{9,8},{10,11... | collective-permute-start | bytes 7864328 | tf_op jit(solution)/shard_map/ppermute | solution.py:61
  96.8 15.0 %copy-start.17 = (bf16[160,1024]{1,0:T(8,128)(2,1)S(1)}, bf16[160,1024]{1,0:T(8,128)(2,1)}, u32[]{:S(2)}) copy-start(bf16[160,1024]{1,0:T(8,128)(2,1)} %get-tuple-element.78) | copy-start | bytes 983044
  96.8 36.8 %all-to-all-start.1 = ((bf16[8,160,1024]{2,1,0:T(8,128)(2,1)}), bf16[8,160,1024]{2,1,0:T(8,128)(2,1)}, u32[]{:S(2)}, u32[]{:S(2)}) async-start(bf16[8,160,1024]{2,1,0:T(8,128)(2,1)} %get-tuple-element.70), calls=%async_computation.1 | async-start | bytes 5242880 | tf_op jit(solution)/shard_map/all_to_all | solution.py:65
  101.4 10.4 %collective-permute-start.9 = (bf16[160,1024]{1,0:T(8,128)(2,1)}, bf16[160,1024]{1,0:T(8,128)(2,1)S(1)}, u32[]{:S(2)}, u32[]{:S(2)}) collective-permute-start(bf16[160,1024]{1,0:T(8,128)(2,1)} %get-tuple-element.74), channel_id=1, source_target_pairs={{0,2},{1,3},{2,4},{3,5},{4,6},{5,7},{6,0},{7,1},{8,10},{9,11},{10,... | collective-permute-start | bytes 983048 | tf_op jit(solution)/shard_map/ppermute | solution.py:61
  101.6 10.2 %collective-permute-start.10 = (bf16[160,1024]{1,0:T(8,128)(2,1)}, bf16[160,1024]{1,0:T(8,128)(2,1)S(1)}, u32[]{:S(2)}, u32[]{:S(2)}) collective-permute-start(bf16[160,1024]{1,0:T(8,128)(2,1)} %get-tuple-element.75), channel_id=1, source_target_pairs={{0,6},{1,7},{2,0},{3,1},{4,2},{5,3},{6,4},{7,5},{8,14},{9,15},{10,... | collective-permute-start | bytes 983048 | tf_op jit(solution)/shard_map/ppermute | solution.py:61
  111.8 9.4 %collective-permute-start.11 = (bf16[160,1024]{1,0:T(8,128)(2,1)S(1)}, bf16[160,1024]{1,0:T(8,128)(2,1)S(1)}, u32[]{:S(2)}, u32[]{:S(2)}) collective-permute-start(bf16[160,1024]{1,0:T(8,128)(2,1)S(1)} %copy-done.17), channel_id=1, source_target_pairs={{0,2},{1,3},{2,4},{3,5},{4,6},{5,7},{6,0},{7,1},{8,10},{9,11},{10,... | collective-permute-start | bytes 983048 | tf_op jit(solution)/shard_map/ppermute | solution.py:61
  115.3 8.9 %collective-permute-start.12 = (bf16[160,1024]{1,0:T(8,128)(2,1)}, bf16[160,1024]{1,0:T(8,128)(2,1)S(1)}, u32[]{:S(2)}, u32[]{:S(2)}) collective-permute-start(bf16[160,1024]{1,0:T(8,128)(2,1)} %shard_map.108), channel_id=1, source_target_pairs={{0,6},{1,7},{2,0},{3,1},{4,2},{5,3},{6,4},{7,5},{8,14},{9,15},{10,... | collective-permute-start | bytes 983048 | tf_op jit(solution)/shard_map/ppermute | solution.py:61
  127.8 14.1 %collective-permute-start.15 = (bf16[160,1024]{1,0:T(8,128)(2,1)}, bf16[160,1024]{1,0:T(8,128)(2,1)S(1)}, u32[]{:S(2)}, u32[]{:S(2)}) collective-permute-start(bf16[160,1024]{1,0:T(8,128)(2,1)} %shard_map.110), channel_id=1, source_target_pairs={{0,24},{1,25},{2,26},{3,27},{4,28},{5,29},{6,30},{7,31},{8,16},{9,... | collective-permute-start | bytes 983048 | tf_op jit(solution)/shard_map/ppermute | solution.py:61
  129.3 12.6 %collective-permute-start.13 = (bf16[160,1024]{1,0:T(8,128)(2,1)}, bf16[160,1024]{1,0:T(8,128)(2,1)}, u32[]{:S(2)}, u32[]{:S(2)}) collective-permute-start(bf16[160,1024]{1,0:T(8,128)(2,1)} %get-tuple-element.84), channel_id=1, source_target_pairs={{0,2},{1,3},{2,4},{3,5},{4,6},{5,7},{6,0},{7,1},{8,10},{9,11},{10,... | collective-permute-start | bytes 983048 | tf_op jit(solution)/shard_map/ppermute | solution.py:61
  129.5 12.5 %collective-permute-start.14 = (bf16[160,1024]{1,0:T(8,128)(2,1)}, bf16[160,1024]{1,0:T(8,128)(2,1)}, u32[]{:S(2)}, u32[]{:S(2)}) collective-permute-start(bf16[160,1024]{1,0:T(8,128)(2,1)} %get-tuple-element.85), channel_id=1, source_target_pairs={{0,6},{1,7},{2,0},{3,1},{4,2},{5,3},{6,4},{7,5},{8,14},{9,15},{10,... | collective-permute-start | bytes 983048 | tf_op jit(solution)/shard_map/ppermute | solution.py:61
  138.5 13.7 %all-to-all-start.2 = ((bf16[8,144,128]{2,1,0:T(8,128)(2,1)}), bf16[8,144,128]{2,1,0:T(8,128)(2,1)S(1)}, u32[]{:S(2)}, u32[]{:S(2)}) async-start(bf16[8,144,128]{2,1,0:T(8,128)(2,1)} %get-tuple-element.71), calls=%async_computation.2 | async-start | bytes 589824 | tf_op jit(solution)/shard_map/all_to_all | solution.py:65
  147.6 6.3 %collective-permute-start.17 = (bf16[144,1152]{1,0:T(8,128)(2,1)}, bf16[144,1152]{1,0:T(8,128)(2,1)}, u32[]{:S(2)}, u32[]{:S(2)}) collective-permute-start(bf16[144,1152]{1,0:T(8,128)(2,1)} %get-tuple-element.89.txt), channel_id=1, source_target_pairs={{0,1},{1,0},{2,3},{3,2},{4,5},{5,4},{6,7},{7,6},{8,9},{9,8},{10,11... | collective-permute-start | bytes 995336 | tf_op jit(solution)/shard_map/ppermute | solution.py:61
  150.3 3.7 %collective-permute-start.16 = (bf16[144,1152]{1,0:T(8,128)(2,1)S(1)}, bf16[144,1152]{1,0:T(8,128)(2,1)}, u32[]{:S(2)}, u32[]{:S(2)}) collective-permute-start(bf16[144,1152]{1,0:T(8,128)(2,1)S(1)} %copy-done.7), channel_id=1, source_target_pairs={{0,1},{1,0},{2,3},{3,2},{4,5},{5,4},{6,7},{7,6},{8,9},{9,8},{10,11... | collective-permute-start | bytes 995336 | tf_op jit(solution)/shard_map/ppermute | solution.py:61
  150.4 7.0 %collective-permute-start.18 = (bf16[4,144,128]{2,1,0:T(8,128)(2,1)}, bf16[4,144,128]{2,1,0:T(8,128)(2,1)}, u32[]{:S(2)}, u32[]{:S(2)}) collective-permute-start(bf16[4,144,128]{2,1,0:T(8,128)(2,1)} %get-tuple-element.90), channel_id=1, source_target_pairs={{0,24},{1,25},{2,26},{3,27},{4,28},{5,29},{6,30},{7,31},{8,16},{9,... | collective-permute-start | bytes 442376 | tf_op jit(solution)/shard_map/ppermute | solution.py:61
  152.2 13.3 %copy-start.14 = (bf16[4,144,128]{2,1,0:T(8,128)(2,1)S(1)}, bf16[4,144,128]{2,1,0:T(8,128)(2,1)}, u32[]{:S(2)}) copy-start(bf16[4,144,128]{2,1,0:T(8,128)(2,1)} %get-tuple-element.92) | copy-start | bytes 442372
  157.3 21.8 %all-to-all-start.3 = ((bf16[64,8,384]{2,1,0:T(8,128)(2,1)}), bf16[64,8,384]{2,1,0:T(8,128)(2,1)S(1)}, u32[]{:S(2)}, u32[]{:S(2)}) async-start(bf16[64,8,384]{2,1,0:T(8,128)(2,1)} %bitcast.49), calls=%async_computation.3 | async-start | bytes 786432 | tf_op jit(solution)/shard_map/all_to_all | solution.py:65
  165.4 11.9 %copy-start.1 = (bf16[1152,1152]{1,0:T(8,128)(2,1)S(1)}, bf16[1152,1152]{1,0:T(8,128)(2,1)}, u32[]{:S(2)}) copy-start(bf16[1152,1152]{1,0:T(8,128)(2,1)} %param.10) | copy-start | bytes 7962628
  166.6 10.6 %collective-permute-start.21 = (bf16[288,128]{1,0:T(8,128)(2,1)S(1)}, bf16[288,128]{1,0:T(8,128)(2,1)S(1)}, u32[]{:S(2)}, u32[]{:S(2)}) collective-permute-start(bf16[288,128]{1,0:T(8,128)(2,1)S(1)} %get-tuple-element.96), channel_id=1, source_target_pairs={{0,2},{1,3},{2,4},{3,5},{4,6},{5,7},{6,0},{7,1},{8,10},{9,11},{10,... | collective-permute-start | bytes 221192 | tf_op jit(solution)/shard_map/ppermute | solution.py:61
  167.7 5.5 %collective-permute-start.19 = (bf16[288,128]{1,0:T(8,128)(2,1)S(1)}, bf16[288,128]{1,0:T(8,128)(2,1)S(1)}, u32[]{:S(2)}, u32[]{:S(2)}) collective-permute-start(bf16[288,128]{1,0:T(8,128)(2,1)S(1)} %get-tuple-element.97), channel_id=1, source_target_pairs={{0,6},{1,7},{2,0},{3,1},{4,2},{5,3},{6,4},{7,5},{8,14},{9,15},{10,... | collective-permute-start | bytes 221192 | tf_op jit(solution)/shard_map/ppermute | solution.py:61
  169.4 7.9 %collective-permute-start.20 = (bf16[288,128]{1,0:T(8,128)(2,1)S(1)}, bf16[288,128]{1,0:T(8,128)(2,1)S(1)}, u32[]{:S(2)}, u32[]{:S(2)}) collective-permute-start(bf16[288,128]{1,0:T(8,128)(2,1)S(1)} %get-tuple-element.98), channel_id=1, source_target_pairs={{0,4},{1,5},{2,6},{3,7},{4,0},{5,1},{6,2},{7,3},{8,12},{9,13},{10,... | collective-permute-start | bytes 221192 | tf_op jit(solution)/shard_map/ppermute | solution.py:61
  (13 other events, 41.8 us)
